TPU v7x, 32 devices: a whole 2x2x4 slice. The times are simulated.
32 devices in a mesh: dp: 4 (over y, x), head: 8 (over z, core).
Axes of the slice: x: 2, y: 2, z: 4, core: 2. Of those that a mesh axis runs over, the one named last changes fastest.
Arguments:
- token_ids: int32 [8192], P('dp'), may hold values from 0 to 31999
- targets: int32 [8192], P('dp'), may hold values from 0 to 31999
- valid: int32 [8192], P('dp'), may hold values from 0 to 1, as said below
- resets: int32 [512], P('dp'), may hold values from 0 to 1, as said below
- owners: int32 [4, 4], replicated, may hold values from 0 to 3, each once within a row
- emb_master: float32 [32000, 2048], P('head', 'dp')
- emb_first: float32 [32000, 2048], P('head', 'dp'), may hold values from -7.6293945e-06 to 7.6293945e-06
- emb_second: float32 [32000, 2048], P('head', 'dp'), may hold values from 1.1180963e-12 to 4.5583927e-12
- qkv_master: float32 [4, 512, 3, 2048], P('dp', None, None, 'head'), may hold values from -0.125 to 0.125
- qkv_left: float32 [4, 8, 512, 512], P('dp', 'head'), as said below
- qkv_right: float32 [4, 8, 768, 768], P('dp', 'head')
- qkv_left_root: float32 [4, 8, 512, 512], P('dp', 'head')
- qkv_right_root: float32 [4, 8, 768, 768], P('dp', 'head')
- out_master: float32 [4, 2048, 512], P('dp', 'head'), may hold values from -0.125 to 0.125
- out_left: float32 [4, 8, 256, 256], P('dp', 'head')
- out_right: float32 [4, 8, 512, 512], P('dp', 'head')
- out_left_root: float32 [4, 8, 256, 256], P('dp', 'head')
- out_right_root: float32 [4, 8, 512, 512], P('dp', 'head')
- gu_master: float32 [4, 512, 2, 5504], P('dp', None, None, 'head'), may hold values from -0.125 to 0.125
- gu_left: float32 [4, 8, 512, 512], P('dp', 'head')
- gu_right: float32 [4, 8, 1376, 1376], P('dp', 'head')
- gu_left_root: float32 [4, 8, 512, 512], P('dp', 'head')
- gu_right_root: float32 [4, 8, 1376, 1376], P('dp', 'head')
- down_master: float32 [4, 5504, 512], P('dp', 'head'), may hold values from -0.078125 to 0.078125
- down_left: float32 [4, 8, 688, 688], P('dp', 'head')
- down_right: float32 [4, 8, 512, 512], P('dp', 'head')
- down_left_root: float32 [4, 8, 688, 688], P('dp', 'head')
- down_right_root: float32 [4, 8, 512, 512], P('dp', 'head')
- inner_init: float32 [32, 64, 64], P('head'), may hold values from -0.375 to 0.375
- inner_first: float32 [32, 64, 64], P('head'), may hold values from -1.5258789e-05 to 1.5258789e-05
- inner_second: float32 [32, 64, 64], P('head'), may hold values from 4.5583927e-12 to 1.8061556e-11
- gains: float32 [4, 2048], P(None, 'head')
- gains_first: float32 [4, 2048], P(None, 'head'), may hold values from -3.8146973e-05 to 3.8146973e-05
- gains_second: float32 [4, 2048], P(None, 'head'), may hold values from 2.8382444e-11 to 1.1180963e-10
Outputs:
- loss_pair: float32 [2], replicated
- grad_norm: float32 [], replicated
- emb_first_new: float32 [32000, 2048], P('head', 'dp')
- emb_second_new: float32 [32000, 2048], P('head', 'dp')
- emb_new: float32 [32000, 2048], P('head', 'dp')
- qkv_grad: float32 [4, 512, 3, 2048], P('dp', None, None, 'head')
- qkv_left_new: float32 [4, 8, 512, 512], P('dp', 'head')
- qkv_right_new: float32 [4, 8, 768, 768], P('dp', 'head')
- qkv_new: float32 [4, 512, 3, 2048], P('dp', None, None, 'head')
- out_grad: float32 [4, 2048, 512], P('dp', 'head')
- out_left_new: float32 [4, 8, 256, 256], P('dp', 'head')
- out_right_new: float32 [4, 8, 512, 512], P('dp', 'head')
- out_new: float32 [4, 2048, 512], P('dp', 'head')
- gu_grad: float32 [4, 512, 2, 5504], P('dp', None, None, 'head')
- gu_left_new: float32 [4, 8, 512, 512], P('dp', 'head')
- gu_right_new: float32 [4, 8, 1376, 1376], P('dp', 'head')
- gu_new: float32 [4, 512, 2, 5504], P('dp', None, None, 'head')
- down_grad: float32 [4, 5504, 512], P('dp', 'head')
- down_left_new: float32 [4, 8, 688, 688], P('dp', 'head')
- down_right_new: float32 [4, 8, 512, 512], P('dp', 'head')
- down_new: float32 [4, 5504, 512], P('dp', 'head')
- inner_first_new: float32 [32, 64, 64], P('head')
- inner_second_new: float32 [32, 64, 64], P('head')
- inner_new: float32 [32, 64, 64], P('head')
- gains_first_new: float32 [4, 2048], P(None, 'head')
- gains_second_new: float32 [4, 2048], P(None, 'head')
- gains_new: float32 [4, 2048], P(None, 'head')
Inputs may be any that keep to these rules, and one draw needn't show every extreme that they name: `valid`: within each sequence the counted positions are a prefix of one or more positions. `resets`: the first mini-batch of every sequence is 1. `owners`: each row is a permutation of the dp indices. `qkv_left`: Symmetric.
All inputs are finite; a program needn't handle non-finite values.
Results may differ from a plain program's by a relative error of at most 0.0085.
The roundings to bfloat16 on the way count: a program that leaves them out, or rounds other values in their place, can miss the bound.
Values may be sent and summed in bfloat16 or wider, within the bound.
A program may use at most 448 MiB of HBM per device.

v0:
```python
import jax
import jax.numpy as jnp
from jax import lax
from jax.sharding import PartitionSpec as P

D = 2048
P_SIZE = 64
MB = 16
STEP = 10


EPSILON = 1e-05
CLIP_LIMIT = 0.05
STAT_DECAY = 0.5
MATRIX_RATE = 0.4
TABLE_RATE = 0.3
INITIAL_RATE = 0.05
GAINS_RATE = 0.3
BETA_ONE = 0.9
BETA_TWO = 0.95
ADAM_EPSILON = 1e-08
WEIGHT_DECAY = 0.01
PRECISE = lax.Precision.HIGHEST


def head_total(values):
    return lax.psum(values, "head")


def spread(rows):
    return lax.all_gather(rows, "head", axis=1, tiled=True)


def spread_grad(rows):
    return lax.all_gather(rows, "head", axis=1, tiled=True)


def fold(partial_value):
    return lax.psum_scatter(partial_value, "head", scatter_dimension=1, tiled=True)


def norm_forward(inputs, gain_row):
    scale = lax.rsqrt(head_total(jnp.sum(inputs * inputs, -1)) / D + EPSILON)
    return ((inputs * scale[:, None] * gain_row).astype(jnp.bfloat16), scale)


def norm_backward(inputs, scale, gain_row, upstream):
    normed = inputs * scale[:, None]
    weighted = upstream * gain_row
    inner = head_total(jnp.sum(weighted * normed, -1)) / D
    return (scale[:, None] * (weighted - normed * inner[:, None]), jnp.sum(upstream * normed, 0))


def mixer(query, key_rows, value_rows, initial, step_rate, markers):
    block_count = query.shape[0] // MB
    head_count = initial.shape[0]
    shaped = [
        piece.reshape(block_count, MB, head_count, P_SIZE)
        for piece in (query, key_rows, value_rows)
    ]
    causal = jnp.tril(jnp.ones((MB, MB), jnp.float32))

    def advance(carried, block):
        query_block, key_block, value_block, marker = block
        carried = jnp.where(marker > 0, initial, carried)
        residue = jnp.einsum("thp,hpc->thc", key_block, carried, precision=PRECISE) - (
            value_block - key_block
        )
        scaled = residue * step_rate
        scores = jnp.einsum("thp,shp->hts", query_block, key_block, precision=PRECISE) * causal
        output = jnp.einsum("thp,hpc->thc", query_block, carried, precision=PRECISE)
        output = output - jnp.einsum("hts,shc->thc", scores, scaled, precision=PRECISE)
        renewed = carried - jnp.einsum("thp,thc->hpc", key_block, scaled, precision=PRECISE)
        return (renewed, output)

    _, outputs = lax.scan(
        advance, jnp.zeros_like(initial), (shaped[0], shaped[1], shaped[2], markers)
    )
    return outputs.reshape(query.shape)


def shampoo(tile_w, tile_g, left, right, left_root, right_root):
    new_left = STAT_DECAY * left + (1.0 - STAT_DECAY) * jnp.einsum(
        "abrc,absc->abrs", tile_g, tile_g, precision=PRECISE
    )
    new_right = STAT_DECAY * right + (1.0 - STAT_DECAY) * jnp.einsum(
        "abrc,abrd->abcd", tile_g, tile_g, precision=PRECISE
    )
    turned = jnp.einsum("abrs,absc->abrc", left_root, tile_g, precision=PRECISE)
    turned = jnp.einsum("abrc,abcd->abrd", turned, right_root, precision=PRECISE)
    return (new_left, new_right, tile_w - MATRIX_RATE * (turned + WEIGHT_DECAY * tile_w))


def refresh(master, grad, left, right, left_root, right_root):
    rows = master.shape[1]
    new_left, new_right, new_w = shampoo(
        master.reshape(1, 1, rows, -1),
        grad.reshape(1, 1, rows, -1),
        left,
        right,
        left_root,
        right_root,
    )
    return (grad, new_left, new_right, new_w.reshape(master.shape))


def adamw(weight, grad, first, second, step_rate):
    new_first = BETA_ONE * first + (1.0 - BETA_ONE) * grad
    new_second = BETA_TWO * second + (1.0 - BETA_TWO) * grad * grad
    moved = (
        new_first
        / (1.0 - BETA_ONE**STEP)
        / (jnp.sqrt(new_second / (1.0 - BETA_TWO**STEP)) + ADAM_EPSILON)
    )
    return (new_first, new_second, weight - step_rate * (moved + WEIGHT_DECAY * weight))


def layer_forward(token_ids, targets, valid, resets, weights, inner_init, gains, head_index):
    w_qkv, w_out, w_gu, w_down, table = weights
    vocab_part = table.shape[0]
    columns = jnp.arange(vocab_part, dtype=jnp.int32)
    local_ids = token_ids - head_index * vocab_part
    inside = (local_ids >= 0) & (local_ids < vocab_part)
    looked = jnp.take(table, jnp.clip(local_ids, 0, vocab_part - 1), axis=0)
    looked_rows = jnp.where(inside[:, None], looked.astype(jnp.float32), 0.0)
    embedded = lax.psum_scatter(
        looked_rows.astype(jnp.bfloat16), "head", scatter_dimension=1, tiled=True
    ).astype(jnp.float32)
    normed_one, scale_one = norm_forward(embedded, gains[0])
    full_one = spread(normed_one)
    mixed = jnp.dot(full_one, w_qkv, preferred_element_type=jnp.float32).astype(jnp.bfloat16)
    tokens = mixed.shape[0]
    heads_here = inner_init.shape[0]
    mixed = mixed.reshape(tokens, 3, heads_here, P_SIZE).astype(jnp.float32)

    def inner(query, key_rows, value_rows, initial, logits_row):
        step_rate = jax.nn.sigmoid(logits_row).reshape(heads_here, P_SIZE) / (8 * P_SIZE)
        return mixer(query, key_rows, value_rows, initial, step_rate, resets)

    inner_out, inner_pull = jax.vjp(
        inner, mixed[:, 0], mixed[:, 1], mixed[:, 2], inner_init, gains[3]
    )
    inner_low = inner_out.reshape(tokens, -1).astype(jnp.bfloat16)
    hidden_one = embedded + fold(jnp.dot(inner_low, w_out, preferred_element_type=jnp.float32))
    normed_two, scale_two = norm_forward(hidden_one, gains[1])
    full_two = spread(normed_two)
    gate_up = jnp.dot(full_two, w_gu, preferred_element_type=jnp.float32)

    def swiglu(paired):
        halves = paired.reshape(tokens, 2, -1)
        return jax.nn.silu(halves[:, 0]) * halves[:, 1]

    activated, act_pull = jax.vjp(swiglu, gate_up)
    act_low = activated.astype(jnp.bfloat16)
    hidden_two = hidden_one + fold(jnp.dot(act_low, w_down, preferred_element_type=jnp.float32))
    normed_end, scale_end = norm_forward(hidden_two, gains[2])
    full_end = spread(normed_end)
    logits = jnp.einsum("td,vd->tv", full_end, table, preferred_element_type=jnp.float32)
    highest = lax.pmax(jnp.max(logits, -1), "head")
    target_hits = columns[None, :] == (targets - head_index * vocab_part)[:, None]
    exp_sum, target_logit = lax.psum(
        (
            jnp.sum(jnp.exp(logits - highest[:, None]), -1),
            jnp.sum(jnp.where(target_hits, logits, 0.0), -1),
        ),
        "head",
    )
    totals = highest + jnp.log(exp_sum)
    counted = valid.astype(jnp.float32)
    kept = (
        embedded,
        scale_one,
        full_one,
        inner_pull,
        inner_low,
        hidden_one,
        scale_two,
        full_two,
        act_pull,
        act_low,
        hidden_two,
        scale_end,
        full_end,
        logits,
        totals,
        target_hits,
        counted,
        local_ids,
    )
    return (jnp.sum((totals - target_logit) * counted), jnp.sum(counted), kept)


def layer_backward(kept, weights, gains):
    (
        embedded,
        scale_one,
        full_one,
        inner_pull,
        inner_low,
        hidden_one,
        scale_two,
        full_two,
        act_pull,
        act_low,
        hidden_two,
        scale_end,
        full_end,
        logits,
        totals,
        target_hits,
        counted,
        local_ids,
    ) = kept
    w_qkv, w_out, w_gu, w_down, table = weights
    tokens = logits.shape[0]
    d_logits = (
        (jnp.exp(logits - totals[:, None]) - target_hits.astype(jnp.float32)) * counted[:, None]
    ).astype(jnp.bfloat16)
    grad_table = jnp.einsum("tv,td->vd", d_logits, full_end, preferred_element_type=jnp.float32)
    d_end = fold(jnp.dot(d_logits, table, preferred_element_type=jnp.float32))
    d_two, gain_end = norm_backward(hidden_two, scale_end, gains[2], d_end)
    d_down_in = spread_grad(d_two.astype(jnp.bfloat16))
    grad_down = jnp.einsum("tf,td->fd", act_low, d_down_in, preferred_element_type=jnp.float32)
    d_act = jnp.einsum("td,fd->tf", d_down_in, w_down, preferred_element_type=jnp.float32)
    d_gate_up = act_pull(d_act)[0].astype(jnp.bfloat16)
    grad_gu = jnp.einsum("td,tc->dc", full_two, d_gate_up, preferred_element_type=jnp.float32)
    d_two_norm = fold(jnp.einsum("tc,dc->td", d_gate_up, w_gu, preferred_element_type=jnp.float32))
    d_middle, gain_two = norm_backward(hidden_one, scale_two, gains[1], d_two_norm)
    d_one = d_two + d_middle
    d_out_in = spread_grad(d_one.astype(jnp.bfloat16))
    grad_out = jnp.einsum("tc,td->cd", inner_low, d_out_in, preferred_element_type=jnp.float32)
    d_inner = jnp.einsum("td,cd->tc", d_out_in, w_out, preferred_element_type=jnp.float32)
    d_query, d_key, d_value, grad_init, grad_rate = inner_pull(d_inner.reshape(tokens, -1, P_SIZE))
    d_mixed = jnp.stack([d_query, d_key, d_value], 1).reshape(tokens, -1).astype(jnp.bfloat16)
    grad_qkv = jnp.einsum("td,tc->dc", full_one, d_mixed, preferred_element_type=jnp.float32)
    d_one_norm = fold(jnp.einsum("tc,dc->td", d_mixed, w_qkv, preferred_element_type=jnp.float32))
    d_base, gain_one = norm_backward(embedded, scale_one, gains[0], d_one_norm)
    d_embed = spread_grad((d_one + d_base).astype(jnp.bfloat16))
    columns = jnp.arange(table.shape[0], dtype=jnp.int32)
    id_onehot = (columns[None, :] == local_ids[:, None]).astype(jnp.bfloat16)
    grad_table = grad_table + jnp.einsum(
        "tv,td->vd", id_onehot, d_embed, preferred_element_type=jnp.float32
    )
    grad_gains = jnp.stack([gain_one, gain_two, gain_end, grad_rate], 0)
    return (grad_qkv, grad_out, grad_gu, grad_down, grad_table, grad_init, grad_gains)


def shards(
    token_ids,
    targets,
    valid,
    resets,
    owners,
    emb_master,
    emb_first,
    emb_second,
    qkv_master,
    qkv_left,
    qkv_right,
    qkv_left_root,
    qkv_right_root,
    out_master,
    out_left,
    out_right,
    out_left_root,
    out_right_root,
    gu_master,
    gu_left,
    gu_right,
    gu_left_root,
    gu_right_root,
    down_master,
    down_left,
    down_right,
    down_left_root,
    down_right_root,
    inner_init,
    inner_first,
    inner_second,
    gains,
    gains_first,
    gains_second,
):
    gathered = (
        lax.all_gather(qkv_master.astype(jnp.bfloat16), "dp", axis=0, tiled=True),
        lax.all_gather(out_master.astype(jnp.bfloat16), "dp", axis=0, tiled=True),
        lax.all_gather(gu_master.astype(jnp.bfloat16), "dp", axis=0, tiled=True),
        lax.all_gather(down_master.astype(jnp.bfloat16), "dp", axis=0, tiled=True),
        lax.all_gather(emb_master.astype(jnp.bfloat16), "dp", axis=1, tiled=True),
    )
    w_qkv = jnp.take(gathered[0], owners[0], axis=0).reshape(D, -1)
    w_out = jnp.take(gathered[1], owners[1], axis=0)
    w_out = jnp.swapaxes(w_out, 0, 1).reshape(w_out.shape[1], D)
    w_gu = jnp.take(gathered[2], owners[2], axis=0).reshape(D, -1)
    w_down = jnp.take(gathered[3], owners[3], axis=0)
    w_down = jnp.swapaxes(w_down, 0, 1).reshape(w_down.shape[1], D)
    weights = (w_qkv, w_out, w_gu, w_down, gathered[4])
    head_index = lax.axis_index("head")
    loss_local, count_local, kept = layer_forward(
        token_ids, targets, valid, resets, weights, inner_init, gains, head_index
    )
    loss_sum, count = lax.psum((loss_local, count_local), "dp")
    grad_qkv, grad_out, grad_gu, grad_down, grad_table, grad_init, grad_gains = layer_backward(
        kept, weights, gains
    )
    parts = lax.axis_size("dp")
    order = jnp.argsort(owners, axis=1)
    slot_qkv = jnp.take(grad_qkv.reshape(parts, -1, 3, grad_qkv.shape[1] // 3), order[0], axis=0)
    slot_out = jnp.take(
        jnp.swapaxes(grad_out.reshape(grad_out.shape[0], parts, -1), 0, 1), order[1], axis=0
    )
    slot_gu = jnp.take(grad_gu.reshape(parts, -1, 2, grad_gu.shape[1] // 2), order[2], axis=0)
    slot_down = jnp.take(
        jnp.swapaxes(grad_down.reshape(grad_down.shape[0], parts, -1), 0, 1), order[3], axis=0
    )
    bundle = (slot_qkv, slot_out, slot_gu, slot_down, grad_table)
    summed = lax.psum((bundle[0], bundle[1], bundle[2], bundle[3], bundle[4]), "dp")
    place = lax.axis_index("dp")
    width_part = emb_master.shape[1]
    owned = tuple((lax.dynamic_slice_in_dim(piece, place, 1, 0) for piece in summed[:4]))
    owned = owned + (lax.dynamic_slice_in_dim(summed[4], place * width_part, width_part, 1),)
    small = lax.psum((grad_init, grad_gains), "dp")
    first_dp = (lax.axis_index("dp") == 0).astype(jnp.float32)
    squares = sum((jnp.sum(piece * piece) for piece in owned))
    squares = squares + first_dp * (jnp.sum(small[0] * small[0]) + jnp.sum(small[1] * small[1]))
    squares_all = lax.psum(squares, ("dp", "head"))
    grad_norm = jnp.sqrt(squares_all) / count
    factor = jnp.minimum(1.0, CLIP_LIMIT / grad_norm) / count
    qkv_out = refresh(
        qkv_master, owned[0] * factor, qkv_left, qkv_right, qkv_left_root, qkv_right_root
    )
    out_out = refresh(
        out_master, owned[1] * factor, out_left, out_right, out_left_root, out_right_root
    )
    gu_out = refresh(gu_master, owned[2] * factor, gu_left, gu_right, gu_left_root, gu_right_root)
    down_out = refresh(
        down_master, owned[3] * factor, down_left, down_right, down_left_root, down_right_root
    )
    table_out = adamw(emb_master, owned[4] * factor, emb_first, emb_second, TABLE_RATE)
    init_out = adamw(inner_init, small[0] * factor, inner_first, inner_second, INITIAL_RATE)
    gain_out = adamw(gains, small[1] * factor, gains_first, gains_second, GAINS_RATE)
    return (
        (jnp.stack([loss_sum, count]), grad_norm)
        + table_out
        + qkv_out
        + out_out
        + gu_out
        + down_out
        + init_out
        + gain_out
    )


def solution(mesh):
    placed = (
        P("dp"),
        P("dp"),
        P("dp"),
        P("dp"),
        P(),
        P("head", "dp"),
        P("head", "dp"),
        P("head", "dp"),
        P("dp", None, None, "head"),
        P("dp", "head", None, None),
        P("dp", "head", None, None),
        P("dp", "head", None, None),
        P("dp", "head", None, None),
        P("dp", "head", None),
        P("dp", "head", None, None),
        P("dp", "head", None, None),
        P("dp", "head", None, None),
        P("dp", "head", None, None),
        P("dp", None, None, "head"),
        P("dp", "head", None, None),
        P("dp", "head", None, None),
        P("dp", "head", None, None),
        P("dp", "head", None, None),
        P("dp", "head", None),
        P("dp", "head", None, None),
        P("dp", "head", None, None),
        P("dp", "head", None, None),
        P("dp", "head", None, None),
        P("head", None, None),
        P("head", None, None),
        P("head", None, None),
        P(None, "head"),
        P(None, "head"),
        P(None, "head"),
    )
    return jax.shard_map(
        shards,
        mesh=mesh,
        in_specs=placed,
        out_specs=(
            P(),
            P(),
            P("head", "dp"),
            P("head", "dp"),
            P("head", "dp"),
            P("dp", None, None, "head"),
            P("dp", "head", None, None),
            P("dp", "head", None, None),
            P("dp", None, None, "head"),
            P("dp", "head", None),
            P("dp", "head", None, None),
            P("dp", "head", None, None),
            P("dp", "head", None),
            P("dp", None, None, "head"),
            P("dp", "head", None, None),
            P("dp", "head", None, None),
            P("dp", None, None, "head"),
            P("dp", "head", None),
            P("dp", "head", None, None),
            P("dp", "head", None, None),
            P("dp", "head", None),
            P("head", None, None),
            P("head", None, None),
            P("head", None, None),
            P(None, "head"),
            P(None, "head"),
            P(None, "head"),
        ),
        check_vma=False,
    )
```

profile of v0, /device:TPU:0, one launch (start us, length us, event | category | flops | bytes accessed | tf_op | source)
XLA Modules:
  0.0 6519.2 jit_solution(148382683950140973)
XLA Ops:
  14.0 156.2 %all-gather.12.cloned.1.call-done = bf16[4000,2048]{1,0:T(8,128)(2,1)} async-done(((bf16[4000,512]{1,0:T(8,128)(2,1)}), bf16[4000,2048]{1,0:T(8,128)(2,1)}) %all-gather.12.cloned.1.call-update) | async-done | bytes 16384016 | tf_op jit(solution)/shard_map/all_gather | solution.py:289
  170.1 24.1 gather_fusion
  194.3 8.4 select_convert_fusion
  207.5 84.9 %reduce-scatter.7.cloned.1.call-done = bf16[2048,256]{1,0:T(8,128)(2,1)} async-done(((bf16[2048,2048]{1,0:T(8,128)(2,1)}), bf16[2048,256]{1,0:T(8,128)(2,1)}) %reduce-scatter.7.cloned.1.call-update) | async-done | bytes 1048592 | tf_op jit(solution)/shard_map/reduce_scatter | solution.py:126
  294.0 13.9 psum.126
  325.4 40.7 all-gather.16.cloned.1.call-done
  381.8 68.9 %all-gather.14.cloned.1.call-done = bf16[2048,2048]{1,0:T(8,128)(2,1)} async-done(((bf16[2048,256]{1,0:T(8,128)(2,1)}), bf16[2048,2048]{1,0:T(8,128)(2,1)}) %all-gather.14.cloned.1.call-update) | async-done | bytes 8388624 | tf_op jit(solution)/shard_map/all_gather | solution.py:31
  450.7 10.1 convolution_convert_fusion
  485.0 1131.9 %while.48 = (s32[]{:T(128)}, f32[4,64,64]{2,1,0:T(8,128)S(1)}, bf16[128,16,4,64]{3,1,2,0:T(8,128)(2,1)}, pred[128]{0:T(512)(128)(4,1)S(1)}, f32[128,4,64,64]{3,2...) while((s32[]{:T(128)}, f32[4,64,64]{2,1,0:T(8,128)S(1)}, ...), condition=%wide.region_4.5_spmd.clone, body=%wide.region_3.4_spmd.clone.sunk | while | flops 11085316 | bytes 1050798 | solution.py:76
  1625.5 9.7 fusion.222
  1641.0 160.8 %reduce-scatter.9.cloned.1.call-done = f32[2048,256]{1,0:T(8,128)} async-done(((f32[2048,2048]{1,0:T(8,128)}), f32[2048,256]{1,0:T(8,128)}) %reduce-scatter.9.cloned.1.call-update) | async-done | bytes 2097168 | tf_op jit(solution)/shard_map/reduce_scatter | solution.py:39
  1805.0 13.9 psum.127
  1822.6 21.3 all-gather.24.cloned.1.call-done
  1852.1 59.0 all-gather.22.cloned.1.call-done
  1917.0 7.0 copy.183
  1929.4 66.4 %all-gather.20.cloned.1.call-done = bf16[2048,2048]{1,0:T(8,128)(2,1)} async-done(((bf16[2048,256]{1,0:T(8,128)(2,1)}), bf16[2048,2048]{1,0:T(8,128)(2,1)}) %all-gather.20.cloned.1.call-update) | async-done | bytes 8388624 | tf_op jit(solution)/shard_map/all_gather | solution.py:31
  1995.8 16.1 fusion.89
  2018.2 10.3 fusion.123
  2028.6 166.5 %reduce-scatter.11.cloned.1.call-done = f32[2048,256]{1,0:T(8,128)} async-done(((f32[2048,2048]{1,0:T(8,128)}), f32[2048,256]{1,0:T(8,128)}) %reduce-scatter.11.cloned.1.call-update) | async-done | bytes 2097168 | tf_op jit(solution)/shard_map/reduce_scatter | solution.py:39
  2198.9 13.9 psum.128
  2215.8 80.8 %all-gather.26.cloned.1.call-done = bf16[2048,2048]{1,0:T(8,128)(2,1)} async-done(((bf16[2048,256]{1,0:T(8,128)(2,1)}), bf16[2048,2048]{1,0:T(8,128)(2,1)}) %all-gather.26.cloned.1.call-update) | async-done | bytes 8388624 | tf_op jit(solution)/shard_map/all_gather | solution.py:31
  2296.6 42.1 fusion.221
  2338.7 14.9 pmax.7
  2353.6 15.4 select_reduce_fusion
  2369.0 13.9 psum.129
  2383.6 47.0 fusion.214
  2430.6 165.8 %reduce-scatter.13.cloned.1.call-done = f32[2048,256]{1,0:T(8,128)} async-done(((f32[2048,2048]{1,0:T(8,128)}), f32[2048,256]{1,0:T(8,128)}) %reduce-scatter.13.cloned.1.call-update) | async-done | bytes 2097168 | tf_op jit(solution)/shard_map/reduce_scatter | solution.py:39
  2600.0 13.9 psum.133
  2621.0 6.8 copy.186
  2627.8 7.6 copy.258
  2635.4 62.7 all-gather.28.cloned.1.call-done
  2698.2 15.9 fusion.103
  2721.7 17.8 fusion.223
  2739.5 166.6 %reduce-scatter.15.cloned.1.call-done = f32[2048,256]{1,0:T(8,128)} async-done(((f32[2048,2048]{1,0:T(8,128)}), f32[2048,256]{1,0:T(8,128)}) %reduce-scatter.15.cloned.1.call-update) | async-done | bytes 2097168 | tf_op jit(solution)/shard_map/reduce_scatter | solution.py:39
  2909.6 13.9 psum.134
  2947.7 62.0 all-gather.30.cloned.1.call-done
  3009.7 8.2 fusion.224
  3022.7 1786.1 %while.49 = (s32[]{:T(128)}, f32[4,64,64]{2,1,0:T(8,128)S(1)}, f32[4,64]{1,0:T(4,128)S(1)}, f32[4,64,64]{2,1,0:T(8,128)S(1)}, bf16[128,16,4,64]{3,1,0,2:T(8,128)...) while((s32[]{:T(128)}, f32[4,64,64]{2,1,0:T(8,128)S(1)}, ...), condition=%wide.region_30.31_spmd.clone, body=%wide.region_28.30_spmd.clone.sunk | while | flops 22275844 | bytes 1619680 | solution.py:76
  4820.9 10.3 fusion.226
  4831.3 166.6 %reduce-scatter.17.cloned.1.call-done = f32[2048,256]{1,0:T(8,128)} async-done(((f32[2048,2048]{1,0:T(8,128)}), f32[2048,256]{1,0:T(8,128)}) %reduce-scatter.17.cloned.1.call-update) | async-done | bytes 2097168 | tf_op jit(solution)/shard_map/reduce_scatter | solution.py:39
  5000.9 25.9 all-reduce.2
  5030.8 12.2 copy.214
  5043.0 11.9 copy.217
  5054.9 12.3 copy.218
  5067.2 10.9 fusion.125
  5084.2 18.5 fusion.97
  5102.7 9.6 gather_fusion.7
  5118.2 10.4 broadcast_select_fusion.1
  5128.6 12.6 copy.216
  5141.1 7.1 convolution_bitcast_fusion.3
  5151.8 11.7 fusion.225
  5163.6 6.4 gather_fusion.5
  5179.6 76.8 %fusion.85 = f32[4000,2048]{1,0:T(8,128)} fusion(bf16[2048,2048]{1,0:T(8,128)(2,1)} %all-gather.32.cloned.1.call-done, s32[2048]{0:T(1024)S(1)} %copy-done.44), kind=kOutput, calls=%fused_computation.121 | convolution fusion | flops 33562624000 | bytes 41164800 | tf_op jit(solution)/shard_map/tv,td->vd/dot_general | solution.py:241
  5256.4 46.1 convolution_add_fusion.4
  5313.7 11.3 all-reduce.3
  5327.5 963.9 %all-reduce.7.cloned.1.call-done = (f32[4,512,3,256]{3,1,2,0:T(8,128)}, f32[4,256,512]{2,1,0:T(8,128)}, f32[4,512,2,688]{1,3,2,0:T(8,128)}, f32[4,688,512]{2,1,0...) async-done(((f32[4,512,3,256]{3,1,2,0:T(8,128)}, f32[4,256,512]{2,1,0:T(8,128)}, f32[4,512,2,688]{1,3,2,0:T(8,128)}, f32[4,688,512]{2,1,0:T(8,128)}, ...) | async-done | bytes 58130448 | tf_op jit(solution)/shard_map/psum | solution.py:317
  6313.7 42.2 psum.143
  6368.3 6.8 fusion.131
  6375.1 6.3 fusion.133
  6391.6 16.8 fusion.88
  6408.4 6.3 fusion.168
  6438.5 8.1 fusion.130
  6457.4 21.8 multiply_subtract_fusion
  6479.2 31.6 fusion.110
  (3306 shorter events, 3212.5 us)
Async XLA Ops:
  7.2 6419.4 %copy-start = (f32[1,1,768,768]{3,2,1,0:T(8,128)S(1)}, f32[1,1,768,768]{3,2,1,0:T(8,128)}, u32[]{:S(2)}) copy-start(f32[1,1,768,768]{3,2,1,0:T(8,128)} %param.50) | copy-start | bytes 7077892
  7.2 162.9 %all-gather.12.cloned.1.call-start = ((), (), s32[]{:S(2)}) async-start(), calls=%async_computation.6 | async-start | bytes 20480000 | tf_op jit(solution)/shard_map/all_gather | solution.py:289
  13.3 279.2 %reduce-scatter.7.cloned.1.call-start = ((), (), s32[]{:S(2)}) async-start(), calls=%async_computation.7 | async-start | bytes 9437184 | tf_op jit(solution)/shard_map/reduce_scatter | solution.py:126
  202.7 108.8 %copy-start.54 = (s32[4,4]{1,0:T(4,128)S(1)}, s32[4,4]{1,0:T(4,128)}, u32[]{:S(2)}) copy-start(s32[4,4]{1,0:T(4,128)} %param.42) | copy-start | bytes 196
  202.7 117.2 %all-gather.18.cloned.1.call-start = ((), (), s32[]{:S(2)}) async-start(), calls=%async_computation.10 | async-start | bytes 1310720 | tf_op jit(solution)/shard_map/all_gather | solution.py:286
  204.5 161.7 %all-gather.16.cloned.1.call-start = ((), (), s32[]{:S(2)}) async-start(), calls=%async_computation.9 | async-start | bytes 3932160 | tf_op jit(solution)/shard_map/all_gather | solution.py:285
  206.9 243.8 %all-gather.14.cloned.1.call-start = ((), (), s32[]{:S(2)}) async-start(), calls=%async_computation.8 | async-start | bytes 9437184 | tf_op jit(solution)/shard_map/all_gather | solution.py:31
  207.5 115.2 %copy-start.57 = (f32[1,256]{1,0:T(1,128)}, f32[1,256]{1,0:T(1,128)S(1)}, u32[]{:S(2)}) copy-start(f32[1,256]{1,0:T(1,128)S(1)} %get-tuple-element.952) | copy-start | bytes 3076
  207.5 1611.4 %copy-start.59 = (f32[1,256]{1,0:T(1,128)}, f32[1,256]{1,0:T(1,128)S(1)}, u32[]{:S(2)}) copy-start(f32[1,256]{1,0:T(1,128)S(1)} %get-tuple-element.949) | copy-start | bytes 3076
  311.1 1490.7 %reduce-scatter.9.cloned.1.call-start = ((), (), s32[]{:S(2)}) async-start(), calls=%async_computation.11 | async-start | bytes 18874368 | tf_op jit(solution)/shard_map/reduce_scatter | solution.py:39
  312.1 10.6 copy-start.68
  324.1 46.5 copy-start.7
  376.9 73.9 %copy-start.84 = (pred[1,4,4,128]{3,1,2,0:T(4,128)(4,1)S(1)}, pred[1,4,4,128]{3,1,2,0:T(4,128)(4,1)}, u32[]{:S(2)}) copy-start(pred[1,4,4,128]{3,1,2,0:T(4,128)(4,1)} %copy.254) | copy-start | bytes 6148
  1617.0 18.2 copy-start.24
  1635.3 166.6 %copy-start.2 = (bf16[2048,256]{1,0:T(8,128)(2,1)S(1)}, bf16[2048,256]{1,0:T(8,128)(2,1)}, u32[]{:S(2)}) copy-start(bf16[2048,256]{1,0:T(8,128)(2,1)} %reduce-scatter.7.cloned.1.call-done) | copy-start | bytes 3145732
  1635.3 208.6 %all-gather.24.cloned.1.call-start = ((), (), s32[]{:S(2)}) async-start(), calls=%async_computation.14 | async-start | bytes 3522560 | tf_op jit(solution)/shard_map/all_gather | solution.py:288
  1637.7 273.3 %all-gather.22.cloned.1.call-start = ((), (), s32[]{:S(2)}) async-start(), calls=%async_computation.13 | async-start | bytes 7045120 | tf_op jit(solution)/shard_map/all_gather | solution.py:287
  1640.9 181.6 %copy-start.83 = (s32[4]{0:T(128)S(1)}, s32[4]{0:T(128)}, u32[]{:S(2)}) copy-start(s32[4]{0:T(128)} %get-tuple-element.957) | copy-start | bytes 52
  1640.9 181.6 %copy-start.82 = (s32[4]{0:T(128)S(1)}, s32[4]{0:T(128)}, u32[]{:S(2)}) copy-start(s32[4]{0:T(128)} %get-tuple-element.960) | copy-start | bytes 52
  1640.9 354.8 %all-gather.20.cloned.1.call-start = ((), (), s32[]{:S(2)}) async-start(), calls=%async_computation.12 | async-start | bytes 9437184 | tf_op jit(solution)/shard_map/all_gather | solution.py:31
  1819.5 28.4 copy-start.80
  1822.5 372.6 %reduce-scatter.11.cloned.1.call-start = ((), (), s32[]{:S(2)}) async-start(), calls=%async_computation.15 | async-start | bytes 18874368 | tf_op jit(solution)/shard_map/reduce_scatter | solution.py:39
  2028.5 187.2 %copy-start.52 = (s32[2048]{0:T(1024)S(1)}, s32[2048]{0:T(1024)}, u32[]{:S(2)}) copy-start(s32[2048]{0:T(1024)} %param.40) | copy-start | bytes 24580
  2028.5 187.3 %copy-start.63 = (s32[2048]{0:T(1024)S(1)}, s32[2048]{0:T(1024)}, u32[]{:S(2)}) copy-start(s32[2048]{0:T(1024)} %param.39) | copy-start | bytes 24580
  2028.6 268.1 %all-gather.26.cloned.1.call-start = ((), (), s32[]{:S(2)}) async-start(), calls=%async_computation.16 | async-start | bytes 9437184 | tf_op jit(solution)/shard_map/all_gather | solution.py:31
  2215.7 380.7 %reduce-scatter.13.cloned.1.call-start = ((), (), s32[]{:S(2)}) async-start(), calls=%async_computation.17 | async-start | bytes 18874368 | tf_op jit(solution)/shard_map/reduce_scatter | solution.py:39
  2215.8 167.1 %copy-start.64 = (f32[2048]{0:T(1024)}, f32[2048]{0:T(1024)S(1)}, u32[]{:S(2)}) copy-start(f32[2048]{0:T(1024)S(1)} %convert_element_type.114) | copy-start | bytes 24580
  2215.8 167.1 %copy-start.47 = (s32[2048]{0:T(1024)}, s32[2048]{0:T(1024)S(1)}, u32[]{:S(2)}) copy-start(s32[2048]{0:T(1024)S(1)} %broadcast_subtract_fusion) | copy-start | bytes 24580
  2430.6 267.6 %all-gather.28.cloned.1.call-start = ((), (), s32[]{:S(2)}) async-start(), calls=%async_computation.18 | async-start | bytes 9437184 | tf_op jit(solution)/shard_map/all_gather | solution.py:35
  2600.0 17.8 copy-start.69
  2617.3 288.8 %reduce-scatter.15.cloned.1.call-start = ((), (), s32[]{:S(2)}) async-start(), calls=%async_computation.19 | async-start | bytes 18874368 | tf_op jit(solution)/shard_map/reduce_scatter | solution.py:39
  2739.5 166.6 %copy-start.40 = (f32[2048]{0:T(1024)S(1)}, f32[2048]{0:T(1024)}, u32[]{:S(2)}) copy-start(f32[2048]{0:T(1024)} %copy-done.39) | copy-start | bytes 24580
  2739.5 166.6 %copy-start.60 = (f32[1,256]{1,0:T(1,128)S(1)}, f32[1,256]{1,0:T(1,128)}, u32[]{:S(2)}) copy-start(f32[1,256]{1,0:T(1,128)} %copy-done.59) | copy-start | bytes 3076
  2739.5 270.2 %all-gather.30.cloned.1.call-start = ((), (), s32[]{:S(2)}) async-start(), calls=%async_computation.20 | async-start | bytes 9437184 | tf_op jit(solution)/shard_map/all_gather | solution.py:35
  2928.8 2069.0 %reduce-scatter.17.cloned.1.call-start = ((), (), s32[]{:S(2)}) async-start(), calls=%async_computation.21 | async-start | bytes 18874368 | tf_op jit(solution)/shard_map/reduce_scatter | solution.py:39
  4831.2 166.6 %copy-start.3 = (bf16[2048,256]{1,0:T(8,128)(2,1)S(1)}, bf16[2048,256]{1,0:T(8,128)(2,1)}, u32[]{:S(2)}) copy-start(bf16[2048,256]{1,0:T(8,128)(2,1)} %reduce-scatter.7.cloned.1.call-done) | copy-start | bytes 3145732
  4831.2 166.6 %copy-start.38 = (f32[2048]{0:T(1024)S(1)}, f32[2048]{0:T(1024)}, u32[]{:S(2)}) copy-start(f32[2048]{0:T(1024)} %copy-done.37) | copy-start | bytes 24580
  4831.2 166.6 %copy-start.58 = (f32[1,256]{1,0:T(1,128)S(1)}, f32[1,256]{1,0:T(1,128)}, u32[]{:S(2)}) copy-start(f32[1,256]{1,0:T(1,128)} %copy-done.57) | copy-start | bytes 3076
  4831.2 169.7 %copy-start.49 = (f32[2048]{0:T(1024)S(1)}, f32[2048]{0:T(1024)}, u32[]{:S(2)}) copy-start(f32[2048]{0:T(1024)} %get-tuple-element.828) | copy-start | bytes 24580
  4831.3 348.3 %all-gather.32.cloned.1.call-start = ((), (), s32[]{:S(2)}) async-start(), calls=%async_computation.22 | async-start | bytes 9437184 | tf_op jit(solution)/shard_map/all_gather | solution.py:35
  5000.9 29.8 copy-start.85
  5000.9 29.8 copy-start.72
  5000.9 29.8 copy-start.73
  5000.9 29.8 copy-start.81
  5000.9 29.9 copy-start.71
  5030.2 1261.1 %all-reduce.7.cloned.1.call-start = ((), (), s32[]{:S(2)}) async-start(), calls=%async_computation.23 | async-start | bytes 116391936 | tf_op jit(solution)/shard_map/psum | solution.py:317
  5128.6 12.6 copy-start.19
  5179.5 76.9 %copy-start.48 = (s32[2048]{0:T(1024)S(1)}, s32[2048]{0:T(1024)}, u32[]{:S(2)}) copy-start(s32[2048]{0:T(1024)} %copy-done.47) | copy-start | bytes 24580
  5179.5 76.9 %copy-start.51 = (f32[2048]{0:T(1024)S(1)}, f32[2048]{0:T(1024)}, u32[]{:S(2)}) copy-start(f32[2048]{0:T(1024)} %copy-done.50) | copy-start | bytes 24580
  5179.5 76.9 %copy-start.65 = (f32[2048]{0:T(1024)S(1)}, f32[2048]{0:T(1024)}, u32[]{:S(2)}) copy-start(f32[2048]{0:T(1024)} %copy-done.64) | copy-start | bytes 24580
  6364.7 53.0 copy-start.9
  6368.3 13.2 copy-start.31
  6368.3 23.2 slice-start
  6375.1 10.3 copy-start.1
  6375.1 10.3 copy-start.28
  6375.1 16.5 slice-start.1
  6391.6 16.8 copy-start.86
  6438.5 12.0 copy-start.56
  6438.5 12.0 copy-start.75
  6438.5 12.0 copy-start.76
  6438.5 12.6 copy-start.17
  6438.5 12.6 copy-start.34
  6438.5 12.5 copy-start.41
  6438.5 12.5 copy-start.42
  (47 other events, 248.9 us)
Sparse Core Ops, SparseCore 0:
  13.4 156.7 all-gather.11
  202.8 89.5 reduce-scatter.6
  294.9 24.9 all-gather.17
  322.2 43.9 all-gather.15
  368.2 82.4 all-gather.13
  1635.4 166.4 reduce-scatter.8
  1804.2 39.6 all-gather.23
  1846.3 64.6 all-gather.21
  1913.2 82.4 all-gather.19
  2028.7 166.4 reduce-scatter.10
  2215.8 80.7 all-gather.25
  2430.7 165.7 reduce-scatter.12
  2617.4 80.7 all-gather.27
  2739.6 166.4 reduce-scatter.14
  2929.0 80.7 all-gather.29
  4831.4 166.4 reduce-scatter.16
  5030.3 80.6 all-gather.31
  5302.6 988.6 all-reduce.6
where the time goes:
time: 6640 us; the launch traced here: 6520 us
  matrix products  2880 us (43%)
  waiting for transfers between devices  2500 us (38%)
  other arithmetic  511 us (8%)
  local copies, waits for them, and re-layouts  418 us (6%)
  blocking collectives  178 us (3%)
    psum x1, waiting for transfers between devices, shards(): lax.psum((bundle[0], bundle[1], bundle[2], bundle[3], bundle[4]), 'dp')  964 us
    reduce_scatter x5, waiting for transfers between devices, fold(): lax.psum_scatter(partial_value, 'head', scatter_dimension=1, tiled=True)  826 us
    dot_general x384, matrix products, advance(): jnp.einsum('thp,hpc->thc', key_block, carried, precision=PRECISE)  684 us
    dot_general x384, matrix products, advance(): jnp.einsum('thp,shp->hts', query_block, key_block, precision=PRECISE)  526 us
    dot_general x384, matrix products, advance(): output = jnp.einsum('thp,hpc->thc', query_block, carried, precision=PRECISE)  433 us
    dot_general x384, matrix products, advance(): jnp.einsum('thp,thc->hpc', key_block, scaled, precision=PRECISE)  412 us
    dot_general x384, matrix products, advance(): jnp.einsum('hts,shc->thc', scores, scaled, precision=PRECISE)  355 us
    dynamic_update_slice x256, other arithmetic, mixer(): lax.scan(advance, jnp.zeros_like(initial), (shaped[0], shaped[1], shaped[...  247 us
  transfers between devices with their start and end apart: 18, of which 17 were waited for; matrix products, arithmetic and copies ran while one was open for 4% of the time, Pallas kernels for 0%

commit v1 on v0

--- a/solution.py
+++ b/solution.py
@@ -1,6 +1,8 @@
 import jax
 import jax.numpy as jnp
 from jax import lax
+from jax.experimental import pallas as pl
+from jax.experimental.pallas import tpu as pltpu
 from jax.sharding import PartitionSpec as P
 
 D = 2048
@@ -20,7 +22,6 @@
 BETA_TWO = 0.95
 ADAM_EPSILON = 1e-08
 WEIGHT_DECAY = 0.01
-PRECISE = lax.Precision.HIGHEST
 
 
 def head_total(values):
@@ -36,7 +37,8 @@
 
 
 def fold(partial_value):
-    return lax.psum_scatter(partial_value, "head", scatter_dimension=1, tiled=True)
+    low = partial_value.astype(jnp.bfloat16)
+    return lax.psum_scatter(low, "head", scatter_dimension=1, tiled=True).astype(jnp.float32)
 
 
 def norm_forward(inputs, gain_row):
@@ -51,43 +53,402 @@
     return (scale[:, None] * (weighted - normed * inner[:, None]), jnp.sum(upstream * normed, 0))
 
 
-def mixer(query, key_rows, value_rows, initial, step_rate, markers):
-    block_count = query.shape[0] // MB
-    head_count = initial.shape[0]
-    shaped = [
-        piece.reshape(block_count, MB, head_count, P_SIZE)
-        for piece in (query, key_rows, value_rows)
-    ]
-    causal = jnp.tril(jnp.ones((MB, MB), jnp.float32))
-
-    def advance(carried, block):
-        query_block, key_block, value_block, marker = block
-        carried = jnp.where(marker > 0, initial, carried)
-        residue = jnp.einsum("thp,hpc->thc", key_block, carried, precision=PRECISE) - (
-            value_block - key_block
+CHUNK = 64
+PAIR = 2 * P_SIZE
+
+
+def dot_ab(left, right):
+    return lax.dot_general(left, right, (((1,), (0,)), ((), ())), preferred_element_type=jnp.float32)
+
+
+def dot_abt(left, right):
+    return lax.dot_general(left, right, (((1,), (1,)), ((), ())), preferred_element_type=jnp.float32)
+
+
+def dot_atb(left, right):
+    return lax.dot_general(left, right, (((0,), (0,)), ((), ())), preferred_element_type=jnp.float32)
+
+
+def halves_of(value):
+    high = value.astype(jnp.bfloat16)
+    return (high, (value - high.astype(jnp.float32)).astype(jnp.bfloat16))
+
+
+def wide(form, left, right):
+    lefts = left if isinstance(left, tuple) else (left,)
+    rights = right if isinstance(right, tuple) else (right,)
+    total = form(lefts[0], rights[0])
+    if len(rights) > 1:
+        total = total + form(lefts[0], rights[1])
+    if len(lefts) > 1:
+        total = total + form(lefts[1], rights[0])
+    return total
+
+
+def each(pieces, change):
+    return tuple(change(piece) for piece in pieces) if isinstance(pieces, tuple) else change(pieces)
+
+
+def mixer_masks(resets, tokens):
+    per_chunk = CHUNK // MB
+    chunks = tokens // CHUNK
+    segment = jnp.cumsum(resets.reshape(chunks, per_chunk), axis=1)
+    segment = jnp.repeat(segment, MB, axis=1)
+    same = segment[:, :, None] == segment[:, None, :]
+    spot = jnp.arange(CHUNK, dtype=jnp.int32)
+    causal = (spot[None, :] <= spot[:, None])[None]
+    earlier = ((spot[None, :] // MB) < (spot[:, None] // MB))[None]
+    causal = (same & causal).astype(jnp.float32)
+    earlier = (same & earlier).astype(jnp.float32)
+    first = (segment == 0).astype(jnp.float32).reshape(tokens, 1)
+    last = (segment == segment[:, -1:]).astype(jnp.float32).reshape(tokens, 1)
+    anew = (segment[:, -1] > 0).astype(jnp.float32)
+    first = jnp.broadcast_to(first, (tokens, PAIR))
+    last = jnp.broadcast_to(last, (tokens, PAIR))
+    anew = jnp.broadcast_to(anew[:, None, None], (chunks, 8, PAIR))
+    return causal, earlier, first, last, anew
+
+
+def lane_helpers(rows):
+    lanes = lax.broadcasted_iota(jnp.int32, (rows, PAIR), 1)
+    low_lane = lanes < P_SIZE
+    low_half = low_lane.astype(jnp.float32)
+    high_half = 1.0 - low_half
+
+    def stack(pieces):
+        def one(piece):
+            kind = piece.dtype
+            return jnp.concatenate(
+                [piece * low_half.astype(kind), piece * high_half.astype(kind)], 0
+            )
+
+        return each(pieces, one)
+
+    def pick(product):
+        return jnp.where(low_lane, product[:rows], product[rows:])
+
+    return stack, pick
+
+
+def diagonal_blocks():
+    rows = lax.broadcasted_iota(jnp.int32, (PAIR, PAIR), 0) // P_SIZE
+    columns = lax.broadcasted_iota(jnp.int32, (PAIR, PAIR), 1) // P_SIZE
+    return (rows == columns).astype(jnp.float32)
+
+
+def solve(matrix, rate_row, value, pick):
+    rows = value.shape[0]
+    powers = [(matrix, rate_row)]
+    reach = 2
+    while reach < CHUNK // MB:
+        last, rate = powers[-1]
+        low, high = halves_of(last[:rows]), halves_of(last[rows:])
+        powers.append(
+            (
+                jnp.concatenate([wide(dot_ab, low, low), wide(dot_ab, high, high)], 0),
+                rate * rate,
+            )
         )
-        scaled = residue * step_rate
-        scores = jnp.einsum("thp,shp->hts", query_block, key_block, precision=PRECISE) * causal
-        output = jnp.einsum("thp,hpc->thc", query_block, carried, precision=PRECISE)
-        output = output - jnp.einsum("hts,shc->thc", scores, scaled, precision=PRECISE)
-        renewed = carried - jnp.einsum("thp,thc->hpc", key_block, scaled, precision=PRECISE)
-        return (renewed, output)
-
-    _, outputs = lax.scan(
-        advance, jnp.zeros_like(initial), (shaped[0], shaped[1], shaped[2], markers)
-    )
-    return outputs.reshape(query.shape)
+        reach = 2 * reach
+    for index in range(len(powers) - 1, -1, -1):
+        factor, rate = powers[index]
+        moved = pick(wide(dot_ab, halves_of(factor), halves_of(value * rate)))
+        value = value - moved if index == 0 else value + moved
+    return value
+
+
+def mixer_forward_kernel(
+    qkv_ref,
+    rate_ref,
+    initial_ref,
+    causal_ref,
+    earlier_ref,
+    first_ref,
+    last_ref,
+    anew_ref,
+    z_ref,
+    residue_ref,
+    states_ref,
+    state,
+):
+    pairs = initial_ref.shape[0]
+    width = pairs * PAIR
+
+    @pl.when(pl.program_id(0) == 0)
+    def _():
+        state[...] = jnp.zeros_like(state)
+
+    stack, pick = lane_helpers(CHUNK)
+    blocks = diagonal_blocks()
+    causal = causal_ref[0]
+    causal = jnp.concatenate([causal, causal], 0)
+    earlier = earlier_ref[0]
+    earlier = jnp.concatenate([earlier, earlier], 0)
+    first = first_ref[...] > 0.0
+    last = last_ref[...]
+    anew = anew_ref[0, 0:1, :]
+    for pair in range(pairs):
+        lanes = slice(pair * PAIR, (pair + 1) * PAIR)
+        query = qkv_ref[:, lanes]
+        key = qkv_ref[:, width + pair * PAIR : width + (pair + 1) * PAIR]
+        value = qkv_ref[:, 2 * width + pair * PAIR : 2 * width + (pair + 1) * PAIR]
+        rate = rate_ref[0:1, lanes]
+        begin = state[pair]
+        initial = initial_ref[pair]
+        states_ref[0, pair] = begin
+        products = dot_abt(jnp.concatenate([stack(key), stack(query)], 0), key)
+        ties = products[: 2 * CHUNK] * earlier
+        scores = products[2 * CHUNK :] * causal
+        both = jnp.concatenate([key, query], 0)
+        seen = wide(dot_ab, both, halves_of(begin))
+        fresh = wide(dot_ab, both, halves_of(initial))
+        key_seen = jnp.where(first, seen[:CHUNK], fresh[:CHUNK])
+        query_seen = jnp.where(first, seen[CHUNK:], fresh[CHUNK:])
+        key_wide = key.astype(jnp.float32)
+        residue = solve(ties, rate, key_seen - (value.astype(jnp.float32) - key_wide), pick)
+        residue_ref[:, lanes] = residue
+        scaled = residue * rate
+        scaled_parts = halves_of(scaled)
+        output = query_seen - pick(wide(dot_ab, halves_of(scores), scaled_parts))
+        z_ref[:, lanes] = output.astype(jnp.bfloat16)
+        key_last = (key_wide * last).astype(jnp.bfloat16)
+        base = jnp.where(anew > 0.0, initial, begin)
+        state[pair] = base - blocks * wide(dot_atb, key_last, scaled_parts)
+
+
+def mixer_backward_kernel(
+    qkv_ref,
+    rate_ref,
+    initial_ref,
+    causal_ref,
+    earlier_ref,
+    causal_turned_ref,
+    earlier_turned_ref,
+    first_ref,
+    last_ref,
+    anew_ref,
+    residue_ref,
+    states_ref,
+    upstream_ref,
+    grad_ref,
+    grad_initial_ref,
+    grad_rate_ref,
+    carried,
+):
+    pairs = initial_ref.shape[0]
+    width = pairs * PAIR
+
+    @pl.when(pl.program_id(0) == 0)
+    def _():
+        carried[...] = jnp.zeros_like(carried)
+        grad_initial_ref[...] = jnp.zeros_like(grad_initial_ref)
+        grad_rate_ref[...] = jnp.zeros_like(grad_rate_ref)
+
+    stack, pick = lane_helpers(CHUNK)
+    blocks = diagonal_blocks()
+
+    def doubled(ref):
+        return jnp.concatenate([ref[0], ref[0]], 0)
+
+    causal, earlier = doubled(causal_ref), doubled(earlier_ref)
+    causal_turned, earlier_turned = doubled(causal_turned_ref), doubled(earlier_turned_ref)
+    first_wide = first_ref[...]
+    first = first_wide > 0.0
+    last = last_ref[...]
+    anew = anew_ref[0, 0:1, :]
+    low = jnp.bfloat16
+    for pair in range(pairs):
+        lanes = slice(pair * PAIR, (pair + 1) * PAIR)
+        query = qkv_ref[:, lanes]
+        key = qkv_ref[:, width + pair * PAIR : width + (pair + 1) * PAIR]
+        rate = rate_ref[0:1, lanes]
+        begin = halves_of(states_ref[0, pair])
+        initial = halves_of(initial_ref[pair])
+        after = carried[pair]
+        after_parts = halves_of(after)
+        residue = residue_ref[:, lanes]
+        scaled = halves_of(residue * rate)
+        upstream = upstream_ref[:, lanes]
+        upstream_parts = halves_of(upstream)
+        key_wide = key.astype(jnp.float32)
+        query_wide = query.astype(jnp.float32)
+        key_last = (key_wide * last).astype(low)
+        key_stack = stack(key)
+        products = dot_abt(key_stack, jnp.concatenate([key, query], 0))
+        ties_turned = products[:, :CHUNK] * earlier_turned
+        scores_turned = products[:, CHUNK:] * causal_turned
+        pulled = pick(wide(dot_ab, halves_of(scores_turned), upstream_parts))
+        pulled = pulled + wide(dot_ab, key_last, after_parts)
+        grad_scaled = solve(ties_turned, rate, -pulled, pick)
+        grad_rate_ref[0:1, lanes] += jnp.sum(grad_scaled * residue, 0, keepdims=True)
+        grad_residue = grad_scaled * rate
+        residue_parts = halves_of(grad_residue)
+        joined = tuple(
+            jnp.concatenate([one, two], 0) for one, two in zip(upstream_parts, residue_parts)
+        )
+        scaled_stack = stack(scaled)
+        turned = wide(dot_abt, scaled_stack, joined)
+        straight = wide(
+            dot_abt,
+            tuple(
+                jnp.concatenate([stack(one), stack(two)], 0)
+                for one, two in zip(upstream_parts, residue_parts)
+            ),
+            scaled,
+        )
+        grad_scores = -straight[: 2 * CHUNK] * causal
+        grad_scores_turned = -turned[:, :CHUNK] * causal_turned
+        grad_ties = -(straight[2 * CHUNK :] * earlier + turned[:, CHUNK:] * earlier_turned)
+        seen = wide(dot_abt, joined, begin)
+        fresh = wide(dot_abt, joined, initial)
+        grad_query = jnp.where(first, seen[:CHUNK], fresh[:CHUNK])
+        grad_query = grad_query + pick(wide(dot_ab, halves_of(grad_scores), key))
+        grad_key = jnp.where(first, seen[CHUNK:], fresh[CHUNK:]) + grad_residue
+        grad_key = grad_key + pick(
+            wide(dot_ab, halves_of(grad_scores_turned), query)
+            + wide(dot_ab, halves_of(grad_ties), key)
+        )
+        grad_key = grad_key - last * wide(dot_abt, scaled, after_parts)
+        grad_ref[:, lanes] = grad_query.astype(low)
+        grad_ref[:, width + pair * PAIR : width + (pair + 1) * PAIR] = grad_key.astype(low)
+        grad_ref[:, 2 * width + pair * PAIR : 2 * width + (pair + 1) * PAIR] = (
+            -grad_residue
+        ).astype(low)
+        fronts = jnp.concatenate([query_wide * first_wide, key_wide * first_wide], 0).astype(low)
+        backs = jnp.concatenate(
+            [query_wide * (1.0 - first_wide), key_wide * (1.0 - first_wide)], 0
+        ).astype(low)
+        kept_after = jnp.where(anew > 0.0, 0.0, after)
+        carried[pair] = kept_after + blocks * wide(dot_atb, fronts, joined)
+        grad_initial_ref[pair] += (after - kept_after) + blocks * wide(dot_atb, backs, joined)
+
+
+def pair_blocks(matrices):
+    heads = matrices.shape[0]
+    split = matrices.reshape(heads // 2, 2, P_SIZE, P_SIZE)
+    empty = jnp.zeros_like(split[:, 0])
+    upper = jnp.concatenate([split[:, 0], empty], 2)
+    lower = jnp.concatenate([empty, split[:, 1]], 2)
+    return jnp.concatenate([upper, lower], 1)
+
+
+def head_blocks(pairs):
+    return jnp.stack([pairs[:, :P_SIZE, :P_SIZE], pairs[:, P_SIZE:, P_SIZE:]], 1).reshape(
+        -1, P_SIZE, P_SIZE
+    )
+
+
+def mixer_forward(qkv, rate, initial, masks):
+    tokens = qkv.shape[0]
+    width = rate.shape[1]
+    pairs = initial.shape[0]
+    chunks = tokens // CHUNK
+    whole = lambda shape: pl.BlockSpec(shape, lambda i: (0,) * len(shape))
+    square = pl.BlockSpec((1, CHUNK, CHUNK), lambda i: (i, 0, 0))
+    column = pl.BlockSpec((CHUNK, PAIR), lambda i: (i, 0))
+    causal, earlier, first, last, anew = masks
+    return pl.pallas_call(
+        mixer_forward_kernel,
+        grid=(chunks,),
+        in_specs=[
+            pl.BlockSpec((CHUNK, 3 * width), lambda i: (i, 0)),
+            whole((1, width)),
+            whole((pairs, PAIR, PAIR)),
+            square,
+            square,
+            column,
+            column,
+            pl.BlockSpec((1, 8, PAIR), lambda i: (i, 0, 0)),
+        ],
+        out_specs=[
+            pl.BlockSpec((CHUNK, width), lambda i: (i, 0)),
+            pl.BlockSpec((CHUNK, width), lambda i: (i, 0)),
+            pl.BlockSpec((1, pairs, PAIR, PAIR), lambda i: (i, 0, 0, 0)),
+        ],
+        out_shape=[
+            jax.ShapeDtypeStruct((tokens, width), jnp.bfloat16),
+            jax.ShapeDtypeStruct((tokens, width), jnp.float32),
+            jax.ShapeDtypeStruct((chunks, pairs, PAIR, PAIR), jnp.float32),
+        ],
+        scratch_shapes=[pltpu.VMEM((pairs, PAIR, PAIR), jnp.float32)],
+        compiler_params=pltpu.CompilerParams(
+            dimension_semantics=("arbitrary",), vmem_limit_bytes=32 * 1024 * 1024
+        ),
+        name="inner_forward",
+    )(qkv, rate, initial, causal, earlier, first, last, anew)
+
+
+def mixer_backward(qkv, rate, initial, masks, residue, states, upstream):
+    tokens = qkv.shape[0]
+    width = rate.shape[1]
+    pairs = initial.shape[0]
+    chunks = tokens // CHUNK
+    whole = lambda shape: pl.BlockSpec(shape, lambda i: (0,) * len(shape))
+    square = pl.BlockSpec((1, CHUNK, CHUNK), lambda i: (chunks - 1 - i, 0, 0))
+    column = pl.BlockSpec((CHUNK, PAIR), lambda i: (chunks - 1 - i, 0))
+    rows = lambda size: pl.BlockSpec((CHUNK, size), lambda i: (chunks - 1 - i, 0))
+    causal, earlier, first, last, anew = masks
+    return pl.pallas_call(
+        mixer_backward_kernel,
+        grid=(chunks,),
+        in_specs=[
+            rows(3 * width),
+            whole((1, width)),
+            whole((pairs, PAIR, PAIR)),
+            square,
+            square,
+            square,
+            square,
+            column,
+            column,
+            pl.BlockSpec((1, 8, PAIR), lambda i: (chunks - 1 - i, 0, 0)),
+            rows(width),
+            pl.BlockSpec((1, pairs, PAIR, PAIR), lambda i: (chunks - 1 - i, 0, 0, 0)),
+            rows(width),
+        ],
+        out_specs=[rows(3 * width), whole((pairs, PAIR, PAIR)), whole((1, width))],
+        out_shape=[
+            jax.ShapeDtypeStruct((tokens, 3 * width), jnp.bfloat16),
+            jax.ShapeDtypeStruct((pairs, PAIR, PAIR), jnp.float32),
+            jax.ShapeDtypeStruct((1, width), jnp.float32),
+        ],
+        scratch_shapes=[pltpu.VMEM((pairs, PAIR, PAIR), jnp.float32)],
+        compiler_params=pltpu.CompilerParams(
+            dimension_semantics=("arbitrary",), vmem_limit_bytes=32 * 1024 * 1024
+        ),
+        name="inner_backward",
+    )(
+        qkv,
+        rate,
+        initial,
+        causal,
+        earlier,
+        jnp.swapaxes(causal, 1, 2),
+        jnp.swapaxes(earlier, 1, 2),
+        first,
+        last,
+        anew,
+        residue,
+        states,
+        upstream,
+    )
 
 
 def shampoo(tile_w, tile_g, left, right, left_root, right_root):
-    new_left = STAT_DECAY * left + (1.0 - STAT_DECAY) * jnp.einsum(
-        "abrc,absc->abrs", tile_g, tile_g, precision=PRECISE
-    )
-    new_right = STAT_DECAY * right + (1.0 - STAT_DECAY) * jnp.einsum(
-        "abrc,abrd->abcd", tile_g, tile_g, precision=PRECISE
-    )
-    turned = jnp.einsum("abrs,absc->abrc", left_root, tile_g, precision=PRECISE)
-    turned = jnp.einsum("abrc,abcd->abrd", turned, right_root, precision=PRECISE)
+    low_g = tile_g.astype(jnp.bfloat16)
+
+    def product(form, one, two):
+        return jnp.einsum(
+            form,
+            one.astype(jnp.bfloat16),
+            two.astype(jnp.bfloat16),
+            preferred_element_type=jnp.float32,
+        )
+
+    new_left = STAT_DECAY * left + (1.0 - STAT_DECAY) * product("abrc,absc->abrs", low_g, low_g)
+    new_right = STAT_DECAY * right + (1.0 - STAT_DECAY) * product("abrc,abrd->abcd", low_g, low_g)
+    turned = product("abrs,absc->abrc", left_root, low_g)
+    turned = product("abrc,abcd->abrd", turned, right_root)
     return (new_left, new_right, tile_w - MATRIX_RATE * (turned + WEIGHT_DECAY * tile_w))
 
 
@@ -130,17 +491,10 @@
     full_one = spread(normed_one)
     mixed = jnp.dot(full_one, w_qkv, preferred_element_type=jnp.float32).astype(jnp.bfloat16)
     tokens = mixed.shape[0]
-    heads_here = inner_init.shape[0]
-    mixed = mixed.reshape(tokens, 3, heads_here, P_SIZE).astype(jnp.float32)
-
-    def inner(query, key_rows, value_rows, initial, logits_row):
-        step_rate = jax.nn.sigmoid(logits_row).reshape(heads_here, P_SIZE) / (8 * P_SIZE)
-        return mixer(query, key_rows, value_rows, initial, step_rate, resets)
-
-    inner_out, inner_pull = jax.vjp(
-        inner, mixed[:, 0], mixed[:, 1], mixed[:, 2], inner_init, gains[3]
-    )
-    inner_low = inner_out.reshape(tokens, -1).astype(jnp.bfloat16)
+    step_rate = jax.nn.sigmoid(gains[3:4]) / (8 * P_SIZE)
+    masks = mixer_masks(resets, tokens)
+    initial_pairs = pair_blocks(inner_init)
+    inner_low, residue, states = mixer_forward(mixed, step_rate, initial_pairs, masks)
     hidden_one = embedded + fold(jnp.dot(inner_low, w_out, preferred_element_type=jnp.float32))
     normed_two, scale_two = norm_forward(hidden_one, gains[1])
     full_two = spread(normed_two)
@@ -156,22 +510,29 @@
     normed_end, scale_end = norm_forward(hidden_two, gains[2])
     full_end = spread(normed_end)
     logits = jnp.einsum("td,vd->tv", full_end, table, preferred_element_type=jnp.float32)
-    highest = lax.pmax(jnp.max(logits, -1), "head")
+    peak = jnp.max(logits, -1)
     target_hits = columns[None, :] == (targets - head_index * vocab_part)[:, None]
-    exp_sum, target_logit = lax.psum(
-        (
-            jnp.sum(jnp.exp(logits - highest[:, None]), -1),
-            jnp.sum(jnp.where(target_hits, logits, 0.0), -1),
+    stats = lax.all_gather(
+        jnp.stack(
+            [
+                peak,
+                jnp.sum(jnp.exp(logits - peak[:, None]), -1),
+                jnp.sum(jnp.where(target_hits, logits, 0.0), -1),
+            ]
         ),
         "head",
-    )
+        axis=0,
+    )
+    highest = jnp.max(stats[:, 0], 0)
+    exp_sum = jnp.sum(stats[:, 1] * jnp.exp(stats[:, 0] - highest[None]), 0)
+    target_logit = jnp.sum(stats[:, 2], 0)
     totals = highest + jnp.log(exp_sum)
     counted = valid.astype(jnp.float32)
     kept = (
         embedded,
         scale_one,
         full_one,
-        inner_pull,
+        (mixed, step_rate, initial_pairs, masks, residue, states),
         inner_low,
         hidden_one,
         scale_two,
@@ -195,7 +556,7 @@
         embedded,
         scale_one,
         full_one,
-        inner_pull,
+        inner_kept,
         inner_low,
         hidden_one,
         scale_two,
@@ -230,8 +591,10 @@
     d_out_in = spread_grad(d_one.astype(jnp.bfloat16))
     grad_out = jnp.einsum("tc,td->cd", inner_low, d_out_in, preferred_element_type=jnp.float32)
     d_inner = jnp.einsum("td,cd->tc", d_out_in, w_out, preferred_element_type=jnp.float32)
-    d_query, d_key, d_value, grad_init, grad_rate = inner_pull(d_inner.reshape(tokens, -1, P_SIZE))
-    d_mixed = jnp.stack([d_query, d_key, d_value], 1).reshape(tokens, -1).astype(jnp.bfloat16)
+    d_mixed, grad_pairs, grad_step = mixer_backward(*inner_kept, d_inner)
+    grad_init = head_blocks(grad_pairs)
+    gate = jax.nn.sigmoid(gains[3])
+    grad_rate = grad_step[0] * gate * (1.0 - gate) / (8 * P_SIZE)
     grad_qkv = jnp.einsum("td,tc->dc", full_one, d_mixed, preferred_element_type=jnp.float32)
     d_one_norm = fold(jnp.einsum("tc,dc->td", d_mixed, w_qkv, preferred_element_type=jnp.float32))
     d_base, gain_one = norm_backward(embedded, scale_one, gains[0], d_one_norm)
@@ -313,12 +676,18 @@
     slot_down = jnp.take(
         jnp.swapaxes(grad_down.reshape(grad_down.shape[0], parts, -1), 0, 1), order[3], axis=0
     )
-    bundle = (slot_qkv, slot_out, slot_gu, slot_down, grad_table)
-    summed = lax.psum((bundle[0], bundle[1], bundle[2], bundle[3], bundle[4]), "dp")
-    place = lax.axis_index("dp")
-    width_part = emb_master.shape[1]
-    owned = tuple((lax.dynamic_slice_in_dim(piece, place, 1, 0) for piece in summed[:4]))
-    owned = owned + (lax.dynamic_slice_in_dim(summed[4], place * width_part, width_part, 1),)
+    low = jnp.bfloat16
+    owned = tuple(
+        lax.psum_scatter(piece.astype(low), "dp", scatter_dimension=0, tiled=True).astype(
+            jnp.float32
+        )
+        for piece in (slot_qkv, slot_out, slot_gu, slot_down)
+    )
+    owned = owned + (
+        lax.psum_scatter(grad_table.astype(low), "dp", scatter_dimension=1, tiled=True).astype(
+            jnp.float32
+        ),
+    )
     small = lax.psum((grad_init, grad_gains), "dp")
     first_dp = (lax.axis_index("dp") == 0).astype(jnp.float32)
     squares = sum((jnp.sum(piece * piece) for piece in owned))

time: 6640 us -> 2370 us (0.36); the launches traced: 6520 us -> 2370 us
  matrix products: 2880 us -> 392 us
  waiting for transfers between devices: 2500 us -> 1370 us
  other arithmetic: 511 us -> 144 us
  local copies, waits for them, and re-layouts: 418 us -> 164 us
  Pallas kernels: 0 us -> 127 us
    dot_general x1936 -> x12, matrix products: 2520 us -> 45.1 us  [product(): jnp.einsum(form, one.astype(jnp.bfloat16), two.astype(jnp.bfloat16), pref...]
    psum x1, waiting for transfers between devices: 964 us -> 0.01 us  [shards(): small = lax.psum((grad_init, grad_gains), 'dp')]
    reduce_scatter x5 -> x6, waiting for transfers between devices: 826 us -> 569 us  [the longest x5 434 us: fold(): lax.psum_scatter(low, 'head', scatter_dimension=1, tiled=True)]
    dynamic_update_slice x256 -> x0, other arithmetic: 247 us -> none  [mixer(): lax.scan(advance, jnp.zeros_like(initial), (shaped[0], shaped[1], shaped[...]
    pallas_call x0 -> x2, Pallas kernels: none -> 127 us  [the longest x1 77.1 us: mixer_backward(): pl.pallas_call(mixer_backward_kernel, grid=(chunks,), in_specs=[rows(3 *...]
    dynamic_update_slice x128 -> x0, local copies, waits for them, and re-layouts: 97.8 us -> none  [mixer(): lax.scan(advance, jnp.zeros_like(initial), (shaped[0], shaped[1], shaped[...]
    dynamic_slice x128 -> x0, local copies, waits for them, and re-layouts: 75.7 us -> none  [mixer(): lax.scan(advance, jnp.zeros_like(initial), (shaped[0], shaped[1], shaped[...]
    gt x128 -> x0, other arithmetic: 75 us -> none  [advance(): carried = jnp.where(marker > 0, initial, carried)]
  transfers between devices with their start and end apart: 18 -> 23, of which waited for: 17 -> 19; matrix products, arithmetic and copies ran while one was open for 4% -> 14% of each run, Pallas kernels for 0% -> 0%
where the time goes in v1:
time: 2370 us
  waiting for transfers between devices  1370 us (58%)
  matrix products  392 us (17%)
  local copies, waits for them, and re-layouts  164 us (7%)
  blocking collectives  147 us (6%)
  other arithmetic  144 us (6%)
  Pallas kernels  127 us (5%)
  between operations  24.3 us (1%)
    reduce_scatter x5, waiting for transfers between devices, fold(): lax.psum_scatter(low, 'head', scatter_dimension=1, tiled=True)  434 us
    all_gather x3, waiting for transfers between devices, spread(): return lax.all_gather(rows, 'head', axis=1, tiled=True)  216 us
    all_gather x1, waiting for transfers between devices, shards(): lax.all_gather(emb_master.astype(jnp.bfloat16), 'dp', axis=1, tiled=True)  156 us
    all_gather x3, waiting for transfers between devices, spread_grad(): return lax.all_gather(rows, 'head', axis=1, tiled=True)  144 us
    reduce_scatter x1, waiting for transfers between devices, shards(): lax.psum_scatter(grad_table.astype(low), 'dp', scatter_dimension=1, tiled...  135 us
    reduce_scatter x1, waiting for transfers between devices, layer_forward(): lax.psum_scatter(looked_rows.astype(jnp.bfloat16), 'head', scatter_dimens...  86.3 us
    psum x6, blocking collectives, head_total(): return lax.psum(values, 'head')  83.4 us
    pallas_call x1, Pallas kernels, mixer_backward(): pl.pallas_call(mixer_backward_kernel, grid=(chunks,), in_specs=[rows(3 *...  77.1 us
  transfers between devices with their start and end apart: 23, of which 19 were waited for; matrix products, arithmetic and copies ran while one was open for 14% of the time, Pallas kernels for 0%

profile of v1, /device:TPU:0, one launch (start us, length us, event | category | flops | bytes accessed | tf_op | source)
XLA Modules:
  0.0 2367.0 jit_solution(17357047503306286109)
XLA Ops:
  7.2 5.8 convert_element_type.273
  14.4 155.6 %all-gather.14.cloned.1.call-done = bf16[4000,2048]{1,0:T(8,128)(2,1)} async-done(((bf16[4000,512]{1,0:T(8,128)(2,1)}), bf16[4000,2048]{1,0:T(8,128)(2,1)}) %all-gather.14.cloned.1.call-update) | async-done | bytes 16384016 | tf_op jit(solution)/shard_map/all_gather | solution.py:652
  170.0 24.1 %gather_fusion = bf16[2048,2048]{1,0:T(8,128)(2,1)} fusion(bf16[4000,2048]{1,0:T(8,128)(2,1)} %all-gather.14.cloned.1.call-done, s32[2048]{0:T(1024)S(1)} %fusion.137), kind=kCustom, calls=%fused_computation | custom fusion | bytes 16785408 | tf_op jit(solution)/shard_map/jit(_take)/gather | solution.py:485
  194.1 8.4 select_convert_fusion
  206.0 86.3 %reduce-scatter.20.cloned.1.call-done = bf16[2048,256]{1,0:T(8,128)(2,1)} async-done(((bf16[2048,2048]{1,0:T(8,128)(2,1)}), bf16[2048,256]{1,0:T(8,128)(2,1)}) %reduce-scatter.20.cloned.1.call-update) | async-done | bytes 1048592 | tf_op jit(solution)/shard_map/reduce_scatter | solution.py:487
  293.9 13.9 psum.77
  314.8 4.9 all-gather.20.cloned.1.call-done
  324.2 41.8 %all-gather.18.cloned.1.call-done = bf16[4,512,3,256]{3,1,2,0:T(8,128)(2,1)} async-done(((bf16[1,512,3,256]{3,1,2,0:T(8,128)(2,1)}), bf16[4,512,3,256]{3,1,2,0:T(8,128)(2,1)}) %all-gather.18.cloned.1.call-update) | async-done | bytes 3145744 | tf_op jit(solution)/shard_map/all_gather | solution.py:648
  370.3 6.2 copy.116
  376.6 5.1 copy.158
  381.7 68.9 %all-gather.16.cloned.1.call-done = bf16[2048,2048]{1,0:T(8,128)(2,1)} async-done(((bf16[2048,256]{1,0:T(8,128)(2,1)}), bf16[2048,2048]{1,0:T(8,128)(2,1)}) %all-gather.16.cloned.1.call-update) | async-done | bytes 8388624 | tf_op jit(solution)/shard_map/all_gather | solution.py:32
  450.6 10.1 convolution_convert_fusion.5.qkv_ref
  461.5 49.9 %inner_forward.1 = (bf16[2048,256]{1,0:T(8,128)(2,1)S(1)}, f32[2048,256]{1,0:T(8,128)S(1)}, f32[32,2,128,128]{3,2,1,0:T(8,128)S(1)}) custom-call(bf16[2048,768]{1,0:T(8,128)(2,1)S(1)} %convolution_convert_fusion.5.qkv_ref, f32[1,256]{1,0:T(1,128)S(1)} %get-tuple-element.182.rate_ref, f32[2,128,128]{2,1,0:T(8,128)S(1)} %select_maximum_fusion.initial_ref, ...), custom_call_target="tpu_custom_call" | custom-call | tf_op jit(solution)/shard_map/inner_forward/pallas_call | solution.py:350
  515.8 5.6 convolution_convert_fusion.4
  527.0 82.3 %reduce-scatter.22.cloned.1.call-done = bf16[2048,256]{1,0:T(8,128)(2,1)} async-done(((bf16[2048,2048]{1,0:T(8,128)(2,1)}), bf16[2048,256]{1,0:T(8,128)(2,1)}) %reduce-scatter.22.cloned.1.call-update) | async-done | bytes 1048592 | tf_op jit(solution)/shard_map/reduce_scatter | solution.py:41
  611.0 13.9 psum.78
  628.5 23.0 all-gather.26.cloned.1.call-done
  659.7 59.0 %all-gather.24.cloned.1.call-done = bf16[4,512,2,688]{1,3,2,0:T(8,128)(2,1)} async-done(((bf16[1,512,2,688]{1,3,2,0:T(8,128)(2,1)}), bf16[4,512,2,688]{1,3,2,0:T(8,128)(2,1)}) %all-gather.24.cloned.1.call-update) | async-done | bytes 5636112 | tf_op jit(solution)/shard_map/all_gather | solution.py:650
  718.6 6.0 gather_fusion.3
  724.6 7.0 copy.123
  737.0 66.4 %all-gather.22.cloned.1.call-done = bf16[2048,2048]{1,0:T(8,128)(2,1)} async-done(((bf16[2048,256]{1,0:T(8,128)(2,1)}), bf16[2048,2048]{1,0:T(8,128)(2,1)}) %all-gather.22.cloned.1.call-update) | async-done | bytes 8388624 | tf_op jit(solution)/shard_map/all_gather | solution.py:32
  803.3 16.2 fusion.5
  825.8 9.1 convolution_convert_fusion.1
  835.0 87.9 %reduce-scatter.24.cloned.1.call-done = bf16[2048,256]{1,0:T(8,128)(2,1)} async-done(((bf16[2048,2048]{1,0:T(8,128)(2,1)}), bf16[2048,256]{1,0:T(8,128)(2,1)}) %reduce-scatter.24.cloned.1.call-update) | async-done | bytes 1048592 | tf_op jit(solution)/shard_map/reduce_scatter | solution.py:41
  924.8 13.9 psum.79
  940.4 80.8 %all-gather.28.cloned.1.call-done = bf16[2048,2048]{1,0:T(8,128)(2,1)} async-done(((bf16[2048,256]{1,0:T(8,128)(2,1)}), bf16[2048,2048]{1,0:T(8,128)(2,1)}) %all-gather.28.cloned.1.call-update) | async-done | bytes 8388624 | tf_op jit(solution)/shard_map/all_gather | solution.py:32
  1021.2 42.3 %fusion.165 = (f32[2048]{0:T(1024)S(1)}, f32[2048,4000]{0,1:T(8,128)}) fusion(bf16[2048,2048]{1,0:T(8,128)(2,1)} %all-gather.28.cloned.1.call-done, bf16[4000,2048]{1,0:T(8,128)(2,1)} %all-gather.14.cloned.1.call-done), kind=kOutput, calls=%fused_computation.308 | convolution fusion | flops 33562621952 | bytes 57548800 | tf_op jit(solution)/shard_map/td,vd->tv/dot_general | solution.py:512
  1063.5 14.8 exponential_reduce_fusion
  1078.3 14.2 all-gather.1
  1093.4 48.5 %convolution_convert_fusion = bf16[2048,2048]{1,0:T(8,128)(2,1)} fusion(bf16[4000,2048]{1,0:T(8,128)(2,1)} %all-gather.14.cloned.1.call-done, f32[2048,4000]{0,1:T(8,128)} %get-tuple-element.218, f32[2048]{0:T(1024)S(1)} %convert_element_type.296, f32[2048]{0:T(1024)S(1)} %get-tuple-element.181, s32[2048]{0:T(1024)S(1)} %broadcast_subtract_fusion), kind=kOutput, calls=%fused_computation.34 | convolution fusion | flops 33607778304 | bytes 57565184 | tf_op jit(solution)/shard_map/dot_general | solution.py:581
  1142.0 87.9 %reduce-scatter.26.cloned.1.call-done = bf16[2048,256]{1,0:T(8,128)(2,1)} async-done(((bf16[2048,2048]{1,0:T(8,128)(2,1)}), bf16[2048,256]{1,0:T(8,128)(2,1)}) %reduce-scatter.26.cloned.1.call-update) | async-done | bytes 1048592 | tf_op jit(solution)/shard_map/reduce_scatter | solution.py:41
  1232.7 13.9 psum.82
  1252.8 6.8 copy.127
  1259.7 7.6 copy.161
  1267.3 63.0 %all-gather.30.cloned.1.call-done = bf16[2048,2048]{1,0:T(8,128)(2,1)} async-done(((bf16[2048,256]{1,0:T(8,128)(2,1)}), bf16[2048,2048]{1,0:T(8,128)(2,1)}) %all-gather.30.cloned.1.call-update) | async-done | bytes 8388624 | tf_op jit(solution)/shard_map/all_gather | solution.py:36
  1330.2 16.1 fusion.19
  1346.3 5.1 add_convert_fusion.1
  1354.0 17.7 convolution_convert_fusion.3
  1371.8 87.9 %reduce-scatter.28.cloned.1.call-done = bf16[2048,256]{1,0:T(8,128)(2,1)} async-done(((bf16[2048,2048]{1,0:T(8,128)(2,1)}), bf16[2048,256]{1,0:T(8,128)(2,1)}) %reduce-scatter.28.cloned.1.call-update) | async-done | bytes 1048592 | tf_op jit(solution)/shard_map/reduce_scatter | solution.py:41
  1462.5 13.9 psum.83
  1481.3 80.8 %all-gather.32.cloned.1.call-done = bf16[2048,2048]{1,0:T(8,128)(2,1)} async-done(((bf16[2048,256]{1,0:T(8,128)(2,1)}), bf16[2048,2048]{1,0:T(8,128)(2,1)}) %all-gather.32.cloned.1.call-update) | async-done | bytes 8388624 | tf_op jit(solution)/shard_map/all_gather | solution.py:36
  1562.2 6.1 fusion.166.upstream_ref
  1569.5 77.1 %inner_backward.1 = (bf16[2048,768]{1,0:T(8,128)(2,1)S(1)}, f32[2,128,128]{2,1,0:T(8,128)S(1)}, f32[1,256]{1,0:T(1,128)S(1)}) custom-call(bf16[2048,768]{1,0:T(8,128)(2,1)S(1)} %copy-done.1, f32[1,256]{1,0:T(1,128)S(1)} %copy-done.23, f32[2,128,128]{2,1,0:T(8,128)S(1)} %copy-done.19, f32[32,64,64]{2,1,0:T(8,128)S(1)} %copy-done.9, ...), custom_call_target="tpu_custom_call" | custom-call | tf_op jit(solution)/shard_map/inner_backward/pallas_call | solution.py:391
  1648.3 8.9 convolution_convert_fusion.2
  1657.3 87.9 %reduce-scatter.30.cloned.1.call-done = bf16[2048,256]{1,0:T(8,128)(2,1)} async-done(((bf16[2048,2048]{1,0:T(8,128)(2,1)}), bf16[2048,256]{1,0:T(8,128)(2,1)}) %reduce-scatter.30.cloned.1.call-update) | async-done | bytes 1048592 | tf_op jit(solution)/shard_map/reduce_scatter | solution.py:41
  1747.9 13.9 psum.84
  1765.5 12.8 copy.148
  1778.4 10.8 fusion.40
  1794.3 12.1 copy.147
  1806.4 17.5 fusion.13
  1823.9 6.2 gather_fusion.7
  1830.1 6.7 select_convert_fusion.1
  1838.0 5.7 fusion.168
  1851.3 10.5 fusion.167
  1876.6 76.9 %fusion = f32[4000,2048]{1,0:T(8,128)} fusion(bf16[2048,2048]{1,0:T(8,128)(2,1)} %all-gather.34.cloned.1.call-done, s32[2048]{0:T(1024)S(1)} %copy-done.63), kind=kOutput, calls=%fused_computation.10 | convolution fusion | flops 33562624000 | bytes 41164800 | tf_op jit(solution)/shard_map/tv,td->vd/dot_general | solution.py:604
  1953.5 45.2 %add_convert_fusion = bf16[4000,2048]{1,0:T(8,128)(2,1)} fusion(f32[4000,2048]{1,0:T(8,128)} %fusion, bf16[2048,2048]{1,0:T(8,128)(2,1)} %all-gather.28.cloned.1.call-done, f32[2048,4000]{0,1:T(8,128)} %get-tuple-element.218, f32[2048]{0:T(1024)S(1)} %copy-done.78, f32[2048]{0:T(1024)S(1)} %copy-done.80, s32[2048]{0:T(1024)S(1)} %copy-done.65), kind=kOutput, calls=%fused_computation.11 | convolution fusion | flops 33619968000 | bytes 90333184 | tf_op jit(solution)/shard_map/tv,td->vd/dot_general | solution.py:580
  2013.2 20.3 reduce-scatter.36.cloned.1.call-done
  2035.2 45.9 %reduce-scatter.34.cloned.1.call-done = bf16[1,512,3,256]{3,1,2,0:T(8,128)(2,1)} async-done(((bf16[4,512,3,256]{3,1,2,0:T(8,128)(2,1)}), bf16[1,512,3,256]{3,1,2,0:T(8,128)(2,1)}) %reduce-scatter.34.cloned.1.call-update) | async-done | bytes 786448
  2086.1 9.8 all-reduce.8
  2099.7 135.2 %reduce-scatter.32.cloned.1.call-done = bf16[4000,512]{1,0:T(8,128)(2,1)} async-done(((bf16[4000,2048]{1,0:T(8,128)(2,1)}), bf16[4000,512]{1,0:T(8,128)(2,1)}) %reduce-scatter.32.cloned.1.call-update) | async-done | bytes 4096016 | tf_op jit(solution)/shard_map/reduce_scatter | solution.py:687
  2241.1 39.6 %psum.87 = f32[]{:T(128)} all-reduce(f32[]{:T(128)S(6)} %add.379), channel_id=1, replica_groups=mesh['dp'=4,'head'=8] {'dp','head'}, use_global_device_ids=true, to_apply=%region_47.48 | all-reduce | flops 1 | bytes 8 | tf_op jit(solution)/shard_map/psum | solution.py:695
  2313.8 8.8 fusion.4
  2327.7 10.1 fusion.29
  2337.9 20.1 multiply_subtract_fusion
  (370 shorter events, 181.8 us)
Async XLA Ops:
  7.2 162.8 %all-gather.14.cloned.1.call-start = ((), (), s32[]{:S(2)}) async-start(), calls=%async_computation.11 | async-start | bytes 20480000 | tf_op jit(solution)/shard_map/all_gather | solution.py:652
  13.1 279.2 %reduce-scatter.20.cloned.1.call-start = ((), (), s32[]{:S(2)}) async-start(), calls=%async_computation.12 | async-start | bytes 9437184 | tf_op jit(solution)/shard_map/reduce_scatter | solution.py:487
  202.5 117.2 %all-gather.20.cloned.1.call-start = ((), (), s32[]{:S(2)}) async-start(), calls=%async_computation.15 | async-start | bytes 1310720 | tf_op jit(solution)/shard_map/all_gather | solution.py:649
  204.3 107.2 %copy-start.67 = (s32[4,4]{1,0:T(4,128)S(1)}, s32[4,4]{1,0:T(4,128)}, u32[]{:S(2)}) copy-start(s32[4,4]{1,0:T(4,128)} %param.38) | copy-start | bytes 196
  204.3 107.8 %copy-start.91 = (s32[128]{0:T(128)S(1)}, s32[128]{0:T(128)}, u32[]{:S(2)}) copy-start(s32[128]{0:T(128)} %param.37) | copy-start | bytes 1540
  204.3 161.7 %all-gather.18.cloned.1.call-start = ((), (), s32[]{:S(2)}) async-start(), calls=%async_computation.14 | async-start | bytes 3932160 | tf_op jit(solution)/shard_map/all_gather | solution.py:648
  205.3 107.6 %copy-start.51 = (f32[4,64,64]{2,1,0:T(8,128)S(1)}, f32[4,64,64]{2,1,0:T(8,128)}, u32[]{:S(2)}) copy-start(f32[4,64,64]{2,1,0:T(8,128)} %param.62) | copy-start | bytes 196612
  205.4 245.2 %all-gather.16.cloned.1.call-start = ((), (), s32[]{:S(2)}) async-start(), calls=%async_computation.13 | async-start | bytes 9437184 | tf_op jit(solution)/shard_map/all_gather | solution.py:32
  206.0 107.2 %copy-start.73 = (f32[1,256]{1,0:T(1,128)}, f32[1,256]{1,0:T(1,128)S(1)}, u32[]{:S(2)}) copy-start(f32[1,256]{1,0:T(1,128)S(1)} %get-tuple-element.205) | copy-start | bytes 3076
  206.0 255.5 %copy-start.22 = (f32[1,256]{1,0:T(1,128)}, f32[1,256]{1,0:T(1,128)S(1)}, u32[]{:S(2)}) copy-start(f32[1,256]{1,0:T(1,128)S(1)} %get-tuple-element.182.rate_ref) | copy-start | bytes 3076
  206.0 419.0 %copy-start.69 = (f32[1,256]{1,0:T(1,128)}, f32[1,256]{1,0:T(1,128)S(1)}, u32[]{:S(2)}) copy-start(f32[1,256]{1,0:T(1,128)S(1)} %get-tuple-element.204) | copy-start | bytes 3076
  311.0 298.4 %reduce-scatter.22.cloned.1.call-start = ((), (), s32[]{:S(2)}) async-start(), calls=%async_computation.16 | async-start | bytes 9437184 | tf_op jit(solution)/shard_map/reduce_scatter | solution.py:41
  312.1 138.5 %copy-start.89 = (pred[1,4,4,128]{3,1,2,0:T(4,128)(4,1)}, pred[1,4,4,128]{3,1,2,0:T(4,128)(4,1)S(1)}, u32[]{:S(2)}) copy-start(pred[1,4,4,128]{3,1,2,0:T(4,128)(4,1)S(1)} %copy.157) | copy-start | bytes 6148
  313.1 148.4 %copy-start.18 = (f32[2,128,128]{2,1,0:T(8,128)}, f32[2,128,128]{2,1,0:T(8,128)S(1)}, u32[]{:S(2)}) copy-start(f32[2,128,128]{2,1,0:T(8,128)S(1)} %select_maximum_fusion.initial_ref) | copy-start | bytes 393220
  314.8 146.7 %copy-start.6 = (f32[32,64,64]{2,1,0:T(8,128)}, f32[32,64,64]{2,1,0:T(8,128)S(1)}, u32[]{:S(2)}) copy-start(f32[32,64,64]{2,1,0:T(8,128)S(1)} %get-tuple-element.199.earlier_ref) | copy-start | bytes 1572868
  314.8 146.7 %copy-start.8 = (f32[32,64,64]{2,1,0:T(8,128)}, f32[32,64,64]{2,1,0:T(8,128)S(1)}, u32[]{:S(2)}) copy-start(f32[32,64,64]{2,1,0:T(8,128)S(1)} %get-tuple-element.200.causal_ref) | copy-start | bytes 1572868
  324.2 190.6 %copy-start.38 = (bf16[256,4,512]{0,2,1:T(8,128)(2,1)}, bf16[256,4,512]{0,2,1:T(8,128)(2,1)S(1)}, u32[]{:S(2)}) copy-start(bf16[256,4,512]{0,2,1:T(8,128)(2,1)S(1)} %copy.122) | copy-start | bytes 3145732
  460.7 50.8 %copy-start = (bf16[2048,768]{1,0:T(8,128)(2,1)}, bf16[2048,768]{1,0:T(8,128)(2,1)S(1)}, u32[]{:S(2)}) copy-start(bf16[2048,768]{1,0:T(8,128)(2,1)S(1)} %convolution_convert_fusion.5.qkv_ref) | copy-start | bytes 9437188
  461.0 50.4 %copy-start.2 = (f32[2048,128]{1,0:T(8,128)}, f32[2048,128]{1,0:T(8,128)S(1)}, u32[]{:S(2)}) copy-start(f32[2048,128]{1,0:T(8,128)S(1)} %broadcast_in_dim.183.first_ref) | copy-start | bytes 3145732
  461.4 50.1 %copy-start.4 = (f32[2048,128]{1,0:T(8,128)}, f32[2048,128]{1,0:T(8,128)S(1)}, u32[]{:S(2)}) copy-start(f32[2048,128]{1,0:T(8,128)S(1)} %broadcast_in_dim.184.last_ref) | copy-start | bytes 3145732
  461.5 50.0 %copy-start.20 = (f32[32,8,128]{2,1,0:T(8,128)}, f32[32,8,128]{2,1,0:T(8,128)S(1)}, u32[]{:S(2)}) copy-start(f32[32,8,128]{2,1,0:T(8,128)S(1)} %broadcast_in_dim.185.anew_ref) | copy-start | bytes 393220
  521.4 130.0 %all-gather.26.cloned.1.call-start = ((), (), s32[]{:S(2)}) async-start(), calls=%async_computation.19 | async-start | bytes 3522560 | tf_op jit(solution)/shard_map/all_gather | solution.py:651
  523.7 85.7 %copy-start.26 = (bf16[2048,256]{1,0:T(8,128)(2,1)S(1)}, bf16[2048,256]{1,0:T(8,128)(2,1)}, u32[]{:S(2)}) copy-start(bf16[2048,256]{1,0:T(8,128)(2,1)} %reduce-scatter.20.cloned.1.call-done) | copy-start | bytes 3145732
  523.7 194.9 %all-gather.24.cloned.1.call-start = ((), (), s32[]{:S(2)}) async-start(), calls=%async_computation.18 | async-start | bytes 7045120 | tf_op jit(solution)/shard_map/all_gather | solution.py:650
  527.0 276.3 %all-gather.22.cloned.1.call-start = ((), (), s32[]{:S(2)}) async-start(), calls=%async_computation.17 | async-start | bytes 9437184 | tf_op jit(solution)/shard_map/all_gather | solution.py:32
  628.2 294.7 %reduce-scatter.24.cloned.1.call-start = ((), (), s32[]{:S(2)}) async-start(), calls=%async_computation.20 | async-start | bytes 9437184 | tf_op jit(solution)/shard_map/reduce_scatter | solution.py:41
  835.0 88.0 %copy-start.28 = (bf16[2048,256]{1,0:T(8,128)(2,1)S(1)}, bf16[2048,256]{1,0:T(8,128)(2,1)}, u32[]{:S(2)}) copy-start(bf16[2048,256]{1,0:T(8,128)(2,1)} %reduce-scatter.22.cloned.1.call-done) | copy-start | bytes 3145732
  835.0 186.2 %all-gather.28.cloned.1.call-start = ((), (), s32[]{:S(2)}) async-start(), calls=%async_computation.21 | async-start | bytes 9437184 | tf_op jit(solution)/shard_map/all_gather | solution.py:32
  940.3 289.6 %reduce-scatter.26.cloned.1.call-start = ((), (), s32[]{:S(2)}) async-start(), calls=%async_computation.22 | async-start | bytes 9437184 | tf_op jit(solution)/shard_map/reduce_scatter | solution.py:41
  940.4 153.1 %copy-start.77 = (f32[2048]{0:T(1024)}, f32[2048]{0:T(1024)S(1)}, u32[]{:S(2)}) copy-start(f32[2048]{0:T(1024)S(1)} %convert_element_type.296) | copy-start | bytes 24580
  940.4 153.0 %copy-start.64 = (s32[2048]{0:T(1024)}, s32[2048]{0:T(1024)S(1)}, u32[]{:S(2)}) copy-start(s32[2048]{0:T(1024)S(1)} %broadcast_subtract_fusion) | copy-start | bytes 24580
  1093.4 48.5 %copy-start.79 = (f32[2048]{0:T(1024)}, f32[2048]{0:T(1024)S(1)}, u32[]{:S(2)}) copy-start(f32[2048]{0:T(1024)S(1)} %get-tuple-element.181) | copy-start | bytes 24580
  1141.9 188.3 %all-gather.30.cloned.1.call-start = ((), (), s32[]{:S(2)}) async-start(), calls=%async_computation.23 | async-start | bytes 9437184 | tf_op jit(solution)/shard_map/all_gather | solution.py:36
  1249.3 210.4 %reduce-scatter.28.cloned.1.call-start = ((), (), s32[]{:S(2)}) async-start(), calls=%async_computation.24 | async-start | bytes 9437184 | tf_op jit(solution)/shard_map/reduce_scatter | solution.py:41
  1371.7 88.0 %copy-start.59 = (f32[2048]{0:T(1024)S(1)}, f32[2048]{0:T(1024)}, u32[]{:S(2)}) copy-start(f32[2048]{0:T(1024)} %copy-done.58) | copy-start | bytes 24580
  1371.7 88.0 %copy-start.70 = (f32[1,256]{1,0:T(1,128)S(1)}, f32[1,256]{1,0:T(1,128)}, u32[]{:S(2)}) copy-start(f32[1,256]{1,0:T(1,128)} %copy-done.69) | copy-start | bytes 3076
  1371.7 190.4 %all-gather.32.cloned.1.call-start = ((), (), s32[]{:S(2)}) async-start(), calls=%async_computation.25 | async-start | bytes 9437184 | tf_op jit(solution)/shard_map/all_gather | solution.py:36
  1481.2 87.1 %copy-start.1 = (bf16[2048,768]{1,0:T(8,128)(2,1)S(1)}, bf16[2048,768]{1,0:T(8,128)(2,1)}, u32[]{:S(2)}) copy-start(bf16[2048,768]{1,0:T(8,128)(2,1)} %copy-done) | copy-start | bytes 9437188
  1481.3 87.1 %copy-start.19 = (f32[2,128,128]{2,1,0:T(8,128)S(1)}, f32[2,128,128]{2,1,0:T(8,128)}, u32[]{:S(2)}) copy-start(f32[2,128,128]{2,1,0:T(8,128)} %copy-done.18) | copy-start | bytes 393220
  1481.3 87.1 %copy-start.21 = (f32[32,8,128]{2,1,0:T(8,128)S(1)}, f32[32,8,128]{2,1,0:T(8,128)}, u32[]{:S(2)}) copy-start(f32[32,8,128]{2,1,0:T(8,128)} %copy-done.20) | copy-start | bytes 393220
  1481.3 87.1 %copy-start.23 = (f32[1,256]{1,0:T(1,128)S(1)}, f32[1,256]{1,0:T(1,128)}, u32[]{:S(2)}) copy-start(f32[1,256]{1,0:T(1,128)} %copy-done.22) | copy-start | bytes 3076
  1481.3 263.9 %reduce-scatter.30.cloned.1.call-start = ((), (), s32[]{:S(2)}) async-start(), calls=%async_computation.26 | async-start | bytes 9437184 | tf_op jit(solution)/shard_map/reduce_scatter | solution.py:41
  1569.5 78.8 %copy-start.39 = (bf16[96,8,4,512]{3,1,2,0:T(8,128)(2,1)S(1)}, bf16[96,8,4,512]{3,1,2,0:T(8,128)(2,1)}, u32[]{:S(2)}) copy-start(bf16[96,8,4,512]{3,1,2,0:T(8,128)(2,1)} %copy.158) | copy-start | bytes 9437188
  1569.5 78.8 %copy-start.90 = (pred[1,4,4,128]{3,1,2,0:T(4,128)(4,1)S(1)}, pred[1,4,4,128]{3,1,2,0:T(4,128)(4,1)}, u32[]{:S(2)}) copy-start(pred[1,4,4,128]{3,1,2,0:T(4,128)(4,1)} %copy-done.89) | copy-start | bytes 6148
  1657.2 88.0 %copy-start.27 = (bf16[2048,256]{1,0:T(8,128)(2,1)S(1)}, bf16[2048,256]{1,0:T(8,128)(2,1)}, u32[]{:S(2)}) copy-start(bf16[2048,256]{1,0:T(8,128)(2,1)} %reduce-scatter.20.cloned.1.call-done) | copy-start | bytes 3145732
  1657.2 88.0 %copy-start.57 = (f32[2048]{0:T(1024)S(1)}, f32[2048]{0:T(1024)}, u32[]{:S(2)}) copy-start(f32[2048]{0:T(1024)} %copy-done.56) | copy-start | bytes 24580
  1657.2 88.0 %copy-start.74 = (f32[1,256]{1,0:T(1,128)S(1)}, f32[1,256]{1,0:T(1,128)}, u32[]{:S(2)}) copy-start(f32[1,256]{1,0:T(1,128)} %copy-done.73) | copy-start | bytes 3076
  1657.2 104.6 %copy-start.33 = (f32[2048,256]{1,0:T(8,128)S(1)}, f32[2048,256]{1,0:T(8,128)}, u32[]{:S(2)}) copy-start(f32[2048,256]{1,0:T(8,128)} %get-tuple-element.180) | copy-start | bytes 6291460
  1657.2 219.0 %all-gather.34.cloned.1.call-start = ((), (), s32[]{:S(2)}) async-start(), calls=%async_computation.27 | async-start | bytes 9437184 | tf_op jit(solution)/shard_map/all_gather | solution.py:36
  1764.5 242.4 %reduce-scatter.40.cloned.1.call-start = ((), (), s32[]{:S(2)}) async-start(), calls=%async_computation.33 | async-start | bytes 3522560
  1794.2 214.8 %reduce-scatter.38.cloned.1.call-start = ((), (), s32[]{:S(2)}) async-start(), calls=%async_computation.32 | async-start | bytes 7045120
  1836.8 174.9 %all-reduce.11.cloned.1.call-start = ((), (), s32[]{:S(2)}) async-start(), calls=%async_computation.29 | async-start | bytes 262144 | tf_op jit(solution)/shard_map/psum | solution.py:691
  1848.6 184.9 %reduce-scatter.36.cloned.1.call-start = ((), (), s32[]{:S(2)}) async-start(), calls=%async_computation.31 | async-start | bytes 1310720
  1851.3 229.8 %reduce-scatter.34.cloned.1.call-start = ((), (), s32[]{:S(2)}) async-start(), calls=%async_computation.30 | async-start | bytes 3932160
  1875.9 77.6 %copy-start.65 = (s32[2048]{0:T(1024)S(1)}, s32[2048]{0:T(1024)}, u32[]{:S(2)}) copy-start(s32[2048]{0:T(1024)} %copy-done.64) | copy-start | bytes 24580
  1875.9 77.6 %copy-start.78 = (f32[2048]{0:T(1024)S(1)}, f32[2048]{0:T(1024)}, u32[]{:S(2)}) copy-start(f32[2048]{0:T(1024)} %copy-done.77) | copy-start | bytes 24580
  1875.9 77.5 %copy-start.80 = (f32[2048]{0:T(1024)S(1)}, f32[2048]{0:T(1024)}, u32[]{:S(2)}) copy-start(f32[2048]{0:T(1024)} %copy-done.79) | copy-start | bytes 24580
  1875.9 359.0 %reduce-scatter.32.cloned.1.call-start = ((), (), s32[]{:S(2)}) async-start(), calls=%async_computation.28 | async-start | bytes 20480000 | tf_op jit(solution)/shard_map/reduce_scatter | solution.py:687
  2006.9 79.2 %copy-start.83 = (f32[256]{0:T(256)S(1)}, f32[256]{0:T(256)}, u32[]{:S(2)}) copy-start(f32[256]{0:T(256)} %get-tuple-element.155) | copy-start | bytes 3076
  2006.9 79.2 %copy-start.84 = (f32[256]{0:T(256)S(1)}, f32[256]{0:T(256)}, u32[]{:S(2)}) copy-start(f32[256]{0:T(256)} %get-tuple-element.153) | copy-start | bytes 3076
  2006.9 79.2 %copy-start.88 = (f32[256]{0:T(256)S(1)}, f32[256]{0:T(256)}, u32[]{:S(2)}) copy-start(f32[256]{0:T(256)} %get-tuple-element.151) | copy-start | bytes 3076
  2301.9 20.6 copy-start.30
  2337.9 20.2 copy-start.60
  2337.9 20.2 copy-start.61
  (52 other events, 261.1 us)
Sparse Core Ops, SparseCore 0:
  13.2 156.7 all-gather.13
  202.7 89.5 reduce-scatter.19
  294.7 24.9 all-gather.19
  322.0 43.9 all-gather.17
  368.0 82.4 all-gather.15
  521.6 87.7 reduce-scatter.21
  611.8 39.6 all-gather.25
  653.9 64.6 all-gather.23
  720.8 82.4 all-gather.21
  835.1 87.7 reduce-scatter.23
  940.4 80.7 all-gather.27
  1142.0 87.8 reduce-scatter.25
  1249.5 80.7 all-gather.29
  1371.8 87.8 reduce-scatter.27
  1481.4 80.7 all-gather.31
  1657.3 87.7 reduce-scatter.29
  1764.6 80.7 all-gather.33
  1848.8 39.4 reduce-scatter.39
  1891.9 64.7 reduce-scatter.37
  1960.0 41.9 all-reduce.10
  2005.7 27.7 reduce-scatter.35
  2037.1 43.9 reduce-scatter.33
  2084.3 150.6 reduce-scatter.31

commit v2 on v1

--- a/solution.py
+++ b/solution.py
@@ -1,3 +1,5 @@
+import functools
+
 import jax
 import jax.numpy as jnp
 from jax import lax
@@ -22,35 +24,6 @@
 BETA_TWO = 0.95
 ADAM_EPSILON = 1e-08
 WEIGHT_DECAY = 0.01
-
-
-def head_total(values):
-    return lax.psum(values, "head")
-
-
-def spread(rows):
-    return lax.all_gather(rows, "head", axis=1, tiled=True)
-
-
-def spread_grad(rows):
-    return lax.all_gather(rows, "head", axis=1, tiled=True)
-
-
-def fold(partial_value):
-    low = partial_value.astype(jnp.bfloat16)
-    return lax.psum_scatter(low, "head", scatter_dimension=1, tiled=True).astype(jnp.float32)
-
-
-def norm_forward(inputs, gain_row):
-    scale = lax.rsqrt(head_total(jnp.sum(inputs * inputs, -1)) / D + EPSILON)
-    return ((inputs * scale[:, None] * gain_row).astype(jnp.bfloat16), scale)
-
-
-def norm_backward(inputs, scale, gain_row, upstream):
-    normed = inputs * scale[:, None]
-    weighted = upstream * gain_row
-    inner = head_total(jnp.sum(weighted * normed, -1)) / D
-    return (scale[:, None] * (weighted - normed * inner[:, None]), jnp.sum(upstream * normed, 0))
 
 
 CHUNK = 64
@@ -434,6 +407,442 @@
     )
 
 
+ROWS = 128
+MESH = pl.DeviceIdType.MESH
+
+
+def across(column, size):
+    return jnp.swapaxes(jnp.broadcast_to(column, (size, size)), 0, 1)[:8]
+
+
+def down(row, size, width):
+    turned = jnp.swapaxes(jnp.broadcast_to(row[:1], (size, size)), 0, 1)
+    return jnp.concatenate([turned] * (width // size), 1) if width > size else turned[:, :width]
+
+
+def transit_kernel(mode, turned, parts, *refs):
+    refs = list(refs)
+    left_hbm, right_ref, inputs_ref, gain_ref = refs[:4]
+    refs = refs[4:]
+    if mode == "norm":
+        own_ref, full_ref, scale_ref = refs[:3]
+        refs = refs[3:]
+    else:
+        given_scale_ref = refs[0]
+        added_ref = None
+        refs = refs[1:]
+        if mode == "grad_add":
+            added_ref = refs[0]
+            refs = refs[1:]
+        own_ref, full_ref, gain_grad_ref = refs[:3]
+        refs = refs[3:]
+    (
+        left_buf,
+        partial,
+        pair_out,
+        pair_in,
+        from_low,
+        from_high,
+        total,
+        sums_out,
+        sums_in,
+        left_sem,
+        pair_out_sem,
+        pair_in_sem,
+        low_out_sem,
+        low_in_sem,
+        high_out_sem,
+        high_in_sem,
+        sums_out_sem,
+        sums_in_sem,
+        up_out_sem,
+        up_in_sem,
+        down_out_sem,
+        down_in_sem,
+        twin_out_sem,
+        twin_in_sem,
+    ) = refs
+    places = parts // 2
+    tokens, size = own_ref.shape
+    chunks = tokens // ROWS
+    ring = partial.shape[0]
+    me = lax.axis_index("head")
+    core = lax.rem(me, 2)
+    spot = me // 2
+    twin = {"head": me + 1 - 2 * core}
+    upper = {"head": lax.rem(me + 2, parts)}
+    lower = {"head": lax.rem(me + parts - 2, parts)}
+
+    def rows_of(chunk):
+        return pl.ds(pl.multiple_of(chunk * ROWS, ROWS), ROWS)
+
+    def shard(index):
+        return pl.ds(pl.multiple_of(index * size, 128), size)
+
+    def remote(source, target, out_sem, in_sem, device):
+        return pltpu.make_async_remote_copy(
+            src_ref=source,
+            dst_ref=target,
+            send_sem=out_sem,
+            recv_sem=in_sem,
+            device_id=device,
+            device_id_type=MESH,
+        )
+
+    def left_copy(chunk):
+        return pltpu.make_async_copy(
+            left_hbm.at[rows_of(chunk)], left_buf.at[lax.rem(chunk, 2)], left_sem.at[lax.rem(chunk, 2)]
+        )
+
+    barrier = pltpu.get_barrier_semaphore()
+    for offset in range(1, parts):
+        pl.semaphore_signal(
+            barrier, inc=1, device_id={"head": lax.rem(me + offset, parts)}, device_id_type=MESH
+        )
+    left_copy(0).start()
+    if mode != "norm":
+        gain_grad_ref[...] = jnp.zeros_like(gain_grad_ref)
+    pl.semaphore_wait(barrier, parts - 1)
+
+    def valid(chunk):
+        return jnp.logical_and(chunk >= 0, chunk < chunks)
+
+    def pair_copy(chunk):
+        slot = lax.rem(chunk, ring)
+        return remote(
+            pair_out.at[slot], pair_in.at[slot], pair_out_sem.at[slot], pair_in_sem.at[slot], twin
+        )
+
+    def rise(chunk, place):
+        slot = lax.rem(chunk, ring)
+        part = from_low.at[slot, :, pl.ds((place + 1) * size, (places - 1 - place) * size)]
+        return remote(part, part, low_out_sem.at[slot], low_in_sem.at[slot], upper)
+
+    def fall(chunk, place):
+        slot = lax.rem(chunk, ring)
+        part = from_high.at[slot, :, pl.ds(0, place * size)]
+        return remote(part, part, high_out_sem.at[slot], high_in_sem.at[slot], lower)
+
+    def sums_copy(chunk, offset):
+        slot = lax.rem(chunk, ring)
+        return remote(
+            sums_out.at[slot],
+            sums_in.at[slot, offset - 1],
+            sums_out_sem.at[slot, offset - 1],
+            sums_in_sem.at[slot],
+            {"head": lax.rem(me + offset, parts)},
+        )
+
+    def climb(chunk, source, hop):
+        part = full_ref.at[rows_of(chunk), shard(2 * source + core)]
+        return remote(
+            part, part, up_out_sem.at[chunk, hop - 1], up_in_sem.at[chunk, hop - 1], upper
+        )
+
+    def sink(chunk, source, hop):
+        part = full_ref.at[rows_of(chunk), shard(2 * source + core)]
+        return remote(
+            part, part, down_out_sem.at[chunk, hop - 1], down_in_sem.at[chunk, hop - 1], lower
+        )
+
+    def mirror(chunk, source):
+        part = full_ref.at[rows_of(chunk), shard(2 * source + core)]
+        return remote(part, part, twin_out_sem.at[chunk, source], twin_in_sem.at[chunk], twin)
+
+    def relay(step):
+        for hop in range(1, places):
+            chunk = step - places - 1 - hop
+            source = spot - hop
+
+            @pl.when(jnp.logical_and(valid(chunk), source >= 0))
+            def _():
+                climb(chunk, source, hop).wait_recv()
+                if hop < places - 1:
+
+                    @pl.when(spot < places - 1)
+                    def _():
+                        climb(chunk, source, hop + 1).start()
+
+                mirror(chunk, source).start()
+
+            source_high = spot + hop
+
+            @pl.when(jnp.logical_and(valid(chunk), source_high < places))
+            def _():
+                sink(chunk, source_high, hop).wait_recv()
+                if hop < places - 1:
+
+                    @pl.when(spot > 0)
+                    def _():
+                        sink(chunk, source_high, hop + 1).start()
+
+                mirror(chunk, source_high).start()
+
+    def finish_shard(step):
+        chunk = step - places - 1
+
+        @pl.when(valid(chunk))
+        def _():
+            slot = lax.rem(chunk, ring)
+            rows = rows_of(chunk)
+            pltpu.make_async_copy(sums_in.at[slot], sums_in.at[slot], sums_in_sem.at[slot]).wait()
+            summed = sums_out[slot]
+            for offset in range(1, parts):
+                summed = summed + sums_in[slot, offset - 1]
+            gain = gain_ref[0:1, :]
+            if mode == "norm":
+                scale = lax.rsqrt(summed / D + EPSILON)
+                scale_ref[chunk] = scale
+                result = own_ref[rows, :] * down(scale, ROWS, size) * gain
+            else:
+                scale = down(given_scale_ref[chunk], ROWS, size)
+                normed = inputs_ref[rows, :] * scale
+                inner = down(summed / D, ROWS, size)
+                result = scale * (own_ref[rows, :] * gain - normed * inner)
+                if mode == "grad_add":
+                    result = result + added_ref[rows, :]
+                own_ref[rows, :] = result
+            full_ref[rows, shard(me)] = result.astype(jnp.bfloat16)
+            mirror(chunk, spot).start()
+
+            @pl.when(spot < places - 1)
+            def _():
+                climb(chunk, spot, 1).start()
+
+            @pl.when(spot > 0)
+            def _():
+                sink(chunk, spot, 1).start()
+
+    def add_pair(step):
+        chunk = step - 1
+
+        @pl.when(valid(chunk))
+        def _():
+            slot = lax.rem(chunk, ring)
+            pair_copy(chunk).wait_recv()
+            partial[slot] = partial[slot] + pair_in[slot].astype(jnp.float32)
+
+    def pass_on(step):
+        for place in range(places):
+            if place < places - 1:
+                up_chunk = step - 1 - place
+
+                @pl.when(jnp.logical_and(valid(up_chunk), spot == place))
+                def _():
+                    slot = lax.rem(up_chunk, ring)
+                    above = pl.ds((place + 1) * size, (places - 1 - place) * size)
+                    values = partial[slot, :, above]
+                    if place > 0:
+                        rise(up_chunk, place - 1).wait_recv()
+                        values = values + from_low[slot, :, above].astype(jnp.float32)
+                    from_low[slot, :, above] = values.astype(jnp.bfloat16)
+                    rise(up_chunk, place).start()
+
+            if place > 0:
+                down_chunk = step - places + place
+
+                @pl.when(jnp.logical_and(valid(down_chunk), spot == place))
+                def _():
+                    slot = lax.rem(down_chunk, ring)
+                    below = pl.ds(0, place * size)
+                    values = partial[slot, :, below]
+                    if place < places - 1:
+                        fall(down_chunk, place + 1).wait_recv()
+                        values = values + from_high[slot, :, below].astype(jnp.float32)
+                    from_high[slot, :, below] = values.astype(jnp.bfloat16)
+                    fall(down_chunk, place).start()
+
+    def settle(step):
+        chunk = step - places - 1
+
+        @pl.when(valid(chunk))
+        def _():
+            pair_copy(chunk).wait_send()
+            for place in range(places):
+
+                @pl.when(spot == place)
+                def _():
+                    if place < places - 1:
+                        rise(chunk, place).wait_send()
+                    if place > 0:
+                        fall(chunk, place).wait_send()
+
+            for offset in range(1, parts):
+                sums_copy(chunk, offset).wait_send()
+
+    def sum_shard(step):
+        chunk = step - places
+
+        @pl.when(valid(chunk))
+        def _():
+            slot = lax.rem(chunk, ring)
+            rows = rows_of(chunk)
+            mine = shard(spot)
+
+            @pl.when(spot == places - 1)
+            def _():
+                rise(chunk, places - 2).wait_recv()
+
+            @pl.when(spot == 0)
+            def _():
+                fall(chunk, 1).wait_recv()
+
+            total[...] = partial[slot, :, mine]
+
+            @pl.when(spot > 0)
+            def _():
+                total[...] += from_low[slot, :, mine].astype(jnp.float32)
+
+            @pl.when(spot < places - 1)
+            def _():
+                total[...] += from_high[slot, :, mine].astype(jnp.float32)
+
+            value = total[...]
+            if mode == "norm":
+                value = value + inputs_ref[rows, :]
+                column = jnp.sum(value * value, 1, keepdims=True)
+            else:
+                scale = down(given_scale_ref[chunk], ROWS, size)
+                normed = inputs_ref[rows, :] * scale
+                gain_grad_ref[0:1, :] += jnp.sum(value * normed, 0, keepdims=True)
+                column = jnp.sum(value * gain_ref[0:1, :] * normed, 1, keepdims=True)
+            own_ref[rows, :] = value
+            sums_out[slot] = across(column, ROWS)
+            for offset in range(1, parts):
+                sums_copy(chunk, offset).start()
+
+    def produce(step):
+        chunk = step
+
+        @pl.when(valid(chunk))
+        def _():
+            slot = lax.rem(chunk, ring)
+            half = lax.rem(chunk, 2)
+            left_copy(chunk).wait()
+
+            @pl.when(chunk + 1 < chunks)
+            def _():
+                left_copy(chunk + 1).start()
+
+            def term(index):
+                if turned:
+                    return dot_abt(left_buf[half], right_ref[shard(index), :])
+                return dot_ab(left_buf[half], right_ref[:, shard(index)])
+
+            for place in range(places):
+                lanes = pl.ds(place * size, size)
+                pair_out[slot, :, lanes] = term(2 * place + 1 - core).astype(jnp.bfloat16)
+            pair_copy(chunk).start()
+            for place in range(places):
+                lanes = pl.ds(place * size, size)
+                partial[slot, :, lanes] = term(2 * place + core)
+
+    def close(step):
+        chunk = step - 2 * places - 1
+
+        @pl.when(valid(chunk))
+        def _():
+            arrived = full_ref.at[rows_of(chunk), pl.ds(0, places * size)]
+            pltpu.make_async_copy(arrived, arrived, twin_in_sem.at[chunk]).wait()
+            for source in range(places):
+                mirror(chunk, source).wait_send()
+            for hop in range(1, places):
+                source = spot - hop + 1
+
+                @pl.when(jnp.logical_and(source >= 0, spot < places - 1))
+                def _():
+                    climb(chunk, source, hop).wait_send()
+
+                source_high = spot + hop - 1
+
+                @pl.when(jnp.logical_and(source_high < places, spot > 0))
+                def _():
+                    sink(chunk, source_high, hop).wait_send()
+
+    def advance(step, carried):
+        relay(step)
+        finish_shard(step)
+        add_pair(step)
+        pass_on(step)
+        settle(step)
+        sum_shard(step)
+        produce(step)
+        close(step)
+        return carried
+
+    lax.fori_loop(0, chunks + 2 * places + 1, advance, 0)
+
+
+def transit(mode, number, parts, left, right, inputs, gain, scale=None, added=None, turned=False):
+    tokens, size = inputs.shape
+    depth = left.shape[1]
+    width = parts * size
+    chunks = tokens // ROWS
+    places = parts // 2
+    ring = min(chunks, 2 * places)
+    dma = pltpu.SemaphoreType.DMA
+    low = jnp.bfloat16
+    vmem = pl.BlockSpec(memory_space=pltpu.VMEM)
+    operands = [left, right, inputs, gain]
+    specs = [pl.BlockSpec(memory_space=pl.ANY), vmem, vmem, vmem]
+    shapes = [
+        jax.ShapeDtypeStruct((tokens, size), jnp.float32),
+        jax.ShapeDtypeStruct((tokens, width), low),
+    ]
+    if mode == "norm":
+        shapes.append(jax.ShapeDtypeStruct((chunks, 8, ROWS), jnp.float32))
+    else:
+        operands.append(scale)
+        specs.append(vmem)
+        if mode == "grad_add":
+            operands.append(added)
+            specs.append(vmem)
+        shapes.append(jax.ShapeDtypeStruct((8, size), jnp.float32))
+    span = places * size
+    hops = max(places - 1, 1)
+    return pl.pallas_call(
+        functools.partial(transit_kernel, mode, turned, parts),
+        in_specs=specs,
+        out_specs=[vmem] * len(shapes),
+        out_shape=shapes,
+        scratch_shapes=[
+            pltpu.VMEM((2, ROWS, depth), low),
+            pltpu.VMEM((ring, ROWS, span), jnp.float32),
+            pltpu.VMEM((ring, ROWS, span), low),
+            pltpu.VMEM((ring, ROWS, span), low),
+            pltpu.VMEM((ring, ROWS, span), low),
+            pltpu.VMEM((ring, ROWS, span), low),
+            pltpu.VMEM((ROWS, size), jnp.float32),
+            pltpu.VMEM((ring, 8, ROWS), jnp.float32),
+            pltpu.VMEM((ring, parts - 1, 8, ROWS), jnp.float32),
+            dma((2,)),
+            dma((ring,)),
+            dma((ring,)),
+            dma((ring,)),
+            dma((ring,)),
+            dma((ring,)),
+            dma((ring,)),
+            dma((ring, parts - 1)),
+            dma((ring,)),
+            dma((chunks, hops)),
+            dma((chunks, hops)),
+            dma((chunks, hops)),
+            dma((chunks, hops)),
+            dma((chunks, places)),
+            dma((chunks,)),
+        ],
+        compiler_params=pltpu.CompilerParams(
+            collective_id=number, has_side_effects=True, vmem_limit_bytes=60 * 1024 * 1024
+        ),
+        cost_estimate=pl.CostEstimate(
+            flops=2 * tokens * depth * width,
+            bytes_accessed=2 * (tokens * depth + depth * width + tokens * width),
+            transcendentals=0,
+        ),
+        name="transit_" + mode,
+    )(*operands)
+
+
 def shampoo(tile_w, tile_g, left, right, left_root, right_root):
     low_g = tile_g.astype(jnp.bfloat16)
 
@@ -478,26 +887,24 @@
 
 def layer_forward(token_ids, targets, valid, resets, weights, inner_init, gains, head_index):
     w_qkv, w_out, w_gu, w_down, table = weights
+    parts = lax.axis_size("head")
     vocab_part = table.shape[0]
+    tokens = token_ids.shape[0]
     columns = jnp.arange(vocab_part, dtype=jnp.int32)
     local_ids = token_ids - head_index * vocab_part
-    inside = (local_ids >= 0) & (local_ids < vocab_part)
-    looked = jnp.take(table, jnp.clip(local_ids, 0, vocab_part - 1), axis=0)
-    looked_rows = jnp.where(inside[:, None], looked.astype(jnp.float32), 0.0)
-    embedded = lax.psum_scatter(
-        looked_rows.astype(jnp.bfloat16), "head", scatter_dimension=1, tiled=True
-    ).astype(jnp.float32)
-    normed_one, scale_one = norm_forward(embedded, gains[0])
-    full_one = spread(normed_one)
+    id_onehot = (columns[None, :] == local_ids[:, None]).astype(jnp.bfloat16)
+    nothing = jnp.zeros((tokens, gains.shape[1]), jnp.float32)
+    embedded, full_one, scale_one = transit(
+        "norm", 1, parts, id_onehot, table, nothing, gains[0:1]
+    )
     mixed = jnp.dot(full_one, w_qkv, preferred_element_type=jnp.float32).astype(jnp.bfloat16)
-    tokens = mixed.shape[0]
     step_rate = jax.nn.sigmoid(gains[3:4]) / (8 * P_SIZE)
     masks = mixer_masks(resets, tokens)
     initial_pairs = pair_blocks(inner_init)
     inner_low, residue, states = mixer_forward(mixed, step_rate, initial_pairs, masks)
-    hidden_one = embedded + fold(jnp.dot(inner_low, w_out, preferred_element_type=jnp.float32))
-    normed_two, scale_two = norm_forward(hidden_one, gains[1])
-    full_two = spread(normed_two)
+    hidden_one, full_two, scale_two = transit(
+        "norm", 2, parts, inner_low, w_out, embedded, gains[1:2]
+    )
     gate_up = jnp.dot(full_two, w_gu, preferred_element_type=jnp.float32)
 
     def swiglu(paired):
@@ -506,9 +913,9 @@
 
     activated, act_pull = jax.vjp(swiglu, gate_up)
     act_low = activated.astype(jnp.bfloat16)
-    hidden_two = hidden_one + fold(jnp.dot(act_low, w_down, preferred_element_type=jnp.float32))
-    normed_end, scale_end = norm_forward(hidden_two, gains[2])
-    full_end = spread(normed_end)
+    hidden_two, full_end, scale_end = transit(
+        "norm", 3, parts, act_low, w_down, hidden_one, gains[2:3]
+    )
     logits = jnp.einsum("td,vd->tv", full_end, table, preferred_element_type=jnp.float32)
     peak = jnp.max(logits, -1)
     target_hits = columns[None, :] == (targets - head_index * vocab_part)[:, None]
@@ -528,6 +935,9 @@
     target_logit = jnp.sum(stats[:, 2], 0)
     totals = highest + jnp.log(exp_sum)
     counted = valid.astype(jnp.float32)
+    d_logits = (
+        (jnp.exp(logits - totals[:, None]) - target_hits.astype(jnp.float32)) * counted[:, None]
+    ).astype(jnp.bfloat16)
     kept = (
         embedded,
         scale_one,
@@ -542,11 +952,8 @@
         hidden_two,
         scale_end,
         full_end,
-        logits,
-        totals,
-        target_hits,
-        counted,
-        local_ids,
+        d_logits,
+        id_onehot,
     )
     return (jnp.sum((totals - target_logit) * counted), jnp.sum(counted), kept)
 
@@ -566,45 +973,36 @@
         hidden_two,
         scale_end,
         full_end,
-        logits,
-        totals,
-        target_hits,
-        counted,
-        local_ids,
+        d_logits,
+        id_onehot,
     ) = kept
     w_qkv, w_out, w_gu, w_down, table = weights
-    tokens = logits.shape[0]
-    d_logits = (
-        (jnp.exp(logits - totals[:, None]) - target_hits.astype(jnp.float32)) * counted[:, None]
-    ).astype(jnp.bfloat16)
+    parts = lax.axis_size("head")
+    d_two, d_down_in, gain_end = transit(
+        "grad", 4, parts, d_logits, table, hidden_two, gains[2:3], scale_end
+    )
     grad_table = jnp.einsum("tv,td->vd", d_logits, full_end, preferred_element_type=jnp.float32)
-    d_end = fold(jnp.dot(d_logits, table, preferred_element_type=jnp.float32))
-    d_two, gain_end = norm_backward(hidden_two, scale_end, gains[2], d_end)
-    d_down_in = spread_grad(d_two.astype(jnp.bfloat16))
-    grad_down = jnp.einsum("tf,td->fd", act_low, d_down_in, preferred_element_type=jnp.float32)
     d_act = jnp.einsum("td,fd->tf", d_down_in, w_down, preferred_element_type=jnp.float32)
     d_gate_up = act_pull(d_act)[0].astype(jnp.bfloat16)
+    d_one, d_out_in, gain_two = transit(
+        "grad_add", 5, parts, d_gate_up, w_gu, hidden_one, gains[1:2], scale_two, d_two, True
+    )
+    grad_down = jnp.einsum("tf,td->fd", act_low, d_down_in, preferred_element_type=jnp.float32)
     grad_gu = jnp.einsum("td,tc->dc", full_two, d_gate_up, preferred_element_type=jnp.float32)
-    d_two_norm = fold(jnp.einsum("tc,dc->td", d_gate_up, w_gu, preferred_element_type=jnp.float32))
-    d_middle, gain_two = norm_backward(hidden_one, scale_two, gains[1], d_two_norm)
-    d_one = d_two + d_middle
-    d_out_in = spread_grad(d_one.astype(jnp.bfloat16))
-    grad_out = jnp.einsum("tc,td->cd", inner_low, d_out_in, preferred_element_type=jnp.float32)
     d_inner = jnp.einsum("td,cd->tc", d_out_in, w_out, preferred_element_type=jnp.float32)
     d_mixed, grad_pairs, grad_step = mixer_backward(*inner_kept, d_inner)
     grad_init = head_blocks(grad_pairs)
     gate = jax.nn.sigmoid(gains[3])
     grad_rate = grad_step[0] * gate * (1.0 - gate) / (8 * P_SIZE)
+    _, d_embed, gain_one = transit(
+        "grad_add", 6, parts, d_mixed, w_qkv, embedded, gains[0:1], scale_one, d_one, True
+    )
+    grad_out = jnp.einsum("tc,td->cd", inner_low, d_out_in, preferred_element_type=jnp.float32)
     grad_qkv = jnp.einsum("td,tc->dc", full_one, d_mixed, preferred_element_type=jnp.float32)
-    d_one_norm = fold(jnp.einsum("tc,dc->td", d_mixed, w_qkv, preferred_element_type=jnp.float32))
-    d_base, gain_one = norm_backward(embedded, scale_one, gains[0], d_one_norm)
-    d_embed = spread_grad((d_one + d_base).astype(jnp.bfloat16))
-    columns = jnp.arange(table.shape[0], dtype=jnp.int32)
-    id_onehot = (columns[None, :] == local_ids[:, None]).astype(jnp.bfloat16)
     grad_table = grad_table + jnp.einsum(
         "tv,td->vd", id_onehot, d_embed, preferred_element_type=jnp.float32
     )
-    grad_gains = jnp.stack([gain_one, gain_two, gain_end, grad_rate], 0)
+    grad_gains = jnp.stack([gain_one[0], gain_two[0], gain_end[0], grad_rate], 0)
     return (grad_qkv, grad_out, grad_gu, grad_down, grad_table, grad_init, grad_gains)
 
 

time: 2370 us -> 2270 us (0.958)
  Pallas kernels: 127 us -> 1160 us
  waiting for transfers between devices: 1370 us -> 348 us
  matrix products: 392 us -> 307 us
  blocking collectives: 147 us -> 63.8 us
  local copies, waits for them, and re-layouts: 164 us -> 195 us
    pallas_call x0 -> x6, Pallas kernels: none -> 1040 us  [transit(): pl.pallas_call(functools.partial(transit_kernel, mode, turned, parts), in...]
    reduce_scatter x6 -> x0, waiting for transfers between devices: 520 us -> none  [the longest x5 434 us: fold(): lax.psum_scatter(low, 'head', scatter_dimension=1, tiled=True)]
    all_gather x6 -> x0, waiting for transfers between devices: 360 us -> none  [the longest x3 216 us: spread(): return lax.all_gather(rows, 'head', axis=1, tiled=True)]
    dot_general x5 -> x0, matrix products: 89.8 us -> none  [the longest x1 48.5 us: layer_backward(): d_end = fold(jnp.dot(d_logits, table, preferred_element_type=jnp.float32))]
    psum x6 -> x0, blocking collectives: 83.4 us -> none  [head_total(): return lax.psum(values, 'head')]
    unnamed x27 -> x15, waiting for transfers between devices: 66.5 us -> 0.23 us
    all_gather x1, waiting for transfers between devices: 156 us -> 99.6 us  [shards(): lax.all_gather(emb_master.astype(jnp.bfloat16), 'dp', axis=1, tiled=True)]
    dot_general x0 -> x2, local copies, waits for them, and re-layouts: none -> 38.9 us  [the longest x1 30.7 us: layer_forward(): jnp.einsum('td,vd->tv', full_end, table, preferred_element_type=jnp.float32)]
  transfers between devices with their start and end apart: 23 -> 11, of which waited for: 19 -> 6; matrix products, arithmetic and copies ran while one was open for 14% -> 16% of each run, Pallas kernels for 0% -> 8%
where the time goes in v2:
time: 2270 us; the launch traced here: 2260 us
  Pallas kernels  1160 us (51%)
  waiting for transfers between devices  348 us (15%)
  matrix products  307 us (14%)
  local copies, waits for them, and re-layouts  195 us (9%)
  other arithmetic  161 us (7%)
  blocking collectives  63.8 us (3%)
  between operations  23.7 us (1%)
    pallas_call x6, Pallas kernels, transit(): pl.pallas_call(functools.partial(transit_kernel, mode, turned, parts), in...  1040 us
    reduce_scatter x1, waiting for transfers between devices, shards(): lax.psum_scatter(grad_table.astype(low), 'dp', scatter_dimension=1, tiled...  113 us
    all_gather x1, waiting for transfers between devices, shards(): lax.all_gather(emb_master.astype(jnp.bfloat16), 'dp', axis=1, tiled=True)  99.6 us
    dot_general x1, matrix products, layer_backward(): jnp.einsum('tv,td->vd', id_onehot, d_embed, preferred_element_type=jnp.fl...  77 us
    pallas_call x1, Pallas kernels, mixer_backward(): pl.pallas_call(mixer_backward_kernel, grid=(chunks,), in_specs=[rows(3 *...  76.9 us
    all_gather x1, waiting for transfers between devices, shards(): lax.all_gather(gu_master.astype(jnp.bfloat16), 'dp', axis=0, tiled=True)  55.3 us
    pallas_call x1, Pallas kernels, mixer_forward(): pl.pallas_call(mixer_forward_kernel, grid=(chunks,), in_specs=[pl.BlockSp...  50 us
    dot_general x12, matrix products, product(): jnp.einsum(form, one.astype(jnp.bfloat16), two.astype(jnp.bfloat16), pref...  46.9 us
  transfers between devices with their start and end apart: 11, of which 6 were waited for; matrix products, arithmetic and copies ran while one was open for 16% of the time, Pallas kernels for 8%

profile of v2, /device:TPU:0, one launch (start us, length us, event | category | flops | bytes accessed | tf_op | source)
XLA Modules:
  0.0 2260.5 jit_solution(4150044627293788206)
XLA Ops:
  15.5 5.9 convert_element_type.217
  29.7 6.5 fusion.1.refs_0_
  36.2 3.6 all-gather.12.cloned.1.call-done
  45.2 38.4 %all-gather.16.cloned.1.call-done = bf16[4,688,512]{2,1,0:T(8,128)(2,1)} async-done(((bf16[1,688,512]{2,1,0:T(8,128)(2,1)}), bf16[4,688,512]{2,1,0:T(8,128)(2,1)}) %all-gather.16.cloned.1.call-update) | async-done | bytes 2818064 | tf_op jit(solution)/shard_map/all_gather | solution.py:1049
  83.6 4.1 gather_fusion.3
  91.8 38.2 %all-gather.10.cloned.1.call-done = bf16[4,512,3,256]{3,1,2,0:T(8,128)(2,1)} async-done(((bf16[1,512,3,256]{3,1,2,0:T(8,128)(2,1)}), bf16[4,512,3,256]{3,1,2,0:T(8,128)(2,1)}) %all-gather.10.cloned.1.call-update) | async-done | bytes 3145744 | tf_op jit(solution)/shard_map/all_gather | solution.py:1046
  130.0 4.3 gather_fusion
  134.3 4.6 copy.163
  141.7 55.3 %all-gather.14.cloned.1.call-done = bf16[4,512,2,688]{1,3,2,0:T(8,128)(2,1)} async-done(((bf16[1,512,2,688]{1,3,2,0:T(8,128)(2,1)}), bf16[4,512,2,688]{1,3,2,0:T(8,128)(2,1)}) %all-gather.14.cloned.1.call-update) | async-done | bytes 5636112 | tf_op jit(solution)/shard_map/all_gather | solution.py:1048
  197.0 6.0 gather_fusion.2
  203.0 16.5 copy.164
  219.5 13.6 reshape.807
  233.1 5.9 fusion.162
  239.0 8.2 copy.128
  247.2 5.9 broadcast_select_fusion.refs_1_
  253.1 99.6 %all-gather.8.cloned.1.call-done.refs_1_ = bf16[4000,2048]{1,0:T(8,128)(2,1)} async-done(((bf16[4000,512]{1,0:T(8,128)(2,1)}), bf16[4000,2048]{1,0:T(8,128)(2,1)}) %all-gather.8.cloned.1.call-update) | async-done | bytes 16384016 | tf_op jit(solution)/shard_map/all_gather | solution.py:1050
  354.2 176.8 %transit_norm.3 = (f32[2048,256]{1,0:T(8,128)}, bf16[2048,2048]{1,0:T(8,128)(2,1)}, f32[16,8,128]{2,1,0:T(8,128)}) custom-call(bf16[2048,4000]{1,0:T(8,128)(2,1)} %fusion.1.refs_0_, bf16[4000,2048]{1,0:T(8,128)(2,1)} %all-gather.8.cloned.1.call-done.refs_1_, f32[2048,256]{1,0:T(8,128)} %broadcast_in_dim.135.refs_2_, f32[1,256]{1,0:T(1,128)} %get-tuple-element.203.refs_3_), custom_call_target="tpu_custom_call" | custom-call | flops 33554432000 | bytes 41156608 | tf_op jit(solution)/shard_map/transit_norm/pallas_call | solution.py:803
  531.0 10.0 convolution_convert_fusion.qkv_ref
  541.8 50.0 %inner_forward.1 = (bf16[2048,256]{1,0:T(8,128)(2,1)S(1)}, f32[2048,256]{1,0:T(8,128)S(1)}, f32[32,2,128,128]{3,2,1,0:T(8,128)S(1)}) custom-call(bf16[2048,768]{1,0:T(8,128)(2,1)S(1)} %convolution_convert_fusion.qkv_ref, f32[1,256]{1,0:T(1,128)S(1)} %get-tuple-element.201.rate_ref, f32[2,128,128]{2,1,0:T(8,128)S(1)} %select_maximum_fusion.initial_ref, ...), custom_call_target="tpu_custom_call" | custom-call | tf_op jit(solution)/shard_map/inner_forward/pallas_call | solution.py:323
  597.8 169.2 %transit_norm.4 = (f32[2048,256]{1,0:T(8,128)}, bf16[2048,2048]{1,0:T(8,128)(2,1)}, f32[16,8,128]{2,1,0:T(8,128)}) custom-call(bf16[2048,256]{1,0:T(8,128)(2,1)} %copy-done.9, bf16[256,2048]{1,0:T(8,128)(2,1)} %bitcast.345, f32[2048,256]{1,0:T(8,128)} %get-tuple-element.53.refs_2_, f32[1,256]{1,0:T(1,128)} %get-tuple-element.200.refs_3_), custom_call_target="tpu_custom_call" | custom-call | flops 2147483648 | bytes 10485760 | tf_op jit(solution)/shard_map/transit_norm/pallas_call | solution.py:803
  767.0 17.7 fusion.6
  784.7 3.5 fusion.14.refs_0_
  790.1 170.4 %transit_norm.5 = (f32[2048,256]{1,0:T(8,128)}, bf16[2048,2048]{1,0:T(8,128)(2,1)}, f32[16,8,128]{2,1,0:T(8,128)}) custom-call(bf16[2048,688]{1,0:T(8,128)(2,1)} %fusion.14.refs_0_, bf16[688,2048]{1,0:T(8,128)(2,1)} %bitcast.343, f32[2048,256]{1,0:T(8,128)} %get-tuple-element.55.refs_2_, f32[1,256]{1,0:T(1,128)} %get-tuple-element.199.refs_3_), custom_call_target="tpu_custom_call" | custom-call | flops 5771362304 | bytes 14024704 | tf_op jit(solution)/shard_map/transit_norm/pallas_call | solution.py:803
  960.6 42.1 %fusion.134 = (f32[2048]{0:T(1024)S(1)}, f32[2048,4000]{0,1:T(8,128)}) fusion(bf16[2048,2048]{1,0:T(8,128)(2,1)} %get-tuple-element.56, bf16[4000,2048]{1,0:T(8,128)(2,1)} %all-gather.8.cloned.1.call-done.refs_1_), kind=kOutput, calls=%fused_computation.250 | convolution fusion | flops 33562621952 | bytes 57548800 | tf_op jit(solution)/shard_map/td,vd->tv/dot_general | solution.py:919
  1002.6 30.7 %copy.132 = f32[2048,4000]{1,0:T(8,128)} copy(f32[2048,4000]{0,1:T(8,128)} %get-tuple-element.215) | data formatting | bytes 65536000 | tf_op jit(solution)/shard_map/td,vd->tv/dot_general | solution.py:919
  1033.4 16.0 exponential_reduce_fusion
  1049.4 15.4 select_reduce_fusion
  1064.9 14.2 all-gather.1
  1080.0 14.0 multiply_convert_fusion.refs_0_
  1094.0 174.7 %transit_grad.1 = (f32[2048,256]{1,0:T(8,128)}, bf16[2048,2048]{1,0:T(8,128)(2,1)}, f32[8,256]{1,0:T(8,128)}) custom-call(bf16[2048,4000]{1,0:T(8,128)(2,1)} %multiply_convert_fusion.refs_0_, bf16[4000,2048]{1,0:T(8,128)(2,1)} %all-gather.8.cloned.1.call-done.refs_1_, f32[2048,256]{1,0:T(8,128)} %get-tuple-element.60.refs_2_, ...), custom_call_target="tpu_custom_call" | custom-call | flops 33554432000 | bytes 41156608 | tf_op jit(solution)/shard_map/transit_grad/pallas_call | solution.py:803
  1268.7 16.9 multiply_bitcast_fusion
  1285.6 7.9 add_convert_fusion.1
  1293.6 8.3 copy.138
  1301.9 8.3 copy.139.refs_0_
  1310.2 173.0 %transit_grad_add.2 = (f32[2048,256]{1,0:T(8,128)}, bf16[2048,2048]{1,0:T(8,128)(2,1)}, f32[8,256]{1,0:T(8,128)}) custom-call(bf16[2048,1376]{1,0:T(8,128)(2,1)} %copy.139.refs_0_, bf16[2048,1376]{1,0:T(8,128)(2,1)} %broadcast_select_fusion.refs_1_, f32[2048,256]{1,0:T(8,128)} %get-tuple-element.55.refs_2_, f32[1,256]{1,0:T(1,128)} %get-tuple-element.200.refs_3_, ...), custom_call_target="tpu_custom_call" | custom-call | flops 11542724608 | bytes 19660800 | tf_op jit(solution)/shard_map/transit_grad_add/pallas_call | solution.py:803
  1483.3 6.2 fusion.135.upstream_ref
  1489.7 3.3 fusion.137
  1494.7 76.9 %inner_backward.1 = (bf16[2048,768]{1,0:T(8,128)(2,1)S(1)}, f32[2,128,128]{2,1,0:T(8,128)S(1)}, f32[1,256]{1,0:T(1,128)S(1)}) custom-call(bf16[2048,768]{1,0:T(8,128)(2,1)S(1)} %copy-done.1, f32[1,256]{1,0:T(1,128)S(1)} %get-tuple-element.201.rate_ref, f32[2,128,128]{2,1,0:T(8,128)S(1)} %select_maximum_fusion.initial_ref, ...), custom_call_target="tpu_custom_call" | custom-call | tf_op jit(solution)/shard_map/inner_backward/pallas_call | solution.py:364
  1577.6 12.4 copy.167
  1590.0 13.6 fusion.35
  1606.0 4.3 select_convert_fusion.2
  1610.5 10.4 fusion.136
  1620.9 4.9 reshape.711
  1625.8 3.9 copy.141
  1635.4 12.6 copy.165
  1648.0 17.6 fusion.18
  1665.5 6.2 gather_fusion.6
  1671.7 6.8 select_convert_fusion
  1678.5 171.4 %transit_grad_add.3 = (f32[2048,256]{1,0:T(8,128)}, bf16[2048,2048]{1,0:T(8,128)(2,1)}, f32[8,256]{1,0:T(8,128)}) custom-call(bf16[2048,768]{1,0:T(8,128)(2,1)} %copy-done.15, bf16[2048,768]{1,0:T(8,128)(2,1)} %broadcast_select_fusion.1.refs_1_, f32[2048,256]{1,0:T(8,128)} %get-tuple-element.53.refs_2_, f32[1,256]{1,0:T(1,128)} %get-tuple-element.203.refs_3_, ...), custom_call_target="tpu_custom_call" | custom-call | flops 6442450944 | bytes 14680064 | tf_op jit(solution)/shard_map/transit_grad_add/pallas_call | solution.py:803
  1850.5 77.0 %fusion = f32[4000,2048]{1,0:T(8,128)} fusion(bf16[2048,2048]{1,0:T(8,128)(2,1)} %get-tuple-element.69, s32[2048]{0:T(1024)S(1)} %copy-done.39), kind=kOutput, calls=%fused_computation.12 | convolution fusion | flops 33562624000 | bytes 41164800 | tf_op jit(solution)/shard_map/tv,td->vd/dot_general | solution.py:1002
  1927.5 45.1 %add_convert_fusion = bf16[4000,2048]{1,0:T(8,128)(2,1)} fusion(f32[4000,2048]{1,0:T(8,128)} %fusion, bf16[2048,4000]{1,0:T(8,128)(2,1)} %multiply_convert_fusion.refs_0_, bf16[2048,2048]{1,0:T(8,128)(2,1)} %get-tuple-element.56), kind=kOutput, calls=%fused_computation.14 | convolution fusion | flops 33570816000 | bytes 73924608 | tf_op jit(solution)/shard_map/tv,td->vd/dot_general | solution.py:984
  1972.7 3.2 copy.150
  1975.9 3.0 copy.152
  1982.9 10.1 all-reduce.8
  2010.2 112.5 %reduce-scatter.14.cloned.1.call-done = bf16[4000,512]{1,0:T(8,128)(2,1)} async-done(((bf16[4000,2048]{1,0:T(8,128)(2,1)}), bf16[4000,512]{1,0:T(8,128)(2,1)}) %reduce-scatter.14.cloned.1.call-update) | async-done | bytes 4096016 | tf_op jit(solution)/shard_map/reduce_scatter | solution.py:1085
  2122.7 4.9 fusion.9
  2128.9 39.5 %psum.39 = f32[]{:T(128)} all-reduce(f32[]{:T(128)S(6)} %add.319), channel_id=1, replica_groups=mesh['dp'=4,'head'=8] {'dp','head'}, use_global_device_ids=true, to_apply=%region_26.27 | all-reduce | flops 1 | bytes 8 | tf_op jit(solution)/shard_map/psum | solution.py:1093
  2179.9 5.2 multiply_subtract_fusion.1
  2188.1 3.0 copy.155
  2191.1 3.9 fusion.38
  2201.5 4.5 fusion.43
  2210.0 8.9 fusion.5
  2221.3 10.2 fusion.29
  2232.3 20.1 multiply_subtract_fusion
  (259 shorter events, 99.6 us)
Async XLA Ops:
  7.2 6.9 copy-start.20
  7.2 32.6 %all-gather.12.cloned.1.call-start = ((), (), s32[]{:S(2)}) async-start(), calls=%async_computation.7 | async-start | bytes 1310720 | tf_op jit(solution)/shard_map/all_gather | solution.py:1047
  9.2 74.3 %all-gather.16.cloned.1.call-start = ((), (), s32[]{:S(2)}) async-start(), calls=%async_computation.9 | async-start | bytes 3522560 | tf_op jit(solution)/shard_map/all_gather | solution.py:1049
  11.6 118.4 %all-gather.10.cloned.1.call-start = ((), (), s32[]{:S(2)}) async-start(), calls=%async_computation.6 | async-start | bytes 3932160 | tf_op jit(solution)/shard_map/all_gather | solution.py:1046
  14.0 183.0 %all-gather.14.cloned.1.call-start = ((), (), s32[]{:S(2)}) async-start(), calls=%async_computation.8 | async-start | bytes 7045120 | tf_op jit(solution)/shard_map/all_gather | solution.py:1048
  15.4 6.1 copy-start.42
  15.4 6.3 copy-start.52
  15.4 7.1 copy-start.40
  15.4 10.3 copy-start.30
  15.4 11.5 copy-start.43
  15.4 12.2 copy-start.45
  15.4 12.2 copy-start.46
  15.5 337.3 %all-gather.8.cloned.1.call-start = ((), (), s32[]{:S(2)}) async-start(), calls=%async_computation.5 | async-start | bytes 20480000 | tf_op jit(solution)/shard_map/all_gather | solution.py:1050
  21.4 1974.1 %all-reduce.11.cloned.1.call-start = ((), (), s32[]{:S(2)}) async-start(), calls=%async_computation.11 | async-start | bytes 262144 | tf_op jit(solution)/shard_map/psum | solution.py:1089
  541.3 50.5 %copy-start.2 = (f32[2048,128]{1,0:T(8,128)}, f32[2048,128]{1,0:T(8,128)S(1)}, u32[]{:S(2)}) copy-start(f32[2048,128]{1,0:T(8,128)S(1)} %broadcast_in_dim.141.first_ref) | copy-start | bytes 3145732
  541.7 56.2 %copy-start.4 = (f32[2048,128]{1,0:T(8,128)}, f32[2048,128]{1,0:T(8,128)S(1)}, u32[]{:S(2)}) copy-start(f32[2048,128]{1,0:T(8,128)S(1)} %broadcast_in_dim.142.last_ref) | copy-start | bytes 3145732
  541.8 56.1 %copy-start.13 = (f32[32,8,128]{2,1,0:T(8,128)}, f32[32,8,128]{2,1,0:T(8,128)S(1)}, u32[]{:S(2)}) copy-start(f32[32,8,128]{2,1,0:T(8,128)S(1)} %broadcast_in_dim.143.anew_ref) | copy-start | bytes 393220
  784.7 5.4 copy-start.19
  1033.4 16.0 copy-start.36
  1033.4 46.6 %slice-start = ((s8[33554432]{0:T(1024)(128)(4,1)}), s8[4194304]{0:T(1024)(128)(4,1)S(1)}, s32[]{:S(2)}) async-start(s8[33554432]{0:T(1024)(128)(4,1)} %bitcast.324), calls=%async_computation.16 | async-start | bytes 8388608
  1033.4 46.6 %slice-start.1 = ((s8[33554432]{0:T(1024)(128)(4,1)}), s8[4194304]{0:T(1024)(128)(4,1)S(1)}, s32[]{:S(2)}) async-start(s8[33554432]{0:T(1024)(128)(4,1)} %bitcast.324), calls=%async_computation.17 | async-start | bytes 8388608
  1033.4 46.6 %slice-start.2 = ((s8[33554432]{0:T(1024)(128)(4,1)}), s8[4194304]{0:T(1024)(128)(4,1)S(1)}, s32[]{:S(2)}) async-start(s8[33554432]{0:T(1024)(128)(4,1)} %bitcast.324), calls=%async_computation.18 | async-start | bytes 8388608
  1033.4 46.6 %slice-start.3 = ((s8[33554432]{0:T(1024)(128)(4,1)}), s8[4194304]{0:T(1024)(128)(4,1)S(1)}, s32[]{:S(2)}) async-start(s8[33554432]{0:T(1024)(128)(4,1)} %bitcast.324), calls=%async_computation.19 | async-start | bytes 8388608
  1049.4 29.9 %copy-start.41 = (s32[2048]{0:T(1024)S(1)}, s32[2048]{0:T(1024)}, u32[]{:S(2)}) copy-start(s32[2048]{0:T(1024)} %param.36) | copy-start | bytes 24580
  1049.4 30.6 %slice-start.4 = ((s8[33554432]{0:T(1024)(128)(4,1)}), s8[4194304]{0:T(1024)(128)(4,1)S(1)}, s32[]{:S(2)}) async-start(s8[33554432]{0:T(1024)(128)(4,1)} %bitcast.324), calls=%async_computation.20 | async-start | bytes 8388608
  1049.4 30.6 %slice-start.5 = ((s8[33554432]{0:T(1024)(128)(4,1)}), s8[4194304]{0:T(1024)(128)(4,1)S(1)}, s32[]{:S(2)}) async-start(s8[33554432]{0:T(1024)(128)(4,1)} %bitcast.324), calls=%async_computation.21 | async-start | bytes 8388608
  1049.4 30.6 %slice-start.6 = ((s8[33554432]{0:T(1024)(128)(4,1)}), s8[4194304]{0:T(1024)(128)(4,1)S(1)}, s32[]{:S(2)}) async-start(s8[33554432]{0:T(1024)(128)(4,1)} %bitcast.324), calls=%async_computation.22 | async-start | bytes 8388608
  1049.4 30.6 %slice-start.7 = ((s8[33554432]{0:T(1024)(128)(4,1)}), s8[4194304]{0:T(1024)(128)(4,1)S(1)}, s32[]{:S(2)}) async-start(s8[33554432]{0:T(1024)(128)(4,1)} %bitcast.324), calls=%async_computation.23 | async-start | bytes 8388608
  1049.4 30.6 %copy-start.37 = (f32[2048]{0:T(1024)S(1)}, f32[2048]{0:T(1024)}, u32[]{:S(2)}) copy-start(f32[2048]{0:T(1024)} %convert_element_type.229) | copy-start | bytes 24580
  1483.3 6.2 copy-start.10
  1483.3 6.4 copy-start.18
  1489.7 3.4 copy-start.1
  1489.7 3.4 copy-start.3
  1489.7 3.4 copy-start.5
  1489.7 4.1 copy-start.7
  1489.7 4.4 copy-start.8
  1489.7 5.0 copy-start.12
  1489.7 5.0 copy-start.14
  1494.7 81.5 %copy-start.51 = (pred[4]{0:T(512)(128)(4,1)S(1)}, pred[4]{0:T(512)(128)(4,1)}, u32[]{:S(2)}) copy-start(pred[4]{0:T(512)(128)(4,1)} %compare_and_fusion.6) | copy-start | bytes 16
  1574.1 424.3 %reduce-scatter.18.cloned.1.call-start = ((), (), s32[]{:S(2)}) async-start(), calls=%async_computation.13 | async-start | bytes 1310720
  1590.0 410.2 %reduce-scatter.22.cloned.1.call-start = ((), (), s32[]{:S(2)}) async-start(), calls=%async_computation.15 | async-start | bytes 3522560
  1606.0 4.4 copy-start.54
  1606.0 4.5 copy-start.16
  1610.4 391.8 %reduce-scatter.16.cloned.1.call-start = ((), (), s32[]{:S(2)}) async-start(), calls=%async_computation.12 | async-start | bytes 3932160
  1635.3 370.8 %reduce-scatter.20.cloned.1.call-start = ((), (), s32[]{:S(2)}) async-start(), calls=%async_computation.14 | async-start | bytes 7045120
  1849.9 272.8 %reduce-scatter.14.cloned.1.call-start = ((), (), s32[]{:S(2)}) async-start(), calls=%async_computation.10 | async-start | bytes 20480000 | tf_op jit(solution)/shard_map/reduce_scatter | solution.py:1085
  1972.7 6.2 copy-start.21
  1972.7 10.2 copy-start.49
  2002.2 169.7 %copy-start.24 = (bf16[1,688,512]{2,1,0:T(8,128)(2,1)S(1)}, bf16[1,688,512]{2,1,0:T(8,128)(2,1)}, u32[]{:S(2)}) copy-start(bf16[1,688,512]{2,1,0:T(8,128)(2,1)} %reduce-scatter.22.cloned.1.call-done) | copy-start | bytes 2113540
  2171.9 5.6 copy-start.28
  2171.9 5.7 copy-start.27
  2172.7 28.8 %copy-start.17 = (f32[1,688,512]{2,1,0:T(8,128)}, f32[1,688,512]{2,1,0:T(8,128)S(1)}, u32[]{:S(2)}) copy-start(f32[1,688,512]{2,1,0:T(8,128)S(1)} %convert_multiply_fusion.6) | copy-start | bytes 4227076
  2172.7 6.3 copy-start.33
  2177.6 41.3 %copy-start.22 = (f32[1,256,512]{2,1,0:T(8,128)}, f32[1,256,512]{2,1,0:T(8,128)S(1)}, u32[]{:S(2)}) copy-start(f32[1,256,512]{2,1,0:T(8,128)S(1)} %convert_multiply_fusion.8) | copy-start | bytes 1572868
  2191.1 9.8 copy-start.44
  2191.1 9.8 copy-start.47
  2191.1 9.8 copy-start.48
  2200.9 5.1 copy-start.23
  2210.0 8.9 copy-start.26
  2210.0 8.9 copy-start.29
  2221.3 10.2 copy-start.31
  2221.3 10.2 copy-start.32
  2221.3 10.2 copy-start.34
  2221.3 10.2 copy-start.35
  (11 other events, 19.3 us)
Sparse Core Ops, SparseCore 0:
  10.5 29.3 all-gather.11
  42.3 41.2 all-gather.15
  86.0 43.9 all-gather.9
  132.3 64.6 all-gather.13
  198.7 154.0 all-gather.7
  1574.2 40.4 all-reduce.10
  1618.5 27.6 reduce-scatter.17
  1649.8 41.2 reduce-scatter.21
  1694.7 43.8 reduce-scatter.15
  1850.0 63.5 reduce-scatter.19
  1972.8 149.8 reduce-scatter.13

commit v3 on v2

--- a/solution.py
+++ b/solution.py
@@ -408,6 +408,7 @@
 
 
 ROWS = 128
+LAG = 2
 MESH = pl.DeviceIdType.MESH
 
 
@@ -420,58 +421,28 @@
     return jnp.concatenate([turned] * (width // size), 1) if width > size else turned[:, :width]
 
 
-def transit_kernel(mode, turned, parts, *refs):
-    refs = list(refs)
-    left_hbm, right_ref, inputs_ref, gain_ref = refs[:4]
-    refs = refs[4:]
-    if mode == "norm":
-        own_ref, full_ref, scale_ref = refs[:3]
-        refs = refs[3:]
-    else:
-        given_scale_ref = refs[0]
-        added_ref = None
-        refs = refs[1:]
-        if mode == "grad_add":
-            added_ref = refs[0]
-            refs = refs[1:]
-        own_ref, full_ref, gain_grad_ref = refs[:3]
-        refs = refs[3:]
-    (
-        left_buf,
-        partial,
-        pair_out,
-        pair_in,
-        from_low,
-        from_high,
-        total,
-        sums_out,
-        sums_in,
-        left_sem,
-        pair_out_sem,
-        pair_in_sem,
-        low_out_sem,
-        low_in_sem,
-        high_out_sem,
-        high_in_sem,
-        sums_out_sem,
-        sums_in_sem,
-        up_out_sem,
-        up_in_sem,
-        down_out_sem,
-        down_in_sem,
-        twin_out_sem,
-        twin_in_sem,
-    ) = refs
+def transit_kernel(mode, form, parts, slabs, names, *all_refs):
+    ref = dict(zip(names, all_refs))
+    full_ref, partial, total = ref["full"], ref["partial"], ref["total"]
+    pair_out, pair_in = ref["pair_out"], ref["pair_in"]
+    from_low, from_high = ref["from_low"], ref["from_high"]
     places = parts // 2
-    tokens, size = own_ref.shape
-    chunks = tokens // ROWS
+    cross = form in ("lookup", "table")
+    summing = mode != "plain"
+    size = total.shape[1]
     ring = partial.shape[0]
     me = lax.axis_index("head")
+    mine_dp = lax.axis_index("dp")
     core = lax.rem(me, 2)
     spot = me // 2
     twin = {"head": me + 1 - 2 * core}
     upper = {"head": lax.rem(me + 2, parts)}
     lower = {"head": lax.rem(me + parts - 2, parts)}
+    chunks = ref["up_in_sem"].shape[0]
+    sum_at = LAG * places
+    finish_at = sum_at + (LAG if summing else 0)
+    reach_at = finish_at + LAG * (places - 1)
+    close_at = reach_at + (2 * LAG if cross else LAG)
 
     def rows_of(chunk):
         return pl.ds(pl.multiple_of(chunk * ROWS, ROWS), ROWS)
@@ -490,8 +461,9 @@
         )
 
     def left_copy(chunk):
+        half = lax.rem(chunk, 2)
         return pltpu.make_async_copy(
-            left_hbm.at[rows_of(chunk)], left_buf.at[lax.rem(chunk, 2)], left_sem.at[lax.rem(chunk, 2)]
+            ref["left"].at[rows_of(chunk)], ref["left_buf"].at[half], ref["left_sem"].at[half]
         )
 
     barrier = pltpu.get_barrier_semaphore()
@@ -499,10 +471,21 @@
         pl.semaphore_signal(
             barrier, inc=1, device_id={"head": lax.rem(me + offset, parts)}, device_id_type=MESH
         )
-    left_copy(0).start()
-    if mode != "norm":
-        gain_grad_ref[...] = jnp.zeros_like(gain_grad_ref)
-    pl.semaphore_wait(barrier, parts - 1)
+    if cross:
+        for offset in range(1, slabs):
+            pl.semaphore_signal(
+                barrier,
+                inc=1,
+                device_id={"dp": lax.rem(mine_dp + offset, slabs)},
+                device_id_type=MESH,
+            )
+    if form != "lookup":
+        left_copy(0).start()
+    if mode in ("grad", "grad_add"):
+        ref["gain_grad"][...] = jnp.zeros_like(ref["gain_grad"])
+    if form == "table":
+        ref["table_grad"][...] = jnp.zeros_like(ref["table_grad"])
+    pl.semaphore_wait(barrier, parts - 1 + (slabs - 1 if cross else 0))
 
     def valid(chunk):
         return jnp.logical_and(chunk >= 0, chunk < chunks)
@@ -510,48 +493,117 @@
     def pair_copy(chunk):
         slot = lax.rem(chunk, ring)
         return remote(
-            pair_out.at[slot], pair_in.at[slot], pair_out_sem.at[slot], pair_in_sem.at[slot], twin
+            pair_out.at[slot],
+            pair_in.at[slot],
+            ref["pair_out_sem"].at[slot],
+            ref["pair_in_sem"].at[slot],
+            twin,
         )
 
     def rise(chunk, place):
         slot = lax.rem(chunk, ring)
         part = from_low.at[slot, :, pl.ds((place + 1) * size, (places - 1 - place) * size)]
-        return remote(part, part, low_out_sem.at[slot], low_in_sem.at[slot], upper)
+        return remote(part, part, ref["low_out_sem"].at[slot], ref["low_in_sem"].at[slot], upper)
 
     def fall(chunk, place):
         slot = lax.rem(chunk, ring)
         part = from_high.at[slot, :, pl.ds(0, place * size)]
-        return remote(part, part, high_out_sem.at[slot], high_in_sem.at[slot], lower)
+        return remote(part, part, ref["high_out_sem"].at[slot], ref["high_in_sem"].at[slot], lower)
 
     def sums_copy(chunk, offset):
         slot = lax.rem(chunk, ring)
         return remote(
-            sums_out.at[slot],
-            sums_in.at[slot, offset - 1],
-            sums_out_sem.at[slot, offset - 1],
-            sums_in_sem.at[slot],
+            ref["sums_out"].at[slot],
+            ref["sums_in"].at[slot, offset - 1],
+            ref["sums_out_sem"].at[slot, offset - 1],
+            ref["sums_in_sem"].at[slot],
             {"head": lax.rem(me + offset, parts)},
         )
 
+    def piece(chunk, source):
+        if cross:
+            return ref["stage"].at[rows_of(chunk), shard(source)]
+        return full_ref.at[rows_of(chunk), shard(2 * source + core)]
+
     def climb(chunk, source, hop):
-        part = full_ref.at[rows_of(chunk), shard(2 * source + core)]
+        part = piece(chunk, source)
         return remote(
-            part, part, up_out_sem.at[chunk, hop - 1], up_in_sem.at[chunk, hop - 1], upper
+            part,
+            part,
+            ref["up_out_sem"].at[chunk, hop - 1],
+            ref["up_in_sem"].at[chunk, hop - 1],
+            upper,
         )
 
     def sink(chunk, source, hop):
-        part = full_ref.at[rows_of(chunk), shard(2 * source + core)]
+        part = piece(chunk, source)
         return remote(
-            part, part, down_out_sem.at[chunk, hop - 1], down_in_sem.at[chunk, hop - 1], lower
+            part,
+            part,
+            ref["down_out_sem"].at[chunk, hop - 1],
+            ref["down_in_sem"].at[chunk, hop - 1],
+            lower,
         )
 
-    def mirror(chunk, source):
-        part = full_ref.at[rows_of(chunk), shard(2 * source + core)]
-        return remote(part, part, twin_out_sem.at[chunk, source], twin_in_sem.at[chunk], twin)
+    def target(chunk, giver):
+        if form == "lookup":
+            return full_ref.at[rows_of(chunk), shard(2 * giver + core)]
+        return full_ref.at[chunk, rows_of(giver), shard(core)]
+
+    def mirror(chunk, index):
+        part = target(chunk, index) if cross else piece(chunk, index)
+        return remote(
+            part, part, ref["twin_out_sem"].at[chunk, index], ref["twin_in_sem"].at[chunk], twin
+        )
+
+    def hand_over(chunk, source):
+        return remote(
+            piece(chunk, source),
+            target(chunk, mine_dp),
+            ref["cross_out_sem"].at[chunk, source],
+            ref["cross_in_sem"].at[chunk, mine_dp],
+            {"dp": source},
+        )
+
+    def have(chunk, source):
+        if not cross:
+            mirror(chunk, source).start()
+            return
+
+        @pl.when(source != mine_dp)
+        def _():
+            hand_over(chunk, source).start()
+
+        @pl.when(source == mine_dp)
+        def _():
+            values = ref["stage"][rows_of(chunk), shard(source)]
+            if form == "lookup":
+                full_ref[rows_of(chunk), shard(2 * mine_dp + core)] = values
+            else:
+                full_ref[chunk, rows_of(mine_dp), shard(core)] = values
+            mirror(chunk, mine_dp).start()
+
+    def receive(step):
+        for hop in range(places):
+            chunk = step - finish_at - LAG * (hop + 1)
+
+            @pl.when(jnp.logical_and(valid(chunk), jnp.abs(spot - mine_dp) == hop))
+            def _():
+                for offset in range(1, slabs):
+                    giver = lax.rem(mine_dp + offset, slabs)
+                    part = target(chunk, giver)
+                    remote(
+                        part,
+                        part,
+                        ref["cross_out_sem"].at[chunk, giver],
+                        ref["cross_in_sem"].at[chunk, giver],
+                        twin,
+                    ).wait_recv()
+                    mirror(chunk, giver).start()
 
     def relay(step):
         for hop in range(1, places):
-            chunk = step - places - 1 - hop
+            chunk = step - finish_at - LAG * hop
             source = spot - hop
 
             @pl.when(jnp.logical_and(valid(chunk), source >= 0))
@@ -563,7 +615,7 @@
                     def _():
                         climb(chunk, source, hop + 1).start()
 
-                mirror(chunk, source).start()
+                have(chunk, source)
 
             source_high = spot + hop
 
@@ -576,34 +628,43 @@
                     def _():
                         sink(chunk, source_high, hop + 1).start()
 
-                mirror(chunk, source_high).start()
+                have(chunk, source_high)
 
     def finish_shard(step):
-        chunk = step - places - 1
+        chunk = step - finish_at
 
         @pl.when(valid(chunk))
         def _():
             slot = lax.rem(chunk, ring)
             rows = rows_of(chunk)
-            pltpu.make_async_copy(sums_in.at[slot], sums_in.at[slot], sums_in_sem.at[slot]).wait()
-            summed = sums_out[slot]
-            for offset in range(1, parts):
-                summed = summed + sums_in[slot, offset - 1]
-            gain = gain_ref[0:1, :]
-            if mode == "norm":
+            if summing:
+                sums_in = ref["sums_in"]
+                pltpu.make_async_copy(
+                    sums_in.at[slot], sums_in.at[slot], ref["sums_in_sem"].at[slot]
+                ).wait()
+                summed = ref["sums_out"][slot]
+                for offset in range(1, parts):
+                    summed = summed + sums_in[slot, offset - 1]
+                gain = ref["gain"][0:1, :]
+            if mode == "plain":
+                result = total[...]
+            elif mode == "norm":
                 scale = lax.rsqrt(summed / D + EPSILON)
-                scale_ref[chunk] = scale
-                result = own_ref[rows, :] * down(scale, ROWS, size) * gain
+                ref["scale"][chunk] = scale
+                result = ref["own"][rows, :] * down(scale, ROWS, size) * gain
             else:
-                scale = down(given_scale_ref[chunk], ROWS, size)
-                normed = inputs_ref[rows, :] * scale
+                scale = down(ref["scale"][chunk], ROWS, size)
+                normed = ref["inputs"][rows, :] * scale
                 inner = down(summed / D, ROWS, size)
-                result = scale * (own_ref[rows, :] * gain - normed * inner)
+                result = scale * (ref["own"][rows, :] * gain - normed * inner)
                 if mode == "grad_add":
-                    result = result + added_ref[rows, :]
-                own_ref[rows, :] = result
-            full_ref[rows, shard(me)] = result.astype(jnp.bfloat16)
-            mirror(chunk, spot).start()
+                    result = result + ref["added"][rows, :]
+                if form != "table":
+                    ref["own"][rows, :] = result
+            if cross:
+                ref["stage"][rows, shard(spot)] = result.astype(jnp.bfloat16)
+            else:
+                full_ref[rows, shard(me)] = result.astype(jnp.bfloat16)
 
             @pl.when(spot < places - 1)
             def _():
@@ -613,8 +674,10 @@
             def _():
                 sink(chunk, spot, 1).start()
 
+            have(chunk, spot)
+
     def add_pair(step):
-        chunk = step - 1
+        chunk = step - LAG
 
         @pl.when(valid(chunk))
         def _():
@@ -625,7 +688,7 @@
     def pass_on(step):
         for place in range(places):
             if place < places - 1:
-                up_chunk = step - 1 - place
+                up_chunk = step - LAG * (1 + place)
 
                 @pl.when(jnp.logical_and(valid(up_chunk), spot == place))
                 def _():
@@ -639,7 +702,7 @@
                     rise(up_chunk, place).start()
 
             if place > 0:
-                down_chunk = step - places + place
+                down_chunk = step - LAG * (places - place)
 
                 @pl.when(jnp.logical_and(valid(down_chunk), spot == place))
                 def _():
@@ -653,7 +716,7 @@
                     fall(down_chunk, place).start()
 
     def settle(step):
-        chunk = step - places - 1
+        chunk = step - sum_at - LAG
 
         @pl.when(valid(chunk))
         def _():
@@ -667,11 +730,12 @@
                     if place > 0:
                         fall(chunk, place).wait_send()
 
-            for offset in range(1, parts):
-                sums_copy(chunk, offset).wait_send()
+            if summing:
+                for offset in range(1, parts):
+                    sums_copy(chunk, offset).wait_send()
 
     def sum_shard(step):
-        chunk = step - places
+        chunk = step - sum_at
 
         @pl.when(valid(chunk))
         def _():
@@ -697,17 +761,19 @@
             def _():
                 total[...] += from_high[slot, :, mine].astype(jnp.float32)
 
+            if not summing:
+                return
             value = total[...]
             if mode == "norm":
-                value = value + inputs_ref[rows, :]
+                value = value + ref["inputs"][rows, :]
                 column = jnp.sum(value * value, 1, keepdims=True)
             else:
-                scale = down(given_scale_ref[chunk], ROWS, size)
-                normed = inputs_ref[rows, :] * scale
-                gain_grad_ref[0:1, :] += jnp.sum(value * normed, 0, keepdims=True)
-                column = jnp.sum(value * gain_ref[0:1, :] * normed, 1, keepdims=True)
-            own_ref[rows, :] = value
-            sums_out[slot] = across(column, ROWS)
+                scale = down(ref["scale"][chunk], ROWS, size)
+                normed = ref["inputs"][rows, :] * scale
+                ref["gain_grad"][0:1, :] += jnp.sum(value * normed, 0, keepdims=True)
+                column = jnp.sum(value * ref["gain"][0:1, :] * normed, 1, keepdims=True)
+            ref["own"][rows, :] = value
+            ref["sums_out"][slot] = across(column, ROWS)
             for offset in range(1, parts):
                 sums_copy(chunk, offset).start()
 
@@ -717,6 +783,20 @@
         @pl.when(valid(chunk))
         def _():
             slot = lax.rem(chunk, ring)
+            right_ref = ref["right"]
+            if form == "lookup":
+                entries = right_ref.shape[0]
+                for group in range(slabs):
+                    ids = ref["ids"][group, rows_of(chunk), 0:1]
+                    spots = lax.broadcasted_iota(jnp.int32, (ROWS, entries), 1)
+                    hits = (spots == ids).astype(jnp.bfloat16)
+                    lanes = pl.ds(group * size, size)
+                    pair_out[slot, :, lanes] = dot_ab(hits, right_ref[:, shard(1 - core)]).astype(
+                        jnp.bfloat16
+                    )
+                    partial[slot, :, lanes] = dot_ab(hits, right_ref[:, shard(core)])
+                pair_copy(chunk).start()
+                return
             half = lax.rem(chunk, 2)
             left_copy(chunk).wait()
 
@@ -725,9 +805,9 @@
                 left_copy(chunk + 1).start()
 
             def term(index):
-                if turned:
-                    return dot_abt(left_buf[half], right_ref[shard(index), :])
-                return dot_ab(left_buf[half], right_ref[:, shard(index)])
+                if form in ("turned", "table"):
+                    return dot_abt(ref["left_buf"][half], right_ref[shard(index), :])
+                return dot_ab(ref["left_buf"][half], right_ref[:, shard(index)])
 
             for place in range(places):
                 lanes = pl.ds(place * size, size)
@@ -738,14 +818,20 @@
                 partial[slot, :, lanes] = term(2 * place + core)
 
     def close(step):
-        chunk = step - 2 * places - 1
+        chunk = step - close_at
 
         @pl.when(valid(chunk))
         def _():
-            arrived = full_ref.at[rows_of(chunk), pl.ds(0, places * size)]
-            pltpu.make_async_copy(arrived, arrived, twin_in_sem.at[chunk]).wait()
-            for source in range(places):
-                mirror(chunk, source).wait_send()
+            if form == "table":
+                arrived = full_ref.at[chunk, :, pl.ds(0, size)]
+            else:
+                arrived = full_ref.at[rows_of(chunk), pl.ds(0, places * size)]
+            pltpu.make_async_copy(arrived, arrived, ref["twin_in_sem"].at[chunk]).wait()
+            for index in range(places):
+                mirror(chunk, index).wait_send()
+            if cross:
+                for offset in range(1, slabs):
+                    hand_over(chunk, lax.rem(mine_dp + offset, slabs)).wait_send()
             for hop in range(1, places):
                 source = spot - hop + 1
 
@@ -759,88 +845,142 @@
                 def _():
                     sink(chunk, source_high, hop).wait_send()
 
+            if form == "table":
+                table_grad = ref["table_grad"]
+                entries = table_grad.shape[0]
+                pieces = 5 if entries % 80 == 0 else 1
+                block = entries // pieces
+                ids = ref["ids"][chunk, 0:1, :]
+                values = full_ref[chunk]
+                for index in range(pieces):
+                    spots = index * block + lax.broadcasted_iota(
+                        jnp.int32, (block, ids.shape[1]), 0
+                    )
+                    hits = (spots == ids).astype(jnp.bfloat16)
+                    span = pl.ds(index * block, block)
+                    table_grad[span, :] += dot_ab(hits, values)
+
     def advance(step, carried):
         relay(step)
-        finish_shard(step)
+        if summing:
+            finish_shard(step)
+        if cross:
+            receive(step)
         add_pair(step)
         pass_on(step)
         settle(step)
         sum_shard(step)
+        if not summing:
+            finish_shard(step)
         produce(step)
         close(step)
         return carried
 
-    lax.fori_loop(0, chunks + 2 * places + 1, advance, 0)
-
-
-def transit(mode, number, parts, left, right, inputs, gain, scale=None, added=None, turned=False):
-    tokens, size = inputs.shape
-    depth = left.shape[1]
-    width = parts * size
+    lax.fori_loop(0, chunks + close_at, advance, 0)
+
+
+def transit(
+    mode,
+    form,
+    number,
+    parts,
+    slabs,
+    right,
+    tokens,
+    size,
+    left=None,
+    inputs=None,
+    gain=None,
+    scale=None,
+    added=None,
+    ids=None,
+    entries=None,
+):
     chunks = tokens // ROWS
     places = parts // 2
-    ring = min(chunks, 2 * places)
+    cross = form in ("lookup", "table")
+    summing = mode != "plain"
+    ring = min(chunks, LAG * (places + 1) + 2) if summing else chunks
     dma = pltpu.SemaphoreType.DMA
-    low = jnp.bfloat16
+    low, wide_kind = jnp.bfloat16, jnp.float32
     vmem = pl.BlockSpec(memory_space=pltpu.VMEM)
-    operands = [left, right, inputs, gain]
-    specs = [pl.BlockSpec(memory_space=pl.ANY), vmem, vmem, vmem]
-    shapes = [
-        jax.ShapeDtypeStruct((tokens, size), jnp.float32),
-        jax.ShapeDtypeStruct((tokens, width), low),
-    ]
+    operands, specs, outputs, scratch = {}, [], {}, {}
+
+    def take(name, array, spec=vmem):
+        operands[name] = array
+        specs.append(spec)
+
+    take("right", right)
+    if left is not None:
+        take("left", left, pl.BlockSpec(memory_space=pl.ANY))
+    if ids is not None:
+        take("ids", ids)
+    if summing:
+        take("inputs", inputs)
+        take("gain", gain)
+    if mode in ("grad", "grad_add"):
+        take("scale", scale)
+    if mode == "grad_add":
+        take("added", added)
+
+    if summing and form != "table":
+        outputs["own"] = ((tokens, size), wide_kind)
+    if form != "table":
+        outputs["full"] = ((tokens, parts * size), low)
     if mode == "norm":
-        shapes.append(jax.ShapeDtypeStruct((chunks, 8, ROWS), jnp.float32))
-    else:
-        operands.append(scale)
-        specs.append(vmem)
-        if mode == "grad_add":
-            operands.append(added)
-            specs.append(vmem)
-        shapes.append(jax.ShapeDtypeStruct((8, size), jnp.float32))
+        outputs["scale"] = ((chunks, 8, ROWS), wide_kind)
+    if mode in ("grad", "grad_add"):
+        outputs["gain_grad"] = ((8, size), wide_kind)
+    if form == "table":
+        outputs["table_grad"] = ((entries, 2 * size), wide_kind)
+
     span = places * size
     hops = max(places - 1, 1)
-    return pl.pallas_call(
-        functools.partial(transit_kernel, mode, turned, parts),
+    if form == "table":
+        scratch["own"] = pltpu.VMEM((tokens, size), wide_kind)
+        scratch["full"] = pltpu.VMEM((chunks, slabs * ROWS, 2 * size), low)
+    if left is not None:
+        scratch["left_buf"] = pltpu.VMEM((2, ROWS, left.shape[1]), low)
+        scratch["left_sem"] = dma((2,))
+    if cross:
+        scratch["stage"] = pltpu.VMEM((tokens, span), low)
+        scratch["cross_out_sem"] = dma((chunks, slabs))
+        scratch["cross_in_sem"] = dma((chunks, slabs))
+    if summing:
+        scratch["sums_out"] = pltpu.VMEM((ring, 8, ROWS), wide_kind)
+        scratch["sums_in"] = pltpu.VMEM((ring, parts - 1, 8, ROWS), wide_kind)
+        scratch["sums_out_sem"] = dma((ring, parts - 1))
+        scratch["sums_in_sem"] = dma((ring,))
+    scratch["total"] = pltpu.VMEM((ROWS, size), wide_kind)
+    scratch["partial"] = pltpu.VMEM((ring, ROWS, span), wide_kind)
+    for name in ("pair_out", "pair_in", "from_low", "from_high"):
+        scratch[name] = pltpu.VMEM((ring, ROWS, span), low)
+    for name in ("pair_out", "pair_in", "low_out", "low_in", "high_out", "high_in"):
+        scratch[name + "_sem"] = dma((ring,))
+    for name in ("up_out", "up_in", "down_out", "down_in"):
+        scratch[name + "_sem"] = dma((chunks, hops))
+    scratch["twin_out_sem"] = dma((chunks, places))
+    scratch["twin_in_sem"] = dma((chunks,))
+
+    depth = right.shape[1] if form in ("turned", "table") else right.shape[0]
+    names = tuple(operands) + tuple(outputs) + tuple(scratch)
+    results = pl.pallas_call(
+        functools.partial(transit_kernel, mode, form, parts, slabs, names),
         in_specs=specs,
-        out_specs=[vmem] * len(shapes),
-        out_shape=shapes,
-        scratch_shapes=[
-            pltpu.VMEM((2, ROWS, depth), low),
-            pltpu.VMEM((ring, ROWS, span), jnp.float32),
-            pltpu.VMEM((ring, ROWS, span), low),
-            pltpu.VMEM((ring, ROWS, span), low),
-            pltpu.VMEM((ring, ROWS, span), low),
-            pltpu.VMEM((ring, ROWS, span), low),
-            pltpu.VMEM((ROWS, size), jnp.float32),
-            pltpu.VMEM((ring, 8, ROWS), jnp.float32),
-            pltpu.VMEM((ring, parts - 1, 8, ROWS), jnp.float32),
-            dma((2,)),
-            dma((ring,)),
-            dma((ring,)),
-            dma((ring,)),
-            dma((ring,)),
-            dma((ring,)),
-            dma((ring,)),
-            dma((ring, parts - 1)),
-            dma((ring,)),
-            dma((chunks, hops)),
-            dma((chunks, hops)),
-            dma((chunks, hops)),
-            dma((chunks, hops)),
-            dma((chunks, places)),
-            dma((chunks,)),
-        ],
+        out_specs=[vmem] * len(outputs),
+        out_shape=[jax.ShapeDtypeStruct(shape, kind) for shape, kind in outputs.values()],
+        scratch_shapes=list(scratch.values()),
         compiler_params=pltpu.CompilerParams(
             collective_id=number, has_side_effects=True, vmem_limit_bytes=60 * 1024 * 1024
         ),
         cost_estimate=pl.CostEstimate(
-            flops=2 * tokens * depth * width,
-            bytes_accessed=2 * (tokens * depth + depth * width + tokens * width),
+            flops=2 * tokens * depth * parts * size,
+            bytes_accessed=128 * tokens * parts * size,
             transcendentals=0,
         ),
-        name="transit_" + mode,
-    )(*operands)
+        name="transit_" + form,
+    )(*operands.values())
+    return dict(zip(outputs, results))
 
 
 def shampoo(tile_w, tile_g, left, right, left_root, right_root):
@@ -885,26 +1025,45 @@
     return (new_first, new_second, weight - step_rate * (moved + WEIGHT_DECAY * weight))
 
 
-def layer_forward(token_ids, targets, valid, resets, weights, inner_init, gains, head_index):
+def layer_forward(
+    token_ids, targets, valid, resets, emb_low, weights, inner_init, gains, head_index
+):
     w_qkv, w_out, w_gu, w_down, table = weights
-    parts = lax.axis_size("head")
+    parts, slabs = lax.axis_size("head"), lax.axis_size("dp")
     vocab_part = table.shape[0]
-    tokens = token_ids.shape[0]
+    tokens, size = token_ids.shape[0], gains.shape[1]
+    chunks = tokens // ROWS
     columns = jnp.arange(vocab_part, dtype=jnp.int32)
-    local_ids = token_ids - head_index * vocab_part
-    id_onehot = (columns[None, :] == local_ids[:, None]).astype(jnp.bfloat16)
-    nothing = jnp.zeros((tokens, gains.shape[1]), jnp.float32)
-    embedded, full_one, scale_one = transit(
-        "norm", 1, parts, id_onehot, table, nothing, gains[0:1]
-    )
+    local_ids = lax.all_gather(token_ids, "dp", axis=0) - head_index * vocab_part
+    spread_ids = jnp.broadcast_to(local_ids[:, :, None], (slabs, tokens, 128))
+    first = transit("plain", "lookup", 1, parts, slabs, emb_low, tokens, size, ids=spread_ids)
+    low_embedded = first["full"]
+    wide_embedded = low_embedded.astype(jnp.float32)
+    scale_one = lax.rsqrt(jnp.mean(wide_embedded * wide_embedded, -1) + EPSILON)
+    gain_one = lax.all_gather(gains[0], "head", axis=0, tiled=True)
+    full_one = (wide_embedded * scale_one[:, None] * gain_one[None]).astype(jnp.bfloat16)
+    embedded = lax.dynamic_slice_in_dim(low_embedded, head_index * size, size, 1)
+    embedded = embedded.astype(jnp.float32)
+    scale_one = jnp.broadcast_to(scale_one.reshape(chunks, 1, ROWS), (chunks, 8, ROWS))
     mixed = jnp.dot(full_one, w_qkv, preferred_element_type=jnp.float32).astype(jnp.bfloat16)
     step_rate = jax.nn.sigmoid(gains[3:4]) / (8 * P_SIZE)
     masks = mixer_masks(resets, tokens)
     initial_pairs = pair_blocks(inner_init)
     inner_low, residue, states = mixer_forward(mixed, step_rate, initial_pairs, masks)
-    hidden_one, full_two, scale_two = transit(
-        "norm", 2, parts, inner_low, w_out, embedded, gains[1:2]
-    )
+    second = transit(
+        "norm",
+        "rows",
+        2,
+        parts,
+        slabs,
+        w_out,
+        tokens,
+        size,
+        left=inner_low,
+        inputs=embedded,
+        gain=gains[1:2],
+    )
+    hidden_one, full_two, scale_two = second["own"], second["full"], second["scale"]
     gate_up = jnp.dot(full_two, w_gu, preferred_element_type=jnp.float32)
 
     def swiglu(paired):
@@ -913,9 +1072,20 @@
 
     activated, act_pull = jax.vjp(swiglu, gate_up)
     act_low = activated.astype(jnp.bfloat16)
-    hidden_two, full_end, scale_end = transit(
-        "norm", 3, parts, act_low, w_down, hidden_one, gains[2:3]
-    )
+    third = transit(
+        "norm",
+        "rows",
+        3,
+        parts,
+        slabs,
+        w_down,
+        tokens,
+        size,
+        left=act_low,
+        inputs=hidden_one,
+        gain=gains[2:3],
+    )
+    hidden_two, full_end, scale_end = third["own"], third["full"], third["scale"]
     logits = jnp.einsum("td,vd->tv", full_end, table, preferred_element_type=jnp.float32)
     peak = jnp.max(logits, -1)
     target_hits = columns[None, :] == (targets - head_index * vocab_part)[:, None]
@@ -953,12 +1123,28 @@
         scale_end,
         full_end,
         d_logits,
-        id_onehot,
+        local_ids,
     )
     return (jnp.sum((totals - target_logit) * counted), jnp.sum(counted), kept)
 
 
-def layer_backward(kept, weights, gains):
+def slots_of(grad, order, kinds):
+    parts = lax.axis_size("dp")
+    shaped = grad.astype(jnp.bfloat16).reshape(parts, -1, kinds, grad.shape[1] // kinds)
+    return jnp.take(shaped, order, axis=0, mode="clip")
+
+
+def column_slots_of(grad, order):
+    parts = lax.axis_size("dp")
+    shaped = grad.astype(jnp.bfloat16).reshape(grad.shape[0], parts, -1)
+    return jnp.take(jnp.swapaxes(shaped, 0, 1), order, axis=0, mode="clip")
+
+
+def scatter_dp(grad, dimension):
+    return lax.psum_scatter(grad, "dp", scatter_dimension=dimension, tiled=True)
+
+
+def layer_backward(kept, weights, gains, order):
     (
         embedded,
         scale_one,
@@ -974,36 +1160,98 @@
         scale_end,
         full_end,
         d_logits,
-        id_onehot,
+        local_ids,
     ) = kept
     w_qkv, w_out, w_gu, w_down, table = weights
-    parts = lax.axis_size("head")
-    d_two, d_down_in, gain_end = transit(
-        "grad", 4, parts, d_logits, table, hidden_two, gains[2:3], scale_end
-    )
-    grad_table = jnp.einsum("tv,td->vd", d_logits, full_end, preferred_element_type=jnp.float32)
-    d_act = jnp.einsum("td,fd->tf", d_down_in, w_down, preferred_element_type=jnp.float32)
+    parts, slabs = lax.axis_size("head"), lax.axis_size("dp")
+    tokens, size = embedded.shape
+    chunks = tokens // ROWS
+    wide_kind = jnp.float32
+    fourth = transit(
+        "grad",
+        "rows",
+        4,
+        parts,
+        slabs,
+        table,
+        tokens,
+        size,
+        left=d_logits,
+        inputs=hidden_two,
+        gain=gains[2:3],
+        scale=scale_end,
+    )
+    d_two, d_down_in = fourth["own"], fourth["full"]
+    grad_table = jnp.einsum("tv,td->vd", d_logits, full_end, preferred_element_type=wide_kind)
+    grad_table = grad_table.astype(jnp.bfloat16)
+    d_act = jnp.einsum("td,fd->tf", d_down_in, w_down, preferred_element_type=wide_kind)
     d_gate_up = act_pull(d_act)[0].astype(jnp.bfloat16)
-    d_one, d_out_in, gain_two = transit(
-        "grad_add", 5, parts, d_gate_up, w_gu, hidden_one, gains[1:2], scale_two, d_two, True
-    )
-    grad_down = jnp.einsum("tf,td->fd", act_low, d_down_in, preferred_element_type=jnp.float32)
-    grad_gu = jnp.einsum("td,tc->dc", full_two, d_gate_up, preferred_element_type=jnp.float32)
-    d_inner = jnp.einsum("td,cd->tc", d_out_in, w_out, preferred_element_type=jnp.float32)
+    grad_down = jnp.einsum("tf,td->fd", act_low, d_down_in, preferred_element_type=wide_kind)
+    slot_down = column_slots_of(grad_down, order[3])
+    d_gate_up, grad_table, slot_down = lax.optimization_barrier(
+        (d_gate_up, grad_table, slot_down)
+    )
+    owned_table = scatter_dp(grad_table, 1)
+    owned_down = scatter_dp(slot_down, 0)
+    fifth = transit(
+        "grad_add",
+        "turned",
+        5,
+        parts,
+        slabs,
+        w_gu,
+        tokens,
+        size,
+        left=d_gate_up,
+        inputs=hidden_one,
+        gain=gains[1:2],
+        scale=scale_two,
+        added=d_two,
+    )
+    d_one, d_out_in = fifth["own"], fifth["full"]
+    d_inner = jnp.einsum("td,cd->tc", d_out_in, w_out, preferred_element_type=wide_kind)
+    grad_gu = jnp.einsum("td,tc->dc", full_two, d_gate_up, preferred_element_type=wide_kind)
+    slot_gu = slots_of(grad_gu, order[2], 2)
+    d_inner, slot_gu = lax.optimization_barrier((d_inner, slot_gu))
+    owned_gu = scatter_dp(slot_gu, 0)
     d_mixed, grad_pairs, grad_step = mixer_backward(*inner_kept, d_inner)
     grad_init = head_blocks(grad_pairs)
     gate = jax.nn.sigmoid(gains[3])
     grad_rate = grad_step[0] * gate * (1.0 - gate) / (8 * P_SIZE)
-    _, d_embed, gain_one = transit(
-        "grad_add", 6, parts, d_mixed, w_qkv, embedded, gains[0:1], scale_one, d_one, True
-    )
-    grad_out = jnp.einsum("tc,td->cd", inner_low, d_out_in, preferred_element_type=jnp.float32)
-    grad_qkv = jnp.einsum("td,tc->dc", full_one, d_mixed, preferred_element_type=jnp.float32)
-    grad_table = grad_table + jnp.einsum(
-        "tv,td->vd", id_onehot, d_embed, preferred_element_type=jnp.float32
-    )
-    grad_gains = jnp.stack([gain_one[0], gain_two[0], gain_end[0], grad_rate], 0)
-    return (grad_qkv, grad_out, grad_gu, grad_down, grad_table, grad_init, grad_gains)
+    grad_out = jnp.einsum("tc,td->cd", inner_low, d_out_in, preferred_element_type=wide_kind)
+    grad_qkv = jnp.einsum("td,tc->dc", full_one, d_mixed, preferred_element_type=wide_kind)
+    slot_out = column_slots_of(grad_out, order[1])
+    slot_qkv = slots_of(grad_qkv, order[0], 3)
+    d_mixed, slot_out, slot_qkv = lax.optimization_barrier((d_mixed, slot_out, slot_qkv))
+    owned_out = scatter_dp(slot_out, 0)
+    owned_qkv = scatter_dp(slot_qkv, 0)
+    row_ids = jnp.swapaxes(local_ids.reshape(slabs, chunks, ROWS), 0, 1)
+    row_ids = jnp.broadcast_to(
+        row_ids.reshape(chunks, 1, slabs * ROWS), (chunks, 8, slabs * ROWS)
+    )
+    sixth = transit(
+        "grad_add",
+        "table",
+        6,
+        parts,
+        slabs,
+        w_qkv,
+        tokens,
+        size,
+        left=d_mixed,
+        inputs=embedded,
+        gain=gains[0:1],
+        scale=scale_one,
+        added=d_one,
+        ids=row_ids,
+        entries=table.shape[0],
+    )
+    owned_table = owned_table.astype(wide_kind) + sixth["table_grad"]
+    gain_rows = [sixth["gain_grad"][0], fifth["gain_grad"][0], fourth["gain_grad"][0], grad_rate]
+    owned = tuple(
+        piece.astype(wide_kind) for piece in (owned_qkv, owned_out, owned_gu, owned_down)
+    )
+    return owned + (owned_table,), grad_init, jnp.stack(gain_rows, 0)
 
 
 def shards(
@@ -1042,50 +1290,29 @@
     gains_first,
     gains_second,
 ):
+    low = jnp.bfloat16
+    emb_low = emb_master.astype(low)
     gathered = (
-        lax.all_gather(qkv_master.astype(jnp.bfloat16), "dp", axis=0, tiled=True),
-        lax.all_gather(out_master.astype(jnp.bfloat16), "dp", axis=0, tiled=True),
-        lax.all_gather(gu_master.astype(jnp.bfloat16), "dp", axis=0, tiled=True),
-        lax.all_gather(down_master.astype(jnp.bfloat16), "dp", axis=0, tiled=True),
-        lax.all_gather(emb_master.astype(jnp.bfloat16), "dp", axis=1, tiled=True),
-    )
-    w_qkv = jnp.take(gathered[0], owners[0], axis=0).reshape(D, -1)
-    w_out = jnp.take(gathered[1], owners[1], axis=0)
+        lax.all_gather(qkv_master.astype(low), "dp", axis=0, tiled=True),
+        lax.all_gather(out_master.astype(low), "dp", axis=0, tiled=True),
+        lax.all_gather(gu_master.astype(low), "dp", axis=0, tiled=True),
+        lax.all_gather(down_master.astype(low), "dp", axis=0, tiled=True),
+        lax.all_gather(emb_low, "dp", axis=1, tiled=True),
+    )
+    w_qkv = jnp.take(gathered[0], owners[0], axis=0, mode="clip").reshape(D, -1)
+    w_out = jnp.take(gathered[1], owners[1], axis=0, mode="clip")
     w_out = jnp.swapaxes(w_out, 0, 1).reshape(w_out.shape[1], D)
-    w_gu = jnp.take(gathered[2], owners[2], axis=0).reshape(D, -1)
-    w_down = jnp.take(gathered[3], owners[3], axis=0)
+    w_gu = jnp.take(gathered[2], owners[2], axis=0, mode="clip").reshape(D, -1)
+    w_down = jnp.take(gathered[3], owners[3], axis=0, mode="clip")
     w_down = jnp.swapaxes(w_down, 0, 1).reshape(w_down.shape[1], D)
     weights = (w_qkv, w_out, w_gu, w_down, gathered[4])
     head_index = lax.axis_index("head")
     loss_local, count_local, kept = layer_forward(
-        token_ids, targets, valid, resets, weights, inner_init, gains, head_index
+        token_ids, targets, valid, resets, emb_low, weights, inner_init, gains, head_index
     )
     loss_sum, count = lax.psum((loss_local, count_local), "dp")
-    grad_qkv, grad_out, grad_gu, grad_down, grad_table, grad_init, grad_gains = layer_backward(
-        kept, weights, gains
-    )
-    parts = lax.axis_size("dp")
     order = jnp.argsort(owners, axis=1)
-    slot_qkv = jnp.take(grad_qkv.reshape(parts, -1, 3, grad_qkv.shape[1] // 3), order[0], axis=0)
-    slot_out = jnp.take(
-        jnp.swapaxes(grad_out.reshape(grad_out.shape[0], parts, -1), 0, 1), order[1], axis=0
-    )
-    slot_gu = jnp.take(grad_gu.reshape(parts, -1, 2, grad_gu.shape[1] // 2), order[2], axis=0)
-    slot_down = jnp.take(
-        jnp.swapaxes(grad_down.reshape(grad_down.shape[0], parts, -1), 0, 1), order[3], axis=0
-    )
-    low = jnp.bfloat16
-    owned = tuple(
-        lax.psum_scatter(piece.astype(low), "dp", scatter_dimension=0, tiled=True).astype(
-            jnp.float32
-        )
-        for piece in (slot_qkv, slot_out, slot_gu, slot_down)
-    )
-    owned = owned + (
-        lax.psum_scatter(grad_table.astype(low), "dp", scatter_dimension=1, tiled=True).astype(
-            jnp.float32
-        ),
-    )
+    owned, grad_init, grad_gains = layer_backward(kept, weights, gains, order)
     small = lax.psum((grad_init, grad_gains), "dp")
     first_dp = (lax.axis_index("dp") == 0).astype(jnp.float32)
     squares = sum((jnp.sum(piece * piece) for piece in owned))

time: 2270 us -> 1910 us (0.84)
  waiting for transfers between devices: 348 us -> 176 us
  Pallas kernels: 1160 us -> 1040 us
  matrix products: 307 us -> 227 us
  blocking collectives: 63.8 us -> 93 us
  other arithmetic: 161 us -> 136 us
    all_gather x5, waiting for transfers between devices: 235 us -> 0.05 us  [the longest x1 0.02 us: shards(): lax.all_gather(gu_master.astype(low), 'dp', axis=0, tiled=True)]
    pallas_call x6, Pallas kernels: 1040 us -> 911 us  [transit(): pl.pallas_call(functools.partial(transit_kernel, mode, form, parts, slabs...]
    dot_general x8 -> x7, matrix products: 190 us -> 110 us  [the longest x1 41.9 us: layer_backward(): jnp.einsum('tv,td->vd', d_logits, full_end, preferred_element_type=wide_k...]
    reduce_scatter x1, waiting for transfers between devices: 113 us -> 150 us  [scatter_dp(): return lax.psum_scatter(grad, 'dp', scatter_dimension=dimension, tiled=True)]
    dot_general x3 -> x0, local copies, waits for them, and re-layouts: 33.1 us -> none  [the longest x1 12.6 us: layer_backward(): jnp.einsum('td,tc->dc', full_two, d_gate_up, preferred_element_type=jnp.f...]
    reshape x3 -> x8, local copies, waits for them, and re-layouts: 10.1 us -> 42.7 us  [the longest x4 29.9 us: slots_of(): grad.astype(jnp.bfloat16).reshape(parts, -1, kinds, grad.shape[1] // kinds)]
    unnamed x15, waiting for transfers between devices: 0.23 us -> 26.4 us
    gather x11 -> x10, local copies, waits for them, and re-layouts: 64 us -> 44.6 us  [the longest x2 12.9 us: shards(): w_gu = jnp.take(gathered[2], owners[2], axis=0, mode='clip').reshape(D, -1)]
  transfers between devices with their start and end apart: 11 -> 11, of which waited for: 6 -> 2; matrix products, arithmetic and copies ran while one was open for 16% -> 10% of each run, Pallas kernels for 8% -> 35%
where the time goes in v3:
time: 1910 us; the launch traced here: 1900 us
  Pallas kernels  1040 us (54%)
  matrix products  227 us (12%)
  local copies, waits for them, and re-layouts  205 us (11%)
  waiting for transfers between devices  176 us (9%)
  other arithmetic  136 us (7%)
  blocking collectives  93 us (5%)
  between operations  23.5 us (1%)
    pallas_call x6, Pallas kernels, transit(): pl.pallas_call(functools.partial(transit_kernel, mode, form, parts, slabs...  911 us
    reduce_scatter x1, waiting for transfers between devices, scatter_dp(): return lax.psum_scatter(grad, 'dp', scatter_dimension=dimension, tiled=True)  150 us
    pallas_call x1, Pallas kernels, mixer_backward(): pl.pallas_call(mixer_backward_kernel, grid=(chunks,), in_specs=[rows(3 *...  77.1 us
    pallas_call x1, Pallas kernels, mixer_forward(): pl.pallas_call(mixer_forward_kernel, grid=(chunks,), in_specs=[pl.BlockSp...  50.4 us
    dot_general x12, matrix products, product(): jnp.einsum(form, one.astype(jnp.bfloat16), two.astype(jnp.bfloat16), pref...  46.9 us
    dot_general x1, matrix products, layer_forward(): jnp.einsum('td,vd->tv', full_end, table, preferred_element_type=jnp.float32)  42.1 us
    dot_general x1, matrix products, layer_backward(): jnp.einsum('tv,td->vd', d_logits, full_end, preferred_element_type=wide_k...  41.9 us
    unnamed x165, local copies, waits for them, and re-layouts  40.4 us
  transfers between devices with their start and end apart: 11, of which 2 were waited for; matrix products, arithmetic and copies ran while one was open for 10% of the time, Pallas kernels for 35%

profile of v3, /device:TPU:0, one launch (start us, length us, event | category | flops | bytes accessed | tf_op | source)
XLA Modules:
  0.0 1899.8 jit_solution(3234326258084707495)
XLA Ops:
  15.5 5.9 convert_element_type.221.all_refs_0_
  21.4 9.7 all-gather
  33.9 12.0 all-gather.1
  47.5 3.8 broadcast_in_dim.92.all_refs_1_
  51.3 145.9 %transit_lookup.1 = bf16[2048,2048]{1,0:T(8,128)(2,1)} custom-call(bf16[4000,512]{1,0:T(8,128)(2,1)} %convert_element_type.221.all_refs_0_, s32[4,2048,128]{2,1,0:T(8,128)} %broadcast_in_dim.92.all_refs_1_), custom_call_target="tpu_custom_call" | custom-call | flops 33554432000 | bytes 536870912 | tf_op jit(solution)/shard_map/transit_lookup/pallas_call | solution.py:967
  197.3 5.1 fusion
  211.8 4.1 gather_fusion
  215.9 3.8 copy.205
  219.6 4.3 gather_fusion.2
  223.9 6.2 copy.155
  233.0 10.3 convolution_convert_fusion.2.qkv_ref
  244.2 50.4 %inner_forward.1 = (bf16[2048,256]{1,0:T(8,128)(2,1)S(1)}, f32[2048,256]{1,0:T(8,128)S(1)}, f32[32,2,128,128]{3,2,1,0:T(8,128)S(1)}) custom-call(bf16[2048,768]{1,0:T(8,128)(2,1)S(1)} %convolution_convert_fusion.2.qkv_ref, f32[1,256]{1,0:T(1,128)S(1)} %get-tuple-element.240.rate_ref, f32[2,128,128]{2,1,0:T(8,128)S(1)} %select_maximum_fusion.initial_ref, ...), custom_call_target="tpu_custom_call" | custom-call | tf_op jit(solution)/shard_map/inner_forward/pallas_call | solution.py:323
  300.6 149.4 %transit_rows.3 = (f32[2048,256]{1,0:T(8,128)}, bf16[2048,2048]{1,0:T(8,128)(2,1)}, f32[16,8,128]{2,1,0:T(8,128)}) custom-call(bf16[256,2048]{1,0:T(8,128)(2,1)} %bitcast.297, bf16[2048,256]{1,0:T(8,128)(2,1)} %copy-done.14, f32[2048,256]{1,0:T(8,128)} %dynamic-slice_convert_fusion.all_refs_2_.all_refs_3_, f32[1,256]{1,0:T(1,128)} %get-tuple-element.239.all_refs_3_), custom_call_target="tpu_custom_call" | custom-call | flops 2147483648 | bytes 536870912 | tf_op jit(solution)/shard_map/transit_rows/pallas_call | solution.py:967
  450.0 6.0 gather_fusion.3
  456.0 6.9 copy.161
  462.9 4.9 copy.209
  467.8 8.3 copy.172.all_refs_0_
  476.1 17.7 fusion.5
  493.9 3.4 multiply_convert_fusion.1.all_refs_1_
  499.3 146.1 %transit_rows.4 = (f32[2048,256]{1,0:T(8,128)}, bf16[2048,2048]{1,0:T(8,128)(2,1)}, f32[16,8,128]{2,1,0:T(8,128)}) custom-call(bf16[688,2048]{1,0:T(8,128)(2,1)} %bitcast.294, bf16[2048,688]{1,0:T(8,128)(2,1)} %multiply_convert_fusion.1.all_refs_1_, f32[2048,256]{1,0:T(8,128)} %get-tuple-element.58.all_refs_2_, f32[1,256]{1,0:T(1,128)} %get-tuple-element.238.all_refs_3_), custom_call_target="tpu_custom_call" | custom-call | flops 5771362304 | bytes 536870912 | tf_op jit(solution)/shard_map/transit_rows/pallas_call | solution.py:967
  645.4 42.1 %fusion.114 = (f32[2048]{0:T(1024)S(1)}, f32[2048,4000]{0,1:T(8,128)}) fusion(bf16[2048,2048]{1,0:T(8,128)(2,1)} %get-tuple-element.59, bf16[4000,2048]{1,0:T(8,128)(2,1)} %all-gather.18.cloned.1.call-done.all_refs_0_), kind=kOutput, calls=%fused_computation.209 | convolution fusion | flops 33562621952 | bytes 57548800 | tf_op jit(solution)/shard_map/td,vd->tv/dot_general | solution.py:1089
  687.5 30.7 %copy.164 = f32[2048,4000]{1,0:T(8,128)} copy(f32[2048,4000]{0,1:T(8,128)} %get-tuple-element.250) | data formatting | bytes 65536000 | tf_op jit(solution)/shard_map/td,vd->tv/dot_general | solution.py:1089
  718.2 16.0 exponential_reduce_fusion
  734.3 15.4 select_reduce_fusion
  749.7 14.2 all-gather.3
  764.8 14.0 multiply_convert_fusion.all_refs_1_
  778.8 41.9 %convolution_convert_fusion = bf16[4000,2048]{1,0:T(8,128)(2,1)} fusion(bf16[2048,4000]{1,0:T(8,128)(2,1)} %multiply_convert_fusion.all_refs_1_, bf16[2048,2048]{1,0:T(8,128)(2,1)} %get-tuple-element.59), kind=kOutput, calls=%fused_computation.17 | convolution fusion | flops 33562624000 | bytes 41156608 | tf_op jit(solution)/shard_map/tv,td->vd/dot_general | solution.py:1185
  820.7 154.1 %transit_rows.5 = (f32[2048,256]{1,0:T(8,128)}, bf16[2048,2048]{1,0:T(8,128)(2,1)}, f32[8,256]{1,0:T(8,128)}) custom-call(bf16[4000,2048]{1,0:T(8,128)(2,1)} %all-gather.18.cloned.1.call-done.all_refs_0_, bf16[2048,4000]{1,0:T(8,128)(2,1)} %multiply_convert_fusion.all_refs_1_, f32[2048,256]{1,0:T(8,128)} %get-tuple-element.62.all_refs_2_, ...), custom_call_target="tpu_custom_call" | custom-call | flops 33554432000 | bytes 536870912 | tf_op jit(solution)/shard_map/transit_rows/pallas_call | solution.py:967
  974.8 9.1 convolution_convert_fusion.4
  983.9 16.7 multiply_bitcast_fusion
  1000.8 7.9 add_convert_fusion
  1008.8 8.3 copy.169
  1019.5 17.5 convolution_convert_fusion.1
  1037.0 8.3 copy.173.all_refs_1_
  1045.3 12.8 reshape.474
  1058.1 10.3 copy.174
  1068.5 150.2 %transit_turned.1 = (f32[2048,256]{1,0:T(8,128)}, bf16[2048,2048]{1,0:T(8,128)(2,1)}, f32[8,256]{1,0:T(8,128)}) custom-call(bf16[2048,1376]{1,0:T(8,128)(2,1)} %copy.172.all_refs_0_, bf16[2048,1376]{1,0:T(8,128)(2,1)} %copy.173.all_refs_1_, f32[2048,256]{1,0:T(8,128)} %get-tuple-element.58.all_refs_2_, f32[1,256]{1,0:T(1,128)} %get-tuple-element.239.all_refs_3_, ...), custom_call_target="tpu_custom_call" | custom-call | flops 11542724608 | bytes 536870912 | tf_op jit(solution)/shard_map/transit_turned/pallas_call | solution.py:967
  1218.7 7.1 fusion.115.upstream_ref
  1225.8 6.7 gather_fusion.5
  1245.2 77.1 %inner_backward.1 = (bf16[2048,768]{1,0:T(8,128)(2,1)S(1)}, f32[2,128,128]{2,1,0:T(8,128)S(1)}, f32[1,256]{1,0:T(1,128)S(1)}) custom-call(bf16[2048,768]{1,0:T(8,128)(2,1)S(1)} %copy-done.1, f32[1,256]{1,0:T(1,128)S(1)} %copy-done.24, f32[2,128,128]{2,1,0:T(8,128)S(1)} %copy-done.20, f32[32,64,64]{2,1,0:T(8,128)S(1)} %copy-done.9, ...), custom_call_target="tpu_custom_call" | custom-call | tf_op jit(solution)/shard_map/inner_backward/pallas_call | solution.py:364
  1324.9 11.1 convolution_convert_fusion.3
  1336.0 6.7 convolution_convert_fusion.6
  1342.7 4.0 reshape.581
  1353.1 2.9 gather_fusion.6
  1357.6 8.4 copy.179
  1366.8 3.2 copy.185
  1369.9 3.0 copy.187
  1373.0 3.7 bitcast_multiply_fusion
  1376.6 3.2 copy.181.all_refs_0_
  1381.2 165.1 %transit_table.1 = (f32[8,256]{1,0:T(8,128)}, f32[4000,512]{1,0:T(8,128)}) custom-call(bf16[2048,768]{1,0:T(8,128)(2,1)} %copy.181.all_refs_0_, bf16[2048,768]{1,0:T(8,128)(2,1)} %copy-done.25, s32[16,8,512]{2,1,0:T(8,128)} %broadcast_in_dim.107.all_refs_2_, f32[2048,256]{1,0:T(8,128)} %dynamic-slice_convert_fusion.all_refs_2_.all_refs_3_, ...), custom_call_target="tpu_custom_call" | custom-call | flops 6442450944 | bytes 536870912 | tf_op jit(solution)/shard_map/transit_table/pallas_call | solution.py:967
  1548.4 17.7 all-reduce.8
  1578.9 24.2 %reduce-scatter.20.cloned.1.call-done = bf16[1,512,2,688]{1,3,2,0:T(8,128)(2,1)} async-done(((bf16[4,512,2,688]{1,3,2,0:T(8,128)(2,1)}), bf16[1,512,2,688]{1,3,2,0:T(8,128)(2,1)}) %reduce-scatter.20.cloned.1.call-update) | async-done | bytes 1409040
  1607.0 149.8 %reduce-scatter.14.cloned.1.call-done = bf16[4000,512]{1,0:T(8,128)(2,1)} async-done(((bf16[4000,2048]{1,0:T(8,128)(2,1)}), bf16[4000,512]{1,0:T(8,128)(2,1)}) %reduce-scatter.14.cloned.1.call-update) | async-done | bytes 4096016 | tf_op jit(solution)/shard_map/reduce_scatter | solution.py:1144
  1756.9 7.3 multiply_reduce_fusion
  1765.5 39.5 %psum.39 = f32[]{:T(128)} all-reduce(f32[]{:T(128)S(6)} %add.200), channel_id=1, replica_groups=mesh['dp'=4,'head'=8] {'dp','head'}, use_global_device_ids=true, to_apply=%region_27.28 | all-reduce | flops 1 | bytes 8 | tf_op jit(solution)/shard_map/psum | solution.py:1320
  1816.5 5.2 multiply_subtract_fusion.1
  1821.6 3.0 copy.188
  1824.6 3.0 copy.190
  1827.7 3.9 fusion.27
  1831.6 3.0 copy.189
  1838.1 4.5 fusion.32
  1846.6 8.9 fusion.4
  1857.9 10.1 fusion.21
  1868.8 23.1 %multiply_subtract_fusion = (f32[4000,512]{1,0:T(8,128)}, f32[4000,512]{1,0:T(8,128)}, f32[4000,512]{1,0:T(8,128)}) fusion(f32[4000,512]{1,0:T(8,128)} %param.39, f32[]{:T(128)S(6)} %div.104, f32[4000,512]{1,0:T(8,128)} %get-tuple-element.79, bf16[4000,512]{1,0:T(8,128)(2,1)} %reduce-scatter.14.cloned.1.call-done, f32[4000,512]{1,0:T(8,128)} %param.41, ...), kind=kLoop, calls=%fused_computation.27 | loop fusion | flops 36864000 | bytes 61440004 | tf_op jit(solution)/shard_map/sub | solution.py:1025
  (277 shorter events, 97.5 us)
Async XLA Ops:
  7.2 6.9 copy-start.30
  7.2 200.9 %all-gather.12.cloned.1.call-start = ((), (), s32[]{:S(2)}) async-start(), calls=%async_computation.6 | async-start | bytes 1310720 | tf_op jit(solution)/shard_map/all_gather | solution.py:1297
  9.2 202.6 %all-gather.10.cloned.1.call-start = ((), (), s32[]{:S(2)}) async-start(), calls=%async_computation.5 | async-start | bytes 3522560 | tf_op jit(solution)/shard_map/all_gather | solution.py:1299
  11.6 208.1 %all-gather.14.cloned.1.call-start = ((), (), s32[]{:S(2)}) async-start(), calls=%async_computation.7 | async-start | bytes 3932160 | tf_op jit(solution)/shard_map/all_gather | solution.py:1296
  14.0 436.0 %all-gather.16.cloned.1.call-start = ((), (), s32[]{:S(2)}) async-start(), calls=%async_computation.8 | async-start | bytes 7045120 | tf_op jit(solution)/shard_map/all_gather | solution.py:1298
  15.4 15.8 copy-start.69
  15.4 16.6 copy-start.54
  15.4 17.2 copy-start.64
  15.4 17.9 copy-start.56
  15.4 32.0 %copy-start.43 = (f32[4,64,64]{2,1,0:T(8,128)S(1)}, f32[4,64,64]{2,1,0:T(8,128)}, u32[]{:S(2)}) copy-start(f32[4,64,64]{2,1,0:T(8,128)} %param.62) | copy-start | bytes 196612
  15.4 630.0 %all-gather.18.cloned.1.call-start = ((), (), s32[]{:S(2)}) async-start(), calls=%async_computation.9 | async-start | bytes 20480000 | tf_op jit(solution)/shard_map/all_gather | solution.py:1300
  21.4 1547.1 %all-reduce.11.cloned.1.call-start = ((), (), s32[]{:S(2)}) async-start(), calls=%async_computation.11 | async-start | bytes 262144 | tf_op jit(solution)/shard_map/psum | solution.py:1316
  31.1 166.1 %copy-start.46 = (s32[8192]{0:T(1024)}, s32[8192]{0:T(1024)S(1)}, u32[]{:S(2)}) copy-start(s32[8192]{0:T(1024)S(1)} %broadcast_subtract_fusion) | copy-start | bytes 98308
  33.9 163.4 %copy-start.68 = (f32[1,256]{1,0:T(1,128)}, f32[1,256]{1,0:T(1,128)S(1)}, u32[]{:S(2)}) copy-start(f32[1,256]{1,0:T(1,128)S(1)} %get-tuple-element.242.all_refs_4_) | copy-start | bytes 3076
  33.9 210.2 %copy-start.23 = (f32[1,256]{1,0:T(1,128)}, f32[1,256]{1,0:T(1,128)S(1)}, u32[]{:S(2)}) copy-start(f32[1,256]{1,0:T(1,128)S(1)} %get-tuple-element.240.rate_ref) | copy-start | bytes 3076
  45.9 187.1 %copy-start.61 = (f32[1,2048]{1,0:T(1,128)}, f32[1,2048]{1,0:T(1,128)S(1)}, u32[]{:S(2)}) copy-start(f32[1,2048]{1,0:T(1,128)S(1)} %all-gather.1) | copy-start | bytes 24580
  47.5 196.6 %copy-start.19 = (f32[2,128,128]{2,1,0:T(8,128)}, f32[2,128,128]{2,1,0:T(8,128)S(1)}, u32[]{:S(2)}) copy-start(f32[2,128,128]{2,1,0:T(8,128)S(1)} %select_maximum_fusion.initial_ref) | copy-start | bytes 393220
  203.0 30.0 %copy-start.59 = (f32[2048]{0:T(1024)}, f32[2048]{0:T(1024)S(1)}, u32[]{:S(2)}) copy-start(f32[2048]{0:T(1024)S(1)} %get-tuple-element.235) | copy-start | bytes 24580
  208.1 36.1 %copy-start.6 = (f32[32,64,64]{2,1,0:T(8,128)}, f32[32,64,64]{2,1,0:T(8,128)S(1)}, u32[]{:S(2)}) copy-start(f32[32,64,64]{2,1,0:T(8,128)S(1)} %get-tuple-element.231.earlier_ref) | copy-start | bytes 1572868
  208.1 36.1 %copy-start.8 = (f32[32,64,64]{2,1,0:T(8,128)}, f32[32,64,64]{2,1,0:T(8,128)S(1)}, u32[]{:S(2)}) copy-start(f32[32,64,64]{2,1,0:T(8,128)S(1)} %get-tuple-element.232.causal_ref) | copy-start | bytes 1572868
  233.0 10.3 copy-start.27
  243.7 50.9 %copy-start.2 = (f32[2048,128]{1,0:T(8,128)}, f32[2048,128]{1,0:T(8,128)S(1)}, u32[]{:S(2)}) copy-start(f32[2048,128]{1,0:T(8,128)S(1)} %broadcast_in_dim.95.first_ref) | copy-start | bytes 3145732
  244.0 56.6 %copy-start.4 = (f32[2048,128]{1,0:T(8,128)}, f32[2048,128]{1,0:T(8,128)S(1)}, u32[]{:S(2)}) copy-start(f32[2048,128]{1,0:T(8,128)S(1)} %broadcast_in_dim.96.last_ref) | copy-start | bytes 3145732
  244.2 56.5 %copy-start.21 = (f32[32,8,128]{2,1,0:T(8,128)}, f32[32,8,128]{2,1,0:T(8,128)S(1)}, u32[]{:S(2)}) copy-start(f32[32,8,128]{2,1,0:T(8,128)S(1)} %broadcast_in_dim.97.anew_ref) | copy-start | bytes 393220
  718.2 16.0 copy-start.51
  718.2 46.6 %slice-start = ((s8[33554432]{0:T(1024)(128)(4,1)}), s8[4194304]{0:T(1024)(128)(4,1)S(1)}, s32[]{:S(2)}) async-start(s8[33554432]{0:T(1024)(128)(4,1)} %bitcast.272), calls=%async_computation.16 | async-start | bytes 8388608
  718.2 46.6 %slice-start.1 = ((s8[33554432]{0:T(1024)(128)(4,1)}), s8[4194304]{0:T(1024)(128)(4,1)S(1)}, s32[]{:S(2)}) async-start(s8[33554432]{0:T(1024)(128)(4,1)} %bitcast.272), calls=%async_computation.17 | async-start | bytes 8388608
  718.2 46.6 %slice-start.2 = ((s8[33554432]{0:T(1024)(128)(4,1)}), s8[4194304]{0:T(1024)(128)(4,1)S(1)}, s32[]{:S(2)}) async-start(s8[33554432]{0:T(1024)(128)(4,1)} %bitcast.272), calls=%async_computation.18 | async-start | bytes 8388608
  718.2 46.6 %slice-start.3 = ((s8[33554432]{0:T(1024)(128)(4,1)}), s8[4194304]{0:T(1024)(128)(4,1)S(1)}, s32[]{:S(2)}) async-start(s8[33554432]{0:T(1024)(128)(4,1)} %bitcast.272), calls=%async_computation.19 | async-start | bytes 8388608
  734.2 29.9 %copy-start.55 = (s32[2048]{0:T(1024)S(1)}, s32[2048]{0:T(1024)}, u32[]{:S(2)}) copy-start(s32[2048]{0:T(1024)} %param.36) | copy-start | bytes 24580
  734.2 30.6 %slice-start.4 = ((s8[33554432]{0:T(1024)(128)(4,1)}), s8[4194304]{0:T(1024)(128)(4,1)S(1)}, s32[]{:S(2)}) async-start(s8[33554432]{0:T(1024)(128)(4,1)} %bitcast.272), calls=%async_computation.20 | async-start | bytes 8388608
  734.2 30.6 %slice-start.5 = ((s8[33554432]{0:T(1024)(128)(4,1)}), s8[4194304]{0:T(1024)(128)(4,1)S(1)}, s32[]{:S(2)}) async-start(s8[33554432]{0:T(1024)(128)(4,1)} %bitcast.272), calls=%async_computation.21 | async-start | bytes 8388608
  734.2 30.6 %slice-start.6 = ((s8[33554432]{0:T(1024)(128)(4,1)}), s8[4194304]{0:T(1024)(128)(4,1)S(1)}, s32[]{:S(2)}) async-start(s8[33554432]{0:T(1024)(128)(4,1)} %bitcast.272), calls=%async_computation.22 | async-start | bytes 8388608
  734.2 30.6 %slice-start.7 = ((s8[33554432]{0:T(1024)(128)(4,1)}), s8[4194304]{0:T(1024)(128)(4,1)S(1)}, s32[]{:S(2)}) async-start(s8[33554432]{0:T(1024)(128)(4,1)} %bitcast.272), calls=%async_computation.23 | async-start | bytes 8388608
  734.2 30.6 %copy-start.52 = (f32[2048]{0:T(1024)S(1)}, f32[2048]{0:T(1024)}, u32[]{:S(2)}) copy-start(f32[2048]{0:T(1024)} %convert_element_type.234) | copy-start | bytes 24580
  820.7 154.1 %copy-start.34 = (bf16[2048,688]{1,0:T(8,128)(2,1)S(1)}, bf16[2048,688]{1,0:T(8,128)(2,1)}, u32[]{:S(2)}) copy-start(bf16[2048,688]{1,0:T(8,128)(2,1)} %multiply_convert_fusion.1.all_refs_1_) | copy-start | bytes 8454148
  974.8 9.1 copy-start.35
  1068.4 150.2 %copy-start.40 = (bf16[4,32,8,512]{3,2,0,1:T(8,128)(2,1)S(1)}, bf16[4,32,8,512]{3,2,0,1:T(8,128)(2,1)}, u32[]{:S(2)}) copy-start(bf16[4,32,8,512]{3,2,0,1:T(8,128)(2,1)} %copy.206) | copy-start | bytes 3145732
  1225.8 6.7 copy-start.20
  1225.8 6.7 copy-start.22
  1225.8 6.7 copy-start.24
  1245.2 79.6 %copy-start.60 = (f32[2048]{0:T(1024)S(1)}, f32[2048]{0:T(1024)}, u32[]{:S(2)}) copy-start(f32[2048]{0:T(1024)} %copy-done.59) | copy-start | bytes 24580
  1245.2 79.6 %copy-start.62 = (f32[1,2048]{1,0:T(1,128)S(1)}, f32[1,2048]{1,0:T(1,128)}, u32[]{:S(2)}) copy-start(f32[1,2048]{1,0:T(1,128)} %copy-done.61) | copy-start | bytes 24580
  1324.8 246.6 %reduce-scatter.18.cloned.1.call-start = ((), (), s32[]{:S(2)}) async-start(), calls=%async_computation.13 | async-start | bytes 1310720
  1324.9 11.2 copy-start.15
  1356.1 217.0 %reduce-scatter.22.cloned.1.call-start = ((), (), s32[]{:S(2)}) async-start(), calls=%async_computation.15 | async-start | bytes 3522560
  1356.8 218.3 %reduce-scatter.16.cloned.1.call-start = ((), (), s32[]{:S(2)}) async-start(), calls=%async_computation.12 | async-start | bytes 3932160
  1357.6 245.5 %reduce-scatter.20.cloned.1.call-start = ((), (), s32[]{:S(2)}) async-start(), calls=%async_computation.14 | async-start | bytes 7045120
  1366.0 390.9 %reduce-scatter.14.cloned.1.call-start = ((), (), s32[]{:S(2)}) async-start(), calls=%async_computation.10 | async-start | bytes 20480000 | tf_op jit(solution)/shard_map/reduce_scatter | solution.py:1144
  1366.8 9.9 copy-start.28
  1373.0 6.8 copy-start.53
  1381.2 167.2 %copy-start.67 = (f32[1,256]{1,0:T(1,128)S(1)}, f32[1,256]{1,0:T(1,128)}, u32[]{:S(2)}) copy-start(f32[1,256]{1,0:T(1,128)} %get-tuple-element.241) | copy-start | bytes 3076
  1756.9 51.6 %copy-start.36 = (bf16[1,688,512]{2,1,0:T(8,128)(2,1)S(1)}, bf16[1,688,512]{2,1,0:T(8,128)(2,1)}, u32[]{:S(2)}) copy-start(bf16[1,688,512]{2,1,0:T(8,128)(2,1)} %reduce-scatter.22.cloned.1.call-done) | copy-start | bytes 2113540
  1809.2 28.9 %copy-start.26 = (f32[1,688,512]{2,1,0:T(8,128)}, f32[1,688,512]{2,1,0:T(8,128)S(1)}, u32[]{:S(2)}) copy-start(f32[1,688,512]{2,1,0:T(8,128)S(1)} %convert_multiply_fusion.6) | copy-start | bytes 4227076
  1814.2 41.3 %copy-start.31 = (f32[1,256,512]{2,1,0:T(8,128)}, f32[1,256,512]{2,1,0:T(8,128)S(1)}, u32[]{:S(2)}) copy-start(f32[1,256,512]{2,1,0:T(8,128)S(1)} %convert_multiply_fusion.8) | copy-start | bytes 1572868
  1827.7 9.8 copy-start.57
  1827.7 9.8 copy-start.65
  1827.7 9.8 copy-start.66
  1846.6 8.9 copy-start.38
  1846.6 8.9 copy-start.42
  1857.9 10.1 copy-start.44
  1857.9 10.1 copy-start.45
  1857.9 10.1 copy-start.49
  1857.9 10.1 copy-start.50
  (26 other events, 78.0 us)
Sparse Core Ops, SparseCore 0:
  10.5 29.3 all-gather.11
  42.2 45.1 all-gather.9
  89.8 67.9 all-gather.13
  160.1 78.3 all-gather.15
  240.7 154.1 all-gather.17
  1324.9 42.5 all-reduce.10
  1371.2 27.7 reduce-scatter.17
  1402.6 50.7 reduce-scatter.21
  1457.0 71.0 reduce-scatter.15
  1531.6 71.4 reduce-scatter.19
  1606.3 150.5 reduce-scatter.13

commit v4 on v3

--- a/solution.py
+++ b/solution.py
@@ -347,6 +347,9 @@
         compiler_params=pltpu.CompilerParams(
             dimension_semantics=("arbitrary",), vmem_limit_bytes=32 * 1024 * 1024
         ),
+        cost_estimate=pl.CostEstimate(
+            flops=0, bytes_accessed=90000 * tokens, transcendentals=0
+        ),
         name="inner_forward",
     )(qkv, rate, initial, causal, earlier, first, last, anew)
 
@@ -389,6 +392,9 @@
         compiler_params=pltpu.CompilerParams(
             dimension_semantics=("arbitrary",), vmem_limit_bytes=32 * 1024 * 1024
         ),
+        cost_estimate=pl.CostEstimate(
+            flops=0, bytes_accessed=140000 * tokens, transcendentals=0
+        ),
         name="inner_backward",
     )(
         qkv,
@@ -407,18 +413,18 @@
     )
 
 
-ROWS = 128
+ROWS = 64
 LAG = 2
 MESH = pl.DeviceIdType.MESH
 
 
-def across(column, size):
-    return jnp.swapaxes(jnp.broadcast_to(column, (size, size)), 0, 1)[:8]
-
-
-def down(row, size, width):
-    turned = jnp.swapaxes(jnp.broadcast_to(row[:1], (size, size)), 0, 1)
-    return jnp.concatenate([turned] * (width // size), 1) if width > size else turned[:, :width]
+def across(column):
+    return jnp.swapaxes(jnp.broadcast_to(column, (column.shape[0], 128)), 0, 1)[:8]
+
+
+def down(row, width):
+    turned = jnp.swapaxes(jnp.broadcast_to(row[:1], (128, row.shape[1])), 0, 1)
+    return jnp.concatenate([turned] * (width // 128), 1) if width > 128 else turned
 
 
 def transit_kernel(mode, form, parts, slabs, names, *all_refs):
@@ -515,7 +521,7 @@
         return remote(
             ref["sums_out"].at[slot],
             ref["sums_in"].at[slot, offset - 1],
-            ref["sums_out_sem"].at[slot, offset - 1],
+            ref["sums_out_sem"].at[slot],
             ref["sums_in_sem"].at[slot],
             {"head": lax.rem(me + offset, parts)},
         )
@@ -548,12 +554,12 @@
     def target(chunk, giver):
         if form == "lookup":
             return full_ref.at[rows_of(chunk), shard(2 * giver + core)]
-        return full_ref.at[chunk, rows_of(giver), shard(core)]
+        return full_ref.at[chunk // 2, rows_of(lax.rem(chunk, 2) * slabs + giver), shard(core)]
 
     def mirror(chunk, index):
         part = target(chunk, index) if cross else piece(chunk, index)
         return remote(
-            part, part, ref["twin_out_sem"].at[chunk, index], ref["twin_in_sem"].at[chunk], twin
+            part, part, ref["twin_out_sem"].at[chunk], ref["twin_in_sem"].at[chunk], twin
         )
 
     def hand_over(chunk, source):
@@ -580,7 +586,8 @@
             if form == "lookup":
                 full_ref[rows_of(chunk), shard(2 * mine_dp + core)] = values
             else:
-                full_ref[chunk, rows_of(mine_dp), shard(core)] = values
+                place_rows = rows_of(lax.rem(chunk, 2) * slabs + mine_dp)
+                full_ref[chunk // 2, place_rows, shard(core)] = values
             mirror(chunk, mine_dp).start()
 
     def receive(step):
@@ -651,11 +658,11 @@
             elif mode == "norm":
                 scale = lax.rsqrt(summed / D + EPSILON)
                 ref["scale"][chunk] = scale
-                result = ref["own"][rows, :] * down(scale, ROWS, size) * gain
+                result = ref["own"][rows, :] * down(scale, size) * gain
             else:
-                scale = down(ref["scale"][chunk], ROWS, size)
+                scale = down(ref["scale"][chunk], size)
                 normed = ref["inputs"][rows, :] * scale
-                inner = down(summed / D, ROWS, size)
+                inner = down(summed / D, size)
                 result = scale * (ref["own"][rows, :] * gain - normed * inner)
                 if mode == "grad_add":
                     result = result + ref["added"][rows, :]
@@ -731,8 +738,11 @@
                         fall(chunk, place).wait_send()
 
             if summing:
-                for offset in range(1, parts):
-                    sums_copy(chunk, offset).wait_send()
+                slot = lax.rem(chunk, ring)
+                sums_in = ref["sums_in"]
+                pltpu.make_async_copy(
+                    sums_in.at[slot], sums_in.at[slot], ref["sums_out_sem"].at[slot]
+                ).wait()
 
     def sum_shard(step):
         chunk = step - sum_at
@@ -768,12 +778,12 @@
                 value = value + ref["inputs"][rows, :]
                 column = jnp.sum(value * value, 1, keepdims=True)
             else:
-                scale = down(ref["scale"][chunk], ROWS, size)
+                scale = down(ref["scale"][chunk], size)
                 normed = ref["inputs"][rows, :] * scale
                 ref["gain_grad"][0:1, :] += jnp.sum(value * normed, 0, keepdims=True)
                 column = jnp.sum(value * ref["gain"][0:1, :] * normed, 1, keepdims=True)
             ref["own"][rows, :] = value
-            ref["sums_out"][slot] = across(column, ROWS)
+            ref["sums_out"][slot] = across(column)
             for offset in range(1, parts):
                 sums_copy(chunk, offset).start()
 
@@ -786,16 +796,22 @@
             right_ref = ref["right"]
             if form == "lookup":
                 entries = right_ref.shape[0]
+                ids = jnp.concatenate(
+                    [ref["ids"][group, rows_of(chunk), 0:1] for group in range(slabs)], 0
+                )
+                spots = lax.broadcasted_iota(jnp.int32, (slabs * ROWS, entries), 1)
+                hits = (spots == ids).astype(jnp.bfloat16)
+                other = dot_ab(hits, right_ref[:, shard(1 - core)]).astype(jnp.bfloat16)
                 for group in range(slabs):
-                    ids = ref["ids"][group, rows_of(chunk), 0:1]
-                    spots = lax.broadcasted_iota(jnp.int32, (ROWS, entries), 1)
-                    hits = (spots == ids).astype(jnp.bfloat16)
-                    lanes = pl.ds(group * size, size)
-                    pair_out[slot, :, lanes] = dot_ab(hits, right_ref[:, shard(1 - core)]).astype(
-                        jnp.bfloat16
-                    )
-                    partial[slot, :, lanes] = dot_ab(hits, right_ref[:, shard(core)])
+                    pair_out[slot, :, pl.ds(group * size, size)] = other[
+                        group * ROWS : (group + 1) * ROWS
+                    ]
                 pair_copy(chunk).start()
+                here = dot_ab(hits, right_ref[:, shard(core)])
+                for group in range(slabs):
+                    partial[slot, :, pl.ds(group * size, size)] = here[
+                        group * ROWS : (group + 1) * ROWS
+                    ]
                 return
             half = lax.rem(chunk, 2)
             left_copy(chunk).wait()
@@ -823,12 +839,11 @@
         @pl.when(valid(chunk))
         def _():
             if form == "table":
-                arrived = full_ref.at[chunk, :, pl.ds(0, size)]
+                arrived = full_ref.at[chunk // 2, pl.ds(0, slabs * ROWS), pl.ds(0, size)]
             else:
                 arrived = full_ref.at[rows_of(chunk), pl.ds(0, places * size)]
             pltpu.make_async_copy(arrived, arrived, ref["twin_in_sem"].at[chunk]).wait()
-            for index in range(places):
-                mirror(chunk, index).wait_send()
+            pltpu.make_async_copy(arrived, arrived, ref["twin_out_sem"].at[chunk]).wait()
             if cross:
                 for offset in range(1, slabs):
                     hand_over(chunk, lax.rem(mine_dp + offset, slabs)).wait_send()
@@ -846,19 +861,21 @@
                     sink(chunk, source_high, hop).wait_send()
 
             if form == "table":
-                table_grad = ref["table_grad"]
-                entries = table_grad.shape[0]
-                pieces = 5 if entries % 80 == 0 else 1
-                block = entries // pieces
-                ids = ref["ids"][chunk, 0:1, :]
-                values = full_ref[chunk]
-                for index in range(pieces):
-                    spots = index * block + lax.broadcasted_iota(
-                        jnp.int32, (block, ids.shape[1]), 0
-                    )
-                    hits = (spots == ids).astype(jnp.bfloat16)
-                    span = pl.ds(index * block, block)
-                    table_grad[span, :] += dot_ab(hits, values)
+                @pl.when(lax.rem(chunk, 2) == 1)
+                def _():
+                    table_grad = ref["table_grad"]
+                    entries = table_grad.shape[0]
+                    pieces = 5 if entries % 80 == 0 else 1
+                    block = entries // pieces
+                    ids = ref["ids"][chunk // 2, 0:1, :]
+                    values = full_ref[chunk // 2]
+                    for index in range(pieces):
+                        spots = index * block + lax.broadcasted_iota(
+                            jnp.int32, (block, ids.shape[1]), 0
+                        )
+                        hits = (spots == ids).astype(jnp.bfloat16)
+                        span = pl.ds(index * block, block)
+                        table_grad[span, :] += dot_ab(hits, values)
 
     def advance(step, carried):
         relay(step)
@@ -938,7 +955,7 @@
     hops = max(places - 1, 1)
     if form == "table":
         scratch["own"] = pltpu.VMEM((tokens, size), wide_kind)
-        scratch["full"] = pltpu.VMEM((chunks, slabs * ROWS, 2 * size), low)
+        scratch["full"] = pltpu.VMEM((chunks // 2, 2 * slabs * ROWS, 2 * size), low)
     if left is not None:
         scratch["left_buf"] = pltpu.VMEM((2, ROWS, left.shape[1]), low)
         scratch["left_sem"] = dma((2,))
@@ -949,7 +966,7 @@
     if summing:
         scratch["sums_out"] = pltpu.VMEM((ring, 8, ROWS), wide_kind)
         scratch["sums_in"] = pltpu.VMEM((ring, parts - 1, 8, ROWS), wide_kind)
-        scratch["sums_out_sem"] = dma((ring, parts - 1))
+        scratch["sums_out_sem"] = dma((ring,))
         scratch["sums_in_sem"] = dma((ring,))
     scratch["total"] = pltpu.VMEM((ROWS, size), wide_kind)
     scratch["partial"] = pltpu.VMEM((ring, ROWS, span), wide_kind)
@@ -959,7 +976,7 @@
         scratch[name + "_sem"] = dma((ring,))
     for name in ("up_out", "up_in", "down_out", "down_in"):
         scratch[name + "_sem"] = dma((chunks, hops))
-    scratch["twin_out_sem"] = dma((chunks, places))
+    scratch["twin_out_sem"] = dma((chunks,))
     scratch["twin_in_sem"] = dma((chunks,))
 
     depth = right.shape[1] if form in ("turned", "table") else right.shape[0]
@@ -983,6 +1000,127 @@
     return dict(zip(outputs, results))
 
 
+def share_kernel(axes, block_ref, all_ref, out_sem, in_sem):
+    counts = [lax.axis_size(axis) for axis in axes]
+    places = [lax.axis_index(axis) for axis in axes]
+    members = 1
+    me = 0
+    for count, place in zip(counts, places):
+        members = members * count
+        me = me * count + place
+
+    def partner(offset):
+        device, rest = {}, offset
+        for axis, count, place in reversed(list(zip(axes, counts, places))):
+            device[axis] = lax.rem(place + lax.rem(rest, count), count)
+            rest = rest // count
+        return device
+
+    def send(offset):
+        return pltpu.make_async_remote_copy(
+            src_ref=block_ref,
+            dst_ref=all_ref.at[me],
+            send_sem=out_sem,
+            recv_sem=in_sem,
+            device_id=partner(offset),
+            device_id_type=MESH,
+        )
+
+    barrier = pltpu.get_barrier_semaphore()
+
+    def greet(offset, carried):
+        pl.semaphore_signal(barrier, inc=1, device_id=partner(offset), device_id_type=MESH)
+        return carried
+
+    def start(offset, carried):
+        send(offset).start()
+        return carried
+
+    lax.fori_loop(1, members, greet, 0)
+    all_ref[me] = block_ref[...]
+    pl.semaphore_wait(barrier, members - 1)
+    lax.fori_loop(1, members, start, 0)
+    arrived = all_ref.at[pl.ds(0, members - 1)]
+    pltpu.make_async_copy(arrived, arrived, in_sem).wait()
+    pltpu.make_async_copy(arrived, arrived, out_sem).wait()
+
+
+def share(number, block, axes):
+    members = 1
+    for axis in axes:
+        members = members * lax.axis_size(axis)
+    vmem = pl.BlockSpec(memory_space=pltpu.VMEM)
+    return pl.pallas_call(
+        functools.partial(share_kernel, axes),
+        in_specs=[vmem],
+        out_specs=vmem,
+        out_shape=jax.ShapeDtypeStruct((members,) + block.shape, block.dtype),
+        scratch_shapes=[pltpu.SemaphoreType.DMA, pltpu.SemaphoreType.DMA],
+        compiler_params=pltpu.CompilerParams(
+            collective_id=number, has_side_effects=True, vmem_limit_bytes=16 * 1024 * 1024
+        ),
+        cost_estimate=pl.CostEstimate(
+            flops=0, bytes_accessed=16 * 1024 * 1024, transcendentals=0
+        ),
+        name="share",
+    )(block)
+
+
+SCORE_ROWS = 256
+
+
+def scores_kernel(rows_ref, table_ref, goal_ref, logits_ref, stats_ref):
+    entries = table_ref.shape[0]
+    edges = list(range(0, entries, 1024)) + [entries]
+    peak = jnp.full((SCORE_ROWS, 1), -jnp.inf, jnp.float32)
+    for low, high in zip(edges, edges[1:]):
+        values = dot_abt(rows_ref[...], table_ref[low:high, :])
+        logits_ref[:, low:high] = values
+        peak = jnp.maximum(peak, jnp.max(values, 1, keepdims=True))
+    exp_sum = jnp.zeros((SCORE_ROWS, 1), jnp.float32)
+    picked = jnp.zeros((SCORE_ROWS, 1), jnp.float32)
+    goal = goal_ref[:, 0:1]
+    for low, high in zip(edges, edges[1:]):
+        values = logits_ref[:, low:high]
+        exp_sum = exp_sum + jnp.sum(jnp.exp(values - peak), 1, keepdims=True)
+        spots = low + lax.broadcasted_iota(jnp.int32, values.shape, 1)
+        picked = picked + jnp.sum(jnp.where(spots == goal, values, 0.0), 1, keepdims=True)
+    stats_ref[0] = jnp.broadcast_to(peak, (SCORE_ROWS, 128))
+    stats_ref[1] = jnp.broadcast_to(exp_sum, (SCORE_ROWS, 128))
+    stats_ref[2] = jnp.broadcast_to(picked, (SCORE_ROWS, 128))
+
+
+def scores(rows, table, goals):
+    tokens, width = rows.shape
+    entries = table.shape[0]
+    return pl.pallas_call(
+        scores_kernel,
+        grid=(tokens // SCORE_ROWS,),
+        in_specs=[
+            pl.BlockSpec((SCORE_ROWS, width), lambda i: (i, 0)),
+            pl.BlockSpec(memory_space=pltpu.VMEM),
+            pl.BlockSpec((SCORE_ROWS, 128), lambda i: (i, 0)),
+        ],
+        out_specs=[
+            pl.BlockSpec((SCORE_ROWS, entries), lambda i: (i, 0)),
+            pl.BlockSpec((3, SCORE_ROWS, 128), lambda i: (0, i, 0)),
+        ],
+        out_shape=[
+            jax.ShapeDtypeStruct((tokens, entries), jnp.float32),
+            jax.ShapeDtypeStruct((3, tokens, 128), jnp.float32),
+        ],
+        compiler_params=pltpu.CompilerParams(
+            dimension_semantics=("arbitrary",), vmem_limit_bytes=56 * 1024 * 1024
+        ),
+        cost_estimate=pl.CostEstimate(
+            flops=2 * tokens * entries * width,
+            bytes_accessed=2 * entries * width + 4 * tokens * entries,
+            transcendentals=tokens * entries,
+        ),
+        name="scores",
+    )(rows, table, goals)
+
+
 def shampoo(tile_w, tile_g, left, right, left_root, right_root):
     low_g = tile_g.astype(jnp.bfloat16)
 
@@ -1011,7 +1149,7 @@
         left_root,
         right_root,
     )
-    return (grad, new_left, new_right, new_w.reshape(master.shape))
+    return (grad.reshape(master.shape), new_left, new_right, new_w.reshape(master.shape))
 
 
 def adamw(weight, grad, first, second, step_rate):
@@ -1026,21 +1164,19 @@
 
 
 def layer_forward(
-    token_ids, targets, valid, resets, emb_low, weights, inner_init, gains, head_index
+    local_ids, targets, valid, resets, emb_low, weights, inner_init, gains, gain_one, head_index
 ):
     w_qkv, w_out, w_gu, w_down, table = weights
     parts, slabs = lax.axis_size("head"), lax.axis_size("dp")
     vocab_part = table.shape[0]
-    tokens, size = token_ids.shape[0], gains.shape[1]
+    tokens, size = targets.shape[0], gains.shape[1]
     chunks = tokens // ROWS
     columns = jnp.arange(vocab_part, dtype=jnp.int32)
-    local_ids = lax.all_gather(token_ids, "dp", axis=0) - head_index * vocab_part
     spread_ids = jnp.broadcast_to(local_ids[:, :, None], (slabs, tokens, 128))
     first = transit("plain", "lookup", 1, parts, slabs, emb_low, tokens, size, ids=spread_ids)
     low_embedded = first["full"]
     wide_embedded = low_embedded.astype(jnp.float32)
     scale_one = lax.rsqrt(jnp.mean(wide_embedded * wide_embedded, -1) + EPSILON)
-    gain_one = lax.all_gather(gains[0], "head", axis=0, tiled=True)
     full_one = (wide_embedded * scale_one[:, None] * gain_one[None]).astype(jnp.bfloat16)
     embedded = lax.dynamic_slice_in_dim(low_embedded, head_index * size, size, 1)
     embedded = embedded.astype(jnp.float32)
@@ -1086,20 +1222,12 @@
         gain=gains[2:3],
     )
     hidden_two, full_end, scale_end = third["own"], third["full"], third["scale"]
-    logits = jnp.einsum("td,vd->tv", full_end, table, preferred_element_type=jnp.float32)
-    peak = jnp.max(logits, -1)
-    target_hits = columns[None, :] == (targets - head_index * vocab_part)[:, None]
-    stats = lax.all_gather(
-        jnp.stack(
-            [
-                peak,
-                jnp.sum(jnp.exp(logits - peak[:, None]), -1),
-                jnp.sum(jnp.where(target_hits, logits, 0.0), -1),
-            ]
-        ),
-        "head",
-        axis=0,
-    )
+    local_targets = targets - head_index * vocab_part
+    target_hits = columns[None, :] == local_targets[:, None]
+    logits, stats = scores(
+        full_end, table, jnp.broadcast_to(local_targets[:, None], (tokens, 128))
+    )
+    stats = share(7, stats[:, :, 0].reshape(-1, 128), ("head",)).reshape(parts, 3, tokens)
     highest = jnp.max(stats[:, 0], 0)
     exp_sum = jnp.sum(stats[:, 1] * jnp.exp(stats[:, 0] - highest[None]), 0)
     target_logit = jnp.sum(stats[:, 2], 0)
@@ -1128,9 +1256,9 @@
     return (jnp.sum((totals - target_logit) * counted), jnp.sum(counted), kept)
 
 
-def slots_of(grad, order, kinds):
+def slots_of(grad, order):
     parts = lax.axis_size("dp")
-    shaped = grad.astype(jnp.bfloat16).reshape(parts, -1, kinds, grad.shape[1] // kinds)
+    shaped = grad.astype(jnp.bfloat16).reshape(parts, -1, grad.shape[1])
     return jnp.take(shaped, order, axis=0, mode="clip")
 
 
@@ -1209,9 +1337,10 @@
         added=d_two,
     )
     d_one, d_out_in = fifth["own"], fifth["full"]
+    d_out_in, owned_down = lax.optimization_barrier((d_out_in, owned_down))
     d_inner = jnp.einsum("td,cd->tc", d_out_in, w_out, preferred_element_type=wide_kind)
     grad_gu = jnp.einsum("td,tc->dc", full_two, d_gate_up, preferred_element_type=wide_kind)
-    slot_gu = slots_of(grad_gu, order[2], 2)
+    slot_gu = slots_of(grad_gu, order[2])
     d_inner, slot_gu = lax.optimization_barrier((d_inner, slot_gu))
     owned_gu = scatter_dp(slot_gu, 0)
     d_mixed, grad_pairs, grad_step = mixer_backward(*inner_kept, d_inner)
@@ -1221,13 +1350,15 @@
     grad_out = jnp.einsum("tc,td->cd", inner_low, d_out_in, preferred_element_type=wide_kind)
     grad_qkv = jnp.einsum("td,tc->dc", full_one, d_mixed, preferred_element_type=wide_kind)
     slot_out = column_slots_of(grad_out, order[1])
-    slot_qkv = slots_of(grad_qkv, order[0], 3)
-    d_mixed, slot_out, slot_qkv = lax.optimization_barrier((d_mixed, slot_out, slot_qkv))
+    slot_qkv = slots_of(grad_qkv, order[0])
+    d_mixed, slot_out, slot_qkv, owned_table, owned_gu = lax.optimization_barrier(
+        (d_mixed, slot_out, slot_qkv, owned_table, owned_gu)
+    )
     owned_out = scatter_dp(slot_out, 0)
     owned_qkv = scatter_dp(slot_qkv, 0)
-    row_ids = jnp.swapaxes(local_ids.reshape(slabs, chunks, ROWS), 0, 1)
+    row_ids = jnp.moveaxis(local_ids.reshape(slabs, chunks // 2, 2, ROWS), 0, 2)
     row_ids = jnp.broadcast_to(
-        row_ids.reshape(chunks, 1, slabs * ROWS), (chunks, 8, slabs * ROWS)
+        row_ids.reshape(chunks // 2, 1, 2 * slabs * ROWS), (chunks // 2, 8, 2 * slabs * ROWS)
     )
     sixth = transit(
         "grad_add",
@@ -1291,11 +1422,25 @@
     gains_second,
 ):
     low = jnp.bfloat16
+    dp_size, head_size = lax.axis_size("dp"), lax.axis_size("head")
+    head_index = lax.axis_index("head")
+    ids_rows = token_ids.astype(jnp.float32).reshape(-1, 128)
+    gain_rows = jnp.pad(gains[0].reshape(-1, 128), ((0, 8 - gains.shape[1] // 128), (0, 0)))
+    opening = share(8, jnp.concatenate([ids_rows, gain_rows], 0), ("dp", "head"))
+    opening = opening.reshape(dp_size, head_size, -1, 128)
+    local_ids = opening[:, 0, : ids_rows.shape[0]].reshape(dp_size, -1).astype(jnp.int32)
+    local_ids = local_ids - head_index * emb_master.shape[0]
+    gain_one = opening[0, :, ids_rows.shape[0] :].reshape(head_size, -1)
+    gain_one = gain_one[:, : gains.shape[1]].reshape(-1)
     emb_low = emb_master.astype(low)
+
+    def flat(array):
+        return array.reshape(array.shape[1], -1)
+
     gathered = (
-        lax.all_gather(qkv_master.astype(low), "dp", axis=0, tiled=True),
+        lax.all_gather(flat(qkv_master).astype(low), "dp", axis=0),
         lax.all_gather(out_master.astype(low), "dp", axis=0, tiled=True),
-        lax.all_gather(gu_master.astype(low), "dp", axis=0, tiled=True),
+        lax.all_gather(flat(gu_master).astype(low), "dp", axis=0),
         lax.all_gather(down_master.astype(low), "dp", axis=0, tiled=True),
         lax.all_gather(emb_low, "dp", axis=1, tiled=True),
     )
@@ -1306,18 +1451,25 @@
     w_down = jnp.take(gathered[3], owners[3], axis=0, mode="clip")
     w_down = jnp.swapaxes(w_down, 0, 1).reshape(w_down.shape[1], D)
     weights = (w_qkv, w_out, w_gu, w_down, gathered[4])
-    head_index = lax.axis_index("head")
     loss_local, count_local, kept = layer_forward(
-        token_ids, targets, valid, resets, emb_low, weights, inner_init, gains, head_index
-    )
-    loss_sum, count = lax.psum((loss_local, count_local), "dp")
+        local_ids, targets, valid, resets, emb_low, weights, inner_init, gains, gain_one, head_index
+    )
     order = jnp.argsort(owners, axis=1)
     owned, grad_init, grad_gains = layer_backward(kept, weights, gains, order)
-    small = lax.psum((grad_init, grad_gains), "dp")
+    init_rows = grad_init.size // 128
+    numbers = jnp.zeros((8, 128), jnp.float32).at[0, 0].set(loss_local).at[0, 1].set(count_local)
+    pieces = (grad_init.reshape(-1, 128), grad_gains.reshape(-1, 128), numbers)
+    small = jnp.sum(share(9, jnp.concatenate(pieces, 0), ("dp",)), 0)
+    loss_sum, count = small[-8, 0], small[-8, 1]
+    small = (
+        small[:init_rows].reshape(grad_init.shape),
+        small[init_rows:-8].reshape(grad_gains.shape),
+    )
     first_dp = (lax.axis_index("dp") == 0).astype(jnp.float32)
     squares = sum((jnp.sum(piece * piece) for piece in owned))
     squares = squares + first_dp * (jnp.sum(small[0] * small[0]) + jnp.sum(small[1] * small[1]))
-    squares_all = lax.psum(squares, ("dp", "head"))
+    squares = share(10, jnp.broadcast_to(squares, (8, 128)), ("dp", "head"))
+    squares_all = jnp.sum(squares[:, 0, 0])
     grad_norm = jnp.sqrt(squares_all) / count
     factor = jnp.minimum(1.0, CLIP_LIMIT / grad_norm) / count
     qkv_out = refresh(

time: 1910 us -> 1730 us (0.906)
  Pallas kernels: 1040 us -> 1140 us
  blocking collectives: 93 us -> 0 us
  local copies, waits for them, and re-layouts: 205 us -> 143 us
  waiting for transfers between devices: 176 us -> 117 us
  matrix products: 227 us -> 180 us
  other arithmetic: 136 us -> 110 us
    pallas_call x0 -> x5, Pallas kernels: none -> 91.2 us  [the longest x1 52.5 us: scores(): pl.pallas_call(scores_kernel, grid=(tokens // SCORE_ROWS,), in_specs=[pl....]
    psum x2 -> x0, blocking collectives: 57.1 us -> none  [the longest x1 39.5 us: shards(): squares_all = lax.psum(squares, ('dp', 'head'))]
    dot_general x1 -> x0, matrix products: 42.1 us -> none  [layer_forward(): jnp.einsum('td,vd->tv', full_end, table, preferred_element_type=jnp.float32)]
    all_gather x3 -> x0, blocking collectives: 35.9 us -> none  [the longest x1 14.2 us: layer_forward(): lax.all_gather(jnp.stack([peak, jnp.sum(jnp.exp(logits - peak[:, None]),...]
    reduce_scatter x1, waiting for transfers between devices: 150 us -> 116 us  [scatter_dp(): return lax.psum_scatter(grad, 'dp', scatter_dimension=dimension, tiled=True)]
    reshape x6 -> x3, local copies, waits for them, and re-layouts: 41.4 us -> 9.16 us  [the longest x1 8.37 us: slots_of(): shaped = grad.astype(jnp.bfloat16).reshape(parts, -1, grad.shape[1])]
    reduce_sum x2 -> x3, other arithmetic: 31.3 us -> 2.11 us  [the longest x1 1.46 us: layer_forward(): target_logit = jnp.sum(stats[:, 2], 0)]
    unnamed x15 -> x12, waiting for transfers between devices: 26.4 us -> 1.36 us
  transfers between devices with their start and end apart: 11 -> 10, of which waited for: 2 -> 1; matrix products, arithmetic and copies ran while one was open for 10% -> 11% of each run, Pallas kernels for 35% -> 52%
where the time goes in v4:
time: 1730 us; the launch traced here: 1720 us
  Pallas kernels  1140 us (66%)
  matrix products  180 us (10%)
  local copies, waits for them, and re-layouts  143 us (8%)
  waiting for transfers between devices  117 us (7%)
  other arithmetic  110 us (6%)
  between operations  24.3 us (1%)
    pallas_call x6, Pallas kernels, transit(): pl.pallas_call(functools.partial(transit_kernel, mode, form, parts, slabs...  923 us
    reduce_scatter x1, waiting for transfers between devices, scatter_dp(): return lax.psum_scatter(grad, 'dp', scatter_dimension=dimension, tiled=True)  116 us
    pallas_call x1, Pallas kernels, mixer_backward(): pl.pallas_call(mixer_backward_kernel, grid=(chunks,), in_specs=[rows(3 *...  77 us
    pallas_call x1, Pallas kernels, scores(): pl.pallas_call(scores_kernel, grid=(tokens // SCORE_ROWS,), in_specs=[pl....  52.5 us
    pallas_call x1, Pallas kernels, mixer_forward(): pl.pallas_call(mixer_forward_kernel, grid=(chunks,), in_specs=[pl.BlockSp...  50.2 us
    dot_general x12, matrix products, product(): jnp.einsum(form, one.astype(jnp.bfloat16), two.astype(jnp.bfloat16), pref...  44.6 us
    dot_general x1, matrix products, layer_backward(): jnp.einsum('tv,td->vd', d_logits, full_end, preferred_element_type=wide_k...  41.3 us
    pallas_call x4, Pallas kernels, share(): pl.pallas_call(functools.partial(share_kernel, axes), in_specs=[vmem], ou...  38.7 us
  transfers between devices with their start and end apart: 10, of which 1 were waited for; matrix products, arithmetic and copies ran while one was open for 11% of the time, Pallas kernels for 52%

profile of v4, /device:TPU:0, one launch (start us, length us, event | category | flops | bytes accessed | tf_op | source)
XLA Modules:
  0.0 1715.3 jit_solution(2923289921170528656)
XLA Ops:
  13.5 3.1 convert_element_type.269
  16.7 5.9 convert_element_type.254.all_refs_0_
  23.3 17.1 share.4
  44.2 3.6 broadcast_in_dim.94.all_refs_1_
  47.7 143.7 %transit_lookup.1 = bf16[2048,2048]{1,0:T(8,128)(2,1)} custom-call(bf16[4000,512]{1,0:T(8,128)(2,1)} %convert_element_type.254.all_refs_0_, s32[4,2048,128]{2,1,0:T(8,128)} %broadcast_in_dim.94.all_refs_1_), custom_call_target="tpu_custom_call" | custom-call | flops 33554432000 | bytes 536870912 | tf_op jit(solution)/shard_map/transit_lookup/pallas_call | solution.py:984
  191.5 5.1 fusion
  196.7 2.7 dynamic-slice_convert_fusion.all_refs_2_.all_refs_3_
  201.0 2.8 gather_fusion.2
  203.8 2.3 copy.185
  206.1 4.1 gather_fusion.3
  210.2 3.8 copy.186
  214.0 4.3 gather_fusion
  218.2 10.2 convolution_convert_fusion.2.qkv_ref
  229.2 50.2 %inner_forward.1 = (bf16[2048,256]{1,0:T(8,128)(2,1)S(1)}, f32[2048,256]{1,0:T(8,128)S(1)}, f32[32,2,128,128]{3,2,1,0:T(8,128)S(1)}) custom-call(bf16[2048,768]{1,0:T(8,128)(2,1)S(1)} %convolution_convert_fusion.2.qkv_ref, f32[1,256]{1,0:T(1,128)S(1)} %get-tuple-element.267.rate_ref, f32[2,128,128]{2,1,0:T(8,128)S(1)} %select_maximum_fusion.initial_ref, ...), custom_call_target="tpu_custom_call" | custom-call | bytes 184320000 | tf_op jit(solution)/shard_map/inner_forward/pallas_call | solution.py:323
  283.6 149.0 %transit_rows.3 = (f32[2048,256]{1,0:T(8,128)}, bf16[2048,2048]{1,0:T(8,128)(2,1)}, f32[32,8,64]{2,1,0:T(8,128)}) custom-call(bf16[256,2048]{1,0:T(8,128)(2,1)} %bitcast.310, bf16[2048,256]{1,0:T(8,128)(2,1)} %copy-done.9, f32[2048,256]{1,0:T(8,128)} %dynamic-slice_convert_fusion.all_refs_2_.all_refs_3_, f32[1,256]{1,0:T(1,128)} %get-tuple-element.266.all_refs_3_), custom_call_target="tpu_custom_call" | custom-call | flops 2147483648 | bytes 536870912 | tf_op jit(solution)/shard_map/transit_rows/pallas_call | solution.py:984
  432.7 6.0 gather_fusion.1
  438.7 8.2 copy.149
  446.9 8.2 copy.151
  455.1 17.3 %fusion.5 = f32[2048,2,688]{2,0,1:T(8,128)S(1)} fusion(bf16[2,688,2048]{2,1,0:T(8,128)(2,1)} %bitcast.297, bf16[2048,2048]{1,0:T(8,128)(2,1)} %get-tuple-element.89), kind=kOutput, calls=%fused_computation.22 | convolution fusion | flops 11542724608 | bytes 25296896 | tf_op jit(solution)/shard_map/dot_general | solution.py:1203
  472.4 3.4 multiply_convert_fusion.1.all_refs_1_
  477.8 145.3 %transit_rows.4 = (f32[2048,256]{1,0:T(8,128)}, bf16[2048,2048]{1,0:T(8,128)(2,1)}, f32[32,8,64]{2,1,0:T(8,128)}) custom-call(bf16[688,2048]{1,0:T(8,128)(2,1)} %bitcast.306, bf16[2048,688]{1,0:T(8,128)(2,1)} %multiply_convert_fusion.1.all_refs_1_, f32[2048,256]{1,0:T(8,128)} %get-tuple-element.90.all_refs_2_, f32[1,256]{1,0:T(1,128)} %get-tuple-element.265.all_refs_3_), custom_call_target="tpu_custom_call" | custom-call | flops 5771362304 | bytes 536870912 | tf_op jit(solution)/shard_map/transit_rows/pallas_call | solution.py:984
  624.5 52.5 %scores.1 = (f32[2048,4000]{1,0:T(8,128)}, f32[3,2048,128]{2,1,0:T(8,128)}) custom-call(bf16[2048,2048]{1,0:T(8,128)(2,1)} %get-tuple-element.91.rows_ref, bf16[4000,2048]{1,0:T(8,128)(2,1)} %all-gather.12.cloned.1.call-done.table_ref.all_refs_0_, s32[2048,128]{1,0:T(8,128)} %broadcast_in_dim.103.goal_ref), custom_call_target="tpu_custom_call" | custom-call | flops 33554432000 | bytes 49152000 | tf_op jit(solution)/shard_map/scores/pallas_call | solution.py:1096
  677.0 2.8 slice_reduce_fusion
  679.8 6.1 share.5
  688.8 16.6 multiply_convert_fusion.all_refs_1_
  705.5 5.7 copy-done.24
  711.2 41.3 %convolution_convert_fusion = bf16[4000,2048]{1,0:T(8,128)(2,1)} fusion(bf16[2048,4000]{1,0:T(8,128)(2,1)S(1)} %multiply_convert_fusion.all_refs_1_, bf16[2048,2048]{1,0:T(8,128)(2,1)} %get-tuple-element.91.rows_ref), kind=kOutput, calls=%fused_computation.15 | convolution fusion | flops 33562624000 | bytes 41156608 | tf_op jit(solution)/shard_map/tv,td->vd/dot_general | solution.py:1313
  752.5 174.0 %transit_rows.5 = (f32[2048,256]{1,0:T(8,128)}, bf16[2048,2048]{1,0:T(8,128)(2,1)}, f32[8,256]{1,0:T(8,128)}) custom-call(bf16[4000,2048]{1,0:T(8,128)(2,1)} %all-gather.12.cloned.1.call-done.table_ref.all_refs_0_, bf16[2048,4000]{1,0:T(8,128)(2,1)} %copy-done.24, f32[2048,256]{1,0:T(8,128)} %get-tuple-element.94.all_refs_2_, ...), custom_call_target="tpu_custom_call" | custom-call | flops 33554432000 | bytes 536870912 | tf_op jit(solution)/shard_map/transit_rows/pallas_call | solution.py:984
  926.5 9.6 convolution_convert_fusion.4
  936.1 16.7 multiply_bitcast_fusion
  954.6 7.9 add_convert_fusion
  962.5 8.3 copy.158
  970.9 4.2 gather_fusion.4
  975.2 8.7 copy.161.all_refs_1_
  983.9 17.6 %convolution_convert_fusion.1 = bf16[2048,1376]{0,1:T(8,128)(2,1)} fusion(bf16[2048,1376]{0,1:T(8,128)(2,1)} %bitcast.288, bf16[2048,2048]{1,0:T(8,128)(2,1)} %get-tuple-element.89), kind=kOutput, calls=%fused_computation.29 | convolution fusion | flops 11545542656 | bytes 19660800 | tf_op jit(solution)/shard_map/td,tc->dc/dot_general | solution.py:1342
  1001.5 8.4 copy.176
  1009.9 6.5 gather_fusion.5
  1016.4 149.5 %transit_turned.1 = (f32[2048,256]{1,0:T(8,128)}, bf16[2048,2048]{1,0:T(8,128)(2,1)}, f32[8,256]{1,0:T(8,128)}) custom-call(bf16[2048,1376]{1,0:T(8,128)(2,1)} %bitcast.285, bf16[2048,1376]{1,0:T(8,128)(2,1)} %copy.161.all_refs_1_, f32[2048,256]{1,0:T(8,128)} %get-tuple-element.90.all_refs_2_, f32[1,256]{1,0:T(1,128)} %get-tuple-element.266.all_refs_3_, ...), custom_call_target="tpu_custom_call" | custom-call | flops 11542724608 | bytes 536870912 | tf_op jit(solution)/shard_map/transit_turned/pallas_call | solution.py:984
  1165.9 7.3 fusion.130.upstream_ref
  1173.2 8.2 copy.165
  1182.6 6.2 convolution_convert_fusion.6
  1191.8 77.0 %inner_backward.1 = (bf16[2048,768]{1,0:T(8,128)(2,1)S(1)}, f32[2,128,128]{2,1,0:T(8,128)S(1)}, f32[1,256]{1,0:T(1,128)S(1)}) custom-call(bf16[2048,768]{1,0:T(8,128)(2,1)S(1)} %copy-done.1, f32[1,256]{1,0:T(1,128)S(1)} %copy-done.17, f32[2,128,128]{2,1,0:T(8,128)S(1)} %select_maximum_fusion.initial_ref, f32[32,64,64]{2,1,0:T(8,128)S(1)} %get-tuple-element.261.causal_ref, ...), custom_call_target="tpu_custom_call" | custom-call | bytes 286720000 | tf_op jit(solution)/shard_map/inner_backward/pallas_call | solution.py:367
  1268.9 9.1 convolution_convert_fusion.3
  1278.0 4.5 gather_fusion.7
  1284.1 115.7 %reduce-scatter.14.cloned.1.call-done = bf16[4000,512]{1,0:T(8,128)(2,1)} async-done(((bf16[4000,2048]{1,0:T(8,128)(2,1)}), bf16[4000,512]{1,0:T(8,128)(2,1)}) %reduce-scatter.14.cloned.1.call-update) | async-done | bytes 4096016 | tf_op jit(solution)/shard_map/reduce_scatter | solution.py:1272
  1403.7 3.7 bitcast_multiply_fusion
  1414.4 161.1 %transit_table.1 = (f32[8,256]{1,0:T(8,128)}, f32[4000,512]{1,0:T(8,128)}) custom-call(bf16[2048,768]{1,0:T(8,128)(2,1)} %bitcast.303, bf16[2048,768]{1,0:T(8,128)(2,1)} %copy-done.18, s32[16,8,512]{2,1,0:T(8,128)} %broadcast_in_dim.111.all_refs_2_, f32[2048,256]{1,0:T(8,128)} %dynamic-slice_convert_fusion.all_refs_2_.all_refs_3_, f32[1,256]{1,0:T(1,128)} %copy-done.61, ...), custom_call_target="tpu_custom_call" | custom-call | flops 6442450944 | bytes 536870912 | tf_op jit(solution)/shard_map/transit_table/pallas_call | solution.py:984
  1576.2 6.3 share.6
  1589.5 7.2 multiply_reduce_fusion
  1604.1 9.3 share.7
  1618.0 3.5 convert_multiply_fusion.2
  1621.4 2.5 convert_multiply_fusion.4
  1627.5 4.7 fusion.28
  1632.1 2.8 fusion.46
  1635.0 5.6 fusion.4
  1645.0 4.8 multiply_subtract_fusion.1
  1649.8 3.0 copy.171
  1652.8 3.0 copy.173
  1655.8 4.0 fusion.27
  1661.4 3.0 copy.172
  1664.5 4.6 fusion.32
  1669.0 2.7 fusion.55
  1671.8 24.0 %multiply_subtract_fusion = (f32[4000,512]{1,0:T(8,128)}, f32[4000,512]{1,0:T(8,128)}, f32[4000,512]{1,0:T(8,128)}) fusion(f32[4000,512]{1,0:T(8,128)} %param.43, f32[]{:T(128)S(6)} %div.104, f32[4000,512]{1,0:T(8,128)} %get-tuple-element.120, bf16[4000,512]{1,0:T(8,128)(2,1)} %reduce-scatter.14.cloned.1.call-done, f32[4000,512]{1,0:T(8,128)} %param.45, ...), kind=kLoop, calls=%fused_computation.25 | loop fusion | flops 36864000 | bytes 61440004 | tf_op jit(solution)/shard_map/sub | solution.py:1163
  1697.3 9.6 fusion.21
  (281 shorter events, 65.1 us)
Async XLA Ops:
  7.2 193.7 %all-gather.10.cloned.1.call-start = ((), (), s32[]{:S(2)}) async-start(), calls=%async_computation.7 | async-start | bytes 1310720 | tf_op jit(solution)/shard_map/all_gather | solution.py:1442
  9.2 196.9 %all-gather.14.cloned.1.call-start = ((), (), s32[]{:S(2)}) async-start(), calls=%async_computation.9 | async-start | bytes 3522560 | tf_op jit(solution)/shard_map/all_gather | solution.py:1444
  11.5 202.4 %all-gather.6.cloned.1.call-start = ((), (), s32[]{:S(2)}) async-start(), calls=%async_computation.5 | async-start | bytes 3932160 | tf_op jit(solution)/shard_map/all_gather | solution.py:1441
  13.5 419.2 %all-gather.8.cloned.1.call-start = ((), (), s32[]{:S(2)}) async-start(), calls=%async_computation.6 | async-start | bytes 7045120 | tf_op jit(solution)/shard_map/all_gather | solution.py:1443
  16.6 6.1 copy-start.50
  16.6 6.7 copy-start.53
  16.7 606.5 %all-gather.12.cloned.1.call-start = ((), (), s32[]{:S(2)}) async-start(), calls=%async_computation.8 | async-start | bytes 20480000 | tf_op jit(solution)/shard_map/all_gather | solution.py:1445
  22.6 17.9 %copy-start.64 = (s32[128]{0:T(128)S(1)}, s32[128]{0:T(128)}, u32[]{:S(2)}) copy-start(s32[128]{0:T(128)} %param.41) | copy-start | bytes 1540
  22.6 18.7 %copy-start.48 = (s32[2048]{0:T(1024)S(1)}, s32[2048]{0:T(1024)}, u32[]{:S(2)}) copy-start(s32[2048]{0:T(1024)} %param.40) | copy-start | bytes 24580
  22.6 19.3 %copy-start.57 = (s32[4,4]{1,0:T(4,128)S(1)}, s32[4,4]{1,0:T(4,128)}, u32[]{:S(2)}) copy-start(s32[4,4]{1,0:T(4,128)} %param.42) | copy-start | bytes 196
  22.6 21.4 %copy-start.38 = (f32[4,64,64]{2,1,0:T(8,128)S(1)}, f32[4,64,64]{2,1,0:T(8,128)}, u32[]{:S(2)}) copy-start(f32[4,64,64]{2,1,0:T(8,128)} %param.66) | copy-start | bytes 196612
  22.6 1143.3 %reduce-scatter.16.cloned.1.call-start = ((), (), s32[]{:S(2)}) async-start(), calls=%async_computation.11 | async-start | bytes 3522560
  23.3 17.1 copy-start.61
  23.3 205.9 %copy-start.16 = (f32[1,256]{1,0:T(1,128)}, f32[1,256]{1,0:T(1,128)S(1)}, u32[]{:S(2)}) copy-start(f32[1,256]{1,0:T(1,128)S(1)} %get-tuple-element.267.rate_ref) | copy-start | bytes 3076
  40.4 151.1 %copy-start.15 = (f32[32,24,128]{2,1,0:T(8,128)}, f32[32,24,128]{2,1,0:T(8,128)S(1)}, u32[]{:S(2)}) copy-start(f32[32,24,128]{2,1,0:T(8,128)S(1)} %share.4) | copy-start | bytes 1179652
  40.5 177.7 %copy-start.55 = (f32[1,2,8,128]{3,1,2,0:T(2,128)}, f32[1,2,8,128]{3,1,2,0:T(2,128)S(1)}, u32[]{:S(2)}) copy-start(f32[1,2,8,128]{3,1,2,0:T(2,128)S(1)} %copy.189) | copy-start | bytes 24580
  196.6 21.7 %copy-start.46 = (f32[2048]{0:T(1024)}, f32[2048]{0:T(1024)S(1)}, u32[]{:S(2)}) copy-start(f32[2048]{0:T(1024)S(1)} %add_rsqrt_fusion) | copy-start | bytes 24580
  228.4 51.0 %copy-start = (bf16[2048,768]{1,0:T(8,128)(2,1)}, bf16[2048,768]{1,0:T(8,128)(2,1)S(1)}, u32[]{:S(2)}) copy-start(bf16[2048,768]{1,0:T(8,128)(2,1)S(1)} %convolution_convert_fusion.2.qkv_ref) | copy-start | bytes 9437188
  228.7 50.6 %copy-start.2 = (f32[2048,128]{1,0:T(8,128)}, f32[2048,128]{1,0:T(8,128)S(1)}, u32[]{:S(2)}) copy-start(f32[2048,128]{1,0:T(8,128)S(1)} %broadcast_in_dim.97.first_ref) | copy-start | bytes 3145732
  229.1 54.6 %copy-start.4 = (f32[2048,128]{1,0:T(8,128)}, f32[2048,128]{1,0:T(8,128)S(1)}, u32[]{:S(2)}) copy-start(f32[2048,128]{1,0:T(8,128)S(1)} %broadcast_in_dim.98.last_ref) | copy-start | bytes 3145732
  229.2 54.5 %copy-start.13 = (f32[32,8,128]{2,1,0:T(8,128)}, f32[32,8,128]{2,1,0:T(8,128)S(1)}, u32[]{:S(2)}) copy-start(f32[32,8,128]{2,1,0:T(8,128)S(1)} %broadcast_in_dim.99.anew_ref) | copy-start | bytes 393220
  472.4 5.4 copy-start.29
  677.0 11.2 copy-start.49
  677.0 11.8 copy-start.45
  705.4 5.8 copy-start.24
  926.5 9.6 copy-start.32
  975.1 309.0 %reduce-scatter.18.cloned.1.call-start = ((), (), s32[]{:S(2)}) async-start(), calls=%async_computation.12 | async-start | bytes 7045120
  1181.5 218.3 %reduce-scatter.14.cloned.1.call-start = ((), (), s32[]{:S(2)}) async-start(), calls=%async_computation.10 | async-start | bytes 20480000 | tf_op jit(solution)/shard_map/reduce_scatter | solution.py:1272
  1182.3 414.5 %reduce-scatter.22.cloned.1.call-start = ((), (), s32[]{:S(2)}) async-start(), calls=%async_computation.14 | async-start | bytes 1310720
  1182.5 7.4 copy-start.1
  1182.5 7.4 copy-start.3
  1182.5 7.4 copy-start.5
  1182.5 7.4 copy-start.7
  1182.6 8.0 copy-start.8
  1182.6 8.6 copy-start.11
  1182.6 9.2 copy-start.12
  1182.6 9.2 copy-start.14
  1182.6 9.2 copy-start.17
  1182.6 86.2 %slice-start.2 = ((s8[8388608]{0:T(1024)(128)(4,1)}), s8[4194304]{0:T(1024)(128)(4,1)S(1)}, s32[]{:S(2)}) async-start(s8[8388608]{0:T(1024)(128)(4,1)} %bitcast.293), calls=%async_computation.17 | async-start | bytes 8388608
  1188.8 80.0 %slice-start.3 = ((s8[8388608]{0:T(1024)(128)(4,1)}), s8[4194304]{0:T(1024)(128)(4,1)S(1)}, s32[]{:S(2)}) async-start(s8[8388608]{0:T(1024)(128)(4,1)} %bitcast.293), calls=%async_computation.18 | async-start | bytes 8388608
  1191.8 77.0 %copy-start.47 = (f32[2048]{0:T(1024)S(1)}, f32[2048]{0:T(1024)}, u32[]{:S(2)}) copy-start(f32[2048]{0:T(1024)} %copy-done.46) | copy-start | bytes 24580
  1191.8 77.0 %copy-start.56 = (f32[1,2,8,128]{3,1,2,0:T(2,128)S(1)}, f32[1,2,8,128]{3,1,2,0:T(2,128)}, u32[]{:S(2)}) copy-start(f32[1,2,8,128]{3,1,2,0:T(2,128)} %copy-done.55) | copy-start | bytes 24580
  1268.8 9.2 copy-start.18
  1282.6 118.9 %copy-start.26 = (f32[1,512,3,256]{1,3,2,0:T(8,128)S(1)}, f32[1,512,3,256]{1,3,2,0:T(8,128)}, u32[]{:S(2)}) copy-start(f32[1,512,3,256]{1,3,2,0:T(8,128)} %copy-done.25) | copy-start | bytes 4718596
  1399.8 198.6 %reduce-scatter.20.cloned.1.call-start = ((), (), s32[]{:S(2)}) async-start(), calls=%async_computation.13 | async-start | bytes 3932160
  1401.5 10.5 copy-start.33
  1403.1 9.8 copy-start.60
  1414.4 173.8 %copy-start.21 = (bf16[1,512,1376]{1,2,0:T(8,128)(2,1)S(1)}, bf16[1,512,1376]{1,2,0:T(8,128)(2,1)}, u32[]{:S(2)}) copy-start(bf16[1,512,1376]{1,2,0:T(8,128)(2,1)} %reduce-scatter.18.cloned.1.call-done) | copy-start | bytes 4227076
  1599.8 16.9 copy-start.27
  1617.9 17.0 slice-start
  1627.5 7.5 slice-start.1
  1627.5 7.5 copy-start.22
  1635.0 5.6 copy-start.65
  1642.7 26.4 %copy-start.30 = (f32[1,256,512]{2,1,0:T(8,128)}, f32[1,256,512]{2,1,0:T(8,128)S(1)}, u32[]{:S(2)}) copy-start(f32[1,256,512]{2,1,0:T(8,128)S(1)} %convert_multiply_fusion.8) | copy-start | bytes 1572868
  1671.7 24.1 %copy-start.51 = (f32[4,256]{1,0:T(4,128)S(1)}, f32[4,256]{1,0:T(4,128)}, u32[]{:S(2)}) copy-start(f32[4,256]{1,0:T(4,128)} %param.69) | copy-start | bytes 12292
  1671.7 24.1 %copy-start.52 = (f32[4,256]{1,0:T(4,128)S(1)}, f32[4,256]{1,0:T(4,128)}, u32[]{:S(2)}) copy-start(f32[4,256]{1,0:T(4,128)} %mul.447) | copy-start | bytes 12292
  1671.7 24.1 %copy-start.58 = (f32[4,256]{1,0:T(4,128)S(1)}, f32[4,256]{1,0:T(4,128)}, u32[]{:S(2)}) copy-start(f32[4,256]{1,0:T(4,128)} %param.71) | copy-start | bytes 12292
  1671.7 24.1 %copy-start.59 = (f32[4,256]{1,0:T(4,128)S(1)}, f32[4,256]{1,0:T(4,128)}, u32[]{:S(2)}) copy-start(f32[4,256]{1,0:T(4,128)} %param.70) | copy-start | bytes 12292
  1671.7 24.8 %copy-start.39 = (f32[4,64,64]{2,1,0:T(8,128)S(1)}, f32[4,64,64]{2,1,0:T(8,128)}, u32[]{:S(2)}) copy-start(f32[4,64,64]{2,1,0:T(8,128)} %param.66) | copy-start | bytes 196612
  1671.7 24.8 %copy-start.40 = (f32[4,64,64]{2,1,0:T(8,128)S(1)}, f32[4,64,64]{2,1,0:T(8,128)}, u32[]{:S(2)}) copy-start(f32[4,64,64]{2,1,0:T(8,128)} %mul.433) | copy-start | bytes 196612
  1671.7 24.7 %copy-start.43 = (f32[4,64,64]{2,1,0:T(8,128)S(1)}, f32[4,64,64]{2,1,0:T(8,128)}, u32[]{:S(2)}) copy-start(f32[4,64,64]{2,1,0:T(8,128)} %param.68) | copy-start | bytes 196612
  1671.7 24.7 %copy-start.44 = (f32[4,64,64]{2,1,0:T(8,128)S(1)}, f32[4,64,64]{2,1,0:T(8,128)}, u32[]{:S(2)}) copy-start(f32[4,64,64]{2,1,0:T(8,128)} %param.67) | copy-start | bytes 196612
  1671.7 25.5 %copy-start.23 = (bf16[1,512,1376]{1,2,0:T(8,128)(2,1)S(1)}, bf16[1,512,1376]{1,2,0:T(8,128)(2,1)}, u32[]{:S(2)}) copy-start(bf16[1,512,1376]{1,2,0:T(8,128)(2,1)} %reduce-scatter.18.cloned.1.call-done) | copy-start | bytes 4227076
  1671.7 25.5 %copy-start.68 = (f32[1,1,512,512]{3,2,1,0:T(8,128)S(1)}, f32[1,1,512,512]{3,2,1,0:T(8,128)}, u32[]{:S(2)}) copy-start(f32[1,1,512,512]{3,2,1,0:T(8,128)} %param.59) | copy-start | bytes 3145732
  (19 other events, 59.4 us)
Sparse Core Ops, SparseCore 0:
  10.5 32.3 all-gather.9
  45.2 46.8 all-gather.13
  94.5 67.8 all-gather.5
  164.7 67.4 all-gather.7
  234.5 154.1 all-gather.11
  975.2 40.8 reduce-scatter.15
  1181.6 64.3 reduce-scatter.17
  1249.1 150.6 reduce-scatter.13
  1403.5 27.7 reduce-scatter.21
  1434.7 62.0 reduce-scatter.19

commit v5 on v4

--- a/solution.py
+++ b/solution.py
@@ -130,7 +130,7 @@
     return value
 
 
-def mixer_forward_kernel(
+def mixer_forward_chunk(
     qkv_ref,
     rate_ref,
     initial_ref,
@@ -146,10 +146,6 @@
 ):
     pairs = initial_ref.shape[0]
     width = pairs * PAIR
-
-    @pl.when(pl.program_id(0) == 0)
-    def _():
-        state[...] = jnp.zeros_like(state)
 
     stack, pick = lane_helpers(CHUNK)
     blocks = diagonal_blocks()
@@ -311,49 +307,6 @@
     )
 
 
-def mixer_forward(qkv, rate, initial, masks):
-    tokens = qkv.shape[0]
-    width = rate.shape[1]
-    pairs = initial.shape[0]
-    chunks = tokens // CHUNK
-    whole = lambda shape: pl.BlockSpec(shape, lambda i: (0,) * len(shape))
-    square = pl.BlockSpec((1, CHUNK, CHUNK), lambda i: (i, 0, 0))
-    column = pl.BlockSpec((CHUNK, PAIR), lambda i: (i, 0))
-    causal, earlier, first, last, anew = masks
-    return pl.pallas_call(
-        mixer_forward_kernel,
-        grid=(chunks,),
-        in_specs=[
-            pl.BlockSpec((CHUNK, 3 * width), lambda i: (i, 0)),
-            whole((1, width)),
-            whole((pairs, PAIR, PAIR)),
-            square,
-            square,
-            column,
-            column,
-            pl.BlockSpec((1, 8, PAIR), lambda i: (i, 0, 0)),
-        ],
-        out_specs=[
-            pl.BlockSpec((CHUNK, width), lambda i: (i, 0)),
-            pl.BlockSpec((CHUNK, width), lambda i: (i, 0)),
-            pl.BlockSpec((1, pairs, PAIR, PAIR), lambda i: (i, 0, 0, 0)),
-        ],
-        out_shape=[
-            jax.ShapeDtypeStruct((tokens, width), jnp.bfloat16),
-            jax.ShapeDtypeStruct((tokens, width), jnp.float32),
-            jax.ShapeDtypeStruct((chunks, pairs, PAIR, PAIR), jnp.float32),
-        ],
-        scratch_shapes=[pltpu.VMEM((pairs, PAIR, PAIR), jnp.float32)],
-        compiler_params=pltpu.CompilerParams(
-            dimension_semantics=("arbitrary",), vmem_limit_bytes=32 * 1024 * 1024
-        ),
-        cost_estimate=pl.CostEstimate(
-            flops=0, bytes_accessed=90000 * tokens, transcendentals=0
-        ),
-        name="inner_forward",
-    )(qkv, rate, initial, causal, earlier, first, last, anew)
-
-
 def mixer_backward(qkv, rate, initial, masks, residue, states, upstream):
     tokens = qkv.shape[0]
     width = rate.shape[1]
@@ -436,7 +389,7 @@
     cross = form in ("lookup", "table")
     summing = mode != "plain"
     size = total.shape[1]
-    ring = partial.shape[0]
+    ring, band = partial.shape[0], partial.shape[1]
     me = lax.axis_index("head")
     mine_dp = lax.axis_index("dp")
     core = lax.rem(me, 2)
@@ -451,7 +404,7 @@
     close_at = reach_at + (2 * LAG if cross else LAG)
 
     def rows_of(chunk):
-        return pl.ds(pl.multiple_of(chunk * ROWS, ROWS), ROWS)
+        return pl.ds(pl.multiple_of(chunk * band, band), band)
 
     def shard(index):
         return pl.ds(pl.multiple_of(index * size, 128), size)
@@ -485,7 +438,7 @@
                 device_id={"dp": lax.rem(mine_dp + offset, slabs)},
                 device_id_type=MESH,
             )
-    if form != "lookup":
+    if form in ("rows", "turned", "table"):
         left_copy(0).start()
     if mode in ("grad", "grad_add"):
         ref["gain_grad"][...] = jnp.zeros_like(ref["gain_grad"])
@@ -799,28 +752,53 @@
                 ids = jnp.concatenate(
                     [ref["ids"][group, rows_of(chunk), 0:1] for group in range(slabs)], 0
                 )
-                spots = lax.broadcasted_iota(jnp.int32, (slabs * ROWS, entries), 1)
+                spots = lax.broadcasted_iota(jnp.int32, (slabs * band, entries), 1)
                 hits = (spots == ids).astype(jnp.bfloat16)
                 other = dot_ab(hits, right_ref[:, shard(1 - core)]).astype(jnp.bfloat16)
                 for group in range(slabs):
                     pair_out[slot, :, pl.ds(group * size, size)] = other[
-                        group * ROWS : (group + 1) * ROWS
+                        group * band : (group + 1) * band
                     ]
                 pair_copy(chunk).start()
                 here = dot_ab(hits, right_ref[:, shard(core)])
                 for group in range(slabs):
                     partial[slot, :, pl.ds(group * size, size)] = here[
-                        group * ROWS : (group + 1) * ROWS
+                        group * band : (group + 1) * band
                     ]
                 return
             half = lax.rem(chunk, 2)
-            left_copy(chunk).wait()
-
-            @pl.when(chunk + 1 < chunks)
-            def _():
-                left_copy(chunk + 1).start()
+            if form == "mixer":
+                one = pl.ds(chunk, 1)
+                here = rows_of(chunk)
+
+                @pl.when(chunk == 0)
+                def _():
+                    ref["state"][...] = jnp.zeros_like(ref["state"])
+
+                mixer_forward_chunk(
+                    ref["qkv"].at[here],
+                    ref["rate"],
+                    ref["initial"],
+                    ref["causal"].at[one],
+                    ref["earlier"].at[one],
+                    ref["first"].at[here],
+                    ref["last"].at[here],
+                    ref["anew"].at[one],
+                    ref["z"].at[here],
+                    ref["residue"].at[here],
+                    ref["states"].at[one],
+                    ref["state"],
+                )
+            else:
+                left_copy(chunk).wait()
+
+                @pl.when(chunk + 1 < chunks)
+                def _():
+                    left_copy(chunk + 1).start()
 
             def term(index):
+                if form == "mixer":
+                    return dot_ab(ref["z"][rows_of(chunk), :], right_ref[:, shard(index)])
                 if form in ("turned", "table"):
                     return dot_abt(ref["left_buf"][half], right_ref[shard(index), :])
                 return dot_ab(ref["left_buf"][half], right_ref[:, shard(index)])
@@ -839,7 +817,7 @@
         @pl.when(valid(chunk))
         def _():
             if form == "table":
-                arrived = full_ref.at[chunk // 2, pl.ds(0, slabs * ROWS), pl.ds(0, size)]
+                arrived = full_ref.at[chunk // 2, pl.ds(0, slabs * band), pl.ds(0, size)]
             else:
                 arrived = full_ref.at[rows_of(chunk), pl.ds(0, places * size)]
             pltpu.make_async_copy(arrived, arrived, ref["twin_in_sem"].at[chunk]).wait()
@@ -912,8 +890,10 @@
     added=None,
     ids=None,
     entries=None,
+    mixer=None,
+    band=ROWS,
 ):
-    chunks = tokens // ROWS
+    chunks = tokens // band
     places = parts // 2
     cross = form in ("lookup", "table")
     summing = mode != "plain"
@@ -932,6 +912,10 @@
         take("left", left, pl.BlockSpec(memory_space=pl.ANY))
     if ids is not None:
         take("ids", ids)
+    if mixer is not None:
+        for name, array in mixer.items():
+            take(name, array)
+        pairs, width = mixer["initial"].shape[0], mixer["rate"].shape[1]
     if summing:
         take("inputs", inputs)
         take("gain", gain)
@@ -945,33 +929,38 @@
     if form != "table":
         outputs["full"] = ((tokens, parts * size), low)
     if mode == "norm":
-        outputs["scale"] = ((chunks, 8, ROWS), wide_kind)
+        outputs["scale"] = ((chunks, 8, band), wide_kind)
     if mode in ("grad", "grad_add"):
         outputs["gain_grad"] = ((8, size), wide_kind)
     if form == "table":
         outputs["table_grad"] = ((entries, 2 * size), wide_kind)
 
+    if mixer is not None:
+        outputs["z"] = ((tokens, width), low)
+        outputs["residue"] = ((tokens, width), wide_kind)
+        outputs["states"] = ((chunks, pairs, PAIR, PAIR), wide_kind)
+        scratch["state"] = pltpu.VMEM((pairs, PAIR, PAIR), wide_kind)
     span = places * size
     hops = max(places - 1, 1)
     if form == "table":
         scratch["own"] = pltpu.VMEM((tokens, size), wide_kind)
-        scratch["full"] = pltpu.VMEM((chunks // 2, 2 * slabs * ROWS, 2 * size), low)
+        scratch["full"] = pltpu.VMEM((chunks // 2, 2 * slabs * band, 2 * size), low)
     if left is not None:
-        scratch["left_buf"] = pltpu.VMEM((2, ROWS, left.shape[1]), low)
+        scratch["left_buf"] = pltpu.VMEM((2, band, left.shape[1]), low)
         scratch["left_sem"] = dma((2,))
     if cross:
         scratch["stage"] = pltpu.VMEM((tokens, span), low)
         scratch["cross_out_sem"] = dma((chunks, slabs))
         scratch["cross_in_sem"] = dma((chunks, slabs))
     if summing:
-        scratch["sums_out"] = pltpu.VMEM((ring, 8, ROWS), wide_kind)
-        scratch["sums_in"] = pltpu.VMEM((ring, parts - 1, 8, ROWS), wide_kind)
+        scratch["sums_out"] = pltpu.VMEM((ring, 8, band), wide_kind)
+        scratch["sums_in"] = pltpu.VMEM((ring, parts - 1, 8, band), wide_kind)
         scratch["sums_out_sem"] = dma((ring,))
         scratch["sums_in_sem"] = dma((ring,))
-    scratch["total"] = pltpu.VMEM((ROWS, size), wide_kind)
-    scratch["partial"] = pltpu.VMEM((ring, ROWS, span), wide_kind)
+    scratch["total"] = pltpu.VMEM((band, size), wide_kind)
+    scratch["partial"] = pltpu.VMEM((ring, band, span), wide_kind)
     for name in ("pair_out", "pair_in", "from_low", "from_high"):
-        scratch[name] = pltpu.VMEM((ring, ROWS, span), low)
+        scratch[name] = pltpu.VMEM((ring, band, span), low)
     for name in ("pair_out", "pair_in", "low_out", "low_in", "high_out", "high_in"):
         scratch[name + "_sem"] = dma((ring,))
     for name in ("up_out", "up_in", "down_out", "down_in"):
@@ -1185,20 +1174,30 @@
     step_rate = jax.nn.sigmoid(gains[3:4]) / (8 * P_SIZE)
     masks = mixer_masks(resets, tokens)
     initial_pairs = pair_blocks(inner_init)
-    inner_low, residue, states = mixer_forward(mixed, step_rate, initial_pairs, masks)
+    causal, earlier, before, after, anew = masks
     second = transit(
         "norm",
-        "rows",
+        "mixer",
         2,
         parts,
         slabs,
         w_out,
         tokens,
         size,
-        left=inner_low,
+        mixer=dict(
+            qkv=mixed,
+            rate=step_rate,
+            initial=initial_pairs,
+            causal=causal,
+            earlier=earlier,
+            first=before,
+            last=after,
+            anew=anew,
+        ),
         inputs=embedded,
         gain=gains[1:2],
     )
+    inner_low, residue, states = second["z"], second["residue"], second["states"]
     hidden_one, full_two, scale_two = second["own"], second["full"], second["scale"]
     gate_up = jnp.dot(full_two, w_gu, preferred_element_type=jnp.float32)
 
@@ -1272,6 +1271,11 @@
     return lax.psum_scatter(grad, "dp", scatter_dimension=dimension, tiled=True)
 
 
+def rebanded(scale, band):
+    rows = scale[:, 0].reshape(-1, 1, band)
+    return jnp.broadcast_to(rows, (rows.shape[0], 8, band))
+
+
 def layer_backward(kept, weights, gains, order):
     (
         embedded,
@@ -1295,6 +1299,10 @@
     tokens, size = embedded.shape
     chunks = tokens // ROWS
     wide_kind = jnp.float32
+    grad_table = jnp.einsum("tv,td->vd", d_logits, full_end, preferred_element_type=wide_kind)
+    grad_table = grad_table.astype(jnp.bfloat16)
+    owned_table = scatter_dp(grad_table, 1)
+    d_logits, grad_table = lax.optimization_barrier((d_logits, grad_table))
     fourth = transit(
         "grad",
         "rows",
@@ -1307,19 +1315,16 @@
         left=d_logits,
         inputs=hidden_two,
         gain=gains[2:3],
-        scale=scale_end,
+        scale=rebanded(scale_end, 2 * ROWS),
+        band=2 * ROWS,
     )
     d_two, d_down_in = fourth["own"], fourth["full"]
-    grad_table = jnp.einsum("tv,td->vd", d_logits, full_end, preferred_element_type=wide_kind)
-    grad_table = grad_table.astype(jnp.bfloat16)
+    d_down_in, owned_table = lax.optimization_barrier((d_down_in, owned_table))
     d_act = jnp.einsum("td,fd->tf", d_down_in, w_down, preferred_element_type=wide_kind)
     d_gate_up = act_pull(d_act)[0].astype(jnp.bfloat16)
     grad_down = jnp.einsum("tf,td->fd", act_low, d_down_in, preferred_element_type=wide_kind)
     slot_down = column_slots_of(grad_down, order[3])
-    d_gate_up, grad_table, slot_down = lax.optimization_barrier(
-        (d_gate_up, grad_table, slot_down)
-    )
-    owned_table = scatter_dp(grad_table, 1)
+    d_gate_up, slot_down = lax.optimization_barrier((d_gate_up, slot_down))
     owned_down = scatter_dp(slot_down, 0)
     fifth = transit(
         "grad_add",
@@ -1351,8 +1356,8 @@
     grad_qkv = jnp.einsum("td,tc->dc", full_one, d_mixed, preferred_element_type=wide_kind)
     slot_out = column_slots_of(grad_out, order[1])
     slot_qkv = slots_of(grad_qkv, order[0])
-    d_mixed, slot_out, slot_qkv, owned_table, owned_gu = lax.optimization_barrier(
-        (d_mixed, slot_out, slot_qkv, owned_table, owned_gu)
+    d_mixed, slot_out, slot_qkv, owned_gu = lax.optimization_barrier(
+        (d_mixed, slot_out, slot_qkv, owned_gu)
     )
     owned_out = scatter_dp(slot_out, 0)
     owned_qkv = scatter_dp(slot_qkv, 0)

time: 1730 us -> 1540 us (0.89)
  waiting for transfers between devices: 117 us -> 0.78 us
  Pallas kernels: 1140 us -> 1080 us
    reduce_scatter x1, waiting for transfers between devices: 116 us -> 0.02 us  [scatter_dp(): return lax.psum_scatter(grad, 'dp', scatter_dimension=dimension, tiled=True)]
    pallas_call x1 -> x0, Pallas kernels: 50.2 us -> none  [mixer_forward(): pl.pallas_call(mixer_forward_kernel, grid=(chunks,), in_specs=[pl.BlockSp...]
  transfers between devices with their start and end apart: 10 -> 10, of which waited for: 1 -> 0; matrix products, arithmetic and copies ran while one was open for 11% -> 13% of each run, Pallas kernels for 52% -> 66%
where the time goes in v5:
time: 1540 us; the launch traced here: 1530 us
  Pallas kernels  1080 us (70%)
  matrix products  180 us (12%)
  local copies, waits for them, and re-layouts  140 us (9%)
  other arithmetic  109 us (7%)
  between operations  24.2 us (2%)
    pallas_call x6, Pallas kernels, transit(): pl.pallas_call(functools.partial(transit_kernel, mode, form, parts, slabs...  909 us
    pallas_call x1, Pallas kernels, mixer_backward(): pl.pallas_call(mixer_backward_kernel, grid=(chunks,), in_specs=[rows(3 *...  77 us
    pallas_call x1, Pallas kernels, scores(): pl.pallas_call(scores_kernel, grid=(tokens // SCORE_ROWS,), in_specs=[pl....  52.5 us
    dot_general x12, matrix products, product(): jnp.einsum(form, one.astype(jnp.bfloat16), two.astype(jnp.bfloat16), pref...  44.6 us
    dot_general x1, matrix products, layer_backward(): jnp.einsum('tv,td->vd', d_logits, full_end, preferred_element_type=wide_k...  41.3 us
    pallas_call x4, Pallas kernels, share(): pl.pallas_call(functools.partial(share_kernel, axes), in_specs=[vmem], ou...  39.1 us
  transfers between devices with their start and end apart: 10, of which 0 were waited for; matrix products, arithmetic and copies ran while one was open for 13% of the time, Pallas kernels for 66%

profile of v5, /device:TPU:0, one launch (start us, length us, event | category | flops | bytes accessed | tf_op | source)
XLA Modules:
  0.0 1532.8 jit_solution(11924868409572268048)
XLA Ops:
  9.2 2.3 convert_element_type.273
  13.5 3.1 convert_element_type.271
  16.7 5.9 convert_element_type.254.all_refs_0_
  23.3 17.1 %share.4 = f32[32,24,128]{2,1,0:T(8,128)S(1)} custom-call(f32[24,128]{1,0:T(8,128)S(1)} %select_maximum_fusion.1.block_ref), custom_call_target="tpu_custom_call" | custom-call | bytes 16777216 | tf_op jit(solution)/shard_map/share/pallas_call | solution.py:1042
  42.8 3.5 broadcast_in_dim.101.all_refs_1_
  46.4 143.3 %transit_lookup.1 = bf16[2048,2048]{1,0:T(8,128)(2,1)} custom-call(bf16[4000,512]{1,0:T(8,128)(2,1)} %convert_element_type.254.all_refs_0_, s32[4,2048,128]{2,1,0:T(8,128)} %broadcast_in_dim.101.all_refs_1_), custom_call_target="tpu_custom_call" | custom-call | flops 33554432000 | bytes 536870912 | tf_op jit(solution)/shard_map/transit_lookup/pallas_call | solution.py:973
  189.7 5.1 fusion
  194.9 2.7 dynamic-slice_convert_fusion.all_refs_9_.all_refs_3_
  199.4 2.0 gather_fusion.1
  202.5 4.1 gather_fusion.3
  206.6 3.8 copy.186
  210.4 4.4 gather_fusion
  214.7 11.3 convolution_convert_fusion.2.all_refs_1_.qkv_ref
  229.4 154.2 %transit_mixer.1 = (f32[2048,256]{1,0:T(8,128)}, bf16[2048,2048]{1,0:T(8,128)(2,1)}, f32[32,8,64]{2,1,0:T(8,128)}, bf16[2048,256]{1,0:T(8,128)(2,1)}, f32[2048,256]{1,0:T(8,128)}, /*index=5*/f32[32,2,128,128]{3,2,1,0:T(8,128)}) custom-call(bf16[256,2048]{1,0:T(8,128)(2,1)} %bitcast.299, bf16[2048,768]{1,0:T(8,128)(2,1)} %convolution_convert_fusion.2.all_refs_1_.qkv_ref, ...), custom_call_target="tpu_custom_call" | custom-call | flops 2147483648 | bytes 536870912 | tf_op jit(solution)/shard_map/transit_mixer/pallas_call | solution.py:973
  383.6 6.0 gather_fusion.2
  389.6 8.2 copy.150
  397.8 8.2 copy.151
  406.0 17.3 %fusion.5 = f32[2048,2,688]{2,0,1:T(8,128)S(1)} fusion(bf16[2,688,2048]{2,1,0:T(8,128)(2,1)} %bitcast.297, bf16[2048,2048]{1,0:T(8,128)(2,1)} %get-tuple-element.89), kind=kOutput, calls=%fused_computation.22 | convolution fusion | flops 11542724608 | bytes 25296896 | tf_op jit(solution)/shard_map/dot_general | solution.py:1202
  423.3 3.4 multiply_convert_fusion.1.all_refs_1_
  428.7 145.2 %transit_rows.2 = (f32[2048,256]{1,0:T(8,128)}, bf16[2048,2048]{1,0:T(8,128)(2,1)}, f32[32,8,64]{2,1,0:T(8,128)}) custom-call(bf16[688,2048]{1,0:T(8,128)(2,1)} %bitcast.308, bf16[2048,688]{1,0:T(8,128)(2,1)} %multiply_convert_fusion.1.all_refs_1_, f32[2048,256]{1,0:T(8,128)} %get-tuple-element.90.all_refs_2_, f32[1,256]{1,0:T(1,128)} %get-tuple-element.267.all_refs_3_), custom_call_target="tpu_custom_call" | custom-call | flops 5771362304 | bytes 536870912 | tf_op jit(solution)/shard_map/transit_rows/pallas_call | solution.py:973
  575.2 52.5 %scores.1 = (f32[2048,4000]{1,0:T(8,128)}, f32[3,2048,128]{2,1,0:T(8,128)}) custom-call(bf16[2048,2048]{1,0:T(8,128)(2,1)} %get-tuple-element.91.rows_ref, bf16[4000,2048]{1,0:T(8,128)(2,1)} %all-gather.12.cloned.1.call-done.table_ref.all_refs_0_, s32[2048,128]{1,0:T(8,128)} %broadcast_in_dim.110.goal_ref), custom_call_target="tpu_custom_call" | custom-call | flops 33554432000 | bytes 49152000 | tf_op jit(solution)/shard_map/scores/pallas_call | solution.py:1085
  627.8 2.8 slice_reduce_fusion
  630.6 6.1 share.5
  637.6 16.6 %multiply_convert_fusion.all_refs_1_ = bf16[2048,4000]{1,0:T(8,128)(2,1)S(1)} fusion(f32[2048,4000]{1,0:T(8,128)} %get-tuple-element.92, f32[2048]{0:T(1024)S(1)} %copy-done.40, s32[2048]{0:T(1024)S(1)} %broadcast_subtract_fusion, f32[2048]{0:T(1024)S(1)} %get-tuple-element.248), kind=kLoop, calls=%fused_computation.8 | loop fusion | flops 49152000 | bytes 49176576 | tf_op jit(solution)/shard_map/convert_element_type | solution.py:1237
  654.3 5.7 copy-done.18
  660.0 41.3 %convolution_convert_fusion = bf16[4000,2048]{1,0:T(8,128)(2,1)} fusion(bf16[2048,4000]{1,0:T(8,128)(2,1)S(1)} %multiply_convert_fusion.all_refs_1_, bf16[2048,2048]{1,0:T(8,128)(2,1)} %get-tuple-element.91.rows_ref), kind=kOutput, calls=%fused_computation.15 | convolution fusion | flops 33562624000 | bytes 41156608 | tf_op jit(solution)/shard_map/tv,td->vd/dot_general | solution.py:1302
  704.6 154.9 %transit_rows.3 = (f32[2048,256]{1,0:T(8,128)}, bf16[2048,2048]{1,0:T(8,128)(2,1)}, f32[8,256]{1,0:T(8,128)}) custom-call(bf16[4000,2048]{1,0:T(8,128)(2,1)} %all-gather.12.cloned.1.call-done.table_ref.all_refs_0_, bf16[2048,4000]{1,0:T(8,128)(2,1)} %copy-done.18, f32[2048,256]{1,0:T(8,128)} %get-tuple-element.95.all_refs_2_, ...), custom_call_target="tpu_custom_call" | custom-call | flops 33554432000 | bytes 536870912 | tf_op jit(solution)/shard_map/transit_rows/pallas_call | solution.py:973
  859.6 9.6 convolution_convert_fusion.4
  869.2 16.7 %multiply_bitcast_fusion = (f32[2048,1,688]{2,0,1:T(8,128)}, f32[2048,1,688]{2,0,1:T(8,128)}) fusion(f32[2048,2,688]{2,0,1:T(8,128)} %copy-done.23, bf16[2048,2048]{1,0:T(8,128)(2,1)} %get-tuple-element.98, bf16[688,2048]{1,0:T(8,128)(2,1)S(1)} %bitcast.309), kind=kOutput, calls=%fused_computation.35 | convolution fusion | flops 5788270592 | bytes 33751040 | tf_op jit(solution)/shard_map/td,fd->tf/dot_general | solution.py:1323
  887.7 7.9 add_convert_fusion
  895.6 8.3 copy.158
  903.9 4.1 gather_fusion.4
  908.1 8.7 copy.161.all_refs_1_
  916.8 17.5 %convolution_convert_fusion.1 = bf16[2048,1376]{0,1:T(8,128)(2,1)} fusion(bf16[2048,1376]{0,1:T(8,128)(2,1)} %bitcast.288, bf16[2048,2048]{1,0:T(8,128)(2,1)} %get-tuple-element.89), kind=kOutput, calls=%fused_computation.29 | convolution fusion | flops 11545542656 | bytes 19660800 | tf_op jit(solution)/shard_map/td,tc->dc/dot_general | solution.py:1347
  934.2 8.3 copy.176
  942.6 6.3 gather_fusion.5
  948.9 149.9 %transit_turned.1 = (f32[2048,256]{1,0:T(8,128)}, bf16[2048,2048]{1,0:T(8,128)(2,1)}, f32[8,256]{1,0:T(8,128)}) custom-call(bf16[2048,1376]{1,0:T(8,128)(2,1)} %bitcast.285, bf16[2048,1376]{1,0:T(8,128)(2,1)} %copy.161.all_refs_1_, f32[2048,256]{1,0:T(8,128)} %get-tuple-element.90.all_refs_2_, f32[1,256]{1,0:T(1,128)} %get-tuple-element.268.all_refs_10_.all_refs_3_, ...), custom_call_target="tpu_custom_call" | custom-call | flops 11542724608 | bytes 536870912 | tf_op jit(solution)/shard_map/transit_turned/pallas_call | solution.py:973
  1098.9 7.1 fusion.130.upstream_ref
  1106.0 8.2 copy.165
  1115.5 5.9 convolution_convert_fusion.6
  1124.4 77.0 %inner_backward.1 = (bf16[2048,768]{1,0:T(8,128)(2,1)S(1)}, f32[2,128,128]{2,1,0:T(8,128)S(1)}, f32[1,256]{1,0:T(1,128)S(1)}) custom-call(bf16[2048,768]{1,0:T(8,128)(2,1)S(1)} %copy-done, f32[1,256]{1,0:T(1,128)S(1)} %copy-done.11, f32[2,128,128]{2,1,0:T(8,128)S(1)} %copy-done.8, f32[32,64,64]{2,1,0:T(8,128)S(1)} %copy-done.4, f32[32,64,64]{2,1,0:T(8,128)S(1)} %copy-done.3, ...), custom_call_target="tpu_custom_call" | custom-call | bytes 286720000 | tf_op jit(solution)/shard_map/inner_backward/pallas_call | solution.py:320
  1201.4 9.1 convolution_convert_fusion.3
  1210.5 4.3 gather_fusion.7
  1220.4 3.7 bitcast_multiply_fusion
  1225.4 2.3 scatter.9
  1231.0 161.6 %transit_table.1 = (f32[8,256]{1,0:T(8,128)}, f32[4000,512]{1,0:T(8,128)}) custom-call(bf16[2048,768]{1,0:T(8,128)(2,1)} %bitcast.305, bf16[2048,768]{1,0:T(8,128)(2,1)} %copy-done.12, s32[16,8,512]{2,1,0:T(8,128)} %broadcast_in_dim.120.all_refs_2_, f32[2048,256]{1,0:T(8,128)} %dynamic-slice_convert_fusion.all_refs_9_.all_refs_3_, f32[1,256]{1,0:T(1,128)} %copy-done.57, ...), custom_call_target="tpu_custom_call" | custom-call | flops 6442450944 | bytes 536870912 | tf_op jit(solution)/shard_map/transit_table/pallas_call | solution.py:973
  1393.3 6.6 share.6
  1406.9 7.2 multiply_reduce_fusion
  1421.5 9.3 share.7
  1435.4 3.5 convert_multiply_fusion.2
  1438.8 2.5 convert_multiply_fusion.4
  1444.9 4.7 fusion.28
  1449.6 2.8 fusion.46
  1452.4 5.6 fusion.4
  1458.0 2.0 fusion.50
  1462.4 4.8 multiply_subtract_fusion.1
  1467.2 3.0 copy.171
  1470.2 3.0 copy.173
  1473.3 4.0 fusion.27
  1478.8 3.0 copy.172
  1481.9 4.6 fusion.32
  1486.4 2.7 fusion.55
  1489.2 24.0 %multiply_subtract_fusion = (f32[4000,512]{1,0:T(8,128)}, f32[4000,512]{1,0:T(8,128)}, f32[4000,512]{1,0:T(8,128)}) fusion(f32[4000,512]{1,0:T(8,128)} %param.43, f32[]{:T(128)S(6)} %div.104, f32[4000,512]{1,0:T(8,128)} %get-tuple-element.122, bf16[4000,512]{1,0:T(8,128)(2,1)} %reduce-scatter.14.cloned.1.call-done, f32[4000,512]{1,0:T(8,128)} %param.45, ...), kind=kLoop, calls=%fused_computation.25 | loop fusion | flops 36864000 | bytes 61440004 | tf_op jit(solution)/shard_map/sub | solution.py:1152
  1514.7 9.6 fusion.21
  (271 shorter events, 58.3 us)
Async XLA Ops:
  7.2 192.2 %all-gather.8.cloned.1.call-start = ((), (), s32[]{:S(2)}) async-start(), calls=%async_computation.6 | async-start | bytes 1310720 | tf_op jit(solution)/shard_map/all_gather | solution.py:1447
  9.2 193.3 %all-gather.14.cloned.1.call-start = ((), (), s32[]{:S(2)}) async-start(), calls=%async_computation.9 | async-start | bytes 3522560 | tf_op jit(solution)/shard_map/all_gather | solution.py:1449
  11.5 198.8 %all-gather.6.cloned.1.call-start = ((), (), s32[]{:S(2)}) async-start(), calls=%async_computation.5 | async-start | bytes 3932160 | tf_op jit(solution)/shard_map/all_gather | solution.py:1446
  13.5 370.1 %all-gather.10.cloned.1.call-start = ((), (), s32[]{:S(2)}) async-start(), calls=%async_computation.7 | async-start | bytes 7045120 | tf_op jit(solution)/shard_map/all_gather | solution.py:1448
  16.6 6.1 copy-start.45
  16.6 6.7 copy-start.48
  16.7 557.3 %all-gather.12.cloned.1.call-start = ((), (), s32[]{:S(2)}) async-start(), calls=%async_computation.8 | async-start | bytes 20480000 | tf_op jit(solution)/shard_map/all_gather | solution.py:1450
  22.6 17.9 %copy-start.58 = (s32[128]{0:T(128)S(1)}, s32[128]{0:T(128)}, u32[]{:S(2)}) copy-start(s32[128]{0:T(128)} %param.41) | copy-start | bytes 1540
  22.6 18.7 %copy-start.43 = (s32[2048]{0:T(1024)S(1)}, s32[2048]{0:T(1024)}, u32[]{:S(2)}) copy-start(s32[2048]{0:T(1024)} %param.40) | copy-start | bytes 24580
  22.6 19.4 %copy-start.52 = (s32[4,4]{1,0:T(4,128)S(1)}, s32[4,4]{1,0:T(4,128)}, u32[]{:S(2)}) copy-start(s32[4,4]{1,0:T(4,128)} %param.42) | copy-start | bytes 196
  22.6 19.4 %copy-start.33 = (f32[4,64,64]{2,1,0:T(8,128)S(1)}, f32[4,64,64]{2,1,0:T(8,128)}, u32[]{:S(2)}) copy-start(f32[4,64,64]{2,1,0:T(8,128)} %param.66) | copy-start | bytes 196612
  22.6 836.9 %reduce-scatter.14.cloned.1.call-start = ((), (), s32[]{:S(2)}) async-start(), calls=%async_computation.10 | async-start | bytes 20480000 | tf_op jit(solution)/shard_map/reduce_scatter | solution.py:1271
  23.3 17.1 %copy-start.57 = (f32[1,256]{1,0:T(1,128)}, f32[1,256]{1,0:T(1,128)S(1)}, u32[]{:S(2)}) copy-start(f32[1,256]{1,0:T(1,128)S(1)} %get-tuple-element.271.all_refs_4_) | copy-start | bytes 3076
  40.4 149.3 %copy-start.10 = (f32[32,24,128]{2,1,0:T(8,128)}, f32[32,24,128]{2,1,0:T(8,128)S(1)}, u32[]{:S(2)}) copy-start(f32[32,24,128]{2,1,0:T(8,128)S(1)} %share.4) | copy-start | bytes 1179652
  40.5 174.2 %copy-start.50 = (f32[1,2,8,128]{3,1,2,0:T(2,128)}, f32[1,2,8,128]{3,1,2,0:T(2,128)S(1)}, u32[]{:S(2)}) copy-start(f32[1,2,8,128]{3,1,2,0:T(2,128)S(1)} %copy.189) | copy-start | bytes 24580
  189.7 5.1 copy-start.49
  194.8 19.9 %copy-start.41 = (f32[2048]{0:T(1024)}, f32[2048]{0:T(1024)S(1)}, u32[]{:S(2)}) copy-start(f32[2048]{0:T(1024)S(1)} %add_rsqrt_fusion) | copy-start | bytes 24580
  423.3 5.4 copy-start.23
  627.7 9.3 copy-start.44
  627.7 9.9 copy-start.40
  654.3 5.8 copy-start.18
  701.3 397.5 %reduce-scatter.16.cloned.1.call-start = ((), (), s32[]{:S(2)}) async-start(), calls=%async_computation.11 | async-start | bytes 3522560
  859.5 9.6 copy-start.26
  908.0 308.4 %reduce-scatter.18.cloned.1.call-start = ((), (), s32[]{:S(2)}) async-start(), calls=%async_computation.12 | async-start | bytes 7045120
  948.9 150.0 %copy-start.25 = (bf16[4,32,8,512]{3,2,0,1:T(8,128)(2,1)S(1)}, bf16[4,32,8,512]{3,2,0,1:T(8,128)(2,1)}, u32[]{:S(2)}) copy-start(bf16[4,32,8,512]{3,2,0,1:T(8,128)(2,1)} %copy.185) | copy-start | bytes 3145732
  1114.2 299.9 %reduce-scatter.22.cloned.1.call-start = ((), (), s32[]{:S(2)}) async-start(), calls=%async_computation.14 | async-start | bytes 1310720
  1115.4 6.1 copy-start
  1115.4 6.1 copy-start.1
  1115.4 6.1 copy-start.2
  1115.4 6.1 copy-start.3
  1115.4 6.1 copy-start.4
  1115.5 6.8 copy-start.5
  1115.5 8.0 copy-start.6
  1115.5 8.8 copy-start.7
  1115.5 8.8 copy-start.8
  1115.5 8.8 copy-start.9
  1115.5 8.8 copy-start.11
  1115.5 85.8 %slice-start.2 = ((s8[8388608]{0:T(1024)(128)(4,1)}), s8[4194304]{0:T(1024)(128)(4,1)S(1)}, s32[]{:S(2)}) async-start(s8[8388608]{0:T(1024)(128)(4,1)} %bitcast.293), calls=%async_computation.17 | async-start | bytes 8388608
  1121.4 79.9 %slice-start.3 = ((s8[8388608]{0:T(1024)(128)(4,1)}), s8[4194304]{0:T(1024)(128)(4,1)S(1)}, s32[]{:S(2)}) async-start(s8[8388608]{0:T(1024)(128)(4,1)} %bitcast.293), calls=%async_computation.18 | async-start | bytes 8388608
  1124.3 77.0 %copy-start.42 = (f32[2048]{0:T(1024)S(1)}, f32[2048]{0:T(1024)}, u32[]{:S(2)}) copy-start(f32[2048]{0:T(1024)} %copy-done.41) | copy-start | bytes 24580
  1124.3 77.0 %copy-start.51 = (f32[1,2,8,128]{3,1,2,0:T(2,128)S(1)}, f32[1,2,8,128]{3,1,2,0:T(2,128)}, u32[]{:S(2)}) copy-start(f32[1,2,8,128]{3,1,2,0:T(2,128)} %copy-done.50) | copy-start | bytes 24580
  1201.3 9.2 copy-start.12
  1216.5 199.4 %reduce-scatter.20.cloned.1.call-start = ((), (), s32[]{:S(2)}) async-start(), calls=%async_computation.13 | async-start | bytes 3932160
  1218.1 10.5 copy-start.27
  1219.8 9.8 copy-start.56
  1231.0 174.6 %copy-start.15 = (bf16[1,512,1376]{1,2,0:T(8,128)(2,1)S(1)}, bf16[1,512,1376]{1,2,0:T(8,128)(2,1)}, u32[]{:S(2)}) copy-start(bf16[1,512,1376]{1,2,0:T(8,128)(2,1)} %reduce-scatter.18.cloned.1.call-done) | copy-start | bytes 4227076
  1417.2 16.9 %copy-start.21 = (bf16[1,512,768]{1,2,0:T(8,128)(2,1)}, bf16[1,512,768]{1,2,0:T(8,128)(2,1)S(1)}, u32[]{:S(2)}) copy-start(bf16[1,512,768]{1,2,0:T(8,128)(2,1)S(1)} %copy.167) | copy-start | bytes 2359300
  1435.4 17.0 %slice-start = ((s8[7749632]{0:T(1024)(128)(4,1)}), s8[3555328]{0:T(1024)(128)(4,1)S(1)}, s32[]{:S(2)}) async-start(s8[7749632]{0:T(1024)(128)(4,1)} %bitcast.282), calls=%async_computation.15 | async-start | bytes 7110656
  1444.9 4.7 copy-start.13
  1444.9 7.5 slice-start.1
  1444.9 7.5 copy-start.16
  1452.4 5.6 copy-start.59
  1460.1 26.4 %copy-start.24 = (f32[1,256,512]{2,1,0:T(8,128)}, f32[1,256,512]{2,1,0:T(8,128)S(1)}, u32[]{:S(2)}) copy-start(f32[1,256,512]{2,1,0:T(8,128)S(1)} %convert_multiply_fusion.8) | copy-start | bytes 1572868
  1477.3 4.6 copy-start.14
  1489.1 24.1 %copy-start.46 = (f32[4,256]{1,0:T(4,128)S(1)}, f32[4,256]{1,0:T(4,128)}, u32[]{:S(2)}) copy-start(f32[4,256]{1,0:T(4,128)} %param.69) | copy-start | bytes 12292
  1489.1 24.1 %copy-start.47 = (f32[4,256]{1,0:T(4,128)S(1)}, f32[4,256]{1,0:T(4,128)}, u32[]{:S(2)}) copy-start(f32[4,256]{1,0:T(4,128)} %mul.447) | copy-start | bytes 12292
  1489.1 24.1 %copy-start.54 = (f32[4,256]{1,0:T(4,128)S(1)}, f32[4,256]{1,0:T(4,128)}, u32[]{:S(2)}) copy-start(f32[4,256]{1,0:T(4,128)} %param.71) | copy-start | bytes 12292
  1489.1 24.1 %copy-start.55 = (f32[4,256]{1,0:T(4,128)S(1)}, f32[4,256]{1,0:T(4,128)}, u32[]{:S(2)}) copy-start(f32[4,256]{1,0:T(4,128)} %param.70) | copy-start | bytes 12292
  1489.1 24.8 %copy-start.34 = (f32[4,64,64]{2,1,0:T(8,128)S(1)}, f32[4,64,64]{2,1,0:T(8,128)}, u32[]{:S(2)}) copy-start(f32[4,64,64]{2,1,0:T(8,128)} %param.66) | copy-start | bytes 196612
  1489.1 24.8 %copy-start.35 = (f32[4,64,64]{2,1,0:T(8,128)S(1)}, f32[4,64,64]{2,1,0:T(8,128)}, u32[]{:S(2)}) copy-start(f32[4,64,64]{2,1,0:T(8,128)} %mul.433) | copy-start | bytes 196612
  1489.1 24.7 %copy-start.38 = (f32[4,64,64]{2,1,0:T(8,128)S(1)}, f32[4,64,64]{2,1,0:T(8,128)}, u32[]{:S(2)}) copy-start(f32[4,64,64]{2,1,0:T(8,128)} %param.68) | copy-start | bytes 196612
  1489.1 24.7 %copy-start.39 = (f32[4,64,64]{2,1,0:T(8,128)S(1)}, f32[4,64,64]{2,1,0:T(8,128)}, u32[]{:S(2)}) copy-start(f32[4,64,64]{2,1,0:T(8,128)} %param.67) | copy-start | bytes 196612
  1489.2 25.5 %copy-start.17 = (bf16[1,512,1376]{1,2,0:T(8,128)(2,1)S(1)}, bf16[1,512,1376]{1,2,0:T(8,128)(2,1)}, u32[]{:S(2)}) copy-start(bf16[1,512,1376]{1,2,0:T(8,128)(2,1)} %reduce-scatter.18.cloned.1.call-done) | copy-start | bytes 4227076
  1489.2 25.5 %copy-start.62 = (f32[1,1,512,512]{3,2,1,0:T(8,128)S(1)}, f32[1,1,512,512]{3,2,1,0:T(8,128)}, u32[]{:S(2)}) copy-start(f32[1,1,512,512]{3,2,1,0:T(8,128)} %param.59) | copy-start | bytes 3145732
  (13 other events, 39.4 us)
Sparse Core Ops, SparseCore 0:
  10.5 32.3 all-gather.7
  45.2 48.1 all-gather.13
  95.8 67.5 all-gather.5
  165.7 65.4 all-gather.9
  233.4 154.0 all-gather.11
  701.5 153.1 reduce-scatter.13
  908.1 42.6 reduce-scatter.15
  1114.4 65.8 reduce-scatter.17
  1216.6 28.8 reduce-scatter.21
  1248.9 60.1 reduce-scatter.19

commit v6 on v5

--- a/solution.py
+++ b/solution.py
@@ -185,7 +185,7 @@
         state[pair] = base - blocks * wide(dot_atb, key_last, scaled_parts)
 
 
-def mixer_backward_kernel(
+def mixer_backward_chunk(
     qkv_ref,
     rate_ref,
     initial_ref,
@@ -206,12 +206,6 @@
 ):
     pairs = initial_ref.shape[0]
     width = pairs * PAIR
-
-    @pl.when(pl.program_id(0) == 0)
-    def _():
-        carried[...] = jnp.zeros_like(carried)
-        grad_initial_ref[...] = jnp.zeros_like(grad_initial_ref)
-        grad_rate_ref[...] = jnp.zeros_like(grad_rate_ref)
 
     stack, pick = lane_helpers(CHUNK)
     blocks = diagonal_blocks()
@@ -307,65 +301,6 @@
     )
 
 
-def mixer_backward(qkv, rate, initial, masks, residue, states, upstream):
-    tokens = qkv.shape[0]
-    width = rate.shape[1]
-    pairs = initial.shape[0]
-    chunks = tokens // CHUNK
-    whole = lambda shape: pl.BlockSpec(shape, lambda i: (0,) * len(shape))
-    square = pl.BlockSpec((1, CHUNK, CHUNK), lambda i: (chunks - 1 - i, 0, 0))
-    column = pl.BlockSpec((CHUNK, PAIR), lambda i: (chunks - 1 - i, 0))
-    rows = lambda size: pl.BlockSpec((CHUNK, size), lambda i: (chunks - 1 - i, 0))
-    causal, earlier, first, last, anew = masks
-    return pl.pallas_call(
-        mixer_backward_kernel,
-        grid=(chunks,),
-        in_specs=[
-            rows(3 * width),
-            whole((1, width)),
-            whole((pairs, PAIR, PAIR)),
-            square,
-            square,
-            square,
-            square,
-            column,
-            column,
-            pl.BlockSpec((1, 8, PAIR), lambda i: (chunks - 1 - i, 0, 0)),
-            rows(width),
-            pl.BlockSpec((1, pairs, PAIR, PAIR), lambda i: (chunks - 1 - i, 0, 0, 0)),
-            rows(width),
-        ],
-        out_specs=[rows(3 * width), whole((pairs, PAIR, PAIR)), whole((1, width))],
-        out_shape=[
-            jax.ShapeDtypeStruct((tokens, 3 * width), jnp.bfloat16),
-            jax.ShapeDtypeStruct((pairs, PAIR, PAIR), jnp.float32),
-            jax.ShapeDtypeStruct((1, width), jnp.float32),
-        ],
-        scratch_shapes=[pltpu.VMEM((pairs, PAIR, PAIR), jnp.float32)],
-        compiler_params=pltpu.CompilerParams(
-            dimension_semantics=("arbitrary",), vmem_limit_bytes=32 * 1024 * 1024
-        ),
-        cost_estimate=pl.CostEstimate(
-            flops=0, bytes_accessed=140000 * tokens, transcendentals=0
-        ),
-        name="inner_backward",
-    )(
-        qkv,
-        rate,
-        initial,
-        causal,
-        earlier,
-        jnp.swapaxes(causal, 1, 2),
-        jnp.swapaxes(earlier, 1, 2),
-        first,
-        last,
-        anew,
-        residue,
-        states,
-        upstream,
-    )
-
-
 ROWS = 64
 LAG = 2
 MESH = pl.DeviceIdType.MESH
@@ -388,6 +323,7 @@
     places = parts // 2
     cross = form in ("lookup", "table")
     summing = mode != "plain"
+    lefts = sum(name.startswith("left_buf") for name in names)
     size = total.shape[1]
     ring, band = partial.shape[0], partial.shape[1]
     me = lax.axis_index("head")
@@ -403,8 +339,14 @@
     reach_at = finish_at + LAG * (places - 1)
     close_at = reach_at + (2 * LAG if cross else LAG)
 
+    def place_of(chunk):
+        return chunks - 1 - chunk if form == "inner" else chunk
+
+    def band_of(index):
+        return pl.ds(pl.multiple_of(index * band, band), band)
+
     def rows_of(chunk):
-        return pl.ds(pl.multiple_of(chunk * band, band), band)
+        return band_of(place_of(chunk))
 
     def shard(index):
         return pl.ds(pl.multiple_of(index * size, 128), size)
@@ -419,11 +361,16 @@
             device_id_type=MESH,
         )
 
-    def left_copy(chunk):
+    def left_copies(chunk):
         half = lax.rem(chunk, 2)
-        return pltpu.make_async_copy(
-            ref["left"].at[rows_of(chunk)], ref["left_buf"].at[half], ref["left_sem"].at[half]
-        )
+        return [
+            pltpu.make_async_copy(
+                ref["left%d" % part].at[rows_of(chunk)],
+                ref["left_buf%d" % part].at[half],
+                ref["left_sem%d" % part].at[half],
+            )
+            for part in range(lefts)
+        ]
 
     barrier = pltpu.get_barrier_semaphore()
     for offset in range(1, parts):
@@ -438,8 +385,8 @@
                 device_id={"dp": lax.rem(mine_dp + offset, slabs)},
                 device_id_type=MESH,
             )
-    if form in ("rows", "turned", "table"):
-        left_copy(0).start()
+    for copy in left_copies(0):
+        copy.start()
     if mode in ("grad", "grad_add"):
         ref["gain_grad"][...] = jnp.zeros_like(ref["gain_grad"])
     if form == "table":
@@ -507,7 +454,7 @@
     def target(chunk, giver):
         if form == "lookup":
             return full_ref.at[rows_of(chunk), shard(2 * giver + core)]
-        return full_ref.at[chunk // 2, rows_of(lax.rem(chunk, 2) * slabs + giver), shard(core)]
+        return full_ref.at[chunk // 2, band_of(lax.rem(chunk, 2) * slabs + giver), shard(core)]
 
     def mirror(chunk, index):
         part = target(chunk, index) if cross else piece(chunk, index)
@@ -539,7 +486,7 @@
             if form == "lookup":
                 full_ref[rows_of(chunk), shard(2 * mine_dp + core)] = values
             else:
-                place_rows = rows_of(lax.rem(chunk, 2) * slabs + mine_dp)
+                place_rows = band_of(lax.rem(chunk, 2) * slabs + mine_dp)
                 full_ref[chunk // 2, place_rows, shard(core)] = values
             mirror(chunk, mine_dp).start()
 
@@ -613,7 +560,7 @@
                 ref["scale"][chunk] = scale
                 result = ref["own"][rows, :] * down(scale, size) * gain
             else:
-                scale = down(ref["scale"][chunk], size)
+                scale = down(ref["scale"][place_of(chunk)], size)
                 normed = ref["inputs"][rows, :] * scale
                 inner = down(summed / D, size)
                 result = scale * (ref["own"][rows, :] * gain - normed * inner)
@@ -731,7 +678,7 @@
                 value = value + ref["inputs"][rows, :]
                 column = jnp.sum(value * value, 1, keepdims=True)
             else:
-                scale = down(ref["scale"][chunk], size)
+                scale = down(ref["scale"][place_of(chunk)], size)
                 normed = ref["inputs"][rows, :] * scale
                 ref["gain_grad"][0:1, :] += jnp.sum(value * normed, 0, keepdims=True)
                 column = jnp.sum(value * ref["gain"][0:1, :] * normed, 1, keepdims=True)
@@ -746,7 +693,7 @@
         @pl.when(valid(chunk))
         def _():
             slot = lax.rem(chunk, ring)
-            right_ref = ref["right"]
+            right_ref = ref["right0"]
             if form == "lookup":
                 entries = right_ref.shape[0]
                 ids = jnp.concatenate(
@@ -790,18 +737,24 @@
                     ref["state"],
                 )
             else:
-                left_copy(chunk).wait()
+                for copy in left_copies(chunk):
+                    copy.wait()
 
                 @pl.when(chunk + 1 < chunks)
                 def _():
-                    left_copy(chunk + 1).start()
+                    for copy in left_copies(chunk + 1):
+                        copy.start()
 
             def term(index):
                 if form == "mixer":
                     return dot_ab(ref["z"][rows_of(chunk), :], right_ref[:, shard(index)])
-                if form in ("turned", "table"):
-                    return dot_abt(ref["left_buf"][half], right_ref[shard(index), :])
-                return dot_ab(ref["left_buf"][half], right_ref[:, shard(index)])
+                if form == "table":
+                    return dot_abt(ref["left_buf0"][half], right_ref[shard(index), :])
+                terms = [
+                    dot_ab(ref["left_buf%d" % part][half], ref["right%d" % part][:, shard(index)])
+                    for part in range(lefts)
+                ]
+                return sum(terms[1:], terms[0])
 
             for place in range(places):
                 lanes = pl.ds(place * size, size)
@@ -838,6 +791,43 @@
                 def _():
                     sink(chunk, source_high, hop).wait_send()
 
+            if form == "lookup":
+                rows = rows_of(chunk)
+                ref["own"][rows, :] = full_ref[rows, shard(me)].astype(jnp.float32)
+                values = full_ref[rows, :].astype(jnp.float32)
+                scale = lax.rsqrt(jnp.sum(values * values, 1, keepdims=True) / D + EPSILON)
+                ref["scale"][chunk] = across(scale)
+                normed = (values * scale * ref["gain"][0:1, :]).astype(jnp.bfloat16)
+                full_ref[rows, :] = normed
+                ref["mixed"][rows, :] = dot_ab(normed, ref["project"][...]).astype(jnp.bfloat16)
+            if form == "inner":
+                rows, one = rows_of(chunk), pl.ds(place_of(chunk), 1)
+
+                @pl.when(chunk == 0)
+                def _():
+                    for name in ("state", "grad_initial", "grad_rate"):
+                        ref[name][...] = jnp.zeros_like(ref[name])
+
+                ref["upstream"][...] = dot_abt(full_ref[rows, :], ref["project"][...])
+                mixer_backward_chunk(
+                    ref["qkv"].at[rows],
+                    ref["rate"],
+                    ref["initial"],
+                    ref["causal"].at[one],
+                    ref["earlier"].at[one],
+                    ref["causal_turned"].at[one],
+                    ref["earlier_turned"].at[one],
+                    ref["first"].at[rows],
+                    ref["last"].at[rows],
+                    ref["anew"].at[one],
+                    ref["residue"].at[rows],
+                    ref["states"].at[one],
+                    ref["upstream"],
+                    ref["grad_mixed"].at[rows],
+                    ref["grad_initial"],
+                    ref["grad_rate"],
+                    ref["state"],
+                )
             if form == "table":
                 @pl.when(lax.rem(chunk, 2) == 1)
                 def _():
@@ -891,6 +881,7 @@
     ids=None,
     entries=None,
     mixer=None,
+    project=None,
     band=ROWS,
 ):
     chunks = tokens // band
@@ -907,9 +898,14 @@
         operands[name] = array
         specs.append(spec)
 
-    take("right", right)
-    if left is not None:
-        take("left", left, pl.BlockSpec(memory_space=pl.ANY))
+    rights = right if isinstance(right, tuple) else (right,)
+    lefts = left if isinstance(left, tuple) else () if left is None else (left,)
+    for part, array in enumerate(rights):
+        take("right%d" % part, array)
+    for part, array in enumerate(lefts):
+        take("left%d" % part, array, pl.BlockSpec(memory_space=pl.ANY))
+    if project is not None:
+        take("project", project)
     if ids is not None:
         take("ids", ids)
     if mixer is not None:
@@ -918,24 +914,32 @@
         pairs, width = mixer["initial"].shape[0], mixer["rate"].shape[1]
     if summing:
         take("inputs", inputs)
-        take("gain", gain)
+    take("gain", gain)
     if mode in ("grad", "grad_add"):
         take("scale", scale)
     if mode == "grad_add":
         take("added", added)
 
-    if summing and form != "table":
+    if form != "table":
         outputs["own"] = ((tokens, size), wide_kind)
     if form != "table":
         outputs["full"] = ((tokens, parts * size), low)
-    if mode == "norm":
+    if mode in ("norm", "plain"):
         outputs["scale"] = ((chunks, 8, band), wide_kind)
     if mode in ("grad", "grad_add"):
         outputs["gain_grad"] = ((8, size), wide_kind)
     if form == "table":
         outputs["table_grad"] = ((entries, 2 * size), wide_kind)
 
-    if mixer is not None:
+    if form == "lookup":
+        outputs["mixed"] = ((tokens, project.shape[1]), low)
+    if form == "inner":
+        outputs["grad_mixed"] = ((tokens, 3 * width), low)
+        outputs["grad_initial"] = ((pairs, PAIR, PAIR), wide_kind)
+        outputs["grad_rate"] = ((1, width), wide_kind)
+        scratch["state"] = pltpu.VMEM((pairs, PAIR, PAIR), wide_kind)
+        scratch["upstream"] = pltpu.VMEM((band, width), wide_kind)
+    if form == "mixer":
         outputs["z"] = ((tokens, width), low)
         outputs["residue"] = ((tokens, width), wide_kind)
         outputs["states"] = ((chunks, pairs, PAIR, PAIR), wide_kind)
@@ -945,9 +949,9 @@
     if form == "table":
         scratch["own"] = pltpu.VMEM((tokens, size), wide_kind)
         scratch["full"] = pltpu.VMEM((chunks // 2, 2 * slabs * band, 2 * size), low)
-    if left is not None:
-        scratch["left_buf"] = pltpu.VMEM((2, band, left.shape[1]), low)
-        scratch["left_sem"] = dma((2,))
+    for part, array in enumerate(lefts):
+        scratch["left_buf%d" % part] = pltpu.VMEM((2, band, array.shape[1]), low)
+        scratch["left_sem%d" % part] = dma((2,))
     if cross:
         scratch["stage"] = pltpu.VMEM((tokens, span), low)
         scratch["cross_out_sem"] = dma((chunks, slabs))
@@ -968,7 +972,7 @@
     scratch["twin_out_sem"] = dma((chunks,))
     scratch["twin_in_sem"] = dma((chunks,))
 
-    depth = right.shape[1] if form in ("turned", "table") else right.shape[0]
+    depth = sum(array.size for array in rights) // (parts * size)
     names = tuple(operands) + tuple(outputs) + tuple(scratch)
     results = pl.pallas_call(
         functools.partial(transit_kernel, mode, form, parts, slabs, names),
@@ -1141,6 +1145,30 @@
     return (grad.reshape(master.shape), new_left, new_right, new_w.reshape(master.shape))
 
 
+def refresh_rows(master, grad, left, right, left_root, right_root):
+    _, rows, kinds, _ = master.shape
+    low_g = grad.astype(jnp.bfloat16)
+
+    def product(form, one, two):
+        return jnp.einsum(
+            form,
+            one.astype(jnp.bfloat16),
+            two.astype(jnp.bfloat16),
+            preferred_element_type=jnp.float32,
+        )
+
+    def shaped(array):
+        return jnp.transpose(array.reshape(kinds, -1, rows), (2, 0, 1))[None]
+
+    master_rows = jnp.transpose(master[0], (1, 2, 0)).reshape(-1, rows)
+    new_left = STAT_DECAY * left + (1.0 - STAT_DECAY) * product("cr,cs->rs", low_g, low_g)
+    new_right = STAT_DECAY * right + (1.0 - STAT_DECAY) * product("cr,dr->cd", low_g, low_g)
+    turned = product("rs,cs->cr", left_root[0, 0], low_g)
+    turned = product("dr,dc->cr", turned, right_root[0, 0])
+    new_w = master_rows - MATRIX_RATE * (turned + WEIGHT_DECAY * master_rows)
+    return (shaped(grad), new_left, new_right, shaped(new_w))
+
+
 def adamw(weight, grad, first, second, step_rate):
     new_first = BETA_ONE * first + (1.0 - BETA_ONE) * grad
     new_second = BETA_TWO * second + (1.0 - BETA_TWO) * grad * grad
@@ -1153,28 +1181,54 @@
 
 
 def layer_forward(
-    local_ids, targets, valid, resets, emb_low, weights, inner_init, gains, gain_one, head_index
+    local_ids,
+    targets,
+    valid,
+    resets,
+    emb_low,
+    w_qkv,
+    later_weights,
+    inner_init,
+    gains,
+    gain_one,
+    head_index,
 ):
-    w_qkv, w_out, w_gu, w_down, table = weights
     parts, slabs = lax.axis_size("head"), lax.axis_size("dp")
-    vocab_part = table.shape[0]
+    vocab_part = emb_low.shape[0]
     tokens, size = targets.shape[0], gains.shape[1]
     chunks = tokens // ROWS
     columns = jnp.arange(vocab_part, dtype=jnp.int32)
     spread_ids = jnp.broadcast_to(local_ids[:, :, None], (slabs, tokens, 128))
-    first = transit("plain", "lookup", 1, parts, slabs, emb_low, tokens, size, ids=spread_ids)
-    low_embedded = first["full"]
-    wide_embedded = low_embedded.astype(jnp.float32)
-    scale_one = lax.rsqrt(jnp.mean(wide_embedded * wide_embedded, -1) + EPSILON)
-    full_one = (wide_embedded * scale_one[:, None] * gain_one[None]).astype(jnp.bfloat16)
-    embedded = lax.dynamic_slice_in_dim(low_embedded, head_index * size, size, 1)
-    embedded = embedded.astype(jnp.float32)
-    scale_one = jnp.broadcast_to(scale_one.reshape(chunks, 1, ROWS), (chunks, 8, ROWS))
-    mixed = jnp.dot(full_one, w_qkv, preferred_element_type=jnp.float32).astype(jnp.bfloat16)
+    first = transit(
+        "plain",
+        "lookup",
+        1,
+        parts,
+        slabs,
+        emb_low,
+        tokens,
+        size,
+        ids=spread_ids,
+        gain=gain_one[None],
+        project=w_qkv,
+    )
+    embedded, full_one, scale_one = first["own"], first["full"], first["scale"]
+    mixed = first["mixed"]
+    w_out, w_gate, w_up, w_down, table, mixed = later_weights(mixed)
     step_rate = jax.nn.sigmoid(gains[3:4]) / (8 * P_SIZE)
     masks = mixer_masks(resets, tokens)
     initial_pairs = pair_blocks(inner_init)
     causal, earlier, before, after, anew = masks
+    inner = dict(
+        qkv=mixed,
+        rate=step_rate,
+        initial=initial_pairs,
+        causal=causal,
+        earlier=earlier,
+        first=before,
+        last=after,
+        anew=anew,
+    )
     second = transit(
         "norm",
         "mixer",
@@ -1184,28 +1238,22 @@
         w_out,
         tokens,
         size,
-        mixer=dict(
-            qkv=mixed,
-            rate=step_rate,
-            initial=initial_pairs,
-            causal=causal,
-            earlier=earlier,
-            first=before,
-            last=after,
-            anew=anew,
-        ),
+        mixer=inner,
         inputs=embedded,
         gain=gains[1:2],
     )
-    inner_low, residue, states = second["z"], second["residue"], second["states"]
+    inner_low = second["z"]
+    inner = dict(
+        inner,
+        causal_turned=jnp.swapaxes(causal, 1, 2),
+        earlier_turned=jnp.swapaxes(earlier, 1, 2),
+        residue=second["residue"],
+        states=second["states"],
+    )
     hidden_one, full_two, scale_two = second["own"], second["full"], second["scale"]
-    gate_up = jnp.dot(full_two, w_gu, preferred_element_type=jnp.float32)
-
-    def swiglu(paired):
-        halves = paired.reshape(tokens, 2, -1)
-        return jax.nn.silu(halves[:, 0]) * halves[:, 1]
-
-    activated, act_pull = jax.vjp(swiglu, gate_up)
+    gate = jnp.einsum("td,fd->tf", full_two, w_gate, preferred_element_type=jnp.float32)
+    up = jnp.einsum("td,fd->tf", full_two, w_up, preferred_element_type=jnp.float32)
+    activated, act_pull = jax.vjp(lambda one, two: jax.nn.silu(one) * two, gate, up)
     act_low = activated.astype(jnp.bfloat16)
     third = transit(
         "norm",
@@ -1239,7 +1287,7 @@
         embedded,
         scale_one,
         full_one,
-        (mixed, step_rate, initial_pairs, masks, residue, states),
+        inner,
         inner_low,
         hidden_one,
         scale_two,
@@ -1252,7 +1300,8 @@
         d_logits,
         local_ids,
     )
-    return (jnp.sum((totals - target_logit) * counted), jnp.sum(counted), kept)
+    weights = (w_qkv, w_out, w_gate, w_up, w_down, table)
+    return (jnp.sum((totals - target_logit) * counted), jnp.sum(counted), kept, weights)
 
 
 def slots_of(grad, order):
@@ -1281,7 +1330,7 @@
         embedded,
         scale_one,
         full_one,
-        inner_kept,
+        inner,
         inner_low,
         hidden_one,
         scale_two,
@@ -1294,7 +1343,7 @@
         d_logits,
         local_ids,
     ) = kept
-    w_qkv, w_out, w_gu, w_down, table = weights
+    w_qkv, w_out, w_gate, w_up, w_down, table = weights
     parts, slabs = lax.axis_size("head"), lax.axis_size("dp")
     tokens, size = embedded.shape
     chunks = tokens // ROWS
@@ -1321,46 +1370,52 @@
     d_two, d_down_in = fourth["own"], fourth["full"]
     d_down_in, owned_table = lax.optimization_barrier((d_down_in, owned_table))
     d_act = jnp.einsum("td,fd->tf", d_down_in, w_down, preferred_element_type=wide_kind)
-    d_gate_up = act_pull(d_act)[0].astype(jnp.bfloat16)
+    d_gate, d_up = act_pull(d_act)
+    d_gate, d_up = d_gate.astype(jnp.bfloat16), d_up.astype(jnp.bfloat16)
     grad_down = jnp.einsum("tf,td->fd", act_low, d_down_in, preferred_element_type=wide_kind)
     slot_down = column_slots_of(grad_down, order[3])
-    d_gate_up, slot_down = lax.optimization_barrier((d_gate_up, slot_down))
+    grad_gate = jnp.einsum("tf,td->fd", d_gate, full_two, preferred_element_type=wide_kind)
+    grad_up = jnp.einsum("tf,td->fd", d_up, full_two, preferred_element_type=wide_kind)
+    slot_gate = column_slots_of(grad_gate, order[2])
+    slot_up = column_slots_of(grad_up, order[2])
+    d_gate, d_up, slot_down, slot_gate, slot_up = lax.optimization_barrier(
+        (d_gate, d_up, slot_down, slot_gate, slot_up)
+    )
     owned_down = scatter_dp(slot_down, 0)
+    owned_gate = scatter_dp(slot_gate, 0)
+    owned_up = scatter_dp(slot_up, 0)
     fifth = transit(
         "grad_add",
-        "turned",
+        "inner",
         5,
         parts,
         slabs,
-        w_gu,
+        (w_gate, w_up),
         tokens,
         size,
-        left=d_gate_up,
+        left=(d_gate, d_up),
         inputs=hidden_one,
         gain=gains[1:2],
         scale=scale_two,
         added=d_two,
-    )
-    d_one, d_out_in = fifth["own"], fifth["full"]
-    d_out_in, owned_down = lax.optimization_barrier((d_out_in, owned_down))
-    d_inner = jnp.einsum("td,cd->tc", d_out_in, w_out, preferred_element_type=wide_kind)
-    grad_gu = jnp.einsum("td,tc->dc", full_two, d_gate_up, preferred_element_type=wide_kind)
-    slot_gu = slots_of(grad_gu, order[2])
-    d_inner, slot_gu = lax.optimization_barrier((d_inner, slot_gu))
-    owned_gu = scatter_dp(slot_gu, 0)
-    d_mixed, grad_pairs, grad_step = mixer_backward(*inner_kept, d_inner)
-    grad_init = head_blocks(grad_pairs)
+        mixer=inner,
+        project=w_out,
+    )
+    d_one, d_out_in, d_mixed = fifth["own"], fifth["full"], fifth["grad_mixed"]
+    grad_init = head_blocks(fifth["grad_initial"])
     gate = jax.nn.sigmoid(gains[3])
-    grad_rate = grad_step[0] * gate * (1.0 - gate) / (8 * P_SIZE)
+    grad_rate = fifth["grad_rate"][0] * gate * (1.0 - gate) / (8 * P_SIZE)
+    d_mixed, owned_down, owned_gate, owned_up = lax.optimization_barrier(
+        (d_mixed, owned_down, owned_gate, owned_up)
+    )
     grad_out = jnp.einsum("tc,td->cd", inner_low, d_out_in, preferred_element_type=wide_kind)
     grad_qkv = jnp.einsum("td,tc->dc", full_one, d_mixed, preferred_element_type=wide_kind)
     slot_out = column_slots_of(grad_out, order[1])
     slot_qkv = slots_of(grad_qkv, order[0])
-    d_mixed, slot_out, slot_qkv, owned_gu = lax.optimization_barrier(
-        (d_mixed, slot_out, slot_qkv, owned_gu)
-    )
+    d_mixed, slot_out, slot_qkv = lax.optimization_barrier((d_mixed, slot_out, slot_qkv))
     owned_out = scatter_dp(slot_out, 0)
     owned_qkv = scatter_dp(slot_qkv, 0)
+    owned_gu = jnp.concatenate([owned_gate, owned_up], 1)
     row_ids = jnp.moveaxis(local_ids.reshape(slabs, chunks // 2, 2, ROWS), 0, 2)
     row_ids = jnp.broadcast_to(
         row_ids.reshape(chunks // 2, 1, 2 * slabs * ROWS), (chunks // 2, 8, 2 * slabs * ROWS)
@@ -1442,22 +1497,49 @@
     def flat(array):
         return array.reshape(array.shape[1], -1)
 
-    gathered = (
-        lax.all_gather(flat(qkv_master).astype(low), "dp", axis=0),
-        lax.all_gather(out_master.astype(low), "dp", axis=0, tiled=True),
-        lax.all_gather(flat(gu_master).astype(low), "dp", axis=0),
-        lax.all_gather(down_master.astype(low), "dp", axis=0, tiled=True),
-        lax.all_gather(emb_low, "dp", axis=1, tiled=True),
-    )
-    w_qkv = jnp.take(gathered[0], owners[0], axis=0, mode="clip").reshape(D, -1)
-    w_out = jnp.take(gathered[1], owners[1], axis=0, mode="clip")
-    w_out = jnp.swapaxes(w_out, 0, 1).reshape(w_out.shape[1], D)
-    w_gu = jnp.take(gathered[2], owners[2], axis=0, mode="clip").reshape(D, -1)
-    w_down = jnp.take(gathered[3], owners[3], axis=0, mode="clip")
-    w_down = jnp.swapaxes(w_down, 0, 1).reshape(w_down.shape[1], D)
-    weights = (w_qkv, w_out, w_gu, w_down, gathered[4])
-    loss_local, count_local, kept = layer_forward(
-        local_ids, targets, valid, resets, emb_low, weights, inner_init, gains, gain_one, head_index
+    gu_rows = jnp.transpose(gu_master[0], (1, 2, 0)).reshape(-1, gu_master.shape[1])
+    hidden = gu_master.shape[3]
+    all_qkv = lax.all_gather(flat(qkv_master).astype(low), "dp", axis=0)
+    w_qkv = jnp.take(all_qkv, owners[0], axis=0, mode="clip").reshape(D, -1)
+
+    def columns_of(slabs, owner):
+        taken = jnp.take(slabs, owner, axis=0, mode="clip")
+        return jnp.swapaxes(taken, 0, 1).reshape(taken.shape[1], D)
+
+    _, out_low, gu_low, down_low = lax.optimization_barrier(
+        (all_qkv, out_master[0].astype(low), gu_rows.astype(low), down_master[0].astype(low))
+    )
+    all_out = lax.all_gather(out_low, "dp", axis=0)
+    all_gu = lax.all_gather(gu_low, "dp", axis=0)
+    all_down = lax.all_gather(down_low, "dp", axis=0)
+
+    def later_weights(mixed):
+        mixed, wait_out, wait_gu, wait_down, wait_emb = lax.optimization_barrier(
+            (mixed, all_out, all_gu, all_down, emb_low)
+        )
+        table = lax.all_gather(wait_emb, "dp", axis=1, tiled=True)
+        w_gu = columns_of(wait_gu, owners[2])
+        return (
+            columns_of(wait_out, owners[1]),
+            w_gu[:hidden],
+            w_gu[hidden:],
+            columns_of(wait_down, owners[3]),
+            table,
+            mixed,
+        )
+
+    loss_local, count_local, kept, weights = layer_forward(
+        local_ids,
+        targets,
+        valid,
+        resets,
+        emb_low,
+        w_qkv,
+        later_weights,
+        inner_init,
+        gains,
+        gain_one,
+        head_index,
     )
     order = jnp.argsort(owners, axis=1)
     owned, grad_init, grad_gains = layer_backward(kept, weights, gains, order)
@@ -1483,7 +1565,9 @@
     out_out = refresh(
         out_master, owned[1] * factor, out_left, out_right, out_left_root, out_right_root
     )
-    gu_out = refresh(gu_master, owned[2] * factor, gu_left, gu_right, gu_left_root, gu_right_root)
+    gu_out = refresh_rows(
+        gu_master, owned[2][0] * factor, gu_left, gu_right, gu_left_root, gu_right_root
+    )
     down_out = refresh(
         down_master, owned[3] * factor, down_left, down_right, down_left_root, down_right_root
     )

time: 1540 us -> 1480 us (0.961)
  local copies, waits for them, and re-layouts: 140 us -> 88.8 us
  waiting for transfers between devices: 0.78 us -> 45.5 us
  other arithmetic: 109 us -> 85.8 us
  Pallas kernels: 1080 us -> 1060 us
  matrix products: 180 us -> 161 us
    pallas_call x1 -> x0, Pallas kernels: 77 us -> none  [mixer_backward(): pl.pallas_call(mixer_backward_kernel, grid=(chunks,), in_specs=[rows(3 *...]
    pallas_call x6, Pallas kernels: 909 us -> 975 us  [transit(): pl.pallas_call(functools.partial(transit_kernel, mode, form, parts, slabs...]
    all_gather x5, waiting for transfers between devices: 0.05 us -> 42.1 us  [the longest x1 42 us: shards(): all_qkv = lax.all_gather(flat(qkv_master).astype(low), 'dp', axis=0)]
    dot_general x4, matrix products: 53.1 us -> 32 us  [the longest x1 9.66 us: layer_forward(): jnp.einsum('td,fd->tf', full_two, w_up, preferred_element_type=jnp.float32)]
    optimization_barrier x2 -> x0, local copies, waits for them, and re-layouts: 16.9 us -> none  [the longest x1 8.71 us: layer_backward(): d_gate_up, slot_down = lax.optimization_barrier((d_gate_up, slot_down))]
    convert_element_type x7 -> x4, other arithmetic: 21.4 us -> 5.75 us  [the longest x1 3.09 us: shards(): gu_rows.astype(low)]
  transfers between devices with their start and end apart: 10 -> 11, of which waited for: 0 -> 1; matrix products, arithmetic and copies ran while one was open for 13% -> 7% of each run, Pallas kernels for 66% -> 68%
where the time goes in v6:
time: 1480 us; the launch traced here: 1470 us
  Pallas kernels  1060 us (72%)
  matrix products  161 us (11%)
  local copies, waits for them, and re-layouts  88.8 us (6%)
  other arithmetic  85.8 us (6%)
  waiting for transfers between devices  45.5 us (3%)
  between operations  23.4 us (2%)
    pallas_call x6, Pallas kernels, transit(): pl.pallas_call(functools.partial(transit_kernel, mode, form, parts, slabs...  975 us
    pallas_call x1, Pallas kernels, scores(): pl.pallas_call(scores_kernel, grid=(tokens // SCORE_ROWS,), in_specs=[pl....  52.1 us
    dot_general x12, matrix products, product(): jnp.einsum(form, one.astype(jnp.bfloat16), two.astype(jnp.bfloat16), pref...  45.5 us
    all_gather x1, waiting for transfers between devices, shards(): all_qkv = lax.all_gather(flat(qkv_master).astype(low), 'dp', axis=0)  42 us
    dot_general x1, matrix products, layer_backward(): jnp.einsum('tv,td->vd', d_logits, full_end, preferred_element_type=wide_k...  41.3 us
    pallas_call x4, Pallas kernels, share(): pl.pallas_call(functools.partial(share_kernel, axes), in_specs=[vmem], ou...  36.1 us
  transfers between devices with their start and end apart: 11, of which 1 were waited for; matrix products, arithmetic and copies ran while one was open for 7% of the time, Pallas kernels for 68%

profile of v6, /device:TPU:0, one launch (start us, length us, event | category | flops | bytes accessed | tf_op | source)
XLA Modules:
  0.0 1468.2 jit_solution(1724793340184046418)
XLA Ops:
  7.2 1.9 copy.142
  10.1 2.7 copy.143
  14.6 3.1 bitcast_convert_fusion
  17.7 42.0 %all-gather.9.cloned.1.call-done = bf16[4,512,768]{2,1,0:T(8,128)(2,1)} async-done(((bf16[1,512,768]{2,1,0:T(8,128)(2,1)}), bf16[4,512,768]{2,1,0:T(8,128)(2,1)}) %all-gather.9.cloned.1.call-update) | async-done | bytes 3145744 | tf_op jit(solution)/shard_map/all_gather | solution.py:1502
  62.3 14.9 %share.4 = f32[32,24,128]{2,1,0:T(8,128)S(1)} custom-call(f32[24,128]{1,0:T(8,128)S(1)} %select_maximum_fusion.1.block_ref), custom_call_target="tpu_custom_call" | custom-call | bytes 16777216 | tf_op jit(solution)/shard_map/share/pallas_call | solution.py:1046
  78.6 6.0 convert_element_type.239.all_refs_0_
  84.7 2.4 gather_fusion
  87.1 3.5 broadcast_in_dim.103.all_refs_2_
  90.6 160.6 %transit_lookup.1 = (f32[2048,256]{1,0:T(8,128)}, bf16[2048,2048]{1,0:T(8,128)(2,1)}, f32[32,8,64]{2,1,0:T(8,128)}, bf16[2048,768]{1,0:T(8,128)(2,1)}) custom-call(bf16[4000,512]{1,0:T(8,128)(2,1)} %convert_element_type.239.all_refs_0_, bf16[2048,768]{1,0:T(8,128)(2,1)} %bitcast.311, s32[4,2048,128]{2,1,0:T(8,128)} %broadcast_in_dim.103.all_refs_2_, ...), custom_call_target="tpu_custom_call" | custom-call | flops 8388608000 | bytes 536870912 | tf_op jit(solution)/shard_map/transit_lookup/pallas_call | solution.py:977
  253.6 2.4 fusion.49
  257.8 7.3 gather_fusion.1
  265.1 3.3 slice_bitcast_fusion.1
  268.4 1.9 copy.188
  270.3 1.9 copy.189
  272.2 2.6 gather_fusion.2
  274.9 2.0 copy.190
  280.2 155.1 %transit_mixer.1 = (f32[2048,256]{1,0:T(8,128)}, bf16[2048,2048]{1,0:T(8,128)(2,1)}, f32[32,8,64]{2,1,0:T(8,128)}, bf16[2048,256]{1,0:T(8,128)(2,1)}, f32[2048,256]{1,0:T(8,128)}, /*index=5*/f32[32,2,128,128]{3,2,1,0:T(8,128)}) custom-call(bf16[256,2048]{1,0:T(8,128)(2,1)} %bitcast.306, bf16[2048,768]{1,0:T(8,128)(2,1)} %get-tuple-element.109.all_refs_1_.all_refs_5_, ...), custom_call_target="tpu_custom_call" | custom-call | flops 2147483648 | bytes 536870912 | tf_op jit(solution)/shard_map/transit_mixer/pallas_call | solution.py:977
  435.3 9.3 fusion.116
  444.6 9.7 multiply_convert_fusion.2
  454.3 145.7 %transit_rows.2 = (f32[2048,256]{1,0:T(8,128)}, bf16[2048,2048]{1,0:T(8,128)(2,1)}, f32[32,8,64]{2,1,0:T(8,128)}) custom-call(bf16[688,2048]{1,0:T(8,128)(2,1)} %bitcast.320, bf16[2048,688]{1,0:T(8,128)(2,1)} %get-tuple-element.310.all_refs_1_, f32[2048,256]{1,0:T(8,128)} %get-tuple-element.112.all_refs_2_.all_refs_17_, f32[1,256]{1,0:T(1,128)} %get-tuple-element.297.all_refs_3_), custom_call_target="tpu_custom_call" | custom-call | flops 5771362304 | bytes 536870912 | tf_op jit(solution)/shard_map/transit_rows/pallas_call | solution.py:977
  601.3 52.1 %scores.1 = (f32[2048,4000]{1,0:T(8,128)}, f32[3,2048,128]{2,1,0:T(8,128)}) custom-call(bf16[2048,2048]{1,0:T(8,128)(2,1)} %get-tuple-element.113.rows_ref, bf16[4000,2048]{1,0:T(8,128)(2,1)} %all-gather.11.cloned.1.call-done.table_ref.all_refs_0_, s32[2048,128]{1,0:T(8,128)} %broadcast_in_dim.111.goal_ref), custom_call_target="tpu_custom_call" | custom-call | flops 33554432000 | bytes 49152000 | tf_op jit(solution)/shard_map/scores/pallas_call | solution.py:1089
  653.4 2.8 slice_reduce_fusion
  656.2 6.1 share.5
  663.2 16.6 %multiply_convert_fusion.all_refs_1_ = bf16[2048,4000]{1,0:T(8,128)(2,1)S(1)} fusion(f32[2048,4000]{1,0:T(8,128)} %get-tuple-element.114, f32[2048]{0:T(1024)S(1)} %convert_element_type.254, s32[2048]{0:T(1024)S(1)} %broadcast_subtract_fusion, f32[2048]{0:T(1024)S(1)} %get-tuple-element.276), kind=kLoop, calls=%fused_computation.9 | loop fusion | flops 49152000 | bytes 49176576 | tf_op jit(solution)/shard_map/convert_element_type | solution.py:1285
  679.9 5.7 copy-done.2
  685.6 41.3 %convolution_convert_fusion = bf16[4000,2048]{1,0:T(8,128)(2,1)} fusion(bf16[2048,4000]{1,0:T(8,128)(2,1)S(1)} %multiply_convert_fusion.all_refs_1_, bf16[2048,2048]{1,0:T(8,128)(2,1)} %get-tuple-element.113.rows_ref), kind=kOutput, calls=%fused_computation.11 | convolution fusion | flops 33562624000 | bytes 41156608 | tf_op jit(solution)/shard_map/tv,td->vd/dot_general | solution.py:1351
  730.2 154.8 %transit_rows.3 = (f32[2048,256]{1,0:T(8,128)}, bf16[2048,2048]{1,0:T(8,128)(2,1)}, f32[8,256]{1,0:T(8,128)}) custom-call(bf16[4000,2048]{1,0:T(8,128)(2,1)} %all-gather.11.cloned.1.call-done.table_ref.all_refs_0_, bf16[2048,4000]{1,0:T(8,128)(2,1)} %copy-done.2, f32[2048,256]{1,0:T(8,128)} %get-tuple-element.117.all_refs_2_, ...), custom_call_target="tpu_custom_call" | custom-call | flops 33554432000 | bytes 536870912 | tf_op jit(solution)/shard_map/transit_rows/pallas_call | solution.py:977
  885.0 10.7 convolution_convert_fusion.4
  895.7 15.3 %multiply_convert_fusion.1 = (bf16[2048,688]{1,0:T(8,128)(2,1)S(1)}, bf16[2048,688]{1,0:T(8,128)(2,1)}) fusion(f32[2048,688]{1,0:T(8,128)} %copy-done.46, f32[2048,688]{1,0:T(8,128)} %get-tuple-element.311, bf16[2048,2048]{1,0:T(8,128)(2,1)} %get-tuple-element.120, bf16[688,2048]{1,0:T(8,128)(2,1)S(1)} %bitcast.321), kind=kOutput, calls=%fused_computation.25 | convolution fusion | flops 5791088640 | bytes 28114944 | tf_op jit(solution)/shard_map/td,fd->tf/dot_general | solution.py:1372
  911.1 6.8 convolution_convert_fusion.2
  918.1 1.6 copy-done.45
  919.8 6.3 convolution_convert_fusion.3
  926.1 1.8 copy.213
  927.9 2.3 gather_fusion.6
  930.2 4.2 gather_fusion.5
  934.3 2.0 copy.214
  936.4 2.3 gather_fusion.4
  940.2 198.4 %transit_inner.1 = (f32[2048,256]{1,0:T(8,128)}, bf16[2048,2048]{1,0:T(8,128)(2,1)}, f32[8,256]{1,0:T(8,128)}, bf16[2048,768]{1,0:T(8,128)(2,1)}, f32[2,128,128]{2,1,0:T(8,128)}, /*index=5*/f32[1,256]{1,0:T(1,128)}) custom-call(bf16[688,2048]{1,0:T(8,128)(2,1)} %bitcast.315, bf16[688,2048]{1,0:T(8,128)(2,1)} %bitcast.317, ...), custom_call_target="tpu_custom_call" | custom-call | flops 11542724608 | bytes 536870912 | tf_op jit(solution)/shard_map/transit_inner/pallas_call | solution.py:977
  1138.7 5.7 convolution_convert_fusion.6
  1146.1 10.2 convolution_convert_fusion.1
  1156.3 2.4 gather_fusion.8
  1160.5 1.6 copy.171
  1162.7 3.7 bitcast_multiply_fusion
  1167.8 2.1 scatter.9
  1171.6 160.5 %transit_table.1 = (f32[8,256]{1,0:T(8,128)}, f32[4000,512]{1,0:T(8,128)}) custom-call(bf16[2048,768]{1,0:T(8,128)(2,1)} %bitcast.312, bf16[2048,768]{1,0:T(8,128)(2,1)} %get-tuple-element.137.all_refs_1_, s32[16,8,512]{2,1,0:T(8,128)} %broadcast_in_dim.119.all_refs_2_, f32[2048,256]{1,0:T(8,128)} %get-tuple-element.110.all_refs_9_.all_refs_3_, ...), custom_call_target="tpu_custom_call" | custom-call | flops 6442450944 | bytes 536870912 | tf_op jit(solution)/shard_map/transit_table/pallas_call | solution.py:977
  1332.9 6.0 share.6
  1344.0 1.9 pad_maximum_fusion.3
  1346.8 7.2 multiply_reduce_fusion
  1354.0 1.7 fusion.60
  1361.4 9.1 share.7
  1376.9 3.8 fusion.23
  1382.2 2.0 convert_multiply_fusion
  1384.2 9.0 fusion.1
  1393.2 2.0 fusion.32
  1397.5 5.2 multiply_subtract_fusion.1
  1402.7 3.0 copy.172
  1405.7 3.0 copy.174
  1408.7 4.0 fusion.22
  1414.3 3.1 copy.173
  1417.5 4.0 fusion.27
  1421.5 2.9 fusion.39
  1424.4 24.1 %multiply_subtract_fusion = (f32[4000,512]{1,0:T(8,128)}, f32[4000,512]{1,0:T(8,128)}, f32[4000,512]{1,0:T(8,128)}) fusion(f32[4000,512]{1,0:T(8,128)} %param.43, f32[]{:T(128)S(6)} %div.96, f32[4000,512]{1,0:T(8,128)} %get-tuple-element.150, bf16[4000,512]{1,0:T(8,128)(2,1)} %reduce-scatter.17.cloned.1.call-done, f32[4000,512]{1,0:T(8,128)} %param.45, ...), kind=kLoop, calls=%fused_computation.18 | loop fusion | flops 36864000 | bytes 61440004 | tf_op jit(solution)/shard_map/sub | solution.py:1180
  1449.1 1.9 multiply_subtract_fusion.2
  1451.0 9.3 fusion.19
  (228 shorter events, 46.1 us)
Async XLA Ops:
  7.2 52.5 %all-gather.9.cloned.1.call-start = ((), (), s32[]{:S(2)}) async-start(), calls=%async_computation.6 | async-start | bytes 3932160 | tf_op jit(solution)/shard_map/all_gather | solution.py:1502
  9.1 5.5 copy-start.3
  9.1 3.8 copy-start.19
  9.2 4.5 copy-start.11
  12.9 238.4 %all-gather.13.cloned.1.call-start = ((), (), s32[]{:S(2)}) async-start(), calls=%async_computation.9 | async-start | bytes 1310720 | tf_op jit(solution)/shard_map/all_gather | solution.py:1512
  14.6 46.5 %copy-start.29 = (f32[4,256]{1,0:T(4,128)S(1)}, f32[4,256]{1,0:T(4,128)}, u32[]{:S(2)}) copy-start(f32[4,256]{1,0:T(4,128)} %param.69) | copy-start | bytes 12292
  14.6 47.1 %copy-start.31 = (s32[2048]{0:T(1024)S(1)}, s32[2048]{0:T(1024)}, u32[]{:S(2)}) copy-start(s32[2048]{0:T(1024)} %param.38) | copy-start | bytes 24580
  59.7 191.6 %all-gather.17.cloned.1.call-start = ((), (), s32[]{:S(2)}) async-start(), calls=%async_computation.11 | async-start | bytes 3522560 | tf_op jit(solution)/shard_map/all_gather | solution.py:1514
  60.5 190.9 %all-gather.15.cloned.1.call-start = ((), (), s32[]{:S(2)}) async-start(), calls=%async_computation.10 | async-start | bytes 7045120 | tf_op jit(solution)/shard_map/all_gather | solution.py:1513
  61.1 538.9 %all-gather.11.cloned.1.call-start = ((), (), s32[]{:S(2)}) async-start(), calls=%async_computation.7 | async-start | bytes 20480000 | tf_op jit(solution)/shard_map/all_gather | solution.py:1520
  61.7 0.6 copy-start.38
  77.2 7.4 copy-start
  78.6 6.0 copy-start.33
  78.6 6.0 copy-start.13
  84.7 2.4 copy-start.26
  251.2 0.7 copy-start.40
  251.2 1.4 copy-start.28
  251.3 1.5 copy-start.24
  251.3 2.3 copy-start.32
  251.4 4.7 copy-start.20
  251.4 633.6 %reduce-scatter.17.cloned.1.call-start = ((), (), s32[]{:S(2)}) async-start(), calls=%async_computation.8 | async-start | bytes 20480000 | tf_op jit(solution)/shard_map/reduce_scatter | solution.py:1320
  280.2 155.1 %copy-start.14 = (bf16[4,86,8,512]{3,2,0,1:T(8,128)(2,1)S(1)}, bf16[4,86,8,512]{3,2,0,1:T(8,128)(2,1)}, u32[]{:S(2)}) copy-start(bf16[4,86,8,512]{3,2,0,1:T(8,128)(2,1)} %copy.188) | copy-start | bytes 8454148
  435.3 9.3 copy-start.15
  435.3 9.3 copy-start.41
  444.6 9.7 copy-start.46
  679.8 5.7 copy-start.2
  726.9 0.7 copy-start.34
  726.9 419.2 %reduce-scatter.19.cloned.1.call-start = ((), (), s32[]{:S(2)}) async-start(), calls=%async_computation.12 | async-start | bytes 3522560
  885.0 10.7 copy-start.16
  885.0 26.0 %slice-start = ((s8[8388608]{0:T(1024)(128)(4,1)}), s8[4194304]{0:T(1024)(128)(4,1)S(1)}, s32[]{:S(2)}) async-start(s8[8388608]{0:T(1024)(128)(4,1)} %bitcast.336), calls=%async_computation.17 | async-start | bytes 8388608
  895.7 15.3 %slice-start.1 = ((s8[8388608]{0:T(1024)(128)(4,1)}), s8[4194304]{0:T(1024)(128)(4,1)S(1)}, s32[]{:S(2)}) async-start(s8[8388608]{0:T(1024)(128)(4,1)} %bitcast.336), calls=%async_computation.18 | async-start | bytes 8388608
  911.0 6.8 copy-start.44
  917.9 1.9 copy-start.45
  938.7 207.4 %reduce-scatter.21.cloned.1.call-start = ((), (), s32[]{:S(2)}) async-start(), calls=%async_computation.13 | async-start | bytes 3522560
  939.4 206.7 %reduce-scatter.23.cloned.1.call-start = ((), (), s32[]{:S(2)}) async-start(), calls=%async_computation.14 | async-start | bytes 3522560
  940.2 413.9 %reduce-scatter.27.cloned.1.call-start = ((), (), s32[]{:S(2)}) async-start(), calls=%async_computation.16 | async-start | bytes 1310720
  940.2 198.4 %copy-start.18 = (bf16[2048,256]{1,0:T(8,128)(2,1)S(1)}, bf16[2048,256]{1,0:T(8,128)(2,1)}, u32[]{:S(2)}) copy-start(bf16[2048,256]{1,0:T(8,128)(2,1)} %get-tuple-element.134) | copy-start | bytes 3145732
  1158.7 1.8 copy-start.4
  1158.8 197.0 %reduce-scatter.25.cloned.1.call-start = ((), (), s32[]{:S(2)}) async-start(), calls=%async_computation.15 | async-start | bytes 3932160
  1162.7 7.2 copy-start.27
  1162.7 8.1 copy-start.37
  1162.7 8.1 copy-start.39
  1171.6 171.1 %copy-start.7 = (bf16[1,688,512]{2,1,0:T(8,128)(2,1)S(1)}, bf16[1,688,512]{2,1,0:T(8,128)(2,1)}, u32[]{:S(2)}) copy-start(bf16[1,688,512]{2,1,0:T(8,128)(2,1)} %reduce-scatter.21.cloned.1.call-done) | copy-start | bytes 2113540
  1171.6 171.1 %copy-start.9 = (bf16[1,688,512]{2,1,0:T(8,128)(2,1)S(1)}, bf16[1,688,512]{2,1,0:T(8,128)(2,1)}, u32[]{:S(2)}) copy-start(bf16[1,688,512]{2,1,0:T(8,128)(2,1)} %reduce-scatter.23.cloned.1.call-done) | copy-start | bytes 2113540
  1332.1 13.8 copy-start.17
  1373.9 43.5 %copy-start.1 = (f32[1,688,512]{2,1,0:T(8,128)}, f32[1,688,512]{2,1,0:T(8,128)S(1)}, u32[]{:S(2)}) copy-start(f32[1,688,512]{2,1,0:T(8,128)S(1)} %convert_multiply_fusion.3) | copy-start | bytes 4227076
  1376.9 3.8 copy-start.21
  1380.7 1.6 copy-start.10
  1384.2 9.0 copy-start.42
  1393.2 2.0 copy-start.23
  1393.2 2.1 copy-start.22
  1395.2 1.4 copy-start.25
  1395.2 26.3 %copy-start.6 = (f32[1,256,512]{2,1,0:T(8,128)}, f32[1,256,512]{2,1,0:T(8,128)S(1)}, u32[]{:S(2)}) copy-start(f32[1,256,512]{2,1,0:T(8,128)S(1)} %convert_multiply_fusion.5) | copy-start | bytes 1572868
  1408.7 4.0 copy-start.43
  1414.3 3.1 copy-start.12
  1424.4 24.1 %copy-start.30 = (f32[4,256]{1,0:T(4,128)S(1)}, f32[4,256]{1,0:T(4,128)}, u32[]{:S(2)}) copy-start(f32[4,256]{1,0:T(4,128)} %param.69) | copy-start | bytes 12292
  1424.4 24.1 %copy-start.35 = (f32[4,256]{1,0:T(4,128)S(1)}, f32[4,256]{1,0:T(4,128)}, u32[]{:S(2)}) copy-start(f32[4,256]{1,0:T(4,128)} %param.71) | copy-start | bytes 12292
  1424.4 24.1 %copy-start.36 = (f32[4,256]{1,0:T(4,128)S(1)}, f32[4,256]{1,0:T(4,128)}, u32[]{:S(2)}) copy-start(f32[4,256]{1,0:T(4,128)} %param.70) | copy-start | bytes 12292
  1424.4 26.6 %copy-start.5 = (f32[1,512,2,688]{1,3,2,0:T(8,128)S(1)}, f32[1,512,2,688]{1,3,2,0:T(8,128)}, u32[]{:S(2)}) copy-start(f32[1,512,2,688]{1,3,2,0:T(8,128)} %param.56) | copy-start | bytes 8454148
  1424.4 26.6 %copy-start.8 = (bf16[1,688,512]{2,1,0:T(8,128)(2,1)S(1)}, bf16[1,688,512]{2,1,0:T(8,128)(2,1)}, u32[]{:S(2)}) copy-start(bf16[1,688,512]{2,1,0:T(8,128)(2,1)} %reduce-scatter.21.cloned.1.call-done) | copy-start | bytes 2113540
Sparse Core Ops, SparseCore 0:
  13.0 46.6 all-gather.8
  62.1 28.7 all-gather.12
  93.3 52.5 all-gather.16
  148.1 94.4 all-gather.14
  251.5 155.5 all-gather.10
  727.0 151.0 reduce-scatter.16
  938.8 40.6 reduce-scatter.18
  982.8 41.2 reduce-scatter.20
  1028.0 41.2 reduce-scatter.22
  1158.9 27.1 reduce-scatter.26
  1189.6 60.8 reduce-scatter.24

commit v7 on v6

--- a/solution.py
+++ b/solution.py
@@ -249,29 +249,22 @@
         joined = tuple(
             jnp.concatenate([one, two], 0) for one, two in zip(upstream_parts, residue_parts)
         )
-        scaled_stack = stack(scaled)
-        turned = wide(dot_abt, scaled_stack, joined)
-        straight = wide(
-            dot_abt,
-            tuple(
-                jnp.concatenate([stack(one), stack(two)], 0)
-                for one, two in zip(upstream_parts, residue_parts)
-            ),
-            scaled,
+        turned = dot_abt(stack(scaled[0]), joined[0])
+        straight = dot_abt(
+            jnp.concatenate([stack(upstream_parts[0]), stack(residue_parts[0])], 0), scaled[0]
         )
         grad_scores = -straight[: 2 * CHUNK] * causal
         grad_scores_turned = -turned[:, :CHUNK] * causal_turned
         grad_ties = -(straight[2 * CHUNK :] * earlier + turned[:, CHUNK:] * earlier_turned)
-        seen = wide(dot_abt, joined, begin)
-        fresh = wide(dot_abt, joined, initial)
+        seen = dot_abt(joined[0], begin[0])
+        fresh = dot_abt(joined[0], initial[0])
         grad_query = jnp.where(first, seen[:CHUNK], fresh[:CHUNK])
-        grad_query = grad_query + pick(wide(dot_ab, halves_of(grad_scores), key))
+        grad_query = grad_query + pick(dot_ab(grad_scores.astype(low), key))
         grad_key = jnp.where(first, seen[CHUNK:], fresh[CHUNK:]) + grad_residue
         grad_key = grad_key + pick(
-            wide(dot_ab, halves_of(grad_scores_turned), query)
-            + wide(dot_ab, halves_of(grad_ties), key)
+            dot_ab(grad_scores_turned.astype(low), query) + dot_ab(grad_ties.astype(low), key)
         )
-        grad_key = grad_key - last * wide(dot_abt, scaled, after_parts)
+        grad_key = grad_key - last * dot_abt(scaled[0], after_parts[0])
         grad_ref[:, lanes] = grad_query.astype(low)
         grad_ref[:, width + pair * PAIR : width + (pair + 1) * PAIR] = grad_key.astype(low)
         grad_ref[:, 2 * width + pair * PAIR : 2 * width + (pair + 1) * PAIR] = (
@@ -315,7 +308,7 @@
     return jnp.concatenate([turned] * (width // 128), 1) if width > 128 else turned
 
 
-def transit_kernel(mode, form, parts, slabs, names, *all_refs):
+def transit_kernel(mode, form, lag, parts, slabs, names, *all_refs):
     ref = dict(zip(names, all_refs))
     full_ref, partial, total = ref["full"], ref["partial"], ref["total"]
     pair_out, pair_in = ref["pair_out"], ref["pair_in"]
@@ -334,10 +327,10 @@
     upper = {"head": lax.rem(me + 2, parts)}
     lower = {"head": lax.rem(me + parts - 2, parts)}
     chunks = ref["up_in_sem"].shape[0]
-    sum_at = LAG * places
-    finish_at = sum_at + (LAG if summing else 0)
-    reach_at = finish_at + LAG * (places - 1)
-    close_at = reach_at + (2 * LAG if cross else LAG)
+    sum_at = 1 + lag * (places - 1)
+    finish_at = sum_at + (lag if summing else 0)
+    reach_at = finish_at + lag * (places - 1)
+    close_at = reach_at + (lag + 1 if cross else 1)
 
     def place_of(chunk):
         return chunks - 1 - chunk if form == "inner" else chunk
@@ -492,7 +485,7 @@
 
     def receive(step):
         for hop in range(places):
-            chunk = step - finish_at - LAG * (hop + 1)
+            chunk = step - finish_at - lag * (hop + 1)
 
             @pl.when(jnp.logical_and(valid(chunk), jnp.abs(spot - mine_dp) == hop))
             def _():
@@ -510,7 +503,7 @@
 
     def relay(step):
         for hop in range(1, places):
-            chunk = step - finish_at - LAG * hop
+            chunk = step - finish_at - lag * hop
             source = spot - hop
 
             @pl.when(jnp.logical_and(valid(chunk), source >= 0))
@@ -584,7 +577,7 @@
             have(chunk, spot)
 
     def add_pair(step):
-        chunk = step - LAG
+        chunk = step - 1
 
         @pl.when(valid(chunk))
         def _():
@@ -595,7 +588,7 @@
     def pass_on(step):
         for place in range(places):
             if place < places - 1:
-                up_chunk = step - LAG * (1 + place)
+                up_chunk = step - 1 - lag * place
 
                 @pl.when(jnp.logical_and(valid(up_chunk), spot == place))
                 def _():
@@ -609,7 +602,7 @@
                     rise(up_chunk, place).start()
 
             if place > 0:
-                down_chunk = step - LAG * (places - place)
+                down_chunk = step - 1 - lag * (places - 1 - place)
 
                 @pl.when(jnp.logical_and(valid(down_chunk), spot == place))
                 def _():
@@ -623,7 +616,7 @@
                     fall(down_chunk, place).start()
 
     def settle(step):
-        chunk = step - sum_at - LAG
+        chunk = step - sum_at - lag
 
         @pl.when(valid(chunk))
         def _():
@@ -799,7 +792,6 @@
                 ref["scale"][chunk] = across(scale)
                 normed = (values * scale * ref["gain"][0:1, :]).astype(jnp.bfloat16)
                 full_ref[rows, :] = normed
-                ref["mixed"][rows, :] = dot_ab(normed, ref["project"][...]).astype(jnp.bfloat16)
             if form == "inner":
                 rows, one = rows_of(chunk), pl.ds(place_of(chunk), 1)
 
@@ -883,12 +875,13 @@
     mixer=None,
     project=None,
     band=ROWS,
+    lag=LAG,
 ):
     chunks = tokens // band
     places = parts // 2
     cross = form in ("lookup", "table")
     summing = mode != "plain"
-    ring = min(chunks, LAG * (places + 1) + 2) if summing else chunks
+    ring = min(chunks, lag * (places + 1) + 2) if summing else chunks
     dma = pltpu.SemaphoreType.DMA
     low, wide_kind = jnp.bfloat16, jnp.float32
     vmem = pl.BlockSpec(memory_space=pltpu.VMEM)
@@ -931,8 +924,6 @@
     if form == "table":
         outputs["table_grad"] = ((entries, 2 * size), wide_kind)
 
-    if form == "lookup":
-        outputs["mixed"] = ((tokens, project.shape[1]), low)
     if form == "inner":
         outputs["grad_mixed"] = ((tokens, 3 * width), low)
         outputs["grad_initial"] = ((pairs, PAIR, PAIR), wide_kind)
@@ -975,7 +966,7 @@
     depth = sum(array.size for array in rights) // (parts * size)
     names = tuple(operands) + tuple(outputs) + tuple(scratch)
     results = pl.pallas_call(
-        functools.partial(transit_kernel, mode, form, parts, slabs, names),
+        functools.partial(transit_kernel, mode, form, lag, parts, slabs, names),
         in_specs=specs,
         out_specs=[vmem] * len(outputs),
         out_shape=[jax.ShapeDtypeStruct(shape, kind) for shape, kind in outputs.values()],
@@ -1064,20 +1055,19 @@
 
 def scores_kernel(rows_ref, table_ref, goal_ref, logits_ref, stats_ref):
     entries = table_ref.shape[0]
-    edges = list(range(0, entries, 1024)) + [entries]
-    peak = jnp.full((SCORE_ROWS, 1), -jnp.inf, jnp.float32)
+    edges = list(range(0, entries, 512)) + [entries]
+    goal = goal_ref[:, 0:1]
+    picked = jnp.zeros((SCORE_ROWS, 1), jnp.float32)
+    peaks, sums = [], []
     for low, high in zip(edges, edges[1:]):
         values = dot_abt(rows_ref[...], table_ref[low:high, :])
         logits_ref[:, low:high] = values
-        peak = jnp.maximum(peak, jnp.max(values, 1, keepdims=True))
-    exp_sum = jnp.zeros((SCORE_ROWS, 1), jnp.float32)
-    picked = jnp.zeros((SCORE_ROWS, 1), jnp.float32)
-    goal = goal_ref[:, 0:1]
-    for low, high in zip(edges, edges[1:]):
-        values = logits_ref[:, low:high]
-        exp_sum = exp_sum + jnp.sum(jnp.exp(values - peak), 1, keepdims=True)
+        peaks.append(jnp.max(values, 1, keepdims=True))
+        sums.append(jnp.sum(jnp.exp(values - peaks[-1]), 1, keepdims=True))
         spots = low + lax.broadcasted_iota(jnp.int32, values.shape, 1)
         picked = picked + jnp.sum(jnp.where(spots == goal, values, 0.0), 1, keepdims=True)
+    peak = functools.reduce(jnp.maximum, peaks)
+    exp_sum = sum(part * jnp.exp(top - peak) for part, top in zip(sums, peaks))
     stats_ref[0] = jnp.broadcast_to(peak, (SCORE_ROWS, 128))
     stats_ref[1] = jnp.broadcast_to(exp_sum, (SCORE_ROWS, 128))
     stats_ref[2] = jnp.broadcast_to(picked, (SCORE_ROWS, 128))
@@ -1186,7 +1176,6 @@
     valid,
     resets,
     emb_low,
-    w_qkv,
     later_weights,
     inner_init,
     gains,
@@ -1210,11 +1199,11 @@
         size,
         ids=spread_ids,
         gain=gain_one[None],
-        project=w_qkv,
+        lag=3,
     )
     embedded, full_one, scale_one = first["own"], first["full"], first["scale"]
-    mixed = first["mixed"]
-    w_out, w_gate, w_up, w_down, table, mixed = later_weights(mixed)
+    full_one, w_qkv, w_out, w_gate, w_up, w_down, table = later_weights(full_one)
+    mixed = jnp.dot(full_one, w_qkv, preferred_element_type=jnp.float32).astype(jnp.bfloat16)
     step_rate = jax.nn.sigmoid(gains[3:4]) / (8 * P_SIZE)
     masks = mixer_masks(resets, tokens)
     initial_pairs = pair_blocks(inner_init)
@@ -1239,6 +1228,7 @@
         tokens,
         size,
         mixer=inner,
+        lag=3,
         inputs=embedded,
         gain=gains[1:2],
     )
@@ -1399,6 +1389,7 @@
         scale=scale_two,
         added=d_two,
         mixer=inner,
+        lag=3,
         project=w_out,
     )
     d_one, d_out_in, d_mixed = fifth["own"], fifth["full"], fifth["grad_mixed"]
@@ -1500,32 +1491,29 @@
     gu_rows = jnp.transpose(gu_master[0], (1, 2, 0)).reshape(-1, gu_master.shape[1])
     hidden = gu_master.shape[3]
     all_qkv = lax.all_gather(flat(qkv_master).astype(low), "dp", axis=0)
-    w_qkv = jnp.take(all_qkv, owners[0], axis=0, mode="clip").reshape(D, -1)
+    all_out = lax.all_gather(out_master[0].astype(low), "dp", axis=0)
+    all_gu = lax.all_gather(gu_rows.astype(low), "dp", axis=0)
 
     def columns_of(slabs, owner):
         taken = jnp.take(slabs, owner, axis=0, mode="clip")
         return jnp.swapaxes(taken, 0, 1).reshape(taken.shape[1], D)
 
-    _, out_low, gu_low, down_low = lax.optimization_barrier(
-        (all_qkv, out_master[0].astype(low), gu_rows.astype(low), down_master[0].astype(low))
-    )
-    all_out = lax.all_gather(out_low, "dp", axis=0)
-    all_gu = lax.all_gather(gu_low, "dp", axis=0)
-    all_down = lax.all_gather(down_low, "dp", axis=0)
-
-    def later_weights(mixed):
-        mixed, wait_out, wait_gu, wait_down, wait_emb = lax.optimization_barrier(
-            (mixed, all_out, all_gu, all_down, emb_low)
+    def later_weights(rows):
+        rows, wait_qkv, wait_out, wait_gu, down_low, table_low = lax.optimization_barrier(
+            (rows, all_qkv, all_out, all_gu, down_master[0].astype(low), emb_low)
         )
-        table = lax.all_gather(wait_emb, "dp", axis=1, tiled=True)
+        w_qkv = jnp.take(wait_qkv, owners[0], axis=0, mode="clip").reshape(D, -1)
+        all_down = lax.all_gather(down_low, "dp", axis=0)
+        table = lax.all_gather(table_low, "dp", axis=1, tiled=True)
         w_gu = columns_of(wait_gu, owners[2])
         return (
+            rows,
+            w_qkv,
             columns_of(wait_out, owners[1]),
             w_gu[:hidden],
             w_gu[hidden:],
-            columns_of(wait_down, owners[3]),
+            columns_of(all_down, owners[3]),
             table,
-            mixed,
         )
 
     loss_local, count_local, kept, weights = layer_forward(
@@ -1534,7 +1522,6 @@
         valid,
         resets,
         emb_low,
-        w_qkv,
         later_weights,
         inner_init,
         gains,

time: 1480 us -> 1440 us (0.973)
  waiting for transfers between devices: 45.5 us -> 2.81 us
    all_gather x1, waiting for transfers between devices: 42 us -> 0.02 us  [shards(): all_qkv = lax.all_gather(flat(qkv_master).astype(low), 'dp', axis=0)]
  transfers between devices with their start and end apart: 11 -> 11, of which waited for: 1 -> 0; matrix products, arithmetic and copies ran while one was open for 7% -> 8% of each run, Pallas kernels for 68% -> 70%
where the time goes in v7:
time: 1440 us; the launch traced here: 1430 us
  Pallas kernels  1060 us (74%)
  matrix products  172 us (12%)
  local copies, waits for them, and re-layouts  88 us (6%)
  other arithmetic  86 us (6%)
  between operations  23.4 us (2%)
    pallas_call x6, Pallas kernels, transit(): pl.pallas_call(functools.partial(transit_kernel, mode, form, lag, parts,...  973 us
    pallas_call x1, Pallas kernels, scores(): pl.pallas_call(scores_kernel, grid=(tokens // SCORE_ROWS,), in_specs=[pl....  47.9 us
    dot_general x12, matrix products, product(): jnp.einsum(form, one.astype(jnp.bfloat16), two.astype(jnp.bfloat16), pref...  45.5 us
    dot_general x1, matrix products, layer_backward(): jnp.einsum('tv,td->vd', d_logits, full_end, preferred_element_type=wide_k...  41.1 us
    pallas_call x4, Pallas kernels, share(): pl.pallas_call(functools.partial(share_kernel, axes), in_specs=[vmem], ou...  40.5 us
  transfers between devices with their start and end apart: 11, of which 0 were waited for; matrix products, arithmetic and copies ran while one was open for 8% of the time, Pallas kernels for 70%

profile of v7, /device:TPU:0, one launch (start us, length us, event | category | flops | bytes accessed | tf_op | source)
XLA Modules:
  0.0 1434.3 jit_solution(15770325619313108428)
XLA Ops:
  7.2 1.8 convert_element_type.258
  9.1 1.9 copy.143
  12.5 3.1 bitcast_convert_fusion
  16.8 16.6 %share.4 = f32[32,24,128]{2,1,0:T(8,128)S(1)} custom-call(f32[24,128]{1,0:T(8,128)S(1)} %select_maximum_fusion.1.block_ref), custom_call_target="tpu_custom_call" | custom-call | bytes 16777216 | tf_op jit(solution)/shard_map/share/pallas_call | solution.py:1037
  34.2 5.9 convert_element_type.253.all_refs_0_
  41.0 3.5 broadcast_in_dim.102.all_refs_1_
  44.6 159.0 %transit_lookup.1 = (f32[2048,256]{1,0:T(8,128)}, bf16[2048,2048]{1,0:T(8,128)(2,1)}, f32[32,8,64]{2,1,0:T(8,128)}) custom-call(bf16[4000,512]{1,0:T(8,128)(2,1)} %convert_element_type.253.all_refs_0_, s32[4,2048,128]{2,1,0:T(8,128)} %broadcast_in_dim.102.all_refs_1_, f32[1,2048]{1,0:T(1,128)} %bitcast.333), custom_call_target="tpu_custom_call" | custom-call | flops 8388608000 | bytes 536870912 | tf_op jit(solution)/shard_map/transit_lookup/pallas_call | solution.py:968
  206.5 2.4 fusion.49
  210.7 6.4 gather_fusion
  217.1 3.0 slice_bitcast_fusion.1
  220.1 1.9 copy.189
  222.0 1.9 copy.190
  223.9 2.6 gather_fusion.3
  226.6 11.6 convolution_convert_fusion.1.all_refs_1_.all_refs_5_
  241.5 166.0 %transit_mixer.1 = (f32[2048,256]{1,0:T(8,128)}, bf16[2048,2048]{1,0:T(8,128)(2,1)}, f32[32,8,64]{2,1,0:T(8,128)}, bf16[2048,256]{1,0:T(8,128)(2,1)}, f32[2048,256]{1,0:T(8,128)}, /*index=5*/f32[32,2,128,128]{3,2,1,0:T(8,128)}) custom-call(bf16[256,2048]{1,0:T(8,128)(2,1)} %bitcast.306, bf16[2048,768]{1,0:T(8,128)(2,1)} %convolution_convert_fusion.1.all_refs_1_.all_refs_5_, ...), custom_call_target="tpu_custom_call" | custom-call | flops 2147483648 | bytes 536870912 | tf_op jit(solution)/shard_map/transit_mixer/pallas_call | solution.py:968
  407.6 9.3 fusion.116
  416.8 2.7 copy-done.44
  419.5 10.2 multiply_convert_fusion.2
  429.7 2.5 gather_fusion.1
  432.2 2.0 copy.191
  434.2 144.6 %transit_rows.2 = (f32[2048,256]{1,0:T(8,128)}, bf16[2048,2048]{1,0:T(8,128)(2,1)}, f32[32,8,64]{2,1,0:T(8,128)}) custom-call(bf16[688,2048]{1,0:T(8,128)(2,1)} %bitcast.320, bf16[2048,688]{1,0:T(8,128)(2,1)} %get-tuple-element.304.all_refs_1_, f32[2048,256]{1,0:T(8,128)} %get-tuple-element.107.all_refs_2_.all_refs_17_, f32[1,256]{1,0:T(1,128)} %get-tuple-element.291.all_refs_3_), custom_call_target="tpu_custom_call" | custom-call | flops 5771362304 | bytes 536870912 | tf_op jit(solution)/shard_map/transit_rows/pallas_call | solution.py:968
  580.1 47.9 %scores.1 = (f32[2048,4000]{1,0:T(8,128)}, f32[3,2048,128]{2,1,0:T(8,128)}) custom-call(bf16[2048,2048]{1,0:T(8,128)(2,1)} %get-tuple-element.108.rows_ref, bf16[4000,2048]{1,0:T(8,128)(2,1)} %all-gather.13.cloned.1.call-done.table_ref.all_refs_0_, s32[2048,128]{1,0:T(8,128)} %broadcast_in_dim.111.goal_ref), custom_call_target="tpu_custom_call" | custom-call | flops 33554432000 | bytes 49152000 | tf_op jit(solution)/shard_map/scores/pallas_call | solution.py:1079
  628.0 2.8 slice_reduce_fusion
  630.8 6.1 share.5
  637.9 16.8 %multiply_convert_fusion.all_refs_1_ = bf16[2048,4000]{1,0:T(8,128)(2,1)S(1)} fusion(f32[2048,4000]{1,0:T(8,128)} %get-tuple-element.109, f32[2048]{0:T(1024)S(1)} %convert_element_type.270, s32[2048]{0:T(1024)S(1)} %broadcast_subtract_fusion, f32[2048]{0:T(1024)S(1)} %get-tuple-element.270), kind=kLoop, calls=%fused_computation.9 | loop fusion | flops 49152000 | bytes 49176576 | tf_op jit(solution)/shard_map/convert_element_type | solution.py:1275
  654.7 5.7 copy-done.2
  660.4 41.1 %convolution_convert_fusion = bf16[4000,2048]{1,0:T(8,128)(2,1)} fusion(bf16[2048,4000]{1,0:T(8,128)(2,1)S(1)} %multiply_convert_fusion.all_refs_1_, bf16[2048,2048]{1,0:T(8,128)(2,1)} %get-tuple-element.108.rows_ref), kind=kOutput, calls=%fused_computation.11 | convolution fusion | flops 33562624000 | bytes 41156608 | tf_op jit(solution)/shard_map/tv,td->vd/dot_general | solution.py:1341
  704.8 152.2 %transit_rows.3 = (f32[2048,256]{1,0:T(8,128)}, bf16[2048,2048]{1,0:T(8,128)(2,1)}, f32[8,256]{1,0:T(8,128)}) custom-call(bf16[4000,2048]{1,0:T(8,128)(2,1)} %all-gather.13.cloned.1.call-done.table_ref.all_refs_0_, bf16[2048,4000]{1,0:T(8,128)(2,1)} %copy-done.2, f32[2048,256]{1,0:T(8,128)} %get-tuple-element.112.all_refs_2_, ...), custom_call_target="tpu_custom_call" | custom-call | flops 33554432000 | bytes 536870912 | tf_op jit(solution)/shard_map/transit_rows/pallas_call | solution.py:968
  857.1 10.7 convolution_convert_fusion.5
  867.8 15.3 %multiply_convert_fusion.1 = (bf16[2048,688]{1,0:T(8,128)(2,1)S(1)}, bf16[2048,688]{1,0:T(8,128)(2,1)}) fusion(f32[2048,688]{1,0:T(8,128)} %copy-done.44, f32[2048,688]{1,0:T(8,128)} %get-tuple-element.305, bf16[2048,2048]{1,0:T(8,128)(2,1)} %get-tuple-element.115, bf16[688,2048]{1,0:T(8,128)(2,1)S(1)} %bitcast.321), kind=kOutput, calls=%fused_computation.25 | convolution fusion | flops 5791088640 | bytes 28114944 | tf_op jit(solution)/shard_map/td,fd->tf/dot_general | solution.py:1362
  883.1 6.4 convolution_convert_fusion.3
  889.8 1.6 copy-done.43
  891.4 6.3 convolution_convert_fusion.4
  897.7 1.8 copy.214
  899.6 2.3 gather_fusion.6
  901.8 4.2 gather_fusion.5
  906.0 2.0 copy.215
  908.0 2.3 gather_fusion.4
  911.9 192.6 %transit_inner.1 = (f32[2048,256]{1,0:T(8,128)}, bf16[2048,2048]{1,0:T(8,128)(2,1)}, f32[8,256]{1,0:T(8,128)}, bf16[2048,768]{1,0:T(8,128)(2,1)}, f32[2,128,128]{2,1,0:T(8,128)}, /*index=5*/f32[1,256]{1,0:T(1,128)}) custom-call(bf16[688,2048]{1,0:T(8,128)(2,1)} %bitcast.315, bf16[688,2048]{1,0:T(8,128)(2,1)} %bitcast.317, ...), custom_call_target="tpu_custom_call" | custom-call | flops 11542724608 | bytes 536870912 | tf_op jit(solution)/shard_map/transit_inner/pallas_call | solution.py:968
  1104.5 5.7 convolution_convert_fusion.7
  1111.9 10.2 convolution_convert_fusion.2
  1122.2 2.4 gather_fusion.8
  1128.6 3.7 bitcast_multiply_fusion
  1133.7 2.1 scatter.9
  1137.4 158.2 %transit_table.1 = (f32[8,256]{1,0:T(8,128)}, f32[4000,512]{1,0:T(8,128)}) custom-call(bf16[2048,768]{1,0:T(8,128)(2,1)} %bitcast.312, bf16[2048,768]{1,0:T(8,128)(2,1)} %get-tuple-element.131.all_refs_1_, s32[16,8,512]{2,1,0:T(8,128)} %broadcast_in_dim.119.all_refs_2_, f32[2048,256]{1,0:T(8,128)} %get-tuple-element.105.all_refs_9_.all_refs_3_, ...), custom_call_target="tpu_custom_call" | custom-call | flops 6442450944 | bytes 536870912 | tf_op jit(solution)/shard_map/transit_table/pallas_call | solution.py:968
  1296.3 8.6 share.6
  1310.0 1.9 pad_maximum_fusion.3
  1312.8 7.2 multiply_reduce_fusion
  1320.0 1.7 fusion.60
  1327.4 9.3 share.7
  1343.1 3.8 fusion.23
  1348.4 2.0 convert_multiply_fusion
  1350.4 9.0 fusion.1
  1359.3 2.0 fusion.32
  1363.7 5.2 multiply_subtract_fusion.1
  1368.9 3.0 copy.173
  1371.9 3.0 copy.175
  1374.9 4.0 fusion.22
  1380.5 3.1 copy.174
  1383.6 4.0 fusion.27
  1387.7 2.9 fusion.39
  1390.6 24.1 %multiply_subtract_fusion = (f32[4000,512]{1,0:T(8,128)}, f32[4000,512]{1,0:T(8,128)}, f32[4000,512]{1,0:T(8,128)}) fusion(f32[4000,512]{1,0:T(8,128)} %param.43, f32[]{:T(128)S(6)} %div.96, f32[4000,512]{1,0:T(8,128)} %get-tuple-element.144, bf16[4000,512]{1,0:T(8,128)(2,1)} %reduce-scatter.17.cloned.1.call-done, f32[4000,512]{1,0:T(8,128)} %param.45, ...), kind=kLoop, calls=%fused_computation.18 | loop fusion | flops 36864000 | bytes 61440004 | tf_op jit(solution)/shard_map/sub | solution.py:1170
  1415.3 1.9 multiply_subtract_fusion.2
  1417.2 9.3 fusion.19
  (225 shorter events, 45.8 us)
Async XLA Ops:
  7.2 196.5 %all-gather.9.cloned.1.call-start = ((), (), s32[]{:S(2)}) async-start(), calls=%async_computation.7 | async-start | bytes 1310720 | tf_op jit(solution)/shard_map/all_gather | solution.py:1494
  9.1 194.7 %all-gather.7.cloned.1.call-start = ((), (), s32[]{:S(2)}) async-start(), calls=%async_computation.6 | async-start | bytes 3932160 | tf_op jit(solution)/shard_map/all_gather | solution.py:1493
  11.0 4.5 copy-start.3
  12.4 3.2 copy-start.27
  12.4 3.8 copy-start.29
  12.4 191.4 %all-gather.11.cloned.1.call-start = ((), (), s32[]{:S(2)}) async-start(), calls=%async_computation.8 | async-start | bytes 7045120 | tf_op jit(solution)/shard_map/all_gather | solution.py:1495
  15.6 414.1 %all-gather.15.cloned.1.call-start = ((), (), s32[]{:S(2)}) async-start(), calls=%async_computation.11 | async-start | bytes 3522560 | tf_op jit(solution)/shard_map/all_gather | solution.py:1506
  16.2 0.6 copy-start.36
  33.4 6.7 copy-start
  34.2 5.9 copy-start.11
  203.6 1.1 copy-start.38
  203.7 1.9 copy-start.26
  203.7 1.9 copy-start.31
  203.7 2.0 copy-start.23
  203.7 2.8 copy-start.30
  203.8 375.0 %all-gather.13.cloned.1.call-start = ((), (), s32[]{:S(2)}) async-start(), calls=%async_computation.9 | async-start | bytes 20480000 | tf_op jit(solution)/shard_map/all_gather | solution.py:1507
  204.4 4.6 copy-start.19
  204.4 652.7 %reduce-scatter.17.cloned.1.call-start = ((), (), s32[]{:S(2)}) async-start(), calls=%async_computation.10 | async-start | bytes 20480000 | tf_op jit(solution)/shard_map/reduce_scatter | solution.py:1310
  226.6 11.6 copy-start.13
  241.5 166.0 %copy-start.14 = (bf16[4,86,8,512]{3,2,0,1:T(8,128)(2,1)S(1)}, bf16[4,86,8,512]{3,2,0,1:T(8,128)(2,1)}, u32[]{:S(2)}) copy-start(bf16[4,86,8,512]{3,2,0,1:T(8,128)(2,1)} %copy.189) | copy-start | bytes 8454148
  407.5 12.0 copy-start.15
  407.5 12.0 copy-start.39
  416.8 2.7 copy-start.44
  654.7 5.7 copy-start.2
  701.5 0.7 copy-start.32
  701.5 410.4 %reduce-scatter.19.cloned.1.call-start = ((), (), s32[]{:S(2)}) async-start(), calls=%async_computation.12 | async-start | bytes 3522560
  857.1 10.7 copy-start.16
  857.1 26.0 %slice-start = ((s8[8388608]{0:T(1024)(128)(4,1)}), s8[4194304]{0:T(1024)(128)(4,1)S(1)}, s32[]{:S(2)}) async-start(s8[8388608]{0:T(1024)(128)(4,1)} %bitcast.335), calls=%async_computation.17 | async-start | bytes 8388608
  867.8 15.3 %slice-start.1 = ((s8[8388608]{0:T(1024)(128)(4,1)}), s8[4194304]{0:T(1024)(128)(4,1)S(1)}, s32[]{:S(2)}) async-start(s8[8388608]{0:T(1024)(128)(4,1)} %bitcast.335), calls=%async_computation.18 | async-start | bytes 8388608
  883.1 6.4 copy-start.42
  889.5 1.9 copy-start.43
  910.3 201.6 %reduce-scatter.21.cloned.1.call-start = ((), (), s32[]{:S(2)}) async-start(), calls=%async_computation.13 | async-start | bytes 3522560
  911.1 200.8 %reduce-scatter.23.cloned.1.call-start = ((), (), s32[]{:S(2)}) async-start(), calls=%async_computation.14 | async-start | bytes 3522560
  911.8 408.2 %reduce-scatter.27.cloned.1.call-start = ((), (), s32[]{:S(2)}) async-start(), calls=%async_computation.16 | async-start | bytes 1310720
  911.9 192.6 %copy-start.18 = (bf16[2048,256]{1,0:T(8,128)(2,1)S(1)}, bf16[2048,256]{1,0:T(8,128)(2,1)}, u32[]{:S(2)}) copy-start(bf16[2048,256]{1,0:T(8,128)(2,1)} %get-tuple-element.129) | copy-start | bytes 3145732
  1124.6 1.8 copy-start.4
  1124.6 197.1 %reduce-scatter.25.cloned.1.call-start = ((), (), s32[]{:S(2)}) async-start(), calls=%async_computation.15 | async-start | bytes 3932160
  1128.0 7.7 copy-start.25
  1128.6 8.1 copy-start.35
  1128.6 8.1 copy-start.37
  1137.4 171.3 %copy-start.7 = (bf16[1,688,512]{2,1,0:T(8,128)(2,1)S(1)}, bf16[1,688,512]{2,1,0:T(8,128)(2,1)}, u32[]{:S(2)}) copy-start(bf16[1,688,512]{2,1,0:T(8,128)(2,1)} %reduce-scatter.21.cloned.1.call-done) | copy-start | bytes 2113540
  1137.4 171.3 %copy-start.9 = (bf16[1,688,512]{2,1,0:T(8,128)(2,1)S(1)}, bf16[1,688,512]{2,1,0:T(8,128)(2,1)}, u32[]{:S(2)}) copy-start(bf16[1,688,512]{2,1,0:T(8,128)(2,1)} %reduce-scatter.23.cloned.1.call-done) | copy-start | bytes 2113540
  1137.4 174.5 %copy-start.17 = (bf16[1,688,512]{2,1,0:T(8,128)(2,1)S(1)}, bf16[1,688,512]{2,1,0:T(8,128)(2,1)}, u32[]{:S(2)}) copy-start(bf16[1,688,512]{2,1,0:T(8,128)(2,1)} %reduce-scatter.19.cloned.1.call-done) | copy-start | bytes 2113540
  1340.1 43.5 %copy-start.1 = (f32[1,688,512]{2,1,0:T(8,128)}, f32[1,688,512]{2,1,0:T(8,128)S(1)}, u32[]{:S(2)}) copy-start(f32[1,688,512]{2,1,0:T(8,128)S(1)} %convert_multiply_fusion.3) | copy-start | bytes 4227076
  1343.1 3.8 copy-start.20
  1346.8 1.6 copy-start.10
  1350.4 9.0 copy-start.40
  1359.3 2.0 copy-start.22
  1359.3 2.1 copy-start.21
  1359.3 3.4 copy-start.24
  1361.4 26.3 %copy-start.6 = (f32[1,256,512]{2,1,0:T(8,128)}, f32[1,256,512]{2,1,0:T(8,128)S(1)}, u32[]{:S(2)}) copy-start(f32[1,256,512]{2,1,0:T(8,128)S(1)} %convert_multiply_fusion.5) | copy-start | bytes 1572868
  1374.9 4.0 copy-start.41
  1380.5 3.1 copy-start.12
  1390.5 24.1 %copy-start.28 = (f32[4,256]{1,0:T(4,128)S(1)}, f32[4,256]{1,0:T(4,128)}, u32[]{:S(2)}) copy-start(f32[4,256]{1,0:T(4,128)} %param.69) | copy-start | bytes 12292
  1390.5 24.1 %copy-start.33 = (f32[4,256]{1,0:T(4,128)S(1)}, f32[4,256]{1,0:T(4,128)}, u32[]{:S(2)}) copy-start(f32[4,256]{1,0:T(4,128)} %param.71) | copy-start | bytes 12292
  1390.5 24.1 %copy-start.34 = (f32[4,256]{1,0:T(4,128)S(1)}, f32[4,256]{1,0:T(4,128)}, u32[]{:S(2)}) copy-start(f32[4,256]{1,0:T(4,128)} %param.70) | copy-start | bytes 12292
  1390.5 26.6 %copy-start.5 = (f32[1,512,2,688]{1,3,2,0:T(8,128)S(1)}, f32[1,512,2,688]{1,3,2,0:T(8,128)}, u32[]{:S(2)}) copy-start(f32[1,512,2,688]{1,3,2,0:T(8,128)} %param.56) | copy-start | bytes 8454148
  1390.5 26.6 %copy-start.8 = (bf16[1,688,512]{2,1,0:T(8,128)(2,1)S(1)}, bf16[1,688,512]{2,1,0:T(8,128)(2,1)}, u32[]{:S(2)}) copy-start(bf16[1,688,512]{2,1,0:T(8,128)(2,1)} %reduce-scatter.21.cloned.1.call-done) | copy-start | bytes 2113540
Sparse Core Ops, SparseCore 0:
  10.5 31.5 all-gather.8
  44.5 51.0 all-gather.6
  98.0 99.4 all-gather.10
  203.9 42.0 all-gather.14
  248.2 154.2 all-gather.12
  701.7 151.4 reduce-scatter.16
  910.5 41.0 reduce-scatter.18
  954.9 41.2 reduce-scatter.20
  1000.1 41.4 reduce-scatter.22
  1124.7 28.0 reduce-scatter.26
  1156.4 61.4 reduce-scatter.24

commit v8 on v7

--- a/solution.py
+++ b/solution.py
@@ -401,12 +401,12 @@
 
     def rise(chunk, place):
         slot = lax.rem(chunk, ring)
-        part = from_low.at[slot, :, pl.ds((place + 1) * size, (places - 1 - place) * size)]
+        part = from_low.at[slot, pl.ds(place + 1, places - 1 - place)]
         return remote(part, part, ref["low_out_sem"].at[slot], ref["low_in_sem"].at[slot], upper)
 
     def fall(chunk, place):
         slot = lax.rem(chunk, ring)
-        part = from_high.at[slot, :, pl.ds(0, place * size)]
+        part = from_high.at[slot, pl.ds(0, place)]
         return remote(part, part, ref["high_out_sem"].at[slot], ref["high_in_sem"].at[slot], lower)
 
     def sums_copy(chunk, offset):
@@ -421,8 +421,8 @@
 
     def piece(chunk, source):
         if cross:
-            return ref["stage"].at[rows_of(chunk), shard(source)]
-        return full_ref.at[rows_of(chunk), shard(2 * source + core)]
+            return ref["stage"].at[source, rows_of(chunk)]
+        return ref["shards"].at[2 * source + core, rows_of(chunk)]
 
     def climb(chunk, source, hop):
         part = piece(chunk, source)
@@ -446,7 +446,7 @@
 
     def target(chunk, giver):
         if form == "lookup":
-            return full_ref.at[rows_of(chunk), shard(2 * giver + core)]
+            return ref["shards"].at[2 * giver + core, rows_of(chunk)]
         return full_ref.at[chunk // 2, band_of(lax.rem(chunk, 2) * slabs + giver), shard(core)]
 
     def mirror(chunk, index):
@@ -475,9 +475,9 @@
 
         @pl.when(source == mine_dp)
         def _():
-            values = ref["stage"][rows_of(chunk), shard(source)]
+            values = ref["stage"][source, rows_of(chunk), :]
             if form == "lookup":
-                full_ref[rows_of(chunk), shard(2 * mine_dp + core)] = values
+                ref["shards"][2 * mine_dp + core, rows_of(chunk), :] = values
             else:
                 place_rows = band_of(lax.rem(chunk, 2) * slabs + mine_dp)
                 full_ref[chunk // 2, place_rows, shard(core)] = values
@@ -562,9 +562,9 @@
                 if form != "table":
                     ref["own"][rows, :] = result
             if cross:
-                ref["stage"][rows, shard(spot)] = result.astype(jnp.bfloat16)
+                ref["stage"][spot, rows, :] = result.astype(jnp.bfloat16)
             else:
-                full_ref[rows, shard(me)] = result.astype(jnp.bfloat16)
+                ref["shards"][me, rows, :] = result.astype(jnp.bfloat16)
 
             @pl.when(spot < places - 1)
             def _():
@@ -593,12 +593,13 @@
                 @pl.when(jnp.logical_and(valid(up_chunk), spot == place))
                 def _():
                     slot = lax.rem(up_chunk, ring)
-                    above = pl.ds((place + 1) * size, (places - 1 - place) * size)
-                    values = partial[slot, :, above]
                     if place > 0:
                         rise(up_chunk, place - 1).wait_recv()
-                        values = values + from_low[slot, :, above].astype(jnp.float32)
-                    from_low[slot, :, above] = values.astype(jnp.bfloat16)
+                    for above in range(place + 1, places):
+                        values = partial[slot, :, pl.ds(above * size, size)]
+                        if place > 0:
+                            values = values + from_low[slot, above].astype(jnp.float32)
+                        from_low[slot, above] = values.astype(jnp.bfloat16)
                     rise(up_chunk, place).start()
 
             if place > 0:
@@ -607,12 +608,13 @@
                 @pl.when(jnp.logical_and(valid(down_chunk), spot == place))
                 def _():
                     slot = lax.rem(down_chunk, ring)
-                    below = pl.ds(0, place * size)
-                    values = partial[slot, :, below]
                     if place < places - 1:
                         fall(down_chunk, place + 1).wait_recv()
-                        values = values + from_high[slot, :, below].astype(jnp.float32)
-                    from_high[slot, :, below] = values.astype(jnp.bfloat16)
+                    for below in range(place):
+                        values = partial[slot, :, pl.ds(below * size, size)]
+                        if place < places - 1:
+                            values = values + from_high[slot, below].astype(jnp.float32)
+                        from_high[slot, below] = values.astype(jnp.bfloat16)
                     fall(down_chunk, place).start()
 
     def settle(step):
@@ -658,11 +660,11 @@
 
             @pl.when(spot > 0)
             def _():
-                total[...] += from_low[slot, :, mine].astype(jnp.float32)
+                total[...] += from_low[slot, spot].astype(jnp.float32)
 
             @pl.when(spot < places - 1)
             def _():
-                total[...] += from_high[slot, :, mine].astype(jnp.float32)
+                total[...] += from_high[slot, spot].astype(jnp.float32)
 
             if not summing:
                 return
@@ -765,7 +767,7 @@
             if form == "table":
                 arrived = full_ref.at[chunk // 2, pl.ds(0, slabs * band), pl.ds(0, size)]
             else:
-                arrived = full_ref.at[rows_of(chunk), pl.ds(0, places * size)]
+                arrived = ref["shards"].at[pl.ds(0, places), rows_of(chunk)]
             pltpu.make_async_copy(arrived, arrived, ref["twin_in_sem"].at[chunk]).wait()
             pltpu.make_async_copy(arrived, arrived, ref["twin_out_sem"].at[chunk]).wait()
             if cross:
@@ -784,6 +786,11 @@
                 def _():
                     sink(chunk, source_high, hop).wait_send()
 
+            if form != "table":
+                for index in range(parts):
+                    full_ref[rows_of(chunk), pl.ds(index * size, size)] = ref["shards"][
+                        index, rows_of(chunk), :
+                    ]
             if form == "lookup":
                 rows = rows_of(chunk)
                 ref["own"][rows, :] = full_ref[rows, shard(me)].astype(jnp.float32)
@@ -943,8 +950,10 @@
     for part, array in enumerate(lefts):
         scratch["left_buf%d" % part] = pltpu.VMEM((2, band, array.shape[1]), low)
         scratch["left_sem%d" % part] = dma((2,))
+    if form != "table":
+        scratch["shards"] = pltpu.VMEM((parts, tokens, size), low)
     if cross:
-        scratch["stage"] = pltpu.VMEM((tokens, span), low)
+        scratch["stage"] = pltpu.VMEM((places, tokens, size), low)
         scratch["cross_out_sem"] = dma((chunks, slabs))
         scratch["cross_in_sem"] = dma((chunks, slabs))
     if summing:
@@ -954,8 +963,10 @@
         scratch["sums_in_sem"] = dma((ring,))
     scratch["total"] = pltpu.VMEM((band, size), wide_kind)
     scratch["partial"] = pltpu.VMEM((ring, band, span), wide_kind)
-    for name in ("pair_out", "pair_in", "from_low", "from_high"):
+    for name in ("pair_out", "pair_in"):
         scratch[name] = pltpu.VMEM((ring, band, span), low)
+    for name in ("from_low", "from_high"):
+        scratch[name] = pltpu.VMEM((ring, places, band, size), low)
     for name in ("pair_out", "pair_in", "low_out", "low_in", "high_out", "high_in"):
         scratch[name + "_sem"] = dma((ring,))
     for name in ("up_out", "up_in", "down_out", "down_in"):
@@ -1199,7 +1210,6 @@
         size,
         ids=spread_ids,
         gain=gain_one[None],
-        lag=3,
     )
     embedded, full_one, scale_one = first["own"], first["full"], first["scale"]
     full_one, w_qkv, w_out, w_gate, w_up, w_down, table = later_weights(full_one)
@@ -1228,7 +1238,6 @@
         tokens,
         size,
         mixer=inner,
-        lag=3,
         inputs=embedded,
         gain=gains[1:2],
     )
@@ -1389,7 +1398,6 @@
         scale=scale_two,
         added=d_two,
         mixer=inner,
-        lag=3,
         project=w_out,
     )
     d_one, d_out_in, d_mixed = fifth["own"], fifth["full"], fifth["grad_mixed"]

time: 1440 us -> 1420 us (0.986)
  Pallas kernels: 1060 us -> 1040 us
    pallas_call x6, Pallas kernels: 973 us -> 951 us  [transit(): pl.pallas_call(functools.partial(transit_kernel, mode, form, lag, parts,...]
  transfers between devices with their start and end apart: 11 -> 11, of which waited for: 0 -> 1; matrix products, arithmetic and copies ran while one was open for 8% -> 8% of each run, Pallas kernels for 70% -> 69%
where the time goes in v8:
time: 1420 us; the launch traced here: 1410 us
  Pallas kernels  1040 us (73%)
  matrix products  172 us (12%)
  local copies, waits for them, and re-layouts  87.8 us (6%)
  other arithmetic  86.2 us (6%)
  between operations  23.4 us (2%)
    pallas_call x6, Pallas kernels, transit(): pl.pallas_call(functools.partial(transit_kernel, mode, form, lag, parts,...  951 us
    pallas_call x1, Pallas kernels, scores(): pl.pallas_call(scores_kernel, grid=(tokens // SCORE_ROWS,), in_specs=[pl....  47.9 us
    dot_general x12, matrix products, product(): jnp.einsum(form, one.astype(jnp.bfloat16), two.astype(jnp.bfloat16), pref...  45.5 us
    dot_general x1, matrix products, layer_backward(): jnp.einsum('tv,td->vd', d_logits, full_end, preferred_element_type=wide_k...  41.1 us
    pallas_call x4, Pallas kernels, share(): pl.pallas_call(functools.partial(share_kernel, axes), in_specs=[vmem], ou...  39.9 us
  transfers between devices with their start and end apart: 11, of which 1 were waited for; matrix products, arithmetic and copies ran while one was open for 8% of the time, Pallas kernels for 69%

profile of v8, /device:TPU:0, one launch (start us, length us, event | category | flops | bytes accessed | tf_op | source)
XLA Modules:
  0.0 1414.6 jit_solution(7763392818001182801)
XLA Ops:
  7.2 1.8 convert_element_type.258
  9.1 1.9 copy.143
  12.5 3.1 bitcast_convert_fusion
  16.8 16.6 %share.4 = f32[32,24,128]{2,1,0:T(8,128)S(1)} custom-call(f32[24,128]{1,0:T(8,128)S(1)} %select_maximum_fusion.1.block_ref), custom_call_target="tpu_custom_call" | custom-call | bytes 16777216 | tf_op jit(solution)/shard_map/share/pallas_call | solution.py:1048
  34.2 5.9 convert_element_type.253.all_refs_0_
  41.0 3.5 broadcast_in_dim.102.all_refs_1_
  44.6 146.0 %transit_lookup.1 = (f32[2048,256]{1,0:T(8,128)}, bf16[2048,2048]{1,0:T(8,128)(2,1)}, f32[32,8,64]{2,1,0:T(8,128)}) custom-call(bf16[4000,512]{1,0:T(8,128)(2,1)} %convert_element_type.253.all_refs_0_, s32[4,2048,128]{2,1,0:T(8,128)} %broadcast_in_dim.102.all_refs_1_, f32[1,2048]{1,0:T(1,128)} %bitcast.333), custom_call_target="tpu_custom_call" | custom-call | flops 8388608000 | bytes 536870912 | tf_op jit(solution)/shard_map/transit_lookup/pallas_call | solution.py:979
  190.7 3.1 all-gather.11.cloned.1.call-done
  196.5 2.4 fusion.49
  200.6 6.0 gather_fusion
  206.6 3.2 slice_bitcast_fusion.1
  209.9 1.9 copy.189
  211.8 1.9 copy.190
  213.7 2.6 gather_fusion.3
  216.3 11.3 convolution_convert_fusion.1.all_refs_1_.all_refs_5_
  231.0 160.7 %transit_mixer.1 = (f32[2048,256]{1,0:T(8,128)}, bf16[2048,2048]{1,0:T(8,128)(2,1)}, f32[32,8,64]{2,1,0:T(8,128)}, bf16[2048,256]{1,0:T(8,128)(2,1)}, f32[2048,256]{1,0:T(8,128)}, /*index=5*/f32[32,2,128,128]{3,2,1,0:T(8,128)}) custom-call(bf16[256,2048]{1,0:T(8,128)(2,1)} %bitcast.306, bf16[2048,768]{1,0:T(8,128)(2,1)} %convolution_convert_fusion.1.all_refs_1_.all_refs_5_, ...), custom_call_target="tpu_custom_call" | custom-call | flops 2147483648 | bytes 536870912 | tf_op jit(solution)/shard_map/transit_mixer/pallas_call | solution.py:979
  391.7 9.3 fusion.116
  401.0 2.7 copy-done.44
  403.7 10.2 multiply_convert_fusion.2
  413.9 2.5 gather_fusion.1
  416.4 2.0 copy.191
  418.4 144.8 %transit_rows.2 = (f32[2048,256]{1,0:T(8,128)}, bf16[2048,2048]{1,0:T(8,128)(2,1)}, f32[32,8,64]{2,1,0:T(8,128)}) custom-call(bf16[688,2048]{1,0:T(8,128)(2,1)} %bitcast.320, bf16[2048,688]{1,0:T(8,128)(2,1)} %get-tuple-element.304.all_refs_1_, f32[2048,256]{1,0:T(8,128)} %get-tuple-element.107.all_refs_2_.all_refs_17_, f32[1,256]{1,0:T(1,128)} %get-tuple-element.291.all_refs_3_), custom_call_target="tpu_custom_call" | custom-call | flops 5771362304 | bytes 536870912 | tf_op jit(solution)/shard_map/transit_rows/pallas_call | solution.py:979
  564.5 47.9 %scores.1 = (f32[2048,4000]{1,0:T(8,128)}, f32[3,2048,128]{2,1,0:T(8,128)}) custom-call(bf16[2048,2048]{1,0:T(8,128)(2,1)} %get-tuple-element.108.rows_ref, bf16[4000,2048]{1,0:T(8,128)(2,1)} %all-gather.13.cloned.1.call-done.table_ref.all_refs_0_, s32[2048,128]{1,0:T(8,128)} %broadcast_in_dim.111.goal_ref), custom_call_target="tpu_custom_call" | custom-call | flops 33554432000 | bytes 49152000 | tf_op jit(solution)/shard_map/scores/pallas_call | solution.py:1090
  612.4 2.8 slice_reduce_fusion
  615.2 6.1 share.5
  622.3 16.8 %multiply_convert_fusion.all_refs_1_ = bf16[2048,4000]{1,0:T(8,128)(2,1)S(1)} fusion(f32[2048,4000]{1,0:T(8,128)} %get-tuple-element.109, f32[2048]{0:T(1024)S(1)} %convert_element_type.270, s32[2048]{0:T(1024)S(1)} %broadcast_subtract_fusion, f32[2048]{0:T(1024)S(1)} %get-tuple-element.270), kind=kLoop, calls=%fused_computation.9 | loop fusion | flops 49152000 | bytes 49176576 | tf_op jit(solution)/shard_map/convert_element_type | solution.py:1284
  639.0 5.7 copy-done.2
  644.8 41.1 %convolution_convert_fusion = bf16[4000,2048]{1,0:T(8,128)(2,1)} fusion(bf16[2048,4000]{1,0:T(8,128)(2,1)S(1)} %multiply_convert_fusion.all_refs_1_, bf16[2048,2048]{1,0:T(8,128)(2,1)} %get-tuple-element.108.rows_ref), kind=kOutput, calls=%fused_computation.11 | convolution fusion | flops 33562624000 | bytes 41156608 | tf_op jit(solution)/shard_map/tv,td->vd/dot_general | solution.py:1350
  689.2 152.3 %transit_rows.3 = (f32[2048,256]{1,0:T(8,128)}, bf16[2048,2048]{1,0:T(8,128)(2,1)}, f32[8,256]{1,0:T(8,128)}) custom-call(bf16[4000,2048]{1,0:T(8,128)(2,1)} %all-gather.13.cloned.1.call-done.table_ref.all_refs_0_, bf16[2048,4000]{1,0:T(8,128)(2,1)} %copy-done.2, f32[2048,256]{1,0:T(8,128)} %get-tuple-element.112.all_refs_2_, ...), custom_call_target="tpu_custom_call" | custom-call | flops 33554432000 | bytes 536870912 | tf_op jit(solution)/shard_map/transit_rows/pallas_call | solution.py:979
  841.6 10.7 convolution_convert_fusion.5
  852.3 15.3 %multiply_convert_fusion.1 = (bf16[2048,688]{1,0:T(8,128)(2,1)S(1)}, bf16[2048,688]{1,0:T(8,128)(2,1)}) fusion(f32[2048,688]{1,0:T(8,128)} %copy-done.44, f32[2048,688]{1,0:T(8,128)} %get-tuple-element.305, bf16[2048,2048]{1,0:T(8,128)(2,1)} %get-tuple-element.115, bf16[688,2048]{1,0:T(8,128)(2,1)S(1)} %bitcast.321), kind=kOutput, calls=%fused_computation.25 | convolution fusion | flops 5791088640 | bytes 28114944 | tf_op jit(solution)/shard_map/td,fd->tf/dot_general | solution.py:1371
  867.6 6.4 convolution_convert_fusion.3
  875.9 6.3 convolution_convert_fusion.4
  882.3 1.8 copy.214
  884.1 2.3 gather_fusion.6
  886.3 4.2 gather_fusion.5
  890.5 2.0 copy.215
  892.5 2.3 gather_fusion.4
  896.4 190.0 %transit_inner.1 = (f32[2048,256]{1,0:T(8,128)}, bf16[2048,2048]{1,0:T(8,128)(2,1)}, f32[8,256]{1,0:T(8,128)}, bf16[2048,768]{1,0:T(8,128)(2,1)}, f32[2,128,128]{2,1,0:T(8,128)}, /*index=5*/f32[1,256]{1,0:T(1,128)}) custom-call(bf16[688,2048]{1,0:T(8,128)(2,1)} %bitcast.315, bf16[688,2048]{1,0:T(8,128)(2,1)} %bitcast.317, ...), custom_call_target="tpu_custom_call" | custom-call | flops 11542724608 | bytes 536870912 | tf_op jit(solution)/shard_map/transit_inner/pallas_call | solution.py:979
  1086.4 5.7 convolution_convert_fusion.7
  1093.8 10.2 convolution_convert_fusion.2
  1104.1 2.4 gather_fusion.8
  1110.5 3.9 bitcast_multiply_fusion
  1115.7 2.1 scatter.9
  1119.5 157.0 %transit_table.1 = (f32[8,256]{1,0:T(8,128)}, f32[4000,512]{1,0:T(8,128)}) custom-call(bf16[2048,768]{1,0:T(8,128)(2,1)} %bitcast.312, bf16[2048,768]{1,0:T(8,128)(2,1)} %get-tuple-element.131.all_refs_1_, s32[16,8,512]{2,1,0:T(8,128)} %broadcast_in_dim.119.all_refs_2_, f32[2048,256]{1,0:T(8,128)} %get-tuple-element.105.all_refs_9_.all_refs_3_, ...), custom_call_target="tpu_custom_call" | custom-call | flops 6442450944 | bytes 536870912 | tf_op jit(solution)/shard_map/transit_table/pallas_call | solution.py:979
  1277.2 8.0 share.6
  1290.3 1.9 pad_maximum_fusion.3
  1293.2 7.2 multiply_reduce_fusion
  1300.4 1.7 fusion.60
  1307.8 9.2 share.7
  1323.3 3.8 fusion.23
  1328.7 2.0 convert_multiply_fusion
  1330.7 9.0 fusion.1
  1339.6 2.0 fusion.32
  1344.0 5.2 multiply_subtract_fusion.1
  1349.2 3.0 copy.173
  1352.2 3.0 copy.175
  1355.2 4.0 fusion.22
  1360.8 3.1 copy.174
  1363.9 4.0 fusion.27
  1368.0 2.9 fusion.39
  1370.8 24.1 %multiply_subtract_fusion = (f32[4000,512]{1,0:T(8,128)}, f32[4000,512]{1,0:T(8,128)}, f32[4000,512]{1,0:T(8,128)}) fusion(f32[4000,512]{1,0:T(8,128)} %param.43, f32[]{:T(128)S(6)} %div.96, f32[4000,512]{1,0:T(8,128)} %get-tuple-element.144, bf16[4000,512]{1,0:T(8,128)(2,1)} %reduce-scatter.17.cloned.1.call-done, f32[4000,512]{1,0:T(8,128)} %param.45, ...), kind=kLoop, calls=%fused_computation.18 | loop fusion | flops 36864000 | bytes 61440004 | tf_op jit(solution)/shard_map/sub | solution.py:1181
  1395.6 1.9 multiply_subtract_fusion.2
  1397.5 9.3 fusion.19
  (225 shorter events, 47.4 us)
Async XLA Ops:
  7.2 183.4 %all-gather.9.cloned.1.call-start = ((), (), s32[]{:S(2)}) async-start(), calls=%async_computation.7 | async-start | bytes 1310720 | tf_op jit(solution)/shard_map/all_gather | solution.py:1502
  9.1 181.6 %all-gather.7.cloned.1.call-start = ((), (), s32[]{:S(2)}) async-start(), calls=%async_computation.6 | async-start | bytes 3932160 | tf_op jit(solution)/shard_map/all_gather | solution.py:1501
  11.0 4.5 copy-start.3
  12.4 3.2 copy-start.27
  12.4 3.8 copy-start.29
  12.4 181.3 %all-gather.11.cloned.1.call-start = ((), (), s32[]{:S(2)}) async-start(), calls=%async_computation.8 | async-start | bytes 7045120 | tf_op jit(solution)/shard_map/all_gather | solution.py:1503
  15.6 398.3 %all-gather.15.cloned.1.call-start = ((), (), s32[]{:S(2)}) async-start(), calls=%async_computation.11 | async-start | bytes 3522560 | tf_op jit(solution)/shard_map/all_gather | solution.py:1514
  16.2 0.6 copy-start.36
  33.4 6.7 copy-start
  34.2 5.9 copy-start.11
  190.6 4.1 copy-start.38
  190.6 4.9 copy-start.26
  190.6 5.0 copy-start.31
  190.6 5.0 copy-start.23
  190.6 5.8 copy-start.30
  193.8 369.4 %all-gather.13.cloned.1.call-start = ((), (), s32[]{:S(2)}) async-start(), calls=%async_computation.9 | async-start | bytes 20480000 | tf_op jit(solution)/shard_map/all_gather | solution.py:1515
  194.4 4.6 copy-start.19
  194.4 647.2 %reduce-scatter.17.cloned.1.call-start = ((), (), s32[]{:S(2)}) async-start(), calls=%async_computation.10 | async-start | bytes 20480000 | tf_op jit(solution)/shard_map/reduce_scatter | solution.py:1319
  216.3 11.3 copy-start.13
  231.0 160.7 %copy-start.14 = (bf16[4,86,8,512]{3,2,0,1:T(8,128)(2,1)S(1)}, bf16[4,86,8,512]{3,2,0,1:T(8,128)(2,1)}, u32[]{:S(2)}) copy-start(bf16[4,86,8,512]{3,2,0,1:T(8,128)(2,1)} %copy.189) | copy-start | bytes 8454148
  391.7 12.0 copy-start.15
  391.7 12.0 copy-start.39
  401.0 2.7 copy-start.44
  639.0 5.7 copy-start.2
  685.9 0.7 copy-start.32
  685.9 407.9 %reduce-scatter.19.cloned.1.call-start = ((), (), s32[]{:S(2)}) async-start(), calls=%async_computation.12 | async-start | bytes 3522560
  841.6 10.7 copy-start.16
  841.6 26.0 %slice-start = ((s8[8388608]{0:T(1024)(128)(4,1)}), s8[4194304]{0:T(1024)(128)(4,1)S(1)}, s32[]{:S(2)}) async-start(s8[8388608]{0:T(1024)(128)(4,1)} %bitcast.335), calls=%async_computation.17 | async-start | bytes 8388608
  852.3 15.3 %slice-start.1 = ((s8[8388608]{0:T(1024)(128)(4,1)}), s8[4194304]{0:T(1024)(128)(4,1)S(1)}, s32[]{:S(2)}) async-start(s8[8388608]{0:T(1024)(128)(4,1)} %bitcast.335), calls=%async_computation.18 | async-start | bytes 8388608
  867.6 6.4 copy-start.42
  874.0 1.9 copy-start.43
  894.9 199.0 %reduce-scatter.21.cloned.1.call-start = ((), (), s32[]{:S(2)}) async-start(), calls=%async_computation.13 | async-start | bytes 3522560
  895.6 198.2 %reduce-scatter.23.cloned.1.call-start = ((), (), s32[]{:S(2)}) async-start(), calls=%async_computation.14 | async-start | bytes 3522560
  896.3 404.1 %reduce-scatter.27.cloned.1.call-start = ((), (), s32[]{:S(2)}) async-start(), calls=%async_computation.16 | async-start | bytes 1310720
  896.4 190.0 %copy-start.18 = (bf16[2048,256]{1,0:T(8,128)(2,1)S(1)}, bf16[2048,256]{1,0:T(8,128)(2,1)}, u32[]{:S(2)}) copy-start(bf16[2048,256]{1,0:T(8,128)(2,1)} %get-tuple-element.129) | copy-start | bytes 3145732
  1106.5 1.8 copy-start.4
  1106.5 195.6 %reduce-scatter.25.cloned.1.call-start = ((), (), s32[]{:S(2)}) async-start(), calls=%async_computation.15 | async-start | bytes 3932160
  1109.9 7.9 copy-start.25
  1110.5 8.3 copy-start.35
  1110.5 8.3 copy-start.37
  1119.5 169.5 %copy-start.7 = (bf16[1,688,512]{2,1,0:T(8,128)(2,1)S(1)}, bf16[1,688,512]{2,1,0:T(8,128)(2,1)}, u32[]{:S(2)}) copy-start(bf16[1,688,512]{2,1,0:T(8,128)(2,1)} %reduce-scatter.21.cloned.1.call-done) | copy-start | bytes 2113540
  1119.5 169.5 %copy-start.9 = (bf16[1,688,512]{2,1,0:T(8,128)(2,1)S(1)}, bf16[1,688,512]{2,1,0:T(8,128)(2,1)}, u32[]{:S(2)}) copy-start(bf16[1,688,512]{2,1,0:T(8,128)(2,1)} %reduce-scatter.23.cloned.1.call-done) | copy-start | bytes 2113540
  1119.5 172.8 %copy-start.17 = (bf16[1,688,512]{2,1,0:T(8,128)(2,1)S(1)}, bf16[1,688,512]{2,1,0:T(8,128)(2,1)}, u32[]{:S(2)}) copy-start(bf16[1,688,512]{2,1,0:T(8,128)(2,1)} %reduce-scatter.19.cloned.1.call-done) | copy-start | bytes 2113540
  1320.4 43.5 %copy-start.1 = (f32[1,688,512]{2,1,0:T(8,128)}, f32[1,688,512]{2,1,0:T(8,128)S(1)}, u32[]{:S(2)}) copy-start(f32[1,688,512]{2,1,0:T(8,128)S(1)} %convert_multiply_fusion.3) | copy-start | bytes 4227076
  1323.3 3.8 copy-start.20
  1327.1 1.6 copy-start.10
  1330.6 9.0 copy-start.40
  1339.6 2.0 copy-start.22
  1339.6 2.1 copy-start.21
  1339.6 3.4 copy-start.24
  1341.7 26.2 %copy-start.6 = (f32[1,256,512]{2,1,0:T(8,128)}, f32[1,256,512]{2,1,0:T(8,128)S(1)}, u32[]{:S(2)}) copy-start(f32[1,256,512]{2,1,0:T(8,128)S(1)} %convert_multiply_fusion.5) | copy-start | bytes 1572868
  1355.2 4.0 copy-start.41
  1360.8 3.1 copy-start.12
  1370.8 24.1 %copy-start.28 = (f32[4,256]{1,0:T(4,128)S(1)}, f32[4,256]{1,0:T(4,128)}, u32[]{:S(2)}) copy-start(f32[4,256]{1,0:T(4,128)} %param.69) | copy-start | bytes 12292
  1370.8 24.1 %copy-start.33 = (f32[4,256]{1,0:T(4,128)S(1)}, f32[4,256]{1,0:T(4,128)}, u32[]{:S(2)}) copy-start(f32[4,256]{1,0:T(4,128)} %param.71) | copy-start | bytes 12292
  1370.8 24.1 %copy-start.34 = (f32[4,256]{1,0:T(4,128)S(1)}, f32[4,256]{1,0:T(4,128)}, u32[]{:S(2)}) copy-start(f32[4,256]{1,0:T(4,128)} %param.70) | copy-start | bytes 12292
  1370.8 26.6 %copy-start.5 = (f32[1,512,2,688]{1,3,2,0:T(8,128)S(1)}, f32[1,512,2,688]{1,3,2,0:T(8,128)}, u32[]{:S(2)}) copy-start(f32[1,512,2,688]{1,3,2,0:T(8,128)} %param.56) | copy-start | bytes 8454148
  1370.8 26.6 %copy-start.8 = (bf16[1,688,512]{2,1,0:T(8,128)(2,1)S(1)}, bf16[1,688,512]{2,1,0:T(8,128)(2,1)}, u32[]{:S(2)}) copy-start(bf16[1,688,512]{2,1,0:T(8,128)(2,1)} %reduce-scatter.21.cloned.1.call-done) | copy-start | bytes 2113540
Sparse Core Ops, SparseCore 0:
  10.5 31.5 all-gather.8
  44.5 58.5 all-gather.6
  105.5 88.2 all-gather.10
  196.0 44.0 all-gather.14
  242.3 154.1 all-gather.12
  686.0 150.6 reduce-scatter.16
  895.0 40.1 reduce-scatter.18
  938.5 41.2 reduce-scatter.20
  983.7 41.2 reduce-scatter.22
  1106.6 26.1 reduce-scatter.26
  1136.4 62.0 reduce-scatter.24
